TPU v7x, 128 devices: a whole 4x4x4 slice. The times are simulated.
128 devices in a mesh: pipe: 8 (over y, z_hi), dp: 16 (over x, z_lo, core).
Axes of the slice: x: 4, y: 4, z: 4 (z_hi: 2, z_lo: 2; z = z_hi * 2 + z_lo), core: 2. Of those that a mesh axis runs over, the one named last changes fastest.
Arguments:
- inputs_x: bfloat16 [4096, 5120], P('dp'), may hold values from -6 to 6
- cotangent: bfloat16 [4096, 5120], P('dp'), may hold values from -6 to 6
- master_in: float32 [8, 5120, 512], P('pipe', 'dp'), may hold values from -0.078125 to 0.078125
- master_out: float32 [8, 512, 5120], P('pipe', 'dp'), may hold values from -0.25 to 0.25
- moment_in: float32 [8, 5120, 512], P('pipe', 'dp'), may hold values from -60 to 60
- moment_out: float32 [8, 512, 5120], P('pipe', 'dp'), may hold values from -60 to 60
- second_in: float32 [8, 5120, 512], P('pipe', 'dp'), may hold values from 1 to 16
- second_out: float32 [8, 512, 5120], P('pipe', 'dp'), may hold values from 1 to 16
Outputs:
- input_grads: bfloat16 [8, 4096, 5120], P('pipe', 'dp')
- new_master_in: float32 [8, 5120, 512], P('pipe', 'dp')
- new_moment_in: float32 [8, 5120, 512], P('pipe', 'dp')
- new_second_in: float32 [8, 5120, 512], P('pipe', 'dp')
- new_master_out: float32 [8, 512, 5120], P('pipe', 'dp')
- new_moment_out: float32 [8, 512, 5120], P('pipe', 'dp')
- new_second_out: float32 [8, 512, 5120], P('pipe', 'dp')
- rollout_in: bfloat16 [8, 512, 5120], P('pipe', 'dp')
- rollout_out: bfloat16 [8, 5120, 512], P('pipe', 'dp')
All inputs are finite; a program needn't handle non-finite values.
Results may differ from a plain program's by a relative error of at most 0.035.
Values may be sent and summed in bfloat16 or wider, within the bound.
No kernel may reach another device: no remote copies, remote signals or barrier semaphores. Data moves between devices by JAX's collectives and lax.ppermute only.
A program may use at most 128 MiB of HBM per device.

v0:
```python
import jax
import jax.numpy as jnp
from jax import lax
from jax.sharding import PartitionSpec as P

MICRO = 4


norm_eps = 1e-06
beta_one = 0.9
beta_two = 0.999
learn_rate = 0.02
decay_rate = 0.1
adam_eps = 1e-08
adam_step = 100


def passed_along(x, axis, by):
    length = lax.axis_size(axis)
    pairs = [(i, i + by) for i in range(length) if 0 <= i + by < length]
    return lax.ppermute(x, axis, pairs)


def normalize(values):
    return values * lax.rsqrt(jnp.mean(values * values, axis=-1, keepdims=True) + norm_eps)


def contract_rows(left, right):
    return lax.dot_general(
        left, right, (((0,), (0,)), ((), ())), preferred_element_type=jnp.float32
    )


def contract_last(left, right):
    return lax.dot_general(
        left, right, (((1,), (1,)), ((), ())), preferred_element_type=jnp.float32
    )


def section_forward(rows_in, weight_in, weight_out):
    widened = rows_in.astype(jnp.float32)
    normed = normalize(widened).astype(jnp.bfloat16)
    hidden = jnp.dot(normed, weight_in, preferred_element_type=jnp.float32)
    activated = jax.nn.silu(hidden).astype(jnp.bfloat16)
    return (widened + jnp.dot(activated, weight_out, preferred_element_type=jnp.float32)).astype(
        jnp.bfloat16
    )


def section_backward(rows_in, upstream, weight_in, weight_out):
    widened = rows_in.astype(jnp.float32)
    scale_inv = lax.rsqrt(jnp.mean(widened * widened, axis=-1, keepdims=True) + norm_eps)
    normed_full = widened * scale_inv
    normed = normed_full.astype(jnp.bfloat16)
    hidden = jnp.dot(normed, weight_in, preferred_element_type=jnp.float32)
    activated = jax.nn.silu(hidden).astype(jnp.bfloat16)
    grad_act = contract_last(upstream, weight_out)
    sigmoid_h = jax.nn.sigmoid(hidden)
    grad_hidden = (grad_act * sigmoid_h * (1.0 + hidden * (1.0 - sigmoid_h))).astype(jnp.bfloat16)
    grad_normed = contract_last(grad_hidden, weight_in)
    inner = jnp.mean(grad_normed * normed_full, axis=-1, keepdims=True)
    grad_rows = upstream.astype(jnp.float32) + scale_inv * (grad_normed - normed_full * inner)
    return (grad_rows.astype(jnp.bfloat16), normed, grad_hidden, activated)


def adam_update(master, moment, second, grad):
    moment_new = beta_one * moment + (1.0 - beta_one) * grad
    second_new = beta_two * second + (1.0 - beta_two) * grad * grad
    moment_hat = moment_new / (1.0 - beta_one**adam_step)
    second_hat = second_new / (1.0 - beta_two**adam_step)
    master_new = master - learn_rate * (
        moment_hat / (jnp.sqrt(second_hat) + adam_eps) + decay_rate * master
    )
    return (master_new, moment_new, second_new)


def store_block(buffer, rows_new, active_now, slot_index):
    previous = lax.dynamic_index_in_dim(buffer, slot_index, 0, keepdims=False)
    return lax.dynamic_update_index_in_dim(
        buffer, jnp.where(active_now, rows_new, previous), slot_index, 0
    )


def send_back(grad_rows):
    return passed_along(grad_rows, "pipe", -1)


def on_device(
    inputs_x, cotangent, master_in, master_out, moment_in, moment_out, second_in, second_out
):
    section_count = lax.axis_size("pipe")
    section_index = lax.axis_index("pipe")
    group_count = lax.axis_size("dp")
    group_index = lax.axis_index("dp")
    tok_rows, model_width = inputs_x.shape
    block_rows = tok_rows // MICRO
    weight_in, weight_out = (
        lax.all_gather(master_in[0].astype(jnp.bfloat16), "dp", axis=0, tiled=True),
        lax.all_gather(master_out[0].astype(jnp.bfloat16), "dp", axis=0, tiled=True),
    )
    inner_width = weight_in.shape[1]
    own_blocks = inputs_x.reshape(MICRO, block_rows, model_width)
    seed_blocks = cotangent.reshape(MICRO, block_rows, model_width)
    tick_total = MICRO + section_count - 1
    is_last = section_index == section_count - 1

    def forward_tick(tick_index, carry):
        arrived, saved = carry
        position = tick_index - section_index
        active_now = (position >= 0) & (position < MICRO)
        slot_index = jnp.clip(position, 0, MICRO - 1)
        own_rows = lax.dynamic_index_in_dim(own_blocks, slot_index, 0, keepdims=False)
        current = jnp.where(section_index == 0, own_rows, arrived)
        saved = store_block(saved, current, active_now, slot_index)
        produced = lax.cond(
            active_now & jnp.logical_not(is_last),
            lambda rows_now: section_forward(rows_now, weight_in, weight_out),
            jnp.zeros_like,
            current,
        )
        arrived = passed_along(produced, "pipe", 1)
        return (arrived, saved)

    empty_rows = jnp.zeros((block_rows, model_width), jnp.bfloat16)
    empty_blocks = jnp.zeros((MICRO, block_rows, model_width), jnp.bfloat16)
    arrived_end, saved = lax.fori_loop(0, tick_total, forward_tick, (empty_rows, empty_blocks))

    def backward_place(tick_index, arrived):
        position = tick_index - (section_count - 1 - section_index)
        active_now = (position >= 0) & (position < MICRO)
        slot_index = jnp.clip(position, 0, MICRO - 1)
        seed_rows = lax.dynamic_index_in_dim(seed_blocks, slot_index, 0, keepdims=False)
        upstream = jnp.where(is_last, seed_rows, arrived)
        rows_in = lax.dynamic_index_in_dim(saved, slot_index, 0, keepdims=False)
        return (active_now, slot_index, upstream, rows_in)

    def backward_tick(tick_index, carry):
        arrived, grad_blocks, sum_in, sum_out = carry
        active_now, slot_index, upstream, rows_in = backward_place(tick_index, arrived)

        def run_step(operands):
            rows_now, upstream_now, total_in, total_out = operands
            grad_rows, normed, grad_hidden, activated = section_backward(
                rows_now, upstream_now, weight_in, weight_out
            )
            return (
                grad_rows,
                total_in + contract_rows(normed, grad_hidden),
                total_out + contract_rows(activated, upstream_now),
            )

        def skip_step(operands):
            rows_now, upstream_now, total_in, total_out = operands
            return (jnp.zeros_like(upstream_now), total_in, total_out)

        grad_rows, sum_in, sum_out = lax.cond(
            active_now, run_step, skip_step, (rows_in, upstream, sum_in, sum_out)
        )
        grad_blocks = store_block(grad_blocks, grad_rows, active_now, slot_index)
        arrived = send_back(grad_rows)
        return (arrived, grad_blocks, sum_in, sum_out)

    zero_in = jnp.zeros((model_width, inner_width), jnp.float32)
    zero_out = jnp.zeros((inner_width, model_width), jnp.float32)
    arrived_end, grad_blocks, sum_in, sum_out = lax.fori_loop(
        0, tick_total, backward_tick, (empty_rows, empty_blocks, zero_in, zero_out)
    )
    grad_in, grad_out = (
        lax.psum_scatter(sum_in.astype(jnp.bfloat16), "dp", scatter_dimension=0, tiled=True).astype(
            jnp.float32
        ),
        lax.psum_scatter(
            sum_out.astype(jnp.bfloat16), "dp", scatter_dimension=0, tiled=True
        ).astype(jnp.float32),
    )
    new_in, new_moment_in, new_second_in = adam_update(
        master_in[0], moment_in[0], second_in[0], grad_in
    )
    new_out, new_moment_out, new_second_out = adam_update(
        master_out[0], moment_out[0], second_out[0], grad_out
    )
    cast_in = new_in.astype(jnp.bfloat16)
    cast_out = new_out.astype(jnp.bfloat16)
    full_in, full_out = (
        lax.all_gather(cast_in, "dp", axis=0, tiled=True),
        lax.all_gather(cast_out, "dp", axis=0, tiled=True),
    )
    inner_share = inner_width // group_count
    model_share = model_width // group_count
    roll_in = lax.dynamic_slice_in_dim(full_in, group_index * inner_share, inner_share, 1).T
    roll_out = lax.dynamic_slice_in_dim(full_out, group_index * model_share, model_share, 1).T
    return (
        grad_blocks.reshape(1, tok_rows, model_width),
        new_in[None],
        new_moment_in[None],
        new_second_in[None],
        new_out[None],
        new_moment_out[None],
        new_second_out[None],
        roll_in[None],
        roll_out[None],
    )


def solution(mesh):
    in_specs = (
        P("dp", None),
        P("dp", None),
        P("pipe", "dp", None),
        P("pipe", "dp", None),
        P("pipe", "dp", None),
        P("pipe", "dp", None),
        P("pipe", "dp", None),
        P("pipe", "dp", None),
    )
    out_specs = (
        P("pipe", "dp", None),
        P("pipe", "dp", None),
        P("pipe", "dp", None),
        P("pipe", "dp", None),
        P("pipe", "dp", None),
        P("pipe", "dp", None),
        P("pipe", "dp", None),
        P("pipe", "dp", None),
        P("pipe", "dp", None),
    )
    return jax.shard_map(
        on_device, mesh=mesh, in_specs=in_specs, out_specs=out_specs, check_vma=False
    )
```

profile of v0, /device:TPU:1, one launch (start us, length us, event | category | flops | bytes accessed | tf_op | source)
XLA Modules:
  0.0 1035.4 jit_solution(17598767228485181046)
XLA Ops:
  11.1 42.3 %all-gather.5.cloned.1.call-done = bf16[5120,512]{1,0:T(8,128)(2,1)} async-done(((bf16[320,512]{1,0:T(8,128)(2,1)}), bf16[5120,512]{1,0:T(8,128)(2,1)}) %all-gather.5.cloned.1.call-update) | async-done | bytes 5242896 | tf_op jit(solution)/shard_map/all_gather | solution.py:98
  53.4 41.8 %all-gather.7.cloned.1.call-done = bf16[512,5120]{1,0:T(8,128)(2,1)} async-done(((bf16[32,5120]{1,0:T(8,128)(2,1)}), bf16[512,5120]{1,0:T(8,128)(2,1)}) %all-gather.7.cloned.1.call-update) | async-done | bytes 5242896 | tf_op jit(solution)/shard_map/all_gather | solution.py:99
  96.4 257.0 %while.38 = (s32[]{:T(128)}, bf16[64,5120]{1,0:T(8,128)(2,1)}, bf16[4,64,5120]{2,1,0:T(8,128)(2,1)S(1)}, s32[]{:T(128)}, pred[]{:T(512)}, /*index=5*/pred[]{:T(5...) while((s32[]{:T(128)}, bf16[64,5120]{1,0:T(8,128)(2,1)}, ...), condition=%wide.region_4.5_spmd, body=%wide.region_0.4_spmd.sunk | while | flops 674857024 | bytes 22283564 | solution.py:126
  97.8 7.3 conditional.4
  106.4 14.4 %collective-permute-done = bf16[64,5120]{1,0:T(8,128)(2,1)S(1)} collective-permute-done((bf16[64,5120]{1,0:T(8,128)(2,1)}, bf16[64,5120]{1,0:T(8,128)(2,1)S(1)}, u32[]{:S(2)}, u32[]{:S(2)}) %collective-permute-start) | collective-permute-done | bytes 655392 | tf_op jit(solution)/shard_map/while/body/eval_jaxpr/ppermute | solution.py:21
  123.2 7.2 conditional.4
  136.1 13.5 %collective-permute-done = bf16[64,5120]{1,0:T(8,128)(2,1)S(1)} collective-permute-done((bf16[64,5120]{1,0:T(8,128)(2,1)}, bf16[64,5120]{1,0:T(8,128)(2,1)S(1)}, u32[]{:S(2)}, u32[]{:S(2)}) %collective-permute-start) | collective-permute-done | bytes 655392 | tf_op jit(solution)/shard_map/while/body/eval_jaxpr/ppermute | solution.py:21
  152.0 7.3 conditional.4
  165.0 12.6 %collective-permute-done = bf16[64,5120]{1,0:T(8,128)(2,1)S(1)} collective-permute-done((bf16[64,5120]{1,0:T(8,128)(2,1)}, bf16[64,5120]{1,0:T(8,128)(2,1)S(1)}, u32[]{:S(2)}, u32[]{:S(2)}) %collective-permute-start) | collective-permute-done | bytes 655392 | tf_op jit(solution)/shard_map/while/body/eval_jaxpr/ppermute | solution.py:21
  179.9 7.2 conditional.4
  192.9 11.7 %collective-permute-done = bf16[64,5120]{1,0:T(8,128)(2,1)S(1)} collective-permute-done((bf16[64,5120]{1,0:T(8,128)(2,1)}, bf16[64,5120]{1,0:T(8,128)(2,1)S(1)}, u32[]{:S(2)}, u32[]{:S(2)}) %collective-permute-start) | collective-permute-done | bytes 655392 | tf_op jit(solution)/shard_map/while/body/eval_jaxpr/ppermute | solution.py:21
  207.8 12.1 %collective-permute-start = (bf16[64,5120]{1,0:T(8,128)(2,1)}, bf16[64,5120]{1,0:T(8,128)(2,1)S(1)}, u32[]{:S(2)}, u32[]{:S(2)}) collective-permute-start(bf16[64,5120]{1,0:T(8,128)(2,1)} %get-tuple-element.880), channel_id=1, source_target_pairs={{0,16},{16,32},{32,48},{48,64},{64,80},{80,96},{96,112},{1,17},{17... | collective-permute-start | bytes 1966088 | tf_op jit(solution)/shard_map/while/body/eval_jaxpr/ppermute | solution.py:21
  219.9 10.7 %collective-permute-done = bf16[64,5120]{1,0:T(8,128)(2,1)S(1)} collective-permute-done((bf16[64,5120]{1,0:T(8,128)(2,1)}, bf16[64,5120]{1,0:T(8,128)(2,1)S(1)}, u32[]{:S(2)}, u32[]{:S(2)}) %collective-permute-start) | collective-permute-done | bytes 655392 | tf_op jit(solution)/shard_map/while/body/eval_jaxpr/ppermute | solution.py:21
  239.9 10.1 collective-permute-done
  253.3 13.0 %collective-permute-start = (bf16[64,5120]{1,0:T(8,128)(2,1)}, bf16[64,5120]{1,0:T(8,128)(2,1)S(1)}, u32[]{:S(2)}, u32[]{:S(2)}) collective-permute-start(bf16[64,5120]{1,0:T(8,128)(2,1)} %get-tuple-element.880), channel_id=1, source_target_pairs={{0,16},{16,32},{32,48},{48,64},{64,80},{80,96},{96,112},{1,17},{17... | collective-permute-start | bytes 1966088 | tf_op jit(solution)/shard_map/while/body/eval_jaxpr/ppermute | solution.py:21
  266.3 9.2 collective-permute-done
  285.3 8.3 collective-permute-done
  296.8 8.4 collective-permute-start
  305.3 7.8 collective-permute-done
  322.9 7.8 collective-permute-done
  333.9 10.8 %collective-permute-start = (bf16[64,5120]{1,0:T(8,128)(2,1)}, bf16[64,5120]{1,0:T(8,128)(2,1)S(1)}, u32[]{:S(2)}, u32[]{:S(2)}) collective-permute-start(bf16[64,5120]{1,0:T(8,128)(2,1)} %get-tuple-element.880), channel_id=1, source_target_pairs={{0,16},{16,32},{32,48},{48,64},{64,80},{80,96},{96,112},{1,17},{17... | collective-permute-start | bytes 1966088 | tf_op jit(solution)/shard_map/while/body/eval_jaxpr/ppermute | solution.py:21
  344.8 7.8 collective-permute-done
  366.6 412.2 %while.39 = (s32[]{:T(128)}, bf16[64,5120]{1,0:T(8,128)(2,1)}, bf16[4,64,5120]{2,1,0:T(8,128)(2,1)}, f32[5120,512]{1,0:T(8,128)}, f32[512,5120]{1,0:T(8,128)}, /...) while((s32[]{:T(128)}, bf16[64,5120]{1,0:T(8,128)(2,1)}, ...), condition=%wide.region_10.11_spmd, body=%wide.region_5.10_spmd.sunk | while | flops 1690959872 | bytes 184750384 | solution.py:165
  370.9 11.2 %collective-permute-done.1 = bf16[64,5120]{1,0:T(8,128)(2,1)} collective-permute-done((bf16[64,5120]{1,0:T(8,128)(2,1)}, bf16[64,5120]{1,0:T(8,128)(2,1)}, u32[]{:S(2)}, u32[]{:S(2)}) %collective-permute-start.1) | collective-permute-done | bytes 655392 | tf_op jit(solution)/shard_map/while/body/eval_jaxpr/ppermute | solution.py:21
  386.5 12.8 %collective-permute-done.1 = bf16[64,5120]{1,0:T(8,128)(2,1)} collective-permute-done((bf16[64,5120]{1,0:T(8,128)(2,1)}, bf16[64,5120]{1,0:T(8,128)(2,1)}, u32[]{:S(2)}, u32[]{:S(2)}) %collective-permute-start.1) | collective-permute-done | bytes 655392 | tf_op jit(solution)/shard_map/while/body/eval_jaxpr/ppermute | solution.py:21
  403.6 13.0 %collective-permute-done.1 = bf16[64,5120]{1,0:T(8,128)(2,1)} collective-permute-done((bf16[64,5120]{1,0:T(8,128)(2,1)}, bf16[64,5120]{1,0:T(8,128)(2,1)}, u32[]{:S(2)}, u32[]{:S(2)}) %collective-permute-start.1) | collective-permute-done | bytes 655392 | tf_op jit(solution)/shard_map/while/body/eval_jaxpr/ppermute | solution.py:21
  420.9 13.2 %collective-permute-done.1 = bf16[64,5120]{1,0:T(8,128)(2,1)} collective-permute-done((bf16[64,5120]{1,0:T(8,128)(2,1)}, bf16[64,5120]{1,0:T(8,128)(2,1)}, u32[]{:S(2)}, u32[]{:S(2)}) %collective-permute-start.1) | collective-permute-done | bytes 655392 | tf_op jit(solution)/shard_map/while/body/eval_jaxpr/ppermute | solution.py:21
  438.4 17.3 %collective-permute-done.1 = bf16[64,5120]{1,0:T(8,128)(2,1)} collective-permute-done((bf16[64,5120]{1,0:T(8,128)(2,1)}, bf16[64,5120]{1,0:T(8,128)(2,1)}, u32[]{:S(2)}, u32[]{:S(2)}) %collective-permute-start.1) | collective-permute-done | bytes 655392 | tf_op jit(solution)/shard_map/while/body/eval_jaxpr/ppermute | solution.py:21
  460.0 16.0 %collective-permute-done.1 = bf16[64,5120]{1,0:T(8,128)(2,1)} collective-permute-done((bf16[64,5120]{1,0:T(8,128)(2,1)}, bf16[64,5120]{1,0:T(8,128)(2,1)}, u32[]{:S(2)}, u32[]{:S(2)}) %collective-permute-start.1) | collective-permute-done | bytes 655392 | tf_op jit(solution)/shard_map/while/body/eval_jaxpr/ppermute | solution.py:21
  480.4 150.1 %collective-permute-done.1 = bf16[64,5120]{1,0:T(8,128)(2,1)} collective-permute-done((bf16[64,5120]{1,0:T(8,128)(2,1)}, bf16[64,5120]{1,0:T(8,128)(2,1)}, u32[]{:S(2)}, u32[]{:S(2)}) %collective-permute-start.1) | collective-permute-done | bytes 655392 | tf_op jit(solution)/shard_map/while/body/eval_jaxpr/ppermute | solution.py:21
  630.5 23.2 %conditional.5 = (bf16[64,5120]{1,0:T(8,128)(2,1)}, f32[5120,512]{1,0:T(8,128)}, f32[512,5120]{1,0:T(8,128)}) conditional(s32[]{:T(128)} %convert_element_type.163, (f32[5120,512]{1,0:T(8,128)}, f32[512,5120]{1,0:T(8,128)}) %tuple.107, (pred[]{:T(512)}, bf16[4,64,5120]{2,1,0:T(8,128)(2,1)}, s32[]{:T(128)}, bf16[64,5120]{1,0:T(8,128)(2,1)}, ...), branch_computations={%region_6.6_spmd, %region_7.9_spmd} | conditional | flops 1690632192 | bytes 178851296 | solution.py:156
  637.6 9.8 convolution_add_fusion.2
  658.2 9.6 collective-permute-done.1
  667.8 23.3 %conditional.5 = (bf16[64,5120]{1,0:T(8,128)(2,1)}, f32[5120,512]{1,0:T(8,128)}, f32[512,5120]{1,0:T(8,128)}) conditional(s32[]{:T(128)} %convert_element_type.163, (f32[5120,512]{1,0:T(8,128)}, f32[512,5120]{1,0:T(8,128)}) %tuple.107, (pred[]{:T(512)}, bf16[4,64,5120]{2,1,0:T(8,128)(2,1)}, s32[]{:T(128)}, bf16[64,5120]{1,0:T(8,128)(2,1)}, ...), branch_computations={%region_6.6_spmd, %region_7.9_spmd} | conditional | flops 1690632192 | bytes 178851296 | solution.py:156
  674.9 9.8 convolution_add_fusion.2
  695.6 9.5 collective-permute-done.1
  705.1 23.3 %conditional.5 = (bf16[64,5120]{1,0:T(8,128)(2,1)}, f32[5120,512]{1,0:T(8,128)}, f32[512,5120]{1,0:T(8,128)}) conditional(s32[]{:T(128)} %convert_element_type.163, (f32[5120,512]{1,0:T(8,128)}, f32[512,5120]{1,0:T(8,128)}) %tuple.107, (pred[]{:T(512)}, bf16[4,64,5120]{2,1,0:T(8,128)(2,1)}, s32[]{:T(128)}, bf16[64,5120]{1,0:T(8,128)(2,1)}, ...), branch_computations={%region_6.6_spmd, %region_7.9_spmd} | conditional | flops 1690632192 | bytes 178851296 | solution.py:156
  712.2 9.8 convolution_add_fusion.2
  732.9 9.5 collective-permute-done.1
  742.4 23.3 %conditional.5 = (bf16[64,5120]{1,0:T(8,128)(2,1)}, f32[5120,512]{1,0:T(8,128)}, f32[512,5120]{1,0:T(8,128)}) conditional(s32[]{:T(128)} %convert_element_type.163, (f32[5120,512]{1,0:T(8,128)}, f32[512,5120]{1,0:T(8,128)}) %tuple.107, (pred[]{:T(512)}, bf16[4,64,5120]{2,1,0:T(8,128)(2,1)}, s32[]{:T(128)}, bf16[64,5120]{1,0:T(8,128)(2,1)}, ...), branch_computations={%region_6.6_spmd, %region_7.9_spmd} | conditional | flops 1690632192 | bytes 178851296 | solution.py:156
  749.5 9.8 convolution_add_fusion.2
  770.1 8.6 collective-permute-done.1
  778.8 7.0 convert_element_type.89
  786.0 7.1 convert_element_type.91
  793.2 76.2 %reduce-scatter.3.cloned.1.call-done = bf16[320,512]{1,0:T(8,128)(2,1)} async-done(((bf16[5120,512]{1,0:T(8,128)(2,1)}), bf16[320,512]{1,0:T(8,128)(2,1)}) %reduce-scatter.3.cloned.1.call-update) | async-done | bytes 327696 | tf_op jit(solution)/shard_map/reduce_scatter | solution.py:169
  872.4 71.5 %reduce-scatter.5.cloned.1.call-done = bf16[32,5120]{1,0:T(8,128)(2,1)} async-done(((bf16[512,5120]{1,0:T(8,128)(2,1)}), bf16[32,5120]{1,0:T(8,128)(2,1)}) %reduce-scatter.5.cloned.1.call-update) | async-done | bytes 327696 | tf_op jit(solution)/shard_map/reduce_scatter | solution.py:172
  947.0 38.1 %all-gather.9.cloned.1.call-done = bf16[5120,512]{1,0:T(8,128)(2,1)} async-done(((bf16[320,512]{1,0:T(8,128)(2,1)}), bf16[5120,512]{1,0:T(8,128)(2,1)}) %all-gather.9.cloned.1.call-update) | async-done | bytes 5242896 | tf_op jit(solution)/shard_map/all_gather | solution.py:185
  988.1 38.2 %all-gather.11.cloned.1.call-done = bf16[512,5120]{1,0:T(8,128)(2,1)} async-done(((bf16[32,5120]{1,0:T(8,128)(2,1)}), bf16[512,5120]{1,0:T(8,128)(2,1)}) %all-gather.11.cloned.1.call-update) | async-done | bytes 5242896 | tf_op jit(solution)/shard_map/all_gather | solution.py:186
  (260 shorter events, 241.8 us)
Async XLA Ops:
  7.2 46.2 %all-gather.5.cloned.1.call-start = ((), (), s32[]{:S(2)}) async-start(), calls=%async_computation.2 | async-start | bytes 5570560 | tf_op jit(solution)/shard_map/all_gather | solution.py:98
  9.1 86.1 %all-gather.7.cloned.1.call-start = ((), (), s32[]{:S(2)}) async-start(), calls=%async_computation.3 | async-start | bytes 5570560 | tf_op jit(solution)/shard_map/all_gather | solution.py:99
  11.0 858.4 %reduce-scatter.3.cloned.1.call-start = ((), (), s32[]{:S(2)}) async-start(), calls=%async_computation.4 | async-start | bytes 5570560 | tf_op jit(solution)/shard_map/reduce_scatter | solution.py:169
  105.1 15.8 %collective-permute-start = (bf16[64,5120]{1,0:T(8,128)(2,1)}, bf16[64,5120]{1,0:T(8,128)(2,1)S(1)}, u32[]{:S(2)}, u32[]{:S(2)}) collective-permute-start(bf16[64,5120]{1,0:T(8,128)(2,1)} %get-tuple-element.880), channel_id=1, source_target_pairs={{0,16},{16,32},{32,48},{48,64},{64,80},{80,96},{96,112},{1,17},{17... | collective-permute-start | bytes 1966088 | tf_op jit(solution)/shard_map/while/body/eval_jaxpr/ppermute | solution.py:21
  130.4 19.3 %collective-permute-start = (bf16[64,5120]{1,0:T(8,128)(2,1)}, bf16[64,5120]{1,0:T(8,128)(2,1)S(1)}, u32[]{:S(2)}, u32[]{:S(2)}) collective-permute-start(bf16[64,5120]{1,0:T(8,128)(2,1)} %get-tuple-element.880), channel_id=1, source_target_pairs={{0,16},{16,32},{32,48},{48,64},{64,80},{80,96},{96,112},{1,17},{17... | collective-permute-start | bytes 1966088 | tf_op jit(solution)/shard_map/while/body/eval_jaxpr/ppermute | solution.py:21
  159.2 18.3 %collective-permute-start = (bf16[64,5120]{1,0:T(8,128)(2,1)}, bf16[64,5120]{1,0:T(8,128)(2,1)S(1)}, u32[]{:S(2)}, u32[]{:S(2)}) collective-permute-start(bf16[64,5120]{1,0:T(8,128)(2,1)} %get-tuple-element.880), channel_id=1, source_target_pairs={{0,16},{16,32},{32,48},{48,64},{64,80},{80,96},{96,112},{1,17},{17... | collective-permute-start | bytes 1966088 | tf_op jit(solution)/shard_map/while/body/eval_jaxpr/ppermute | solution.py:21
  187.1 17.4 %collective-permute-start = (bf16[64,5120]{1,0:T(8,128)(2,1)}, bf16[64,5120]{1,0:T(8,128)(2,1)S(1)}, u32[]{:S(2)}, u32[]{:S(2)}) collective-permute-start(bf16[64,5120]{1,0:T(8,128)(2,1)} %get-tuple-element.880), channel_id=1, source_target_pairs={{0,16},{16,32},{32,48},{48,64},{64,80},{80,96},{96,112},{1,17},{17... | collective-permute-start | bytes 1966088 | tf_op jit(solution)/shard_map/while/body/eval_jaxpr/ppermute | solution.py:21
  207.8 22.8 %collective-permute-start = (bf16[64,5120]{1,0:T(8,128)(2,1)}, bf16[64,5120]{1,0:T(8,128)(2,1)S(1)}, u32[]{:S(2)}, u32[]{:S(2)}) collective-permute-start(bf16[64,5120]{1,0:T(8,128)(2,1)} %get-tuple-element.880), channel_id=1, source_target_pairs={{0,16},{16,32},{32,48},{48,64},{64,80},{80,96},{96,112},{1,17},{17... | collective-permute-start | bytes 1966088 | tf_op jit(solution)/shard_map/while/body/eval_jaxpr/ppermute | solution.py:21
  233.8 16.3 %collective-permute-start = (bf16[64,5120]{1,0:T(8,128)(2,1)}, bf16[64,5120]{1,0:T(8,128)(2,1)S(1)}, u32[]{:S(2)}, u32[]{:S(2)}) collective-permute-start(bf16[64,5120]{1,0:T(8,128)(2,1)} %get-tuple-element.880), channel_id=1, source_target_pairs={{0,16},{16,32},{32,48},{48,64},{64,80},{80,96},{96,112},{1,17},{17... | collective-permute-start | bytes 1966088 | tf_op jit(solution)/shard_map/while/body/eval_jaxpr/ppermute | solution.py:21
  253.3 22.2 %collective-permute-start = (bf16[64,5120]{1,0:T(8,128)(2,1)}, bf16[64,5120]{1,0:T(8,128)(2,1)S(1)}, u32[]{:S(2)}, u32[]{:S(2)}) collective-permute-start(bf16[64,5120]{1,0:T(8,128)(2,1)} %get-tuple-element.880), channel_id=1, source_target_pairs={{0,16},{16,32},{32,48},{48,64},{64,80},{80,96},{96,112},{1,17},{17... | collective-permute-start | bytes 1966088 | tf_op jit(solution)/shard_map/while/body/eval_jaxpr/ppermute | solution.py:21
  278.7 14.9 %collective-permute-start = (bf16[64,5120]{1,0:T(8,128)(2,1)}, bf16[64,5120]{1,0:T(8,128)(2,1)S(1)}, u32[]{:S(2)}, u32[]{:S(2)}) collective-permute-start(bf16[64,5120]{1,0:T(8,128)(2,1)} %get-tuple-element.880), channel_id=1, source_target_pairs={{0,16},{16,32},{32,48},{48,64},{64,80},{80,96},{96,112},{1,17},{17... | collective-permute-start | bytes 1966088 | tf_op jit(solution)/shard_map/while/body/eval_jaxpr/ppermute | solution.py:21
  296.8 16.2 %collective-permute-start = (bf16[64,5120]{1,0:T(8,128)(2,1)}, bf16[64,5120]{1,0:T(8,128)(2,1)S(1)}, u32[]{:S(2)}, u32[]{:S(2)}) collective-permute-start(bf16[64,5120]{1,0:T(8,128)(2,1)} %get-tuple-element.880), channel_id=1, source_target_pairs={{0,16},{16,32},{32,48},{48,64},{64,80},{80,96},{96,112},{1,17},{17... | collective-permute-start | bytes 1966088 | tf_op jit(solution)/shard_map/while/body/eval_jaxpr/ppermute | solution.py:21
  316.3 14.4 %collective-permute-start = (bf16[64,5120]{1,0:T(8,128)(2,1)}, bf16[64,5120]{1,0:T(8,128)(2,1)S(1)}, u32[]{:S(2)}, u32[]{:S(2)}) collective-permute-start(bf16[64,5120]{1,0:T(8,128)(2,1)} %get-tuple-element.880), channel_id=1, source_target_pairs={{0,16},{16,32},{32,48},{48,64},{64,80},{80,96},{96,112},{1,17},{17... | collective-permute-start | bytes 1966088 | tf_op jit(solution)/shard_map/while/body/eval_jaxpr/ppermute | solution.py:21
  333.9 18.6 %collective-permute-start = (bf16[64,5120]{1,0:T(8,128)(2,1)}, bf16[64,5120]{1,0:T(8,128)(2,1)S(1)}, u32[]{:S(2)}, u32[]{:S(2)}) collective-permute-start(bf16[64,5120]{1,0:T(8,128)(2,1)} %get-tuple-element.880), channel_id=1, source_target_pairs={{0,16},{16,32},{32,48},{48,64},{64,80},{80,96},{96,112},{1,17},{17... | collective-permute-start | bytes 1966088 | tf_op jit(solution)/shard_map/while/body/eval_jaxpr/ppermute | solution.py:21
  367.5 14.7 %collective-permute-start.1 = (bf16[64,5120]{1,0:T(8,128)(2,1)}, bf16[64,5120]{1,0:T(8,128)(2,1)}, u32[]{:S(2)}, u32[]{:S(2)}) collective-permute-start(bf16[64,5120]{1,0:T(8,128)(2,1)} %get-tuple-element.787), channel_id=1, source_target_pairs={{16,0},{32,16},{48,32},{64,48},{80,64},{96,80},{112,96},{17,1},{33... | collective-permute-start | bytes 1966088 | tf_op jit(solution)/shard_map/while/body/eval_jaxpr/ppermute | solution.py:21
  383.0 16.2 %collective-permute-start.1 = (bf16[64,5120]{1,0:T(8,128)(2,1)}, bf16[64,5120]{1,0:T(8,128)(2,1)}, u32[]{:S(2)}, u32[]{:S(2)}) collective-permute-start(bf16[64,5120]{1,0:T(8,128)(2,1)} %get-tuple-element.787), channel_id=1, source_target_pairs={{16,0},{32,16},{48,32},{64,48},{80,64},{96,80},{112,96},{17,1},{33... | collective-permute-start | bytes 1966088 | tf_op jit(solution)/shard_map/while/body/eval_jaxpr/ppermute | solution.py:21
  400.1 16.5 %collective-permute-start.1 = (bf16[64,5120]{1,0:T(8,128)(2,1)}, bf16[64,5120]{1,0:T(8,128)(2,1)}, u32[]{:S(2)}, u32[]{:S(2)}) collective-permute-start(bf16[64,5120]{1,0:T(8,128)(2,1)} %get-tuple-element.787), channel_id=1, source_target_pairs={{16,0},{32,16},{48,32},{64,48},{80,64},{96,80},{112,96},{17,1},{33... | collective-permute-start | bytes 1966088 | tf_op jit(solution)/shard_map/while/body/eval_jaxpr/ppermute | solution.py:21
  417.5 16.6 %collective-permute-start.1 = (bf16[64,5120]{1,0:T(8,128)(2,1)}, bf16[64,5120]{1,0:T(8,128)(2,1)}, u32[]{:S(2)}, u32[]{:S(2)}) collective-permute-start(bf16[64,5120]{1,0:T(8,128)(2,1)} %get-tuple-element.787), channel_id=1, source_target_pairs={{16,0},{32,16},{48,32},{64,48},{80,64},{96,80},{112,96},{17,1},{33... | collective-permute-start | bytes 1966088 | tf_op jit(solution)/shard_map/while/body/eval_jaxpr/ppermute | solution.py:21
  435.0 20.7 %collective-permute-start.1 = (bf16[64,5120]{1,0:T(8,128)(2,1)}, bf16[64,5120]{1,0:T(8,128)(2,1)}, u32[]{:S(2)}, u32[]{:S(2)}) collective-permute-start(bf16[64,5120]{1,0:T(8,128)(2,1)} %get-tuple-element.787), channel_id=1, source_target_pairs={{16,0},{32,16},{48,32},{64,48},{80,64},{96,80},{112,96},{17,1},{33... | collective-permute-start | bytes 1966088 | tf_op jit(solution)/shard_map/while/body/eval_jaxpr/ppermute | solution.py:21
  456.6 19.5 %collective-permute-start.1 = (bf16[64,5120]{1,0:T(8,128)(2,1)}, bf16[64,5120]{1,0:T(8,128)(2,1)}, u32[]{:S(2)}, u32[]{:S(2)}) collective-permute-start(bf16[64,5120]{1,0:T(8,128)(2,1)} %get-tuple-element.787), channel_id=1, source_target_pairs={{16,0},{32,16},{48,32},{64,48},{80,64},{96,80},{112,96},{17,1},{33... | collective-permute-start | bytes 1966088 | tf_op jit(solution)/shard_map/while/body/eval_jaxpr/ppermute | solution.py:21
  476.9 153.6 %collective-permute-start.1 = (bf16[64,5120]{1,0:T(8,128)(2,1)}, bf16[64,5120]{1,0:T(8,128)(2,1)}, u32[]{:S(2)}, u32[]{:S(2)}) collective-permute-start(bf16[64,5120]{1,0:T(8,128)(2,1)} %get-tuple-element.787), channel_id=1, source_target_pairs={{16,0},{32,16},{48,32},{64,48},{80,64},{96,80},{112,96},{17,1},{33... | collective-permute-start | bytes 1966088 | tf_op jit(solution)/shard_map/while/body/eval_jaxpr/ppermute | solution.py:21
  635.9 11.6 %slice-start.2 = ((s8[10485760]{0:T(1024)(128)(4,1)}), s8[4194304]{0:T(1024)(128)(4,1)S(1)}, s32[]{:S(2)}) async-start(s8[10485760]{0:T(1024)(128)(4,1)} %bitcast.115), calls=%async_computation.10 | async-start | bytes 8388608 | tf_op jit(solution)/shard_map/while/body/eval_jaxpr/cond
  637.6 9.8 slice-start.3
  637.6 12.1 %slice-start = ((s8[5242880]{0:T(1024)(128)(4,1)}), s8[1048576]{0:T(1024)(128)(4,1)S(1)}, s32[]{:S(2)}) async-start(s8[5242880]{0:T(1024)(128)(4,1)} %bitcast.113), calls=%async_computation.8 | async-start | bytes 2097152 | tf_op jit(solution)/shard_map/while/body/eval_jaxpr/cond
  653.7 14.1 %collective-permute-start.1 = (bf16[64,5120]{1,0:T(8,128)(2,1)}, bf16[64,5120]{1,0:T(8,128)(2,1)}, u32[]{:S(2)}, u32[]{:S(2)}) collective-permute-start(bf16[64,5120]{1,0:T(8,128)(2,1)} %get-tuple-element.787), channel_id=1, source_target_pairs={{16,0},{32,16},{48,32},{64,48},{80,64},{96,80},{112,96},{17,1},{33... | collective-permute-start | bytes 1966088 | tf_op jit(solution)/shard_map/while/body/eval_jaxpr/ppermute | solution.py:21
  673.2 11.6 %slice-start.2 = ((s8[10485760]{0:T(1024)(128)(4,1)}), s8[4194304]{0:T(1024)(128)(4,1)S(1)}, s32[]{:S(2)}) async-start(s8[10485760]{0:T(1024)(128)(4,1)} %bitcast.115), calls=%async_computation.10 | async-start | bytes 8388608 | tf_op jit(solution)/shard_map/while/body/eval_jaxpr/cond
  674.9 9.8 slice-start.3
  674.9 9.8 slice-start.4
  674.9 12.1 %slice-start = ((s8[5242880]{0:T(1024)(128)(4,1)}), s8[1048576]{0:T(1024)(128)(4,1)S(1)}, s32[]{:S(2)}) async-start(s8[5242880]{0:T(1024)(128)(4,1)} %bitcast.113), calls=%async_computation.8 | async-start | bytes 2097152 | tf_op jit(solution)/shard_map/while/body/eval_jaxpr/cond
  691.1 14.0 %collective-permute-start.1 = (bf16[64,5120]{1,0:T(8,128)(2,1)}, bf16[64,5120]{1,0:T(8,128)(2,1)}, u32[]{:S(2)}, u32[]{:S(2)}) collective-permute-start(bf16[64,5120]{1,0:T(8,128)(2,1)} %get-tuple-element.787), channel_id=1, source_target_pairs={{16,0},{32,16},{48,32},{64,48},{80,64},{96,80},{112,96},{17,1},{33... | collective-permute-start | bytes 1966088 | tf_op jit(solution)/shard_map/while/body/eval_jaxpr/ppermute | solution.py:21
  710.4 11.6 %slice-start.2 = ((s8[10485760]{0:T(1024)(128)(4,1)}), s8[4194304]{0:T(1024)(128)(4,1)S(1)}, s32[]{:S(2)}) async-start(s8[10485760]{0:T(1024)(128)(4,1)} %bitcast.115), calls=%async_computation.10 | async-start | bytes 8388608 | tf_op jit(solution)/shard_map/while/body/eval_jaxpr/cond
  712.2 9.8 slice-start.3
  712.2 9.8 slice-start.4
  712.2 12.1 %slice-start = ((s8[5242880]{0:T(1024)(128)(4,1)}), s8[1048576]{0:T(1024)(128)(4,1)S(1)}, s32[]{:S(2)}) async-start(s8[5242880]{0:T(1024)(128)(4,1)} %bitcast.113), calls=%async_computation.8 | async-start | bytes 2097152 | tf_op jit(solution)/shard_map/while/body/eval_jaxpr/cond
  728.4 14.0 %collective-permute-start.1 = (bf16[64,5120]{1,0:T(8,128)(2,1)}, bf16[64,5120]{1,0:T(8,128)(2,1)}, u32[]{:S(2)}, u32[]{:S(2)}) collective-permute-start(bf16[64,5120]{1,0:T(8,128)(2,1)} %get-tuple-element.787), channel_id=1, source_target_pairs={{16,0},{32,16},{48,32},{64,48},{80,64},{96,80},{112,96},{17,1},{33... | collective-permute-start | bytes 1966088 | tf_op jit(solution)/shard_map/while/body/eval_jaxpr/ppermute | solution.py:21
  747.7 11.6 %slice-start.2 = ((s8[10485760]{0:T(1024)(128)(4,1)}), s8[4194304]{0:T(1024)(128)(4,1)S(1)}, s32[]{:S(2)}) async-start(s8[10485760]{0:T(1024)(128)(4,1)} %bitcast.115), calls=%async_computation.10 | async-start | bytes 8388608 | tf_op jit(solution)/shard_map/while/body/eval_jaxpr/cond
  749.4 9.8 slice-start.3
  749.5 9.8 slice-start.4
  749.5 12.1 %slice-start = ((s8[5242880]{0:T(1024)(128)(4,1)}), s8[1048576]{0:T(1024)(128)(4,1)S(1)}, s32[]{:S(2)}) async-start(s8[5242880]{0:T(1024)(128)(4,1)} %bitcast.113), calls=%async_computation.8 | async-start | bytes 2097152 | tf_op jit(solution)/shard_map/while/body/eval_jaxpr/cond
  765.6 13.1 %collective-permute-start.1 = (bf16[64,5120]{1,0:T(8,128)(2,1)}, bf16[64,5120]{1,0:T(8,128)(2,1)}, u32[]{:S(2)}, u32[]{:S(2)}) collective-permute-start(bf16[64,5120]{1,0:T(8,128)(2,1)} %get-tuple-element.787), channel_id=1, source_target_pairs={{16,0},{32,16},{48,32},{64,48},{80,64},{96,80},{112,96},{17,1},{33... | collective-permute-start | bytes 1966088 | tf_op jit(solution)/shard_map/while/body/eval_jaxpr/ppermute | solution.py:21
  785.8 158.1 %reduce-scatter.5.cloned.1.call-start = ((), (), s32[]{:S(2)}) async-start(), calls=%async_computation.5 | async-start | bytes 5570560 | tf_op jit(solution)/shard_map/reduce_scatter | solution.py:172
  793.1 76.3 %copy-start.3 = (f32[1,320,512]{2,1,0:T(8,128)S(1)}, f32[1,320,512]{2,1,0:T(8,128)}, u32[]{:S(2)}) copy-start(f32[1,320,512]{2,1,0:T(8,128)} %param.18) | copy-start | bytes 1966084
  793.1 76.3 %copy-start.5 = (f32[1,320,512]{2,1,0:T(8,128)S(1)}, f32[1,320,512]{2,1,0:T(8,128)}, u32[]{:S(2)}) copy-start(f32[1,320,512]{2,1,0:T(8,128)} %param.22) | copy-start | bytes 1966084
  793.1 76.3 %copy-start.6 = (f32[1,320,512]{2,1,0:T(8,128)S(1)}, f32[1,320,512]{2,1,0:T(8,128)}, u32[]{:S(2)}) copy-start(f32[1,320,512]{2,1,0:T(8,128)} %param.20) | copy-start | bytes 1966084
  793.2 150.7 %copy-start.4 = (f32[1,32,5120]{2,1,0:T(8,128)S(1)}, f32[1,32,5120]{2,1,0:T(8,128)}, u32[]{:S(2)}) copy-start(f32[1,32,5120]{2,1,0:T(8,128)} %param.19) | copy-start | bytes 1966084
  793.2 150.7 %copy-start.7 = (f32[1,32,5120]{2,1,0:T(8,128)S(1)}, f32[1,32,5120]{2,1,0:T(8,128)}, u32[]{:S(2)}) copy-start(f32[1,32,5120]{2,1,0:T(8,128)} %param.23) | copy-start | bytes 1966084
  793.2 192.0 %all-gather.9.cloned.1.call-start = ((), (), s32[]{:S(2)}) async-start(), calls=%async_computation.6 | async-start | bytes 5570560 | tf_op jit(solution)/shard_map/all_gather | solution.py:185
  872.3 154.1 %all-gather.11.cloned.1.call-start = ((), (), s32[]{:S(2)}) async-start(), calls=%async_computation.7 | async-start | bytes 5570560 | tf_op jit(solution)/shard_map/all_gather | solution.py:186
  (24 other events, 64.6 us)
Sparse Core Ops, SparseCore 0:
  10.3 43.0 all-gather.4
  55.6 39.5 all-gather.6
  785.9 83.4 reduce-scatter.2
  871.7 72.1 reduce-scatter.4
  946.0 39.0 all-gather.8
  986.7 39.6 all-gather.10
where the time goes:
time: 1040 us
  waiting for transfers between devices  693 us (67%)
  matrix products  105 us (10%)
  starting transfers between devices  96.7 us (9%)
  other arithmetic  69.6 us (7%)
  local copies, waits for them, and re-layouts  55.5 us (5%)
  between operations  14.2 us (1%)
    ppermute x22, waiting for transfers between devices, passed_along(): return lax.ppermute(x, axis, pairs)  385 us
    ppermute x22, starting transfers between devices, passed_along(): return lax.ppermute(x, axis, pairs)  96.3 us
    reduce_scatter x1, waiting for transfers between devices, on_device(): lax.psum_scatter(sum_in.astype(jnp.bfloat16), 'dp', scatter_dimension=0,...  76.2 us
    reduce_scatter x1, waiting for transfers between devices, on_device(): lax.psum_scatter(sum_out.astype(jnp.bfloat16), 'dp', scatter_dimension=0,...  71.5 us
    dot_general x8, matrix products, contract_rows(): lax.dot_general(left, right, (((0,), (0,)), ((), ())), preferred_element_...  48.2 us
    all_gather x1, waiting for transfers between devices, on_device(): lax.all_gather(master_in[0].astype(jnp.bfloat16), 'dp', axis=0, tiled=True)  42.3 us
    all_gather x1, waiting for transfers between devices, on_device(): lax.all_gather(master_out[0].astype(jnp.bfloat16), 'dp', axis=0, tiled=True)  41.8 us
    all_gather x1, waiting for transfers between devices, on_device(): lax.all_gather(cast_out, 'dp', axis=0, tiled=True)  38.2 us
  transfers between devices with their start and end apart: 28, of which 28 were waited for; matrix products, arithmetic and copies ran while one was open for 4% of the time, Pallas kernels for 0%

commit v1 on v0

v1 whole, which is shorter than its diff:
```python
import jax
import jax.numpy as jnp
from jax import lax
from jax.sharding import PartitionSpec as P

norm_eps = 1e-06
beta_one = 0.9
beta_two = 0.999
learn_rate = 0.02
decay_rate = 0.1
adam_eps = 1e-08
adam_step = 100

BLOCKS = ((0, 4), (4, 8))


def dot(left, right, dims):
    return lax.dot_general(left, right, (dims, ((), ())), preferred_element_type=jnp.float32)


ROWS = ((1,), (0,))
LAST = ((1,), (1,))
FIRST = ((0,), (0,))


def swap(x, axis):
    return lax.all_to_all(x, axis, 0, 0, tiled=True)


def split_scalars(scalars):
    columns = []
    for value in scalars:
        high = value.astype(jnp.bfloat16)
        columns += [high, (value - high.astype(jnp.float32)).astype(jnp.bfloat16)]
    columns.append(jnp.zeros((scalars[0].shape[0], 128 - len(columns)), jnp.bfloat16))
    return columns


def joined_scalar(packed, at):
    return packed[:, at : at + 1].astype(jnp.float32) + packed[:, at + 1 : at + 2].astype(
        jnp.float32
    )


def sum_to_owner(columns, count):
    packed = jnp.concatenate([c.astype(jnp.bfloat16) for c in columns], axis=1)
    arrived = swap(packed, "pipe").reshape(count, packed.shape[0] // count, packed.shape[1])
    return jnp.sum(arrived.astype(jnp.float32), axis=0)


def gather_rows(columns, count):
    packed = jnp.concatenate(columns, axis=1)
    return swap(jnp.tile(packed, (count, 1)), "pipe")


def adam_update(master, moment, second, grad):
    moment_new = beta_one * moment + (1.0 - beta_one) * grad
    second_new = beta_two * second + (1.0 - beta_two) * grad * grad
    moment_hat = moment_new / (1.0 - beta_one**adam_step)
    second_hat = second_new / (1.0 - beta_two**adam_step)
    master_new = master - learn_rate * (
        moment_hat / (jnp.sqrt(second_hat) + adam_eps) + decay_rate * master
    )
    return (master_new, moment_new, second_new)


def reduce_grads(parts_in, parts_out, n_dp):
    group = len(parts_in)
    chunk, inner = parts_in[0].shape
    rows = group * chunk // n_dp
    share = inner // n_dp
    stacked_in = jnp.concatenate(parts_in, axis=0).reshape(n_dp, rows, inner)
    stacked_out = jnp.stack(parts_out, axis=1).reshape(n_dp, share, group, chunk)
    stacked_out = stacked_out.reshape(n_dp, rows, inner)
    both = jnp.concatenate([stacked_in, stacked_out], axis=1).reshape(n_dp * 2 * rows, inner)
    summed = lax.psum_scatter(both, "dp", scatter_dimension=0, tiled=True)
    return summed[:rows], summed[rows:].reshape(share, group, chunk)


def move_in(summed, first, group, n_pipe, n_dp):
    per = n_pipe // group
    moved = []
    for q in range(per):
        pairs = []
        for i in range(n_pipe):
            for j in range(q, n_dp, per):
                section = j * group // n_dp
                half = j // per % 2
                pairs.append((i * n_dp + j, (first + section) * n_dp + 2 * i + half))
        moved.append(lax.ppermute(summed, ("pipe", "dp"), pairs))
    return jnp.concatenate(moved, axis=0)


def gram_units(first, last):
    units = []
    for j in range(first, last - 1):
        units += [(j, k, False) for k in range(j, last - 1)]
        units += [(j, s, True) for s in range(j + 1, last)]
    return units


def on_device(
    inputs_x, cotangent, master_in, master_out, moment_in, moment_out, second_in, second_out
):
    n_pipe = lax.axis_size("pipe")
    n_dp = lax.axis_size("dp")
    me = lax.axis_index("pipe")
    tok_rows, width = inputs_x.shape
    chunk = width // n_pipe
    inner = master_in.shape[2]
    share_in = master_in.shape[1]
    share_out = master_out.shape[1]

    own_in = master_in[0].astype(jnp.bfloat16)
    own_out = master_out[0].astype(jnp.bfloat16)
    pairs = [
        (s * n_dp + 2 * i + h, i * n_dp + 2 * s + h)
        for s in range(n_pipe)
        for i in range(n_pipe)
        for h in range(2)
    ]
    piece_in = lax.ppermute(own_in, ("pipe", "dp"), pairs)
    piece_out = swap(own_out.reshape(share_out, n_pipe, chunk).transpose(1, 0, 2), "pipe")
    flat_out = piece_out.transpose(1, 0, 2).reshape(share_out, width)
    all_in = lax.all_gather(piece_in, "dp", axis=0, tiled=True)
    all_out = lax.all_gather(flat_out, "dp", axis=0, tiled=True)
    weight_in = [all_in[s * chunk : (s + 1) * chunk] for s in range(n_pipe)]
    weight_out = [all_out[:, s * chunk : (s + 1) * chunk] for s in range(n_pipe)]

    units = [unit for first, last in BLOCKS for unit in gram_units(first, last)]
    padded = -(-len(units) // n_pipe) * n_pipe
    partial = []
    for j, other, down in units:
        if down:
            partial.append(dot(piece_out[j], weight_in[other], ROWS))
        else:
            partial.append(dot(piece_out[j], weight_out[other], LAST))
    partial += [jnp.zeros_like(partial[0])] * (padded - len(units))
    arrived = swap(jnp.stack(partial).astype(jnp.bfloat16), "pipe")
    arrived = arrived.reshape(n_pipe, padded // n_pipe, share_out, inner)
    mine = jnp.sum(arrived.astype(jnp.float32), axis=0).astype(jnp.bfloat16)
    rows_of = swap(jnp.tile(mine, (n_pipe, 1, 1)), "pipe")
    rows_of = rows_of.transpose(1, 0, 2).reshape(share_out, padded * inner)
    gram_all = lax.all_gather(rows_of, "dp", axis=0, tiled=True)
    gram = {
        unit: gram_all[:, at * inner : (at + 1) * inner] for at, unit in enumerate(units)
    }

    rows = lax.dynamic_slice_in_dim(inputs_x, me * chunk, chunk, 1)
    exact = rows.astype(jnp.float32)
    seed = lax.dynamic_slice_in_dim(cotangent, me * chunk, chunk, 1)

    def grad_start(upstream, first, last):
        sums = sum_to_owner(
            [dot(upstream, weight_out[s], LAST) for s in range(first, last)], n_pipe
        )
        return {
            s: sums[:, (s - first) * inner : (s - first + 1) * inner] for s in range(first, last)
        }

    grad_act = grad_start(seed, *BLOCKS[-1])
    saved_rows, saved_act, state = {}, {}, {}

    def forward_block(first, last):
        count = last - first
        columns = [dot(rows, weight_in[s], ROWS) for s in range(first, last)]
        columns += [dot(rows, weight_out[s], LAST) for s in range(first, last - 1)]
        columns += split_scalars([jnp.sum(exact * exact, axis=1, keepdims=True)])
        sums = sum_to_owner(columns, n_pipe)
        raw = {s: sums[:, (s - first) * inner : (s - first + 1) * inner] for s in range(first, last)}
        cross = {
            s: sums[:, (count + s - first) * inner : (count + s - first + 1) * inner]
            for s in range(first, last - 1)
        }
        at = (2 * count - 1) * inner
        square = sums[:, at : at + 1] + sums[:, at + 1 : at + 2]
        for s in range(first, last):
            scale = lax.rsqrt(jnp.maximum(square, 0.0) / width + norm_eps)
            hidden = raw[s] * scale
            gate = jax.nn.sigmoid(hidden)
            act = (hidden * gate).astype(jnp.bfloat16)
            seen = {}
            if s < last - 1:
                added = {}
                for k in range(first, last - 1):
                    if k >= s:
                        added[k] = dot(act, gram[(s, k, False)], ROWS)
                    else:
                        added[k] = dot(act, gram[(k, s, False)], LAST)
                wide = act.astype(jnp.float32)
                square = square + jnp.sum(
                    wide * (2.0 * cross[s] + added[s]), axis=1, keepdims=True
                )
                for k in range(first, last - 1):
                    cross[k] = cross[k] + added[k]
                for t in range(s + 1, last):
                    raw[t] = raw[t] + dot(act, gram[(s, t, True)], ROWS)
                seen = dict(cross)
            state[s] = (hidden, gate, scale, act)
            inputs_cross[s + 1] = seen

    inputs_cross = {}

    def backward_block(first, last):
        packs, pulls = {}, {}
        for s in reversed(range(first, last)):
            hidden, gate, scale, act = state[s]
            grad_hidden = grad_act[s] * gate * (1.0 + hidden * (1.0 - gate))
            mean = jnp.sum(grad_hidden * hidden, axis=1, keepdims=True) / width
            packs[s] = (grad_hidden * scale).astype(jnp.bfloat16)
            pulls[s] = mean * scale * scale
            for t in range(first, s):
                grad_act[t] = (
                    grad_act[t]
                    + dot(packs[s], gram[(t, s, True)], LAST)
                    - pulls[s] * inputs_cross[s][t]
                )
        return packs, pulls

    upstream = seed
    upstream_exact = seed.astype(jnp.float32)
    grads = [None] * n_pipe
    reduced = {}

    def take_rows(act_all, first, last, more):
        nonlocal rows, exact
        for s in range(first, last):
            saved_rows[s] = rows
            saved_act[s] = act_all[:, (s - first) * inner : (s - first + 1) * inner]
            if s < last - 1 or more:
                exact = exact + dot(saved_act[s], weight_out[s], ROWS)
                rows = exact.astype(jnp.bfloat16)

    for first, last in BLOCKS[:-1]:
        forward_block(first, last)
        gathered = gather_rows([state[s][3] for s in range(first, last)], n_pipe)
        take_rows(gathered, first, last, True)

    for number in reversed(range(len(BLOCKS))):
        first, last = BLOCKS[number]
        count = last - first
        is_last = number == len(BLOCKS) - 1
        if is_last:
            forward_block(first, last)
        else:
            grad_act.update(grad_start(upstream, first, last))
        packs, pulls = backward_block(first, last)
        columns = [packs[s] for s in range(first, last)]
        if is_last:
            columns += [state[s][3] for s in range(first, last)]
        columns += split_scalars([pulls[s] for s in range(first, last)])
        gathered = gather_rows(columns, n_pipe)
        if is_last:
            take_rows(gathered[:, count * inner :], first, last, False)
        scalar_at = gathered.shape[1] - 128
        parts_in, parts_out = {}, {}
        for s in reversed(range(first, last)):
            pack = gathered[:, (s - first) * inner : (s - first + 1) * inner]
            pull = joined_scalar(gathered, scalar_at + 2 * (s - first))
            parts_in[s] = dot(saved_rows[s], pack, FIRST).astype(jnp.bfloat16)
            parts_out[s] = dot(saved_act[s], upstream, FIRST).astype(jnp.bfloat16)
            upstream_exact = (
                upstream_exact
                + dot(pack, weight_in[s], LAST)
                - pull * saved_rows[s].astype(jnp.float32)
            )
            upstream = upstream_exact.astype(jnp.bfloat16)
            grads[s] = upstream
        reduced[first] = reduce_grads(
            [parts_in[s] for s in range(first, last)],
            [parts_out[s] for s in range(first, last)],
            n_dp,
        )

    input_grads = swap(jnp.stack(grads), "pipe")
    input_grads = input_grads.transpose(1, 0, 2).reshape(1, tok_rows, width)

    grad_in = jnp.zeros((share_in, inner), jnp.bfloat16)
    outs = []
    for first, last in BLOCKS:
        sum_in, sum_out = reduced[first]
        moved = move_in(sum_in, first, last - first, n_pipe, n_dp)
        grad_in = jnp.where((me >= first) & (me < last), moved, grad_in)
        outs.append(sum_out.transpose(1, 0, 2))
    grad_out = swap(jnp.concatenate(outs, axis=0), "pipe")
    grad_out = grad_out.transpose(1, 0, 2).reshape(share_out, width)

    new_in, new_moment_in, new_second_in = adam_update(
        master_in[0], moment_in[0], second_in[0], grad_in.astype(jnp.float32)
    )
    new_out, new_moment_out, new_second_out = adam_update(
        master_out[0], moment_out[0], second_out[0], grad_out.astype(jnp.float32)
    )
    cast_in = new_in.astype(jnp.bfloat16).T.reshape(n_dp, share_out, share_in)
    cast_out = new_out.astype(jnp.bfloat16).reshape(share_out, n_dp, share_in).transpose(1, 0, 2)
    swapped = swap(jnp.stack([cast_in, cast_out], axis=1), "dp")
    roll_in = swapped[:, 0].transpose(1, 0, 2).reshape(share_out, width)
    roll_out = swapped[:, 1].reshape(inner, share_in).T
    return (
        input_grads,
        new_in[None],
        new_moment_in[None],
        new_second_in[None],
        new_out[None],
        new_moment_out[None],
        new_second_out[None],
        roll_in[None],
        roll_out[None],
    )


def solution(mesh):
    in_specs = (P("dp", None), P("dp", None)) + (P("pipe", "dp", None),) * 6
    out_specs = (P("pipe", "dp", None),) * 9
    return jax.shard_map(
        on_device, mesh=mesh, in_specs=in_specs, out_specs=out_specs, check_vma=False
    )
```

time: 1040 us -> 760 us (0.73)
  waiting for transfers between devices: 693 us -> 299 us
  blocking collectives: 0 us -> 80.7 us
  matrix products: 105 us -> 166 us
  other arithmetic: 69.6 us -> 40 us
  starting transfers between devices: 96.7 us -> 69.1 us
  local copies, waits for them, and re-layouts: 55.5 us -> 75.5 us
    ppermute x22 -> x5, waiting for transfers between devices: 385 us -> 0.01 us  [the longest x4 0.01 us: move_in(): moved.append(lax.ppermute(summed, ('pipe', 'dp'), pairs))]
    reduce_scatter x2 -> x0, waiting for transfers between devices: 148 us -> none  [the longest x1 76.2 us: on_device(): lax.psum_scatter(sum_in.astype(jnp.bfloat16), 'dp', scatter_dimension=0,...]
    all_to_all x0 -> x9, waiting for transfers between devices: none -> 123 us  [swap(): return lax.all_to_all(x, axis, 0, 0, tiled=True)]
    ppermute x22 -> x5, starting transfers between devices: 96.3 us -> 12 us  [the longest x4 11.3 us: move_in(): moved.append(lax.ppermute(summed, ('pipe', 'dp'), pairs))]
    all_to_all x0 -> x4, blocking collectives: none -> 80.7 us  [swap(): return lax.all_to_all(x, axis, 0, 0, tiled=True)]
    dot_general x24 -> x119, matrix products: 105 us -> 166 us  [dot(): lax.dot_general(left, right, (dims, ((), ())), preferred_element_type=jnp...]
    all_to_all x0 -> x9, starting transfers between devices: none -> 56.4 us  [swap(): return lax.all_to_all(x, axis, 0, 0, tiled=True)]
    unnamed x6 -> x7, waiting for transfers between devices: 0.1 us -> 55.3 us
  transfers between devices with their start and end apart: 28 -> 19, of which waited for: 28 -> 11; matrix products, arithmetic and copies ran while one was open for 4% -> 22% of each run, Pallas kernels for 0% -> 0%
where the time goes in v1:
time: 760 us; the launch traced here: 746 us
  waiting for transfers between devices  299 us (39%)
  matrix products  166 us (22%)
  blocking collectives  80.7 us (11%)
  local copies, waits for them, and re-layouts  75.5 us (10%)
  starting transfers between devices  69.1 us (9%)
  other arithmetic  40 us (5%)
  between operations  15.3 us (2%)
    dot_general x119, matrix products, dot(): lax.dot_general(left, right, (dims, ((), ())), preferred_element_type=jnp...  166 us
    all_to_all x9, waiting for transfers between devices, swap(): return lax.all_to_all(x, axis, 0, 0, tiled=True)  123 us
    all_to_all x4, blocking collectives, swap(): return lax.all_to_all(x, axis, 0, 0, tiled=True)  80.7 us
    all_to_all x9, starting transfers between devices, swap(): return lax.all_to_all(x, axis, 0, 0, tiled=True)  56.4 us
    unnamed x7, waiting for transfers between devices  55.3 us
    all_gather x1, waiting for transfers between devices, on_device(): all_in = lax.all_gather(piece_in, 'dp', axis=0, tiled=True)  43 us
    all_gather x1, waiting for transfers between devices, on_device(): all_out = lax.all_gather(flat_out, 'dp', axis=0, tiled=True)  40.7 us
    all_gather x1, waiting for transfers between devices, on_device(): gram_all = lax.all_gather(rows_of, 'dp', axis=0, tiled=True)  37.6 us
  transfers between devices with their start and end apart: 19, of which 11 were waited for; matrix products, arithmetic and copies ran while one was open for 22% of the time, Pallas kernels for 0%

profile of v1, /device:TPU:1, one launch (start us, length us, event | category | flops | bytes accessed | tf_op | source)
XLA Modules:
  0.0 746.2 jit_solution(7318564333119359475)
XLA Ops:
  8.4 16.5 %all_to_all.87 = bf16[8,32,640]{2,1,0:T(8,128)(2,1)S(1)} all-to-all(bf16[8,32,640]{2,1,0:T(8,128)(2,1)S(1)} %copy.307), channel_id=1, replica_groups=mesh['pipe'=8,'dp'=16] {'pipe'}, dimensions={0} | all-to-all | bytes 655360 | tf_op jit(solution)/shard_map/all_to_all | solution.py:27
  28.8 40.7 %all-gather.4.cloned.1.call-done = bf16[512,5120]{1,0:T(8,128)(2,1)} async-done(((bf16[32,5120]{1,0:T(8,128)(2,1)}), bf16[512,5120]{1,0:T(8,128)(2,1)}) %all-gather.4.cloned.1.call-update) | async-done | bytes 5242896 | tf_op jit(solution)/shard_map/all_gather | solution.py:126
  73.6 43.0 %all-gather.6.cloned.1.call-done = bf16[5120,512]{1,0:T(8,128)(2,1)} async-done(((bf16[320,512]{1,0:T(8,128)(2,1)}), bf16[5120,512]{1,0:T(8,128)(2,1)}) %all-gather.6.cloned.1.call-update) | async-done | bytes 5242896 | tf_op jit(solution)/shard_map/all_gather | solution.py:125
  137.8 18.8 %all_to_all.88 = bf16[24,32,512]{2,1,0:T(8,128)(2,1)S(1)} all-to-all(bf16[24,32,512]{2,1,0:T(8,128)(2,1)S(1)} %fusion.101), channel_id=1, replica_groups=mesh['pipe'=8,'dp'=16] {'pipe'}, dimensions={0} | all-to-all | bytes 1572864 | tf_op jit(solution)/shard_map/all_to_all | solution.py:27
  156.8 16.1 %all_to_all.89 = bf16[24,32,512]{2,1,0:T(8,128)(2,1)S(1)} all-to-all(bf16[24,32,512]{2,1,0:T(8,128)(2,1)S(1)} %bitcast.421), channel_id=1, replica_groups=mesh['pipe'=8,'dp'=16] {'pipe'}, dimensions={0} | all-to-all | bytes 1572864 | tf_op jit(solution)/shard_map/all_to_all | solution.py:27
  175.4 2.3 convolution_convert_fusion.29
  186.5 2.2 convolution_convert_fusion.31
  190.9 3.9 concatenate.119
  194.8 3.6 all-to-all-start.2
  198.4 2.3 convolution_convert_fusion.34
  200.7 26.6 %all-to-all-done.2 = bf16[8,32,3712]{2,1,0:T(8,128)(2,1)S(1)} async-done(((bf16[8,32,3712]{2,1,0:T(8,128)(2,1)}), bf16[8,32,3712]{2,1,0:T(8,128)(2,1)S(1)}, u32[]{:S(2)}, u32[]{:S(2)}) %all-to-all-start.2) | async-done | bytes 1900576 | tf_op jit(solution)/shard_map/all_to_all | solution.py:27
  227.9 37.6 %all-gather.8.cloned.1.call-done = bf16[512,12288]{1,0:T(8,128)(2,1)} async-done(((bf16[32,12288]{1,0:T(8,128)(2,1)}), bf16[512,12288]{1,0:T(8,128)(2,1)}) %all-gather.8.cloned.1.call-update) | async-done | bytes 12582928 | tf_op jit(solution)/shard_map/all_gather | solution.py:144
  284.6 6.3 all-to-all-start.5
  296.9 10.0 %all-to-all-done.5 = bf16[8,32,2048]{2,1,0:T(8,128)(2,1)S(1)} async-done(((bf16[8,32,2048]{2,1,0:T(8,128)(2,1)}), bf16[8,32,2048]{2,1,0:T(8,128)(2,1)S(1)}, u32[]{:S(2)}, u32[]{:S(2)}) %all-to-all-start.5) | async-done | bytes 1048608 | tf_op jit(solution)/shard_map/all_to_all | solution.py:27
  306.9 3.9 all-to-all-start.1
  317.7 2.3 multiply_reduce_fusion
  333.5 3.6 concatenate.128
  338.1 6.6 all-to-all-start.6
  346.6 25.1 %all-to-all-done.6 = bf16[8,32,3712]{2,1,0:T(8,128)(2,1)S(1)} async-done(((bf16[8,32,3712]{2,1,0:T(8,128)(2,1)}), bf16[8,32,3712]{2,1,0:T(8,128)(2,1)S(1)}, u32[]{:S(2)}, u32[]{:S(2)}) %all-to-all-start.6) | async-done | bytes 1900576 | tf_op jit(solution)/shard_map/all_to_all | solution.py:27
  402.8 29.3 %all_to_all.90 = bf16[8,32,4224]{2,1,0:T(8,128)(2,1)S(1)} all-to-all(bf16[8,32,4224]{2,1,0:T(8,128)(2,1)S(1)} %tile.13), channel_id=1, replica_groups=mesh['pipe'=8,'dp'=16] {'pipe'}, dimensions={0} | all-to-all | bytes 4325376 | tf_op jit(solution)/shard_map/all_to_all | solution.py:27
  450.3 3.5 copy.338
  453.8 5.8 reshape_reshape.6
  462.1 2.9 pad_maximum_fusion
  465.0 2.5 fusion.304
  474.9 3.7 all-to-all-start.8
  479.9 12.4 %all-to-all-done.8 = bf16[8,32,2048]{2,1,0:T(8,128)(2,1)S(1)} async-done(((bf16[8,32,2048]{2,1,0:T(8,128)(2,1)}), bf16[8,32,2048]{2,1,0:T(8,128)(2,1)S(1)}, u32[]{:S(2)}, u32[]{:S(2)}) %all-to-all-start.8) | async-done | bytes 1048608 | tf_op jit(solution)/shard_map/all_to_all | solution.py:27
  506.6 7.4 all-to-all-start.9
  516.4 16.0 %all-to-all-done.9 = bf16[8,32,2176]{2,1,0:T(8,128)(2,1)S(1)} async-done(((bf16[8,32,2176]{2,1,0:T(8,128)(2,1)}), bf16[8,32,2176]{2,1,0:T(8,128)(2,1)S(1)}, u32[]{:S(2)}, u32[]{:S(2)}) %all-to-all-start.9) | async-done | bytes 1114144 | tf_op jit(solution)/shard_map/all_to_all | solution.py:27
  541.5 3.5 copy.340
  545.0 5.8 reshape_reshape.7
  554.7 2.9 pad_maximum_fusion.1
  559.8 2.2 copy.337
  562.0 2.3 copy.342
  564.3 2.6 fusion.19
  576.4 55.3 %reduce-scatter.9.cloned.1.call-done = bf16[320,512]{1,0:T(8,128)(2,1)} async-done(((bf16[5120,512]{1,0:T(8,128)(2,1)}), bf16[320,512]{1,0:T(8,128)(2,1)}) %reduce-scatter.9.cloned.1.call-update) | async-done | bytes 327696
  635.4 7.9 %all-to-all-start.11 = ((bf16[8,32,640]{2,1,0:T(8,128)(2,1)}), bf16[8,32,640]{2,1,0:T(8,128)(2,1)}, u32[]{:S(2)}, u32[]{:S(2)}) async-start(bf16[8,32,640]{2,1,0:T(8,128)(2,1)} %copy.347), calls=%async_computation.11 | async-start | bytes 655360 | tf_op jit(solution)/shard_map/all_to_all | solution.py:27
  645.9 5.8 collective-permute-start.2
  653.9 2.9 collective-permute-start.4
  658.9 12.4 %all-to-all-start.10 = ((bf16[8,256,640]{2,1,0:T(8,128)(2,1)}), bf16[8,256,640]{2,1,0:T(8,128)(2,1)}, u32[]{:S(2)}, u32[]{:S(2)}) async-start(bf16[8,256,640]{2,1,0:T(8,128)(2,1)} %bitcast_dynamic-update-slice_fusion), calls=%async_computation.10 | async-start | bytes 5242880 | tf_op jit(solution)/shard_map/all_to_all | solution.py:27
  671.3 2.8 fusion.121
  676.7 3.6 multiply_subtract_fusion.1
  680.3 2.2 mul.875
  683.7 2.6 fusion.201
  687.5 31.4 %all-to-all-done.10 = bf16[8,256,640]{2,1,0:T(8,128)(2,1)} async-done(((bf16[8,256,640]{2,1,0:T(8,128)(2,1)}), bf16[8,256,640]{2,1,0:T(8,128)(2,1)}, u32[]{:S(2)}, u32[]{:S(2)}) %all-to-all-start.10) | async-done | bytes 2621472 | tf_op jit(solution)/shard_map/all_to_all | solution.py:27
  718.8 4.5 all-to-all-start.12
  723.3 3.0 copy.336
  726.3 2.8 copy.359
  729.1 2.6 multiply_subtract_fusion
  (347 shorter events, 217.1 us)
Async XLA Ops:
  7.2 62.3 %all-gather.4.cloned.1.call-start = ((), (), s32[]{:S(2)}) async-start(), calls=%async_computation.15 | async-start | bytes 5570560 | tf_op jit(solution)/shard_map/all_gather | solution.py:126
  25.7 90.9 %all-gather.6.cloned.1.call-start = ((), (), s32[]{:S(2)}) async-start(), calls=%async_computation.16 | async-start | bytes 5570560 | tf_op jit(solution)/shard_map/all_gather | solution.py:125
  27.1 0.7 collective-permute-start
  28.8 236.8 %all-gather.8.cloned.1.call-start = ((), (), s32[]{:S(2)}) async-start(), calls=%async_computation.17 | async-start | bytes 13369344 | tf_op jit(solution)/shard_map/all_gather | solution.py:144
  116.6 11.2 %copy-start.22 = (bf16[5120,512]{1,0:T(8,128)(2,1)S(1)}, bf16[5120,512]{1,0:T(8,128)(2,1)}, u32[]{:S(2)}) copy-start(bf16[5120,512]{1,0:T(8,128)(2,1)} %all-gather.6.cloned.1.call-done) | copy-start | bytes 15728644
  156.8 20.9 %copy-start.35 = (bf16[256,5120]{1,0:T(8,128)(2,1)S(1)}, bf16[256,5120]{1,0:T(8,128)(2,1)}, u32[]{:S(2)}) copy-start(bf16[256,5120]{1,0:T(8,128)(2,1)} %param.8) | copy-start | bytes 7864324
  194.8 32.5 %all-to-all-start.2 = ((bf16[8,32,3712]{2,1,0:T(8,128)(2,1)}), bf16[8,32,3712]{2,1,0:T(8,128)(2,1)S(1)}, u32[]{:S(2)}, u32[]{:S(2)}) async-start(bf16[8,32,3712]{2,1,0:T(8,128)(2,1)} %concatenate.119), calls=%async_computation.2 | async-start | bytes 3801088 | tf_op jit(solution)/shard_map/all_to_all | solution.py:27
  227.6 57.1 %copy-start.27 = (f32[32,3712]{1,0:T(8,128)}, f32[32,3712]{1,0:T(8,128)S(1)}, u32[]{:S(2)}) copy-start(f32[32,3712]{1,0:T(8,128)S(1)} %convert_reduce_fusion.1) | copy-start | bytes 1425412
  266.9 211.7 %copy-start.36 = (f32[32,512]{1,0:T(8,128)}, f32[32,512]{1,0:T(8,128)S(1)}, u32[]{:S(2)}) copy-start(f32[32,512]{1,0:T(8,128)S(1)} %get-tuple-element.137) | copy-start | bytes 196612
  268.2 16.5 %copy-start.31 = (f32[32,512]{1,0:T(8,128)}, f32[32,512]{1,0:T(8,128)S(1)}, u32[]{:S(2)}) copy-start(f32[32,512]{1,0:T(8,128)S(1)} %convolution_add_fusion.47) | copy-start | bytes 196612
  272.0 7.7 %copy-start.45 = (f32[32]{0:T(128)}, f32[32]{0:T(128)S(1)}, u32[]{:S(2)}) copy-start(f32[32]{0:T(128)S(1)} %get-tuple-element.99) | copy-start | bytes 388
  272.0 20.5 %copy-start.44 = (f32[32,1]{0,1:T(1,128)}, f32[32,1]{0,1:T(1,128)S(1)}, u32[]{:S(2)}) copy-start(f32[32,1]{0,1:T(1,128)S(1)} %get-tuple-element.100) | copy-start | bytes 388
  275.8 7.7 %copy-start.39 = (f32[32,512]{1,0:T(8,128)}, f32[32,512]{1,0:T(8,128)S(1)}, u32[]{:S(2)}) copy-start(f32[32,512]{1,0:T(8,128)S(1)} %convolution_add_fusion.42) | copy-start | bytes 196612
  277.7 18.0 %copy-start.33 = (bf16[32,512]{1,0:T(8,128)(2,1)}, bf16[32,512]{1,0:T(8,128)(2,1)S(1)}, u32[]{:S(2)}) copy-start(bf16[32,512]{1,0:T(8,128)(2,1)S(1)} %get-tuple-element.142) | copy-start | bytes 98308
  277.7 18.1 %copy-start.41 = (bf16[256,512]{1,0:T(8,128)(2,1)S(1)}, bf16[256,512]{1,0:T(8,128)(2,1)}, u32[]{:S(2)}) copy-start(bf16[256,512]{1,0:T(8,128)(2,1)} %convolution_convert_fusion.34) | copy-start | bytes 786436
  279.7 17.1 %copy-start.42 = (f32[32,1]{0,1:T(1,128)}, f32[32,1]{0,1:T(1,128)S(1)}, u32[]{:S(2)}) copy-start(f32[32,1]{0,1:T(1,128)S(1)} %add_rsqrt_fusion.4) | copy-start | bytes 388
  284.6 22.2 %all-to-all-start.5 = ((bf16[8,32,2048]{2,1,0:T(8,128)(2,1)}), bf16[8,32,2048]{2,1,0:T(8,128)(2,1)S(1)}, u32[]{:S(2)}, u32[]{:S(2)}) async-start(bf16[8,32,2048]{2,1,0:T(8,128)(2,1)} %tile.12), calls=%async_computation.5 | async-start | bytes 2097152 | tf_op jit(solution)/shard_map/all_to_all | solution.py:27
  306.8 13.2 %copy-start.15 = (bf16[8,32,2048]{2,1,0:T(8,128)(2,1)}, bf16[8,32,2048]{2,1,0:T(8,128)(2,1)S(1)}, u32[]{:S(2)}) copy-start(bf16[8,32,2048]{2,1,0:T(8,128)(2,1)S(1)} %all-to-all-done.5) | copy-start | bytes 3145732
  306.9 30.3 %all-to-all-start.1 = ((bf16[8,32,2048]{2,1,0:T(8,128)(2,1)}), bf16[8,32,2048]{2,1,0:T(8,128)(2,1)S(1)}, u32[]{:S(2)}, u32[]{:S(2)}) async-start(bf16[8,32,2048]{2,1,0:T(8,128)(2,1)} %bitcast.418), calls=%async_computation.1 | async-start | bytes 2097152 | tf_op jit(solution)/shard_map/all_to_all | solution.py:27
  338.1 33.5 %all-to-all-start.6 = ((bf16[8,32,3712]{2,1,0:T(8,128)(2,1)}), bf16[8,32,3712]{2,1,0:T(8,128)(2,1)S(1)}, u32[]{:S(2)}, u32[]{:S(2)}) async-start(bf16[8,32,3712]{2,1,0:T(8,128)(2,1)} %concatenate.128), calls=%async_computation.6 | async-start | bytes 3801088 | tf_op jit(solution)/shard_map/all_to_all | solution.py:27
  344.8 229.2 %reduce-scatter.7.cloned.1.call-start = ((), (), s32[]{:S(2)}) async-start(), calls=%async_computation.18 | async-start | bytes 5570560
  469.2 23.3 %copy-start.43 = (f32[32,1]{0,1:T(1,128)S(1)}, f32[32,1]{0,1:T(1,128)}, u32[]{:S(2)}) copy-start(f32[32,1]{0,1:T(1,128)} %copy-done.42) | copy-start | bytes 388
  469.2 23.5 %copy-start.40 = (f32[32,512]{1,0:T(8,128)S(1)}, f32[32,512]{1,0:T(8,128)}, u32[]{:S(2)}) copy-start(f32[32,512]{1,0:T(8,128)} %copy-done.39) | copy-start | bytes 196612
  470.7 24.2 %copy-start.32 = (f32[32,512]{1,0:T(8,128)S(1)}, f32[32,512]{1,0:T(8,128)}, u32[]{:S(2)}) copy-start(f32[32,512]{1,0:T(8,128)} %copy-done.31) | copy-start | bytes 196612
  470.7 24.2 %copy-start.34 = (bf16[32,512]{1,0:T(8,128)(2,1)S(1)}, bf16[32,512]{1,0:T(8,128)(2,1)}, u32[]{:S(2)}) copy-start(bf16[32,512]{1,0:T(8,128)(2,1)} %copy-done.33) | copy-start | bytes 98308
  470.7 24.2 %copy-start.38 = (f32[32,512]{1,0:T(8,128)S(1)}, f32[32,512]{1,0:T(8,128)}, u32[]{:S(2)}) copy-start(f32[32,512]{1,0:T(8,128)} %get-tuple-element.141) | copy-start | bytes 196612
  474.9 24.2 %copy-start.47 = (f32[32,1]{0,1:T(1,128)S(1)}, f32[32,1]{0,1:T(1,128)}, u32[]{:S(2)}) copy-start(f32[32,1]{0,1:T(1,128)} %copy-done.46) | copy-start | bytes 388
  474.9 17.4 %all-to-all-start.8 = ((bf16[8,32,2048]{2,1,0:T(8,128)(2,1)}), bf16[8,32,2048]{2,1,0:T(8,128)(2,1)S(1)}, u32[]{:S(2)}, u32[]{:S(2)}) async-start(bf16[8,32,2048]{2,1,0:T(8,128)(2,1)} %bitcast.74), calls=%async_computation.8 | async-start | bytes 2097152 | tf_op jit(solution)/shard_map/all_to_all | solution.py:27
  479.9 23.1 %copy-start.37 = (f32[32,512]{1,0:T(8,128)S(1)}, f32[32,512]{1,0:T(8,128)}, u32[]{:S(2)}) copy-start(f32[32,512]{1,0:T(8,128)} %copy-done.36) | copy-start | bytes 196612
  492.7 21.6 %copy-start.25 = (bf16[256,640]{1,0:T(8,128)(2,1)S(1)}, bf16[256,640]{1,0:T(8,128)(2,1)}, u32[]{:S(2)}) copy-start(bf16[256,640]{1,0:T(8,128)(2,1)} %copy-done.24) | copy-start | bytes 983044
  504.5 31.8 %copy-start.5 = (f32[256,640]{1,0:T(8,128)S(1)}, f32[256,640]{1,0:T(8,128)}, u32[]{:S(2)}) copy-start(f32[256,640]{1,0:T(8,128)} %copy-done.4) | copy-start | bytes 1966084
  506.6 25.9 %all-to-all-start.9 = ((bf16[8,32,2176]{2,1,0:T(8,128)(2,1)}), bf16[8,32,2176]{2,1,0:T(8,128)(2,1)S(1)}, u32[]{:S(2)}, u32[]{:S(2)}) async-start(bf16[8,32,2176]{2,1,0:T(8,128)(2,1)} %tile.14), calls=%async_computation.9 | async-start | bytes 2228224 | tf_op jit(solution)/shard_map/all_to_all | solution.py:27
  514.0 24.3 %copy-start.3 = (f32[256,640]{1,0:T(8,128)S(1)}, f32[256,640]{1,0:T(8,128)}, u32[]{:S(2)}) copy-start(f32[256,640]{1,0:T(8,128)} %copy-done.2) | copy-start | bytes 1966084
  514.0 117.6 %reduce-scatter.9.cloned.1.call-start = ((), (), s32[]{:S(2)}) async-start(), calls=%async_computation.19 | async-start | bytes 5570560
  557.6 15.6 %copy-start.12 = (f32[256,640]{1,0:T(8,128)S(1)}, f32[256,640]{1,0:T(8,128)}, u32[]{:S(2)}) copy-start(f32[256,640]{1,0:T(8,128)} %copy-done.11) | copy-start | bytes 1966084
  564.3 79.1 %copy-start.10 = (f32[256,640]{1,0:T(8,128)S(1)}, f32[256,640]{1,0:T(8,128)}, u32[]{:S(2)}) copy-start(f32[256,640]{1,0:T(8,128)} %copy-done.9) | copy-start | bytes 1966084
  566.8 91.3 %copy-start.8 = (f32[256,640]{1,0:T(8,128)S(1)}, f32[256,640]{1,0:T(8,128)}, u32[]{:S(2)}) copy-start(f32[256,640]{1,0:T(8,128)} %copy-done.7) | copy-start | bytes 1966084
  632.7 38.7 %copy-start.17 = (f32[1,320,512]{1,2,0:T(8,128)S(1)}, f32[1,320,512]{1,2,0:T(8,128)}, u32[]{:S(2)}) copy-start(f32[1,320,512]{1,2,0:T(8,128)} %copy.337) | copy-start | bytes 1966084
  635.4 23.5 %all-to-all-start.11 = ((bf16[8,32,640]{2,1,0:T(8,128)(2,1)}), bf16[8,32,640]{2,1,0:T(8,128)(2,1)}, u32[]{:S(2)}, u32[]{:S(2)}) async-start(bf16[8,32,640]{2,1,0:T(8,128)(2,1)} %copy.347), calls=%async_computation.11 | async-start | bytes 655360 | tf_op jit(solution)/shard_map/all_to_all | solution.py:27
  644.1 27.3 %copy-start.18 = (f32[1,320,512]{1,2,0:T(8,128)S(1)}, f32[1,320,512]{1,2,0:T(8,128)}, u32[]{:S(2)}) copy-start(f32[1,320,512]{1,2,0:T(8,128)} %copy.342) | copy-start | bytes 1966084
  645.9 25.4 %collective-permute-start.2 = (bf16[160,512]{0,1:T(8,128)(2,1)}, bf16[160,512]{0,1:T(8,128)(2,1)S(1)}, u32[]{:S(2)}, u32[]{:S(2)}) collective-permute-start(bf16[160,512]{0,1:T(8,128)(2,1)} %copy.372), channel_id=1, source_target_pairs={{1,64},{3,65},{5,80},{7,81},{9,96},{11,97},{13,112},{15,113},{17,6... | collective-permute-start | bytes 491528 | tf_op jit(solution)/shard_map/ppermute | solution.py:90
  651.7 19.6 %collective-permute-start.1 = (bf16[160,512]{0,1:T(8,128)(2,1)}, bf16[160,512]{0,1:T(8,128)(2,1)}, u32[]{:S(2)}, u32[]{:S(2)}) collective-permute-start(bf16[160,512]{0,1:T(8,128)(2,1)} %copy.372), channel_id=1, source_target_pairs={{0,64},{2,65},{4,80},{6,81},{8,96},{10,97},{12,112},{14,113},{16,6... | collective-permute-start | bytes 491528 | tf_op jit(solution)/shard_map/ppermute | solution.py:90
  653.9 17.4 %collective-permute-start.4 = (bf16[160,512]{0,1:T(8,128)(2,1)}, bf16[160,512]{0,1:T(8,128)(2,1)}, u32[]{:S(2)}, u32[]{:S(2)}) collective-permute-start(bf16[160,512]{0,1:T(8,128)(2,1)} %copy.373), channel_id=1, source_target_pairs={{1,0},{3,1},{5,16},{7,17},{9,32},{11,33},{13,48},{15,49},{17,2},{1... | collective-permute-start | bytes 491528 | tf_op jit(solution)/shard_map/ppermute | solution.py:90
  656.8 14.5 %collective-permute-start.3 = (bf16[160,512]{0,1:T(8,128)(2,1)}, bf16[160,512]{0,1:T(8,128)(2,1)}, u32[]{:S(2)}, u32[]{:S(2)}) collective-permute-start(bf16[160,512]{0,1:T(8,128)(2,1)} %copy.373), channel_id=1, source_target_pairs={{0,0},{2,1},{4,16},{6,17},{8,32},{10,33},{12,48},{14,49},{16,2},{1... | collective-permute-start | bytes 491528 | tf_op jit(solution)/shard_map/ppermute | solution.py:90
  658.9 60.0 %all-to-all-start.10 = ((bf16[8,256,640]{2,1,0:T(8,128)(2,1)}), bf16[8,256,640]{2,1,0:T(8,128)(2,1)}, u32[]{:S(2)}, u32[]{:S(2)}) async-start(bf16[8,256,640]{2,1,0:T(8,128)(2,1)} %bitcast_dynamic-update-slice_fusion), calls=%async_computation.10 | async-start | bytes 5242880 | tf_op jit(solution)/shard_map/all_to_all | solution.py:27
  676.5 7.2 copy-start.23
  676.7 9.6 %copy-start.29 = (bf16[320,512]{0,1:T(8,128)(2,1)S(1)}, bf16[320,512]{0,1:T(8,128)(2,1)}, u32[]{:S(2)}) copy-start(bf16[320,512]{0,1:T(8,128)(2,1)} %fusion.121) | copy-start | bytes 983044
  718.8 17.4 %all-to-all-start.12 = ((bf16[16,2,32,320]{3,2,1,0:T(8,128)(2,1)}), bf16[16,2,32,320]{3,2,1,0:T(8,128)(2,1)}, u32[]{:S(2)}, u32[]{:S(2)}) async-start(bf16[16,2,32,320]{3,2,1,0:T(8,128)(2,1)} %copy.357), calls=%async_computation.12 | async-start | bytes 1572864 | tf_op jit(solution)/shard_map/all_to_all | solution.py:27
  (19 other events, 48.8 us)
Sparse Core Ops, SparseCore 0:
  25.8 43.6 all-gather.3
  71.7 44.8 all-gather.5
  174.0 91.4 all-gather.7
  465.1 92.3 reduce-scatter.6
  559.8 71.8 reduce-scatter.8

commit v2 on v1

--- a/solution.py
+++ b/solution.py
@@ -12,6 +12,7 @@
 adam_step = 100
 
 BLOCKS = ((0, 4), (4, 8))
+LANES = 128
 
 
 def dot(left, right, dims):
@@ -65,16 +66,27 @@
 
 
 def reduce_grads(parts_in, parts_out, n_dp):
+    chunk, inner = parts_in[0].shape
     group = len(parts_in)
-    chunk, inner = parts_in[0].shape
-    rows = group * chunk // n_dp
     share = inner // n_dp
-    stacked_in = jnp.concatenate(parts_in, axis=0).reshape(n_dp, rows, inner)
-    stacked_out = jnp.stack(parts_out, axis=1).reshape(n_dp, share, group, chunk)
-    stacked_out = stacked_out.reshape(n_dp, rows, inner)
-    both = jnp.concatenate([stacked_in, stacked_out], axis=1).reshape(n_dp * 2 * rows, inner)
-    summed = lax.psum_scatter(both, "dp", scatter_dimension=0, tiled=True)
-    return summed[:rows], summed[rows:].reshape(share, group, chunk)
+    stacked_in = jnp.concatenate(parts_in, axis=0).reshape(n_dp, -1, inner // LANES, LANES)
+    stacked_out = jnp.concatenate(parts_out, axis=1).reshape(n_dp, share, -1, LANES)
+    both = jnp.concatenate(
+        [
+            stacked_in.transpose(0, 2, 1, 3).reshape(n_dp, -1, LANES),
+            stacked_out.transpose(0, 2, 1, 3).reshape(n_dp, -1, LANES),
+        ],
+        axis=1,
+    )
+    half = both.shape[1] // 2
+    summed = lax.psum_scatter(both.reshape(-1, LANES), "dp", scatter_dimension=0, tiled=True)
+
+    def finish(summed):
+        sum_in = summed[:half].reshape(inner // LANES, -1, LANES).transpose(1, 0, 2)
+        sum_out = summed[half:].reshape(group, chunk // LANES, share, LANES)
+        return sum_in.reshape(-1, inner), sum_out.transpose(0, 2, 1, 3).reshape(group, share, chunk)
+
+    return summed, finish
 
 
 def move_in(summed, first, group, n_pipe, n_dp):
@@ -89,14 +101,6 @@
                 pairs.append((i * n_dp + j, (first + section) * n_dp + 2 * i + half))
         moved.append(lax.ppermute(summed, ("pipe", "dp"), pairs))
     return jnp.concatenate(moved, axis=0)
-
-
-def gram_units(first, last):
-    units = []
-    for j in range(first, last - 1):
-        units += [(j, k, False) for k in range(j, last - 1)]
-        units += [(j, s, True) for s in range(j + 1, last)]
-    return units
 
 
 def on_device(
@@ -127,38 +131,54 @@
     weight_in = [all_in[s * chunk : (s + 1) * chunk] for s in range(n_pipe)]
     weight_out = [all_out[:, s * chunk : (s + 1) * chunk] for s in range(n_pipe)]
 
-    units = [unit for first, last in BLOCKS for unit in gram_units(first, last)]
-    padded = -(-len(units) // n_pipe) * n_pipe
-    partial = []
-    for j, other, down in units:
-        if down:
-            partial.append(dot(piece_out[j], weight_in[other], ROWS))
-        else:
-            partial.append(dot(piece_out[j], weight_out[other], LAST))
-    partial += [jnp.zeros_like(partial[0])] * (padded - len(units))
-    arrived = swap(jnp.stack(partial).astype(jnp.bfloat16), "pipe")
-    arrived = arrived.reshape(n_pipe, padded // n_pipe, share_out, inner)
-    mine = jnp.sum(arrived.astype(jnp.float32), axis=0).astype(jnp.bfloat16)
-    rows_of = swap(jnp.tile(mine, (n_pipe, 1, 1)), "pipe")
-    rows_of = rows_of.transpose(1, 0, 2).reshape(share_out, padded * inner)
-    gram_all = lax.all_gather(rows_of, "dp", axis=0, tiled=True)
-    gram = {
-        unit: gram_all[:, at * inner : (at + 1) * inner] for at, unit in enumerate(units)
-    }
+    gram = {}
+
+    def products(first, last):
+        units, partial = [], []
+        for t in range(first + 1, last):
+            left = piece_out[first:t].reshape(-1, chunk)
+            partial.append(dot(left, weight_in[t], ROWS))
+            units += [(k, t, True) for k in range(first, t)]
+        for t in range(first, last - 1):
+            left = piece_out[first : t + 1].reshape(-1, chunk)
+            partial.append(dot(left, weight_out[t], LAST))
+            units += [(k, t, False) for k in range(first, t + 1)]
+        padded = -(-len(units) // n_pipe) * n_pipe
+        partial = [p.astype(jnp.bfloat16) for p in partial]
+        partial.append(jnp.zeros(((padded - len(units)) * share_out, inner), jnp.bfloat16))
+        arrived = swap(jnp.concatenate(partial, axis=0), "pipe")
+        arrived = arrived.reshape(n_pipe, -1, inner)
+        mine = jnp.sum(arrived.astype(jnp.float32), axis=0).astype(jnp.bfloat16)
+        every = swap(jnp.tile(mine, (n_pipe, 1)), "pipe").reshape(padded, share_out, inner)
+        order = sorted(range(len(units)), key=lambda at: units[at])
+        columns = jnp.concatenate([every[at] for at in order], axis=1)
+        whole = lax.all_gather(columns, "dp", axis=0, tiled=True)
+        return [units[at] for at in order], whole
+
+    def unpack(units, whole):
+        for at, unit in enumerate(units):
+            gram[unit] = whole[:, at * inner : (at + 1) * inner]
+
+    made = [products(first, last) for first, last in BLOCKS]
 
     rows = lax.dynamic_slice_in_dim(inputs_x, me * chunk, chunk, 1)
     exact = rows.astype(jnp.float32)
     seed = lax.dynamic_slice_in_dim(cotangent, me * chunk, chunk, 1)
 
-    def grad_start(upstream, first, last):
-        sums = sum_to_owner(
-            [dot(upstream, weight_out[s], LAST) for s in range(first, last)], n_pipe
-        )
+    def grad_start(upstream, first, last, held=None):
+        columns = [dot(upstream, weight_out[s], LAST) for s in range(first, last)]
+        if held is not None:
+            columns, held = lax.optimization_barrier((columns, held))
+        sums = sum_to_owner(columns, n_pipe)
         return {
             s: sums[:, (s - first) * inner : (s - first + 1) * inner] for s in range(first, last)
-        }
-
-    grad_act = grad_start(seed, *BLOCKS[-1])
+        }, held
+
+    grad_act, _ = grad_start(seed, *BLOCKS[-1])
+    whole, grad_act = lax.optimization_barrier((made[0][1], grad_act))
+    unpack(made[0][0], whole)
+    for later, whole in made[1:]:
+        unpack(later, whole)
     saved_rows, saved_act, state = {}, {}, {}
 
     def forward_block(first, last):
@@ -242,17 +262,14 @@
         is_last = number == len(BLOCKS) - 1
         if is_last:
             forward_block(first, last)
-        else:
-            grad_act.update(grad_start(upstream, first, last))
+            acts = gather_rows([state[s][3] for s in range(first, last)], n_pipe)
         packs, pulls = backward_block(first, last)
         columns = [packs[s] for s in range(first, last)]
-        if is_last:
-            columns += [state[s][3] for s in range(first, last)]
         columns += split_scalars([pulls[s] for s in range(first, last)])
         gathered = gather_rows(columns, n_pipe)
         if is_last:
-            take_rows(gathered[:, count * inner :], first, last, False)
-        scalar_at = gathered.shape[1] - 128
+            take_rows(acts, first, last, False)
+        scalar_at = count * inner
         parts_in, parts_out = {}, {}
         for s in reversed(range(first, last)):
             pack = gathered[:, (s - first) * inner : (s - first + 1) * inner]
@@ -266,22 +283,28 @@
             )
             upstream = upstream_exact.astype(jnp.bfloat16)
             grads[s] = upstream
-        reduced[first] = reduce_grads(
-            [parts_in[s] for s in range(first, last)],
-            [parts_out[s] for s in range(first, last)],
-            n_dp,
-        )
+        pending = [parts_in[s] for s in range(first, last)], [
+            parts_out[s] for s in range(first, last)
+        ]
+        if number > 0:
+            following, pending = grad_start(upstream, *BLOCKS[number - 1], pending)
+            grad_act.update(following)
+        reduced[first] = reduce_grads(*pending, n_dp)
 
     input_grads = swap(jnp.stack(grads), "pipe")
+    first = BLOCKS[0][0]
+    input_grads, summed = lax.optimization_barrier((input_grads, reduced[first][0]))
+    reduced[first] = (summed, reduced[first][1])
     input_grads = input_grads.transpose(1, 0, 2).reshape(1, tok_rows, width)
 
     grad_in = jnp.zeros((share_in, inner), jnp.bfloat16)
     outs = []
     for first, last in BLOCKS:
-        sum_in, sum_out = reduced[first]
+        summed, finish = reduced[first]
+        sum_in, sum_out = finish(summed)
         moved = move_in(sum_in, first, last - first, n_pipe, n_dp)
         grad_in = jnp.where((me >= first) & (me < last), moved, grad_in)
-        outs.append(sum_out.transpose(1, 0, 2))
+        outs.append(sum_out)
     grad_out = swap(jnp.concatenate(outs, axis=0), "pipe")
     grad_out = grad_out.transpose(1, 0, 2).reshape(share_out, width)
 

time: 760 us -> 733 us (0.964)
  waiting for transfers between devices: 299 us -> 257 us
  blocking collectives: 80.7 us -> 115 us
  matrix products: 166 us -> 144 us
    unnamed x7 -> x6, waiting for transfers between devices: 55.3 us -> 0.1 us
    reduce_scatter x0 -> x2, waiting for transfers between devices: none -> 53.6 us  [reduce_grads(): lax.psum_scatter(both.reshape(-1, LANES), 'dp', scatter_dimension=0, tile...]
    all_gather x1 -> x2, waiting for transfers between devices: 37.6 us -> 0.04 us  [products(): whole = lax.all_gather(columns, 'dp', axis=0, tiled=True)]
    all_to_all x4 -> x5, blocking collectives: 80.7 us -> 115 us  [swap(): return lax.all_to_all(x, axis, 0, 0, tiled=True)]
    reshape x3 -> x9, local copies, waits for them, and re-layouts: 2.47 us -> 25.5 us  [the longest x4 14.7 us: reduce_grads(): jnp.concatenate(parts_in, axis=0).reshape(n_dp, -1, inner // LANES, LANES)]
    dot_general x119 -> x107, matrix products: 166 us -> 144 us  [dot(): lax.dot_general(left, right, (dims, ((), ())), preferred_element_type=jnp...]
    all_gather x1, waiting for transfers between devices: 43 us -> 23.8 us  [on_device(): all_in = lax.all_gather(piece_in, 'dp', axis=0, tiled=True)]
    all_to_all x9 -> x11, waiting for transfers between devices: 123 us -> 141 us  [swap(): return lax.all_to_all(x, axis, 0, 0, tiled=True)]
  transfers between devices with their start and end apart: 19 -> 22, of which waited for: 11 -> 14; matrix products, arithmetic and copies ran while one was open for 22% -> 24% of each run, Pallas kernels for 0% -> 0%
where the time goes in v2:
time: 733 us; the launch traced here: 720 us
  waiting for transfers between devices  257 us (35%)
  matrix products  144 us (20%)
  blocking collectives  115 us (16%)
  local copies, waits for them, and re-layouts  80.2 us (11%)
  starting transfers between devices  69.2 us (9%)
  other arithmetic  39.2 us (5%)
  between operations  16.3 us (2%)
    dot_general x107, matrix products, dot(): lax.dot_general(left, right, (dims, ((), ())), preferred_element_type=jnp...  144 us
    all_to_all x11, waiting for transfers between devices, swap(): return lax.all_to_all(x, axis, 0, 0, tiled=True)  141 us
    all_to_all x5, blocking collectives, swap(): return lax.all_to_all(x, axis, 0, 0, tiled=True)  115 us
    all_to_all x11, starting transfers between devices, swap(): return lax.all_to_all(x, axis, 0, 0, tiled=True)  57.6 us
    reduce_scatter x2, waiting for transfers between devices, reduce_grads(): lax.psum_scatter(both.reshape(-1, LANES), 'dp', scatter_dimension=0, tile...  53.6 us
    all_gather x1, waiting for transfers between devices, on_device(): all_out = lax.all_gather(flat_out, 'dp', axis=0, tiled=True)  37.9 us
    all_gather x1, waiting for transfers between devices, on_device(): all_in = lax.all_gather(piece_in, 'dp', axis=0, tiled=True)  23.8 us
    unnamed x198, local copies, waits for them, and re-layouts  16.9 us
  transfers between devices with their start and end apart: 22, of which 14 were waited for; matrix products, arithmetic and copies ran while one was open for 24% of the time, Pallas kernels for 0%

profile of v2, /device:TPU:1, one launch (start us, length us, event | category | flops | bytes accessed | tf_op | source)
XLA Modules:
  0.0 720.5 jit_solution(4824511222339306235)
XLA Ops:
  11.1 37.5 %all_to_all.122 = bf16[8,32,640]{2,1,0:T(8,128)(2,1)S(1)} all-to-all(bf16[8,32,640]{2,1,0:T(8,128)(2,1)S(1)} %copy.288), channel_id=1, replica_groups=mesh['pipe'=8,'dp'=16] {'pipe'}, dimensions={0} | all-to-all | bytes 655360 | tf_op jit(solution)/shard_map/all_to_all | solution.py:28
  49.5 23.8 %all-gather.5.cloned.1.call-done = bf16[5120,512]{1,0:T(8,128)(2,1)} async-done(((bf16[320,512]{1,0:T(8,128)(2,1)}), bf16[5120,512]{1,0:T(8,128)(2,1)}) %all-gather.5.cloned.1.call-update) | async-done | bytes 5242896 | tf_op jit(solution)/shard_map/all_gather | solution.py:129
  77.3 37.9 %all-gather.7.cloned.1.call-done = bf16[512,5120]{1,0:T(8,128)(2,1)} async-done(((bf16[32,5120]{1,0:T(8,128)(2,1)}), bf16[512,5120]{1,0:T(8,128)(2,1)}) %all-gather.7.cloned.1.call-update) | async-done | bytes 5242896 | tf_op jit(solution)/shard_map/all_gather | solution.py:130
  119.4 16.0 %all_to_all.123 = bf16[8,64,512]{2,1,0:T(8,128)(2,1)S(1)} all-to-all(bf16[8,64,512]{2,1,0:T(8,128)(2,1)S(1)} %bitcast.370), channel_id=1, replica_groups=mesh['pipe'=8,'dp'=16] {'pipe'}, dimensions={0} | all-to-all | bytes 1048576 | tf_op jit(solution)/shard_map/all_to_all | solution.py:28
  135.5 13.1 %all_to_all.124 = bf16[8,64,512]{2,1,0:T(8,128)(2,1)S(1)} all-to-all(bf16[8,64,512]{2,1,0:T(8,128)(2,1)S(1)} %tile.12), channel_id=1, replica_groups=mesh['pipe'=8,'dp'=16] {'pipe'}, dimensions={0} | all-to-all | bytes 1048576 | tf_op jit(solution)/shard_map/all_to_all | solution.py:28
  172.5 3.5 all-to-all-start.7
  179.2 5.4 all-to-all-done.7
  185.5 6.3 all-to-all-start.8
  197.0 3.4 all-to-all-done.8
  200.4 5.7 all-to-all-start.3
  206.2 15.5 %all-to-all-done.3 = bf16[8,32,2048]{2,1,0:T(8,128)(2,1)S(1)} async-done(((bf16[8,32,2048]{2,1,0:T(8,128)(2,1)}), bf16[8,32,2048]{2,1,0:T(8,128)(2,1)S(1)}, u32[]{:S(2)}, u32[]{:S(2)}) %all-to-all-start.3) | async-done | bytes 1048608 | tf_op jit(solution)/shard_map/all_to_all | solution.py:28
  221.7 3.9 all-to-all-start.4
  230.3 22.5 %all-to-all-done.4 = bf16[8,32,3712]{2,1,0:T(8,128)(2,1)S(1)} async-done(((bf16[8,32,3712]{2,1,0:T(8,128)(2,1)}), bf16[8,32,3712]{2,1,0:T(8,128)(2,1)S(1)}, u32[]{:S(2)}, u32[]{:S(2)}) %all-to-all-start.4) | async-done | bytes 1900576 | tf_op jit(solution)/shard_map/all_to_all | solution.py:28
  273.1 20.3 %all_to_all.125 = bf16[8,32,2048]{2,1,0:T(8,128)(2,1)S(1)} all-to-all(bf16[8,32,2048]{2,1,0:T(8,128)(2,1)S(1)} %tile.13), channel_id=1, replica_groups=mesh['pipe'=8,'dp'=16] {'pipe'}, dimensions={0} | all-to-all | bytes 2097152 | tf_op jit(solution)/shard_map/all_to_all | solution.py:28
  314.6 27.7 %all_to_all.126 = bf16[8,32,3712]{2,1,0:T(8,128)(2,1)S(1)} all-to-all(bf16[8,32,3712]{2,1,0:T(8,128)(2,1)S(1)} %concatenate.151), channel_id=1, replica_groups=mesh['pipe'=8,'dp'=16] {'pipe'}, dimensions={0} | all-to-all | bytes 3801088 | tf_op jit(solution)/shard_map/all_to_all | solution.py:28
  358.4 3.7 all-to-all-start.10
  369.7 5.1 all-to-all-done.10
  375.9 6.7 all-to-all-start.9
  390.0 8.8 %all-to-all-done.9 = bf16[8,32,2176]{2,1,0:T(8,128)(2,1)S(1)} async-done(((bf16[8,32,2176]{2,1,0:T(8,128)(2,1)}), bf16[8,32,2176]{2,1,0:T(8,128)(2,1)S(1)}, u32[]{:S(2)}, u32[]{:S(2)}) %all-to-all-start.9) | async-done | bytes 1114144 | tf_op jit(solution)/shard_map/all_to_all | solution.py:28
  412.1 2.3 fusion.255
  420.5 4.2 reshape.538
  428.5 5.1 reshape.536
  433.6 2.3 copy.317
  435.9 2.6 pad_maximum_fusion.1
  440.8 4.3 all-to-all-start.11
  446.5 19.6 %all-to-all-done.11 = bf16[8,32,2048]{2,1,0:T(8,128)(2,1)S(1)} async-done(((bf16[8,32,2048]{2,1,0:T(8,128)(2,1)}), bf16[8,32,2048]{2,1,0:T(8,128)(2,1)S(1)}, u32[]{:S(2)}, u32[]{:S(2)}) %all-to-all-start.11) | async-done | bytes 1048608 | tf_op jit(solution)/shard_map/all_to_all | solution.py:28
  479.6 5.2 all-to-all-start.12
  487.2 24.8 %all-to-all-done.12 = bf16[8,32,2176]{2,1,0:T(8,128)(2,1)S(1)} async-done(((bf16[8,32,2176]{2,1,0:T(8,128)(2,1)}), bf16[8,32,2176]{2,1,0:T(8,128)(2,1)S(1)}, u32[]{:S(2)}, u32[]{:S(2)}) %all-to-all-start.12) | async-done | bytes 1114144 | tf_op jit(solution)/shard_map/all_to_all | solution.py:28
  522.4 4.2 reshape.532
  532.8 5.1 reshape.530
  537.9 2.3 copy.314
  540.2 2.7 pad_maximum_fusion
  544.0 2.6 fusion.11
  551.9 3.8 all-to-all-start.13
  555.8 2.3 squeeze.7
  560.4 5.9 collective-permute-start.2
  567.6 28.9 %all-to-all-done.13 = bf16[8,256,640]{2,1,0:T(8,128)(2,1)S(1)} async-done(((bf16[8,256,640]{2,1,0:T(8,128)(2,1)}), bf16[8,256,640]{2,1,0:T(8,128)(2,1)S(1)}, u32[]{:S(2)}, u32[]{:S(2)}) %all-to-all-start.13) | async-done | bytes 2621472 | tf_op jit(solution)/shard_map/all_to_all | solution.py:28
  596.5 53.6 %reduce-scatter.3.cloned.1.call-done = bf16[1280,128]{1,0:T(8,128)(2,1)} async-done(((bf16[20480,128]{1,0:T(8,128)(2,1)}), bf16[1280,128]{1,0:T(8,128)(2,1)}) %reduce-scatter.3.cloned.1.call-update) | async-done | bytes 327696 | tf_op jit(solution)/shard_map/reduce_scatter | solution.py:82
  657.1 6.5 all-to-all-start.14
  663.6 2.8 fusion.182
  668.3 4.3 all-to-all-done.14
  676.1 3.6 multiply_subtract_fusion
  684.1 2.8 fusion.181
  689.1 8.0 %all-to-all-start.15 = ((bf16[16,2,32,320]{3,2,1,0:T(8,128)(2,1)}), bf16[16,2,32,320]{3,2,1,0:T(8,128)(2,1)}, u32[]{:S(2)}, u32[]{:S(2)}) async-start(bf16[16,2,32,320]{3,2,1,0:T(8,128)(2,1)} %copy.333), calls=%async_computation.17 | async-start | bytes 1572864 | tf_op jit(solution)/shard_map/all_to_all | solution.py:28
  697.2 2.6 copy.316
  699.8 4.5 copy.335
  704.3 2.7 multiply_subtract_fusion.1
  707.0 2.9 all-to-all-done.15
  (445 shorter events, 214.7 us)
Async XLA Ops:
  7.2 66.1 %all-gather.5.cloned.1.call-start = ((), (), s32[]{:S(2)}) async-start(), calls=%async_computation.18 | async-start | bytes 5570560 | tf_op jit(solution)/shard_map/all_gather | solution.py:129
  8.4 0.7 collective-permute-start
  9.8 105.4 %all-gather.7.cloned.1.call-start = ((), (), s32[]{:S(2)}) async-start(), calls=%async_computation.19 | async-start | bytes 5570560 | tf_op jit(solution)/shard_map/all_gather | solution.py:130
  49.4 204.0 %all-gather.9.cloned.1.call-start = ((), (), s32[]{:S(2)}) async-start(), calls=%async_computation.20 | async-start | bytes 6684672 | tf_op jit(solution)/shard_map/all_gather | solution.py:155
  172.5 12.1 %all-to-all-start.7 = ((bf16[8,64,512]{2,1,0:T(8,128)(2,1)}), bf16[8,64,512]{2,1,0:T(8,128)(2,1)S(1)}, u32[]{:S(2)}, u32[]{:S(2)}) async-start(bf16[8,64,512]{2,1,0:T(8,128)(2,1)} %bitcast.35), calls=%async_computation.7 | async-start | bytes 1048576 | tf_op jit(solution)/shard_map/all_to_all | solution.py:28
  185.5 14.9 %all-to-all-start.8 = ((bf16[8,64,512]{2,1,0:T(8,128)(2,1)}), bf16[8,64,512]{2,1,0:T(8,128)(2,1)S(1)}, u32[]{:S(2)}, u32[]{:S(2)}) async-start(bf16[8,64,512]{2,1,0:T(8,128)(2,1)} %tile.14), calls=%async_computation.8 | async-start | bytes 1048576 | tf_op jit(solution)/shard_map/all_to_all | solution.py:28
  195.0 26.8 %copy-start.49 = (bf16[8,32,126]{2,1,0:T(8,128)(2,1)}, bf16[8,32,126]{2,1,0:T(8,128)(2,1)S(1)}, u32[]{:S(2)}) copy-start(bf16[8,32,126]{2,1,0:T(8,128)(2,1)S(1)} %concatenate.141) | copy-start | bytes 193540
  200.4 21.3 %all-to-all-start.3 = ((bf16[8,32,2048]{2,1,0:T(8,128)(2,1)}), bf16[8,32,2048]{2,1,0:T(8,128)(2,1)S(1)}, u32[]{:S(2)}, u32[]{:S(2)}) async-start(bf16[8,32,2048]{2,1,0:T(8,128)(2,1)} %bitcast.8), calls=%async_computation.3 | async-start | bytes 2097152 | tf_op jit(solution)/shard_map/all_to_all | solution.py:28
  206.2 15.5 %copy-start.54 = (bf16[32,6144]{1,0:T(8,128)(2,1)}, bf16[32,6144]{1,0:T(8,128)(2,1)S(1)}, u32[]{:S(2)}) copy-start(bf16[32,6144]{1,0:T(8,128)(2,1)S(1)} %constant_dynamic-update-slice_fusion.20) | copy-start | bytes 1179652
  221.7 31.0 %all-to-all-start.4 = ((bf16[8,32,3712]{2,1,0:T(8,128)(2,1)}), bf16[8,32,3712]{2,1,0:T(8,128)(2,1)S(1)}, u32[]{:S(2)}, u32[]{:S(2)}) async-start(bf16[8,32,3712]{2,1,0:T(8,128)(2,1)} %concatenate.142), calls=%async_computation.4 | async-start | bytes 3801088 | tf_op jit(solution)/shard_map/all_to_all | solution.py:28
  225.7 117.3 %all-gather.11.cloned.1.call-start = ((), (), s32[]{:S(2)}) async-start(), calls=%async_computation.21 | async-start | bytes 6684672 | tf_op jit(solution)/shard_map/all_gather | solution.py:155
  252.8 40.7 %slice-start = ((s8[5242880]{0:T(1024)(128)(4,1)}), s8[1048576]{0:T(1024)(128)(4,1)S(1)}, s32[]{:S(2)}) async-start(s8[5242880]{0:T(1024)(128)(4,1)} %bitcast.331), calls=%async_computation.24 | async-start | bytes 2097152
  253.0 20.1 %copy-start.46 = (f32[32,3712]{1,0:T(8,128)}, f32[32,3712]{1,0:T(8,128)S(1)}, u32[]{:S(2)}) copy-start(f32[32,3712]{1,0:T(8,128)S(1)} %convert_reduce_fusion.1) | copy-start | bytes 1425412
  256.7 16.3 %copy-start.51 = (f32[32,512]{1,0:T(8,128)}, f32[32,512]{1,0:T(8,128)S(1)}, u32[]{:S(2)}) copy-start(f32[32,512]{1,0:T(8,128)S(1)} %convolution_add_fusion.47) | copy-start | bytes 196612
  260.6 34.5 %copy-start.72 = (f32[32,1]{0,1:T(1,128)}, f32[32,1]{0,1:T(1,128)S(1)}, u32[]{:S(2)}) copy-start(f32[32,1]{0,1:T(1,128)S(1)} %get-tuple-element.138) | copy-start | bytes 388
  263.1 30.3 %slice-start.1 = ((s8[5242880]{0:T(1024)(128)(4,1)}), s8[4194304]{0:T(1024)(128)(4,1)S(1)}, s32[]{:S(2)}) async-start(s8[5242880]{0:T(1024)(128)(4,1)} %bitcast.331), calls=%async_computation.25 | async-start | bytes 8388608
  268.5 27.8 %copy-start.70 = (f32[32,1]{0,1:T(1,128)}, f32[32,1]{0,1:T(1,128)S(1)}, u32[]{:S(2)}) copy-start(f32[32,1]{0,1:T(1,128)S(1)} %add_rsqrt_fusion.4) | copy-start | bytes 388
  299.6 15.0 %copy-start.32 = (bf16[256,640]{1,0:T(8,128)(2,1)}, bf16[256,640]{1,0:T(8,128)(2,1)S(1)}, u32[]{:S(2)}) copy-start(bf16[256,640]{1,0:T(8,128)(2,1)S(1)} %get-tuple-element.148) | copy-start | bytes 983044
  358.4 26.5 %copy-start.45 = (f32[256,640]{1,0:T(8,128)S(1)}, f32[256,640]{1,0:T(8,128)}, u32[]{:S(2)}) copy-start(f32[256,640]{1,0:T(8,128)} %get-tuple-element.194) | copy-start | bytes 1966084
  358.4 16.4 %all-to-all-start.10 = ((bf16[8,32,2048]{2,1,0:T(8,128)(2,1)}), bf16[8,32,2048]{2,1,0:T(8,128)(2,1)S(1)}, u32[]{:S(2)}, u32[]{:S(2)}) async-start(bf16[8,32,2048]{2,1,0:T(8,128)(2,1)} %tile.16), calls=%async_computation.10 | async-start | bytes 2097152 | tf_op jit(solution)/shard_map/all_to_all | solution.py:28
  375.9 22.8 %all-to-all-start.9 = ((bf16[8,32,2176]{2,1,0:T(8,128)(2,1)}), bf16[8,32,2176]{2,1,0:T(8,128)(2,1)S(1)}, u32[]{:S(2)}, u32[]{:S(2)}) async-start(bf16[8,32,2176]{2,1,0:T(8,128)(2,1)} %tile.15), calls=%async_computation.9 | async-start | bytes 2228224 | tf_op jit(solution)/shard_map/all_to_all | solution.py:28
  382.6 175.4 %reduce-scatter.5.cloned.1.call-start = ((), (), s32[]{:S(2)}) async-start(), calls=%async_computation.23 | async-start | bytes 5570560 | tf_op jit(solution)/shard_map/reduce_scatter | solution.py:82
  414.5 70.4 %copy-start.35 = (bf16[256,640]{1,0:T(8,128)(2,1)}, bf16[256,640]{1,0:T(8,128)(2,1)S(1)}, u32[]{:S(2)}) copy-start(bf16[256,640]{1,0:T(8,128)(2,1)S(1)} %get-tuple-element.205) | copy-start | bytes 983044
  438.6 27.7 %copy-start.67 = (f32[32,512]{1,0:T(8,128)S(1)}, f32[32,512]{1,0:T(8,128)}, u32[]{:S(2)}) copy-start(f32[32,512]{1,0:T(8,128)} %get-tuple-element.193) | copy-start | bytes 196612
  438.6 27.7 %copy-start.71 = (f32[32,1]{0,1:T(1,128)S(1)}, f32[32,1]{0,1:T(1,128)}, u32[]{:S(2)}) copy-start(f32[32,1]{0,1:T(1,128)} %copy-done.70) | copy-start | bytes 388
  438.6 27.9 %copy-start.59 = (f32[32,512]{1,0:T(8,128)S(1)}, f32[32,512]{1,0:T(8,128)}, u32[]{:S(2)}) copy-start(f32[32,512]{1,0:T(8,128)} %copy-done.58) | copy-start | bytes 196612
  438.6 27.9 %copy-start.66 = (f32[32,512]{1,0:T(8,128)S(1)}, f32[32,512]{1,0:T(8,128)}, u32[]{:S(2)}) copy-start(f32[32,512]{1,0:T(8,128)} %get-tuple-element.191) | copy-start | bytes 196612
  438.6 27.9 %copy-start.75 = (f32[32]{0:T(128)S(1)}, f32[32]{0:T(128)}, u32[]{:S(2)}) copy-start(f32[32]{0:T(128)} %copy-done.74) | copy-start | bytes 388
  438.6 27.9 %copy-start.78 = (f32[32,512]{1,0:T(8,128)S(1)}, f32[32,512]{1,0:T(8,128)}, u32[]{:S(2)}) copy-start(f32[32,512]{1,0:T(8,128)} %get-tuple-element.189) | copy-start | bytes 196612
  438.6 29.3 %copy-start.73 = (f32[32,1]{0,1:T(1,128)S(1)}, f32[32,1]{0,1:T(1,128)}, u32[]{:S(2)}) copy-start(f32[32,1]{0,1:T(1,128)} %copy-done.72) | copy-start | bytes 388
  438.6 29.3 %copy-start.52 = (f32[32,512]{1,0:T(8,128)S(1)}, f32[32,512]{1,0:T(8,128)}, u32[]{:S(2)}) copy-start(f32[32,512]{1,0:T(8,128)} %copy-done.51) | copy-start | bytes 196612
  438.6 29.3 %copy-start.57 = (f32[32,512]{1,0:T(8,128)S(1)}, f32[32,512]{1,0:T(8,128)}, u32[]{:S(2)}) copy-start(f32[32,512]{1,0:T(8,128)} %get-tuple-element.187) | copy-start | bytes 196612
  439.7 31.0 %copy-start.77 = (f32[32,1]{0,1:T(1,128)S(1)}, f32[32,1]{0,1:T(1,128)}, u32[]{:S(2)}) copy-start(f32[32,1]{0,1:T(1,128)} %copy-done.76) | copy-start | bytes 388
  439.7 31.0 %copy-start.79 = (f32[32,512]{1,0:T(8,128)S(1)}, f32[32,512]{1,0:T(8,128)}, u32[]{:S(2)}) copy-start(f32[32,512]{1,0:T(8,128)} %get-tuple-element.185) | copy-start | bytes 196612
  440.8 25.3 %all-to-all-start.11 = ((bf16[8,32,2048]{2,1,0:T(8,128)(2,1)}), bf16[8,32,2048]{2,1,0:T(8,128)(2,1)S(1)}, u32[]{:S(2)}, u32[]{:S(2)}) async-start(bf16[8,32,2048]{2,1,0:T(8,128)(2,1)} %bitcast.52), calls=%async_computation.11 | async-start | bytes 2097152 | tf_op jit(solution)/shard_map/all_to_all | solution.py:28
  469.3 43.1 %copy-start.17 = (f32[256,640]{1,0:T(8,128)S(1)}, f32[256,640]{1,0:T(8,128)}, u32[]{:S(2)}) copy-start(f32[256,640]{1,0:T(8,128)} %copy-done.16) | copy-start | bytes 1966084
  477.6 38.4 %copy-start.14 = (f32[256,640]{1,0:T(8,128)S(1)}, f32[256,640]{1,0:T(8,128)}, u32[]{:S(2)}) copy-start(f32[256,640]{1,0:T(8,128)} %copy-done.13) | copy-start | bytes 1966084
  479.6 32.3 %all-to-all-start.12 = ((bf16[8,32,2176]{2,1,0:T(8,128)(2,1)}), bf16[8,32,2176]{2,1,0:T(8,128)(2,1)S(1)}, u32[]{:S(2)}, u32[]{:S(2)}) async-start(bf16[8,32,2176]{2,1,0:T(8,128)(2,1)} %tile.17), calls=%async_computation.12 | async-start | bytes 2228224 | tf_op jit(solution)/shard_map/all_to_all | solution.py:28
  484.8 33.2 %copy-start.5 = (f32[256,640]{1,0:T(8,128)S(1)}, f32[256,640]{1,0:T(8,128)}, u32[]{:S(2)}) copy-start(f32[256,640]{1,0:T(8,128)} %copy-done.4) | copy-start | bytes 1966084
  484.8 165.3 %reduce-scatter.3.cloned.1.call-start = ((), (), s32[]{:S(2)}) async-start(), calls=%async_computation.22 | async-start | bytes 5570560 | tf_op jit(solution)/shard_map/reduce_scatter | solution.py:82
  551.9 111.7 %copy-start.26 = (f32[1,320,512]{2,1,0:T(8,128)S(1)}, f32[1,320,512]{2,1,0:T(8,128)}, u32[]{:S(2)}) copy-start(f32[1,320,512]{2,1,0:T(8,128)} %param.10) | copy-start | bytes 1966084
  551.9 44.6 %all-to-all-start.13 = ((bf16[8,256,640]{2,1,0:T(8,128)(2,1)}), bf16[8,256,640]{2,1,0:T(8,128)(2,1)S(1)}, u32[]{:S(2)}, u32[]{:S(2)}) async-start(bf16[8,256,640]{2,1,0:T(8,128)(2,1)} %bitcast_dynamic-update-slice_fusion), calls=%async_computation.13 | async-start | bytes 5242880 | tf_op jit(solution)/shard_map/all_to_all | solution.py:28
  560.4 103.2 %collective-permute-start.2 = (bf16[160,512]{1,0:T(8,128)(2,1)}, bf16[160,512]{1,0:T(8,128)(2,1)S(1)}, u32[]{:S(2)}, u32[]{:S(2)}) collective-permute-start(bf16[160,512]{1,0:T(8,128)(2,1)} %bitcast.287), channel_id=1, source_target_pairs={{1,64},{3,65},{5,80},{7,81},{9,96},{11,97},{13,112},{15,113},{17,6... | collective-permute-start | bytes 491528 | tf_op jit(solution)/shard_map/ppermute | solution.py:102
  566.3 97.3 %collective-permute-start.1 = (bf16[160,512]{1,0:T(8,128)(2,1)}, bf16[160,512]{1,0:T(8,128)(2,1)}, u32[]{:S(2)}, u32[]{:S(2)}) collective-permute-start(bf16[160,512]{1,0:T(8,128)(2,1)} %bitcast.287), channel_id=1, source_target_pairs={{0,64},{2,65},{4,80},{6,81},{8,96},{10,97},{12,112},{14,113},{16,6... | collective-permute-start | bytes 491528 | tf_op jit(solution)/shard_map/ppermute | solution.py:102
  651.9 11.7 %collective-permute-start.4 = (bf16[160,512]{1,0:T(8,128)(2,1)}, bf16[160,512]{1,0:T(8,128)(2,1)}, u32[]{:S(2)}, u32[]{:S(2)}) collective-permute-start(bf16[160,512]{1,0:T(8,128)(2,1)} %bitcast.286), channel_id=1, source_target_pairs={{1,0},{3,1},{5,16},{7,17},{9,32},{11,33},{13,48},{15,49},{17,2},{1... | collective-permute-start | bytes 491528 | tf_op jit(solution)/shard_map/ppermute | solution.py:102
  654.1 9.5 %collective-permute-start.3 = (bf16[160,512]{1,0:T(8,128)(2,1)}, bf16[160,512]{1,0:T(8,128)(2,1)}, u32[]{:S(2)}, u32[]{:S(2)}) collective-permute-start(bf16[160,512]{1,0:T(8,128)(2,1)} %bitcast.286), channel_id=1, source_target_pairs={{0,0},{2,1},{4,16},{6,17},{8,32},{10,33},{12,48},{14,49},{16,2},{1... | collective-permute-start | bytes 491528 | tf_op jit(solution)/shard_map/ppermute | solution.py:102
  657.1 15.5 %all-to-all-start.14 = ((bf16[8,32,640]{2,1,0:T(8,128)(2,1)}), bf16[8,32,640]{2,1,0:T(8,128)(2,1)}, u32[]{:S(2)}, u32[]{:S(2)}) async-start(bf16[8,32,640]{2,1,0:T(8,128)(2,1)} %pad_maximum_fusion.9), calls=%async_computation.16 | async-start | bytes 655360 | tf_op jit(solution)/shard_map/all_to_all | solution.py:28
  689.1 20.8 %all-to-all-start.15 = ((bf16[16,2,32,320]{3,2,1,0:T(8,128)(2,1)}), bf16[16,2,32,320]{3,2,1,0:T(8,128)(2,1)}, u32[]{:S(2)}, u32[]{:S(2)}) async-start(bf16[16,2,32,320]{3,2,1,0:T(8,128)(2,1)} %copy.333), calls=%async_computation.17 | async-start | bytes 1572864 | tf_op jit(solution)/shard_map/all_to_all | solution.py:28
  (58 other events, 316.2 us)
Sparse Core Ops, SparseCore 0:
  10.3 62.9 all-gather.4
  75.6 39.5 all-gather.6
  149.6 49.8 all-gather.8
  229.6 50.0 all-gather.10
  438.8 100.0 reduce-scatter.4
  543.1 107.0 reduce-scatter.2

commit v3 on v2

v3 whole, which is shorter than its diff:
```python
import jax
import jax.numpy as jnp
from jax import lax
from jax.experimental import pallas as pl
from jax.experimental.pallas import tpu as pltpu
from jax.sharding import PartitionSpec as P

norm_eps = 1e-06
beta_one = 0.9
beta_two = 0.999
learn_rate = 0.02
decay_rate = 0.1
adam_eps = 1e-08
adam_step = 100

BLOCKS = ((0, 4), (4, 8))
LANES = 128
VMEM_BYTES = 48 * 1024 * 1024


def dot(left, right, dims):
    return lax.dot_general(left, right, (dims, ((), ())), preferred_element_type=jnp.float32)


ROWS = ((1,), (0,))
LAST = ((1,), (1,))
FIRST = ((0,), (0,))


def swap(x, axis):
    return lax.all_to_all(x, axis, 0, 0, tiled=True)


def split_scalars(scalars):
    columns = []
    for value in scalars:
        high = value.astype(jnp.bfloat16)
        columns += [high, (value - high.astype(jnp.float32)).astype(jnp.bfloat16)]
    columns.append(jnp.zeros((scalars[0].shape[0], 128 - len(columns)), jnp.bfloat16))
    return columns


def exchanged(columns, count):
    packed = columns
    if isinstance(columns, list):
        packed = jnp.concatenate([c.astype(jnp.bfloat16) for c in columns], axis=1)
    return swap(packed, "pipe").reshape(count, packed.shape[0] // count, packed.shape[1])


def adam_update(master, moment, second, grad):
    moment_new = beta_one * moment + (1.0 - beta_one) * grad
    second_new = beta_two * second + (1.0 - beta_two) * grad * grad
    moment_hat = moment_new / (1.0 - beta_one**adam_step)
    second_hat = second_new / (1.0 - beta_two**adam_step)
    master_new = master - learn_rate * (
        moment_hat / (jnp.sqrt(second_hat) + adam_eps) + decay_rate * master
    )
    return (master_new, moment_new, second_new)


def run(kernel, shapes, *operands):
    return pl.pallas_call(
        kernel,
        out_shape=[jax.ShapeDtypeStruct(shape, kind) for shape, kind in shapes],
        compiler_params=pltpu.CompilerParams(vmem_limit_bytes=VMEM_BYTES),
    )(*operands)


def part(ref, at, inner):
    return ref[:, at * inner : (at + 1) * inner]


def scalar_block(scalars):
    lane = lax.broadcasted_iota(jnp.int32, (scalars[0].shape[0], LANES), 1)
    packed = jnp.zeros(lane.shape, jnp.float32)
    for at, value in enumerate(scalars):
        high = value.astype(jnp.bfloat16).astype(jnp.float32)
        packed = jnp.where(lane == 2 * at, high, packed)
        packed = jnp.where(lane == 2 * at + 1, value - high, packed)
    return packed.astype(jnp.bfloat16)


def summed_part(ref, start, size):
    total = ref[0, :, start : start + size].astype(jnp.float32)
    for source in range(1, ref.shape[0]):
        total = total + ref[source, :, start : start + size].astype(jnp.float32)
    return total


def order_of(first, last):
    units = []
    for j in range(first, last - 1):
        units += [(j, t, False) for t in range(j, last - 1)]
        units += [(j, t, True) for t in range(j + 1, last)]
    return units


def forward_chain(first, last, width, inner, down_ref, up_ref, up_start, gram_ref):
    where = {unit: at for at, unit in enumerate(order_of(first, last))}
    count = last - first
    raw = {s: summed_part(down_ref, (s - first) * inner, inner) for s in range(first, last)}
    cross = {
        s: summed_part(up_ref, up_start + (s - first) * inner, inner)
        for s in range(first, last - 1)
    }
    square = summed_part(down_ref, count * inner, LANES)
    square = square[:, 0:1] + square[:, 1:2]
    state, crosses = {}, {}
    for s in range(first, last):
        scale = lax.rsqrt(jnp.maximum(square, 0.0) / width + norm_eps)
        hidden = raw[s] * scale
        gate = jax.nn.sigmoid(hidden)
        act = (hidden * gate).astype(jnp.bfloat16)
        state[s] = (hidden, scale, act)
        if s == last - 1:
            break
        added = {}
        for k in range(first, last - 1):
            if k >= s:
                added[k] = dot(act, part(gram_ref, where[(s, k, False)], inner), ROWS)
            else:
                added[k] = dot(act, part(gram_ref, where[(k, s, False)], inner), LAST)
        wide = act.astype(jnp.float32)
        square = square + jnp.sum(wide * (2.0 * cross[s] + added[s]), axis=1, keepdims=True)
        cross = {k: cross[k] + added[k] for k in cross}
        for t in range(s + 1, last):
            raw[t] = raw[t] + dot(act, part(gram_ref, where[(s, t, True)], inner), ROWS)
        crosses[s + 1] = cross
    return state, crosses


def backward_chain(first, last, width, inner, grad_ref, hidden_of, scale_of, cross_of, gram_ref):
    where = {unit: at for at, unit in enumerate(order_of(first, last))}
    grad_act = {s: summed_part(grad_ref, (s - first) * inner, inner) for s in range(first, last)}
    packs, pulls = {}, {}
    for s in reversed(range(first, last)):
        hidden, scale = hidden_of(s), scale_of(s)
        gate = jax.nn.sigmoid(hidden)
        grad_hidden = grad_act[s] * gate * (1.0 + hidden * (1.0 - gate))
        mean = jnp.sum(grad_hidden * hidden, axis=1, keepdims=True) / width
        packs[s] = (grad_hidden * scale).astype(jnp.bfloat16)
        pulls[s] = mean * scale * scale
        for t in range(first, s):
            grad_act[t] = (
                grad_act[t]
                + dot(packs[s], part(gram_ref, where[(t, s, True)], inner), LAST)
                - pulls[s] * cross_of(s, t)
            )
    return packs, pulls


def kept_crosses(first, last):
    return [(s, t) for s in range(first + 1, last) for t in range(first, s)]


def forward_kernel(first, last, width, inner, copies):
    def kernel(down_ref, up_ref, gram_ref, acts_ref, hidden_ref, scale_ref, cross_ref):
        state, crosses = forward_chain(
            first, last, width, inner, down_ref, up_ref, 0, gram_ref
        )
        rows = down_ref.shape[1]
        for s in range(first, last):
            hidden, scale, act = state[s]
            at = s - first
            for copy in range(copies):
                acts_ref[copy * rows : (copy + 1) * rows, at * inner : (at + 1) * inner] = act
            hidden_ref[at] = hidden
            scale_ref[at] = jnp.broadcast_to(scale, (rows, LANES))
        for at, (s, t) in enumerate(kept_crosses(first, last)):
            cross_ref[at] = crosses[s][t]

    return kernel


def store_packs(ref, packs, pulls, first, last, inner, rows, copies):
    scalars = scalar_block([pulls[s] for s in range(first, last)])
    for copy in range(copies):
        there = slice(copy * rows, (copy + 1) * rows)
        for s in range(first, last):
            ref[there, (s - first) * inner : (s - first + 1) * inner] = packs[s]
        at = (last - first) * inner
        ref[there, at : at + LANES] = scalars


def backward_kernel(first, last, width, inner, copies):
    kept = {pair: at for at, pair in enumerate(kept_crosses(first, last))}

    def kernel(grad_ref, hidden_ref, scale_ref, cross_ref, gram_ref, out_ref):
        packs, pulls = backward_chain(
            first,
            last,
            width,
            inner,
            grad_ref,
            lambda s: hidden_ref[s - first],
            lambda s: scale_ref[s - first][:, 0:1],
            lambda s, t: cross_ref[kept[(s, t)]],
            gram_ref,
        )
        store_packs(out_ref, packs, pulls, first, last, inner, grad_ref.shape[1], copies)

    return kernel


def turning_kernel(first, last, width, inner, copies):
    def kernel(sums_ref, grad_ref, gram_ref, out_ref):
        count = last - first
        state, crosses = forward_chain(
            first, last, width, inner, sums_ref, sums_ref, count * inner + LANES, gram_ref
        )
        packs, pulls = backward_chain(
            first,
            last,
            width,
            inner,
            grad_ref,
            lambda s: state[s][0],
            lambda s: state[s][1],
            lambda s, t: crosses[s][t],
            gram_ref,
        )
        rows = sums_ref.shape[1]
        store_packs(out_ref, packs, pulls, first, last, inner, rows, copies)
        for copy in range(copies):
            for s in range(first, last):
                at = count * inner + LANES + (s - first) * inner
                out_ref[copy * rows : (copy + 1) * rows, at : at + inner] = state[s][2]

    return kernel


def next_rows_kernel(first, last, then, inner, chunk):
    def kernel(rows_ref, acts_ref, in_ref, out_ref, exact_ref, columns_ref):
        exact = rows_ref[...].astype(jnp.float32)
        for s in range(first, last):
            exact = exact + dot(
                part(acts_ref, s - first, inner), part(out_ref, s, chunk), ROWS
            )
        exact_ref[...] = exact
        rows = exact.astype(jnp.bfloat16)
        at = 0
        for s in range(last, then):
            weight = in_ref[(s - last) * chunk : (s - last + 1) * chunk]
            columns_ref[:, at : at + inner] = dot(rows, weight, ROWS).astype(jnp.bfloat16)
            at += inner
        squares = jnp.sum(exact * exact, axis=1, keepdims=True)
        columns_ref[:, at : at + LANES] = scalar_block([squares])
        at += LANES
        for s in range(last, then - 1):
            columns = dot(rows, part(out_ref, s, chunk), LAST)
            columns_ref[:, at : at + inner] = columns.astype(jnp.bfloat16)
            at += inner

    return kernel


def grads_kernel(first, last, before, inner, chunk, n_dp, acts_start):
    group = last - first
    share_in = group * chunk // n_dp
    share_out = inner // n_dp
    lanes_in = inner // LANES
    lanes_out = chunk // LANES

    def kernel(*refs):
        exact_ref, packs_ref, acts_ref, up_ref, in_ref, out_ref = refs[:6]
        grads_ref, packed_ref, up_new_ref = refs[6:9]
        exact = exact_ref[...].astype(jnp.float32)
        rows = {first: exact.astype(jnp.bfloat16)}

        def act_of(s):
            at = acts_start + (s - first) * inner
            return acts_ref[:, at : at + inner]

        for s in range(first, last - 1):
            exact = exact + dot(act_of(s), part(out_ref, s, chunk), ROWS)
            rows[s + 1] = exact.astype(jnp.bfloat16)
        upstream = up_ref[...].astype(jnp.float32)
        narrow = upstream.astype(jnp.bfloat16)
        for s in reversed(range(first, last)):
            pack = part(packs_ref, s - first, inner)
            at = group * inner + 2 * (s - first)
            pull = packs_ref[:, group * inner : group * inner + LANES].astype(jnp.float32)
            at = 2 * (s - first)
            pull = pull[:, at : at + 1] + pull[:, at + 1 : at + 2]
            into = dot(rows[s], pack, FIRST).astype(jnp.bfloat16)
            for piece in range(chunk // share_in):
                device = (s - first) * (chunk // share_in) + piece
                for c in range(lanes_in):
                    packed_ref[device % 2, device // 2, c * share_in : (c + 1) * share_in] = into[
                        piece * share_in : (piece + 1) * share_in, c * LANES : (c + 1) * LANES
                    ]
            onto = dot(act_of(s), narrow, FIRST).astype(jnp.bfloat16)
            base = lanes_in * share_in + (s - first) * lanes_out * share_out
            for device in range(n_dp):
                for c in range(lanes_out):
                    row = base + c * share_out
                    packed_ref[device % 2, device // 2, row : row + share_out] = onto[
                        device * share_out : (device + 1) * share_out, c * LANES : (c + 1) * LANES
                    ]
            weight = in_ref[s * chunk : (s + 1) * chunk]
            upstream = (
                upstream + dot(pack, weight, LAST) - pull * rows[s].astype(jnp.float32)
            )
            narrow = upstream.astype(jnp.bfloat16)
            grads_ref[s - first] = narrow
        up_new_ref[...] = upstream
        if before < first:
            for s in range(before, first):
                columns = dot(narrow, part(out_ref, s, chunk), LAST).astype(jnp.bfloat16)
                refs[9][:, (s - before) * inner : (s - before + 1) * inner] = columns

    return kernel


def unpack_kernel(inner, share_in):
    def kernel(arrived_ref, in_ref, out_ref):
        lanes = inner // LANES
        for c in range(lanes):
            total = arrived_ref[0, c * share_in : (c + 1) * share_in].astype(jnp.float32)
            for source in range(1, arrived_ref.shape[0]):
                total = total + arrived_ref[source, c * share_in : (c + 1) * share_in].astype(
                    jnp.float32
                )
            in_ref[:, c * LANES : (c + 1) * LANES] = total.astype(jnp.bfloat16)
        start = lanes * share_in
        total = arrived_ref[0, start:].astype(jnp.float32)
        for source in range(1, arrived_ref.shape[0]):
            total = total + arrived_ref[source, start:].astype(jnp.float32)
        out_ref[...] = total.astype(jnp.bfloat16)

    return kernel


def adam_out_kernel(share, lanes):
    def kernel(grad_ref, master_ref, moment_ref, second_ref, master_new, moment_new, second_new):
        for device in range(grad_ref.shape[0]):
            for c in range(lanes):
                at = (device * lanes + c) * LANES
                grad = grad_ref[device, c * share : (c + 1) * share].astype(jnp.float32)
                results = adam_update(
                    master_ref[:, at : at + LANES],
                    moment_ref[:, at : at + LANES],
                    second_ref[:, at : at + LANES],
                    grad,
                )
                for ref, value in zip((master_new, moment_new, second_new), results):
                    ref[:, at : at + LANES] = value

    return kernel


def columns_kernel(order):
    def kernel(every_ref, out_ref):
        size = every_ref.shape[2]
        for at, unit in enumerate(order):
            out_ref[:, at * size : (at + 1) * size] = every_ref[unit]

    return kernel


def core_halves(packed, n_dp):
    core = lax.axis_index("dp") % 2
    mine = lax.dynamic_index_in_dim(packed, core, 0, keepdims=False)
    other = lax.dynamic_index_in_dim(packed, 1 - core, 0, keepdims=False)
    other = lax.ppermute(other, "dp", [(j, j + 1 - 2 * (j % 2)) for j in range(n_dp)])
    return (mine.astype(jnp.float32) + other.astype(jnp.float32)).astype(jnp.bfloat16)


def chips_of(n_dp):
    return [list(range(c, n_dp, 2)) for c in range(2)]


def reduce_apart(packed, n_dp):
    mine = core_halves(packed, n_dp)
    rows = mine.shape[1]
    summed = lax.psum_scatter(
        mine.reshape(-1, LANES),
        "dp",
        scatter_dimension=0,
        tiled=True,
        axis_index_groups=chips_of(n_dp),
    )
    return summed.reshape(1, rows, LANES)


def reduce_now(packed, n_dp):
    return lax.all_to_all(
        core_halves(packed, n_dp), "dp", 0, 0, tiled=True, axis_index_groups=chips_of(n_dp)
    )


def move_in(summed, first, group, n_pipe, n_dp):
    per = n_pipe // group
    moved = []
    for q in range(per):
        pairs = []
        for i in range(n_pipe):
            for j in range(q, n_dp, per):
                section = j * group // n_dp
                half = j // per % 2
                pairs.append((i * n_dp + j, (first + section) * n_dp + 2 * i + half))
        moved.append(lax.ppermute(summed, ("pipe", "dp"), pairs))
    return jnp.concatenate(moved, axis=0)


def on_device(
    inputs_x, cotangent, master_in, master_out, moment_in, moment_out, second_in, second_out
):
    n_pipe = lax.axis_size("pipe")
    n_dp = lax.axis_size("dp")
    me = lax.axis_index("pipe")
    tok_rows, width = inputs_x.shape
    chunk = width // n_pipe
    inner = master_in.shape[2]
    share_in = master_in.shape[1]
    share_out = master_out.shape[1]
    block = tok_rows // n_pipe

    own_in = master_in[0].astype(jnp.bfloat16)
    own_out = master_out[0].astype(jnp.bfloat16)
    pairs = [
        (s * n_dp + 2 * i + h, i * n_dp + 2 * s + h)
        for s in range(n_pipe)
        for i in range(n_pipe)
        for h in range(2)
    ]
    piece_in = lax.ppermute(own_in, ("pipe", "dp"), pairs)
    piece_out = swap(own_out.reshape(share_out, n_pipe, chunk).transpose(1, 0, 2), "pipe")
    flat_out = piece_out.transpose(1, 0, 2).reshape(share_out, width)
    all_in = lax.all_gather(piece_in, "dp", axis=0, tiled=True)
    all_out = lax.all_gather(flat_out, "dp", axis=0, tiled=True)
    weight_in = [all_in[s * chunk : (s + 1) * chunk] for s in range(n_pipe)]

    def products(first, last):
        units, partial = [], []
        for t in range(first + 1, last):
            left = piece_out[first:t].reshape(-1, chunk)
            partial.append(dot(left, weight_in[t], ROWS))
            units += [(k, t, True) for k in range(first, t)]
        for t in range(first, last - 1):
            left = piece_out[first : t + 1].reshape(-1, chunk)
            partial.append(dot(left, weight_out[t], LAST))
            units += [(k, t, False) for k in range(first, t + 1)]
        padded = -(-len(units) // n_pipe) * n_pipe
        partial = [p.astype(jnp.bfloat16) for p in partial]
        partial.append(jnp.zeros(((padded - len(units)) * share_out, inner), jnp.bfloat16))
        arrived = swap(jnp.concatenate(partial, axis=0), "pipe")
        arrived = arrived.reshape(n_pipe, -1, inner)
        mine = jnp.sum(arrived.astype(jnp.float32), axis=0).astype(jnp.bfloat16)
        every = swap(jnp.tile(mine, (n_pipe, 1)), "pipe").reshape(padded, share_out, inner)
        order = [units.index(unit) for unit in order_of(first, last)]
        shape = (share_out, len(units) * inner)
        return run(columns_kernel(order), [(shape, jnp.bfloat16)], every)[0]

    rows = lax.dynamic_slice_in_dim(inputs_x, me * chunk, chunk, 1)
    seed = lax.dynamic_slice_in_dim(cotangent, me * chunk, chunk, 1)

    (first, middle), (_, last) = BLOCKS
    count = middle - first
    wide = rows.astype(jnp.float32)
    down = [dot(rows, weight_in[s], ROWS) for s in range(first, middle)]
    down += split_scalars([jnp.sum(wide * wide, axis=1, keepdims=True)])
    down = exchanged(down, n_pipe)
    all_out, down = lax.optimization_barrier((all_out, down))
    weight_out = [all_out[:, s * chunk : (s + 1) * chunk] for s in range(n_pipe)]
    gram_low = lax.all_gather(products(first, middle), "dp", axis=0, tiled=True)
    up = exchanged([dot(rows, weight_out[s], LAST) for s in range(first, middle - 1)], n_pipe)
    columns = products(middle, last)
    gram_low, up, columns = lax.optimization_barrier((gram_low, up, columns))
    gram_high = lax.all_gather(columns, "dp", axis=0, tiled=True)

    kept = len(kept_crosses(first, middle))
    acts, hidden, scale, cross = run(
        forward_kernel(first, middle, width, inner, n_pipe),
        [
            ((tok_rows, count * inner), jnp.bfloat16),
            ((count, block, inner), jnp.float32),
            ((count, block, LANES), jnp.float32),
            ((kept, block, inner), jnp.float32),
        ],
        down,
        up,
        gram_low,
    )
    acts = swap(acts, "pipe")
    late, acts = lax.optimization_barrier((seed, acts))
    exact, columns = run(
        next_rows_kernel(first, middle, last, inner, chunk),
        [
            ((tok_rows, chunk), jnp.float32),
            ((tok_rows, (2 * (last - middle) - 1) * inner + LANES), jnp.bfloat16),
        ],
        rows,
        acts,
        all_in[middle * chunk : last * chunk],
        all_out,
    )
    sums = exchanged(columns, n_pipe)
    grad_high = exchanged([dot(late, weight_out[s], LAST) for s in range(middle, last)], n_pipe)

    turned = run(
        turning_kernel(middle, last, width, inner, n_pipe),
        [((tok_rows, 2 * (last - middle) * inner + LANES), jnp.bfloat16)],
        sums,
        grad_high,
        gram_high,
    )[0]
    turned = swap(turned, "pipe")

    def packed_shape(group):
        rows_packed = 2 * group * chunk * inner // (n_dp * LANES)
        return (2, n_dp // 2, rows_packed, LANES)

    grads_high, packed_high, upstream, columns = run(
        grads_kernel(middle, last, first, inner, chunk, n_dp, (last - middle) * inner + LANES),
        [
            ((last - middle, tok_rows, chunk), jnp.bfloat16),
            (packed_shape(last - middle), jnp.bfloat16),
            ((tok_rows, chunk), jnp.float32),
            ((tok_rows, count * inner), jnp.bfloat16),
        ],
        exact,
        turned,
        turned,
        seed,
        all_in,
        all_out,
    )
    grad_low = exchanged(columns, n_pipe)
    summed_high = reduce_apart(packed_high, n_dp)

    packs = run(
        backward_kernel(first, middle, width, inner, n_pipe),
        [((tok_rows, count * inner + LANES), jnp.bfloat16)],
        grad_low,
        hidden,
        scale,
        cross,
        gram_low,
    )[0]
    packs = swap(packs, "pipe")
    grads_low, packed_low, _ = run(
        grads_kernel(first, middle, first, inner, chunk, n_dp, 0),
        [
            ((count, tok_rows, chunk), jnp.bfloat16),
            (packed_shape(count), jnp.bfloat16),
            ((tok_rows, chunk), jnp.float32),
        ],
        rows,
        packs,
        acts,
        upstream,
        all_in,
        all_out,
    )
    arrived_low = reduce_now(packed_low, n_dp)

    input_grads = swap(jnp.concatenate([grads_low, grads_high], axis=0), "pipe")
    input_grads, arrived_low = lax.optimization_barrier((input_grads, arrived_low))
    input_grads = input_grads.transpose(1, 0, 2).reshape(1, tok_rows, width)

    grad_in = jnp.zeros((share_in, inner), jnp.bfloat16)
    outs = []
    for (low, high), arrived in zip(BLOCKS, (arrived_low, summed_high)):
        group = high - low
        share = group * chunk // n_dp
        sum_in, sum_out = run(
            unpack_kernel(inner, share),
            [
                ((share, inner), jnp.bfloat16),
                ((arrived.shape[1] - share * inner // LANES, LANES), jnp.bfloat16),
            ],
            arrived,
        )
        moved = move_in(sum_in, low, group, n_pipe, n_dp)
        grad_in = jnp.where((me >= low) & (me < high), moved, grad_in)
        outs.append(sum_out.reshape(group, -1, LANES))
    grad_out = swap(jnp.concatenate(outs, axis=0), "pipe")

    new_in, new_moment_in, new_second_in = adam_update(
        master_in[0], moment_in[0], second_in[0], grad_in.astype(jnp.float32)
    )
    shape_out = (share_out, width)
    new_out, new_moment_out, new_second_out = run(
        adam_out_kernel(share_out, chunk // LANES),
        [(shape_out, jnp.float32)] * 3,
        grad_out,
        master_out[0],
        moment_out[0],
        second_out[0],
    )
    cast_in = new_in.astype(jnp.bfloat16).T.reshape(n_dp, share_out, share_in)
    cast_out = new_out.astype(jnp.bfloat16).reshape(share_out, n_dp, share_in).transpose(1, 0, 2)
    swapped = swap(jnp.stack([cast_in, cast_out], axis=1), "dp")
    roll_in = swapped[:, 0].transpose(1, 0, 2).reshape(share_out, width)
    roll_out = swapped[:, 1].reshape(inner, share_in).T
    return (
        input_grads,
        new_in[None],
        new_moment_in[None],
        new_second_in[None],
        new_out[None],
        new_moment_out[None],
        new_second_out[None],
        roll_in[None],
        roll_out[None],
    )


def solution(mesh):
    in_specs = (P("dp", None), P("dp", None)) + (P("pipe", "dp", None),) * 6
    out_specs = (P("pipe", "dp", None),) * 9
    return jax.shard_map(
        on_device, mesh=mesh, in_specs=in_specs, out_specs=out_specs, check_vma=False
    )
```

time: 733 us -> 624 us (0.85); the launches traced: 720 us -> 620 us
  matrix products: 144 us -> 40.1 us
  waiting for transfers between devices: 257 us -> 204 us
  blocking collectives: 115 us -> 164 us
  Pallas kernels: 0 us -> 44.9 us
  local copies, waits for them, and re-layouts: 80.2 us -> 52.2 us
  other arithmetic: 39.2 us -> 28.9 us
    dot_general x107 -> x23, matrix products: 144 us -> 40.1 us  [dot(): lax.dot_general(left, right, (dims, ((), ())), preferred_element_type=jnp...]
    all_to_all x0 -> x1, blocking collectives: none -> 48.8 us  [reduce_now(): lax.all_to_all(core_halves(packed, n_dp), 'dp', 0, 0, tiled=True, axis_in...]
    reduce_scatter x2 -> x1, waiting for transfers between devices: 53.6 us -> 6.3 us  [reduce_apart(): lax.psum_scatter(mine.reshape(-1, LANES), 'dp', scatter_dimension=0, tile...]
    pallas_call x0 -> x11, Pallas kernels: none -> 44.9 us  [run(): pl.pallas_call(kernel, out_shape=[jax.ShapeDtypeStruct(shape, kind) for s...]
    reshape x9 -> x2, local copies, waits for them, and re-layouts: 25.5 us -> 3.13 us  [on_device(): new_out.astype(jnp.bfloat16).reshape(share_out, n_dp, share_in)]
    convert_element_type x4 -> x3, other arithmetic: 1.39 us -> 11.6 us  [the longest x2 9.58 us: core_halves(): (mine.astype(jnp.float32) + other.astype(jnp.float32)).astype(jnp.bfloat16)]
    concatenate x10 -> x3, other arithmetic: 14.2 us -> 4.88 us  [the longest x2 3.12 us: exchanged(): packed = jnp.concatenate([c.astype(jnp.bfloat16) for c in columns], axis=1)]
    all_gather x1, waiting for transfers between devices: 37.9 us -> 29.2 us  [on_device(): all_out = lax.all_gather(flat_out, 'dp', axis=0, tiled=True)]
  transfers between devices with their start and end apart: 22 -> 23, of which waited for: 14 -> 14; matrix products, arithmetic and copies ran while one was open for 24% -> 13% of each run, Pallas kernels for 0% -> 4%
where the time goes in v3:
time: 624 us; the launch traced here: 620 us
  waiting for transfers between devices  204 us (33%)
  blocking collectives  164 us (26%)
  starting transfers between devices  71.5 us (11%)
  local copies, waits for them, and re-layouts  52.2 us (8%)
  Pallas kernels  44.9 us (7%)
  matrix products  40.1 us (6%)
  other arithmetic  28.9 us (5%)
  between operations  14.3 us (2%)
    all_to_all x11, waiting for transfers between devices, swap(): return lax.all_to_all(x, axis, 0, 0, tiled=True)  143 us
    all_to_all x5, blocking collectives, swap(): return lax.all_to_all(x, axis, 0, 0, tiled=True)  116 us
    all_to_all x11, starting transfers between devices, swap(): return lax.all_to_all(x, axis, 0, 0, tiled=True)  55.5 us
    all_to_all x1, blocking collectives, reduce_now(): lax.all_to_all(core_halves(packed, n_dp), 'dp', 0, 0, tiled=True, axis_in...  48.8 us
    pallas_call x11, Pallas kernels, run(): pl.pallas_call(kernel, out_shape=[jax.ShapeDtypeStruct(shape, kind) for s...  44.9 us
    dot_general x23, matrix products, dot(): lax.dot_general(left, right, (dims, ((), ())), preferred_element_type=jnp...  40.1 us
    all_gather x1, waiting for transfers between devices, on_device(): all_out = lax.all_gather(flat_out, 'dp', axis=0, tiled=True)  29.2 us
    unnamed x73, local copies, waits for them, and re-layouts  23.7 us
  transfers between devices with their start and end apart: 23, of which 14 were waited for; matrix products, arithmetic and copies ran while one was open for 13% of the time, Pallas kernels for 4%

profile of v3, /device:TPU:1, one launch (start us, length us, event | category | flops | bytes accessed | tf_op | source)
XLA Modules:
  0.0 620.5 jit_solution(10042559882439701351)
XLA Ops:
  11.2 37.5 %all_to_all.131 = bf16[8,32,640]{2,1,0:T(8,128)(2,1)S(1)} all-to-all(bf16[8,32,640]{2,1,0:T(8,128)(2,1)S(1)} %copy.61), channel_id=1, replica_groups=mesh['pipe'=8,'dp'=16] {'pipe'}, dimensions={0} | all-to-all | bytes 655360 | tf_op jit(solution)/shard_map/all_to_all | solution.py:31
  52.5 21.0 %all-gather.7.cloned.1.call-done.refs_4_ = bf16[5120,512]{1,0:T(8,128)(2,1)} async-done(((bf16[320,512]{1,0:T(8,128)(2,1)}), bf16[5120,512]{1,0:T(8,128)(2,1)}) %all-gather.7.cloned.1.call-update) | async-done | bytes 5242896 | tf_op jit(solution)/shard_map/all_gather | solution.py:430
  82.0 3.2 concatenate.76
  85.2 6.2 all-to-all-start.1
  97.4 29.2 %all-gather.5.cloned.1.call-done.out_ref.refs_5_ = bf16[512,5120]{1,0:T(8,128)(2,1)} async-done(((bf16[32,5120]{1,0:T(8,128)(2,1)}), bf16[512,5120]{1,0:T(8,128)(2,1)}) %all-gather.5.cloned.1.call-update) | async-done | bytes 5242896 | tf_op jit(solution)/shard_map/all_gather | solution.py:431
  133.4 16.7 %all_to_all.132 = bf16[8,64,512]{2,1,0:T(8,128)(2,1)} all-to-all(bf16[8,64,512]{2,1,0:T(8,128)(2,1)} %bitcast.13), channel_id=1, replica_groups=mesh['pipe'=8,'dp'=16] {'pipe'}, dimensions={0} | all-to-all | bytes 1048576 | tf_op jit(solution)/shard_map/all_to_all | solution.py:31
  151.2 13.1 %all_to_all.133 = bf16[8,64,512]{2,1,0:T(8,128)(2,1)S(1)} all-to-all(bf16[8,64,512]{2,1,0:T(8,128)(2,1)S(1)} %tile.4), channel_id=1, replica_groups=mesh['pipe'=8,'dp'=16] {'pipe'}, dimensions={0} | all-to-all | bytes 1048576 | tf_op jit(solution)/shard_map/all_to_all | solution.py:31
  174.1 3.5 all-to-all-start.5
  182.0 4.1 all-to-all-done.5
  187.1 6.0 all-to-all-start.6
  196.6 5.2 all-to-all-done.6
  202.6 6.5 %all-to-all-start.4 = ((bf16[8,32,1536]{2,1,0:T(8,128)(2,1)}), bf16[8,32,1536]{2,1,0:T(8,128)(2,1)S(1)}, u32[]{:S(2)}, u32[]{:S(2)}) async-start(bf16[8,32,1536]{2,1,0:T(8,128)(2,1)} %bitcast.165), calls=%async_computation.4 | async-start | bytes 1572864 | tf_op jit(solution)/shard_map/all_to_all | solution.py:31
  210.9 10.1 %all-to-all-done.4.up_ref = bf16[8,32,1536]{2,1,0:T(8,128)(2,1)S(1)} async-done(((bf16[8,32,1536]{2,1,0:T(8,128)(2,1)}), bf16[8,32,1536]{2,1,0:T(8,128)(2,1)S(1)}, u32[]{:S(2)}, u32[]{:S(2)}) %all-to-all-start.4) | async-done | bytes 786464 | tf_op jit(solution)/shard_map/all_to_all | solution.py:31
  221.0 5.0 all-gather.9.cloned.1.call-done.gram_ref
  226.0 5.1 shard_map.153
  233.6 6.3 %all-to-all-start.7 = ((bf16[8,32,2048]{2,1,0:T(8,128)(2,1)}), bf16[8,32,2048]{2,1,0:T(8,128)(2,1)}, u32[]{:S(2)}, u32[]{:S(2)}) async-start(bf16[8,32,2048]{2,1,0:T(8,128)(2,1)} %bitcast.154), calls=%async_computation.7 | async-start | bytes 2097152 | tf_op jit(solution)/shard_map/all_to_all | solution.py:31
  239.9 18.1 %all-to-all-done.7 = bf16[8,32,2048]{2,1,0:T(8,128)(2,1)} async-done(((bf16[8,32,2048]{2,1,0:T(8,128)(2,1)}), bf16[8,32,2048]{2,1,0:T(8,128)(2,1)}, u32[]{:S(2)}, u32[]{:S(2)}) %all-to-all-start.7) | async-done | bytes 1048608 | tf_op jit(solution)/shard_map/all_to_all | solution.py:31
  265.3 4.3 all-to-all-start.9
  269.6 3.5 slice.111.in_ref
  273.1 6.0 shard_map.154
  279.9 7.5 %all-to-all-done.9.grad_ref = bf16[8,32,2048]{2,1,0:T(8,128)(2,1)} async-done(((bf16[8,32,2048]{2,1,0:T(8,128)(2,1)}), bf16[8,32,2048]{2,1,0:T(8,128)(2,1)}, u32[]{:S(2)}, u32[]{:S(2)}) %all-to-all-start.9) | async-done | bytes 1048608 | tf_op jit(solution)/shard_map/all_to_all | solution.py:31
  287.5 29.1 %all_to_all.134.sums_ref = bf16[8,32,3712]{2,1,0:T(8,128)(2,1)} all-to-all(bf16[8,32,3712]{2,1,0:T(8,128)(2,1)S(1)} %bitcast.153), channel_id=1, replica_groups=mesh['pipe'=8,'dp'=16] {'pipe'}, dimensions={0} | all-to-all | bytes 3801088 | tf_op jit(solution)/shard_map/all_to_all | solution.py:31
  318.1 6.3 %shard_map.155 = bf16[256,4224]{1,0:T(8,128)(2,1)S(1)} custom-call(bf16[8,32,3712]{2,1,0:T(8,128)(2,1)S(1)} %copy-done.3, bf16[8,32,2048]{2,1,0:T(8,128)(2,1)} %all-to-all-done.9.grad_ref, bf16[512,6144]{1,0:T(8,128)(2,1)} %all-gather.11.cloned.1.call-done.gram_ref), custom_call_target="tpu_custom_call" | custom-call | tf_op jit(solution)/shard_map/pallas_call | solution.py:62
  325.8 3.6 all-to-all-start.10
  329.4 29.4 %all-to-all-done.10 = bf16[8,32,4224]{2,1,0:T(8,128)(2,1)S(1)} async-done(((bf16[8,32,4224]{2,1,0:T(8,128)(2,1)}), bf16[8,32,4224]{2,1,0:T(8,128)(2,1)S(1)}, u32[]{:S(2)}, u32[]{:S(2)}) %all-to-all-start.10) | async-done | bytes 2162720 | tf_op jit(solution)/shard_map/all_to_all | solution.py:31
  360.0 9.5 %shard_map.156 = (bf16[4,256,640]{2,1,0:T(8,128)(2,1)S(1)}, bf16[2,8,1280,128]{3,2,1,0:T(8,128)(2,1)}, f32[256,640]{1,0:T(8,128)S(1)}, bf16[256,2048]{1,0:T(8,128)(2,1)S(1)}) custom-call(f32[256,640]{1,0:T(8,128)S(1)} %copy-done.18, bf16[256,4224]{1,0:T(8,128)(2,1)S(1)} %bitcast.146, bf16[256,4224]{1,0:T(8,128)(2,1)S(1)} %bitcast.147, ...), custom_call_target="tpu_custom_call" | custom-call | tf_op jit(solution)/shard_map/pallas_call | solution.py:62
  369.5 4.2 dynamic-slice_bitcast_fusion
  376.1 19.2 %all_to_all.135.grad_ref = bf16[8,32,2048]{2,1,0:T(8,128)(2,1)S(1)} all-to-all(bf16[8,32,2048]{2,1,0:T(8,128)(2,1)S(1)} %bitcast.155), channel_id=1, replica_groups=mesh['pipe'=8,'dp'=16] {'pipe'}, dimensions={0} | all-to-all | bytes 2097152 | tf_op jit(solution)/shard_map/all_to_all | solution.py:31
  395.2 5.1 shard_map.157
  400.4 3.6 all-to-all-start.12
  404.0 16.3 %all-to-all-done.12 = bf16[8,32,2176]{2,1,0:T(8,128)(2,1)S(1)} async-done(((bf16[8,32,2176]{2,1,0:T(8,128)(2,1)}), bf16[8,32,2176]{2,1,0:T(8,128)(2,1)S(1)}, u32[]{:S(2)}, u32[]{:S(2)}) %all-to-all-start.12) | async-done | bytes 1114144 | tf_op jit(solution)/shard_map/all_to_all | solution.py:31
  423.7 10.1 %shard_map.158 = (bf16[4,256,640]{2,1,0:T(8,128)(2,1)S(1)}, bf16[2,8,1280,128]{3,2,1,0:T(8,128)(2,1)}, f32[256,640]{1,0:T(8,128)}) custom-call(bf16[256,640]{1,0:T(8,128)(2,1)S(1)} %copy-done.7, bf16[256,2176]{1,0:T(8,128)(2,1)S(1)} %bitcast.149, bf16[256,2048]{1,0:T(8,128)(2,1)} %bitcast.25.acts_ref.refs_2_, f32[256,640]{1,0:T(8,128)S(1)} %copy-done.22, ...), custom_call_target="tpu_custom_call" | custom-call | tf_op jit(solution)/shard_map/pallas_call | solution.py:62
  434.8 3.5 dynamic-slice_bitcast_fusion.1
  439.9 4.7 fusion
  446.4 3.6 all-to-all-start.13
  450.0 4.9 fusion.1
  454.9 44.2 %all-to-all-done.13 = bf16[8,256,640]{2,1,0:T(8,128)(2,1)S(1)} async-done(((bf16[8,256,640]{2,1,0:T(8,128)(2,1)}), bf16[8,256,640]{2,1,0:T(8,128)(2,1)S(1)}, u32[]{:S(2)}, u32[]{:S(2)}) %all-to-all-start.13) | async-done | bytes 2621472 | tf_op jit(solution)/shard_map/all_to_all | solution.py:31
  500.6 48.8 %all_to_all.136.arrived_ref = bf16[8,1280,128]{2,1,0:T(8,128)(2,1)S(1)} all-to-all(bf16[8,1280,128]{2,1,0:T(8,128)(2,1)} %fusion.1), channel_id=1, replica_groups={{0,2,4,6,8,10,12,14},{1,3,5,7,9,11,13,15},{16,18,20,22,24,26,28,30},{17..., dimensions={0} | all-to-all | bytes 5242880 | tf_op jit(solution)/shard_map/all_to_all | solution.py:387
  549.7 4.0 collective-permute-start.6
  555.1 6.3 %reduce-scatter.2.cloned.1.call-done = bf16[1280,128]{1,0:T(8,128)(2,1)} async-done(((bf16[10240,128]{1,0:T(8,128)(2,1)}), bf16[1280,128]{1,0:T(8,128)(2,1)}) %reduce-scatter.2.cloned.1.call-update) | async-done | bytes 327696 | tf_op jit(solution)/shard_map/reduce_scatter | solution.py:376
  562.4 4.6 collective-permute-start.4
  569.0 5.4 all-to-all-start.15
  577.4 5.1 all-to-all-done.15.grad_ref
  591.4 6.6 %all-to-all-start.16 = ((bf16[16,2,32,320]{3,2,1,0:T(8,128)(2,1)}), bf16[16,2,32,320]{3,2,1,0:T(8,128)(2,1)}, u32[]{:S(2)}, u32[]{:S(2)}) async-start(bf16[16,2,32,320]{3,2,1,0:T(8,128)(2,1)} %copy.69), calls=%async_computation.17 | async-start | bytes 1572864 | tf_op jit(solution)/shard_map/all_to_all | solution.py:31
  597.9 2.6 copy.66
  600.6 4.5 copy.71
  605.1 3.1 multiply_subtract_fusion
  608.2 2.5 all-to-all-done.16
  (159 shorter events, 97.4 us)
Async XLA Ops:
  7.2 232.7 %copy-start = (bf16[256,5120]{1,0:T(8,128)(2,1)S(1)}, bf16[256,5120]{1,0:T(8,128)(2,1)}, u32[]{:S(2)}) copy-start(bf16[256,5120]{1,0:T(8,128)(2,1)} %param.9) | copy-start | bytes 7864324
  7.2 66.3 %all-gather.7.cloned.1.call-start = ((), (), s32[]{:S(2)}) async-start(), calls=%async_computation.19 | async-start | bytes 5570560 | tf_op jit(solution)/shard_map/all_gather | solution.py:430
  8.5 0.7 collective-permute-start
  10.0 116.6 %all-gather.5.cloned.1.call-start = ((), (), s32[]{:S(2)}) async-start(), calls=%async_computation.18 | async-start | bytes 5570560 | tf_op jit(solution)/shard_map/all_gather | solution.py:431
  50.7 142.4 %copy-start.6 = (bf16[256,640]{1,0:T(8,128)(2,1)}, bf16[256,640]{1,0:T(8,128)(2,1)S(1)}, u32[]{:S(2)}) copy-start(bf16[256,640]{1,0:T(8,128)(2,1)S(1)} %get-tuple-element.114.rows_ref.refs_0_) | copy-start | bytes 983044
  85.2 41.4 %all-to-all-start.1 = ((bf16[8,32,2176]{2,1,0:T(8,128)(2,1)}), bf16[8,32,2176]{2,1,0:T(8,128)(2,1)}, u32[]{:S(2)}, u32[]{:S(2)}) async-start(bf16[8,32,2176]{2,1,0:T(8,128)(2,1)} %concatenate.76), calls=%async_computation.1 | async-start | bytes 2228224 | tf_op jit(solution)/shard_map/all_to_all | solution.py:31
  91.4 134.6 %all-gather.9.cloned.1.call-start = ((), (), s32[]{:S(2)}) async-start(), calls=%async_computation.20 | async-start | bytes 6684672 | tf_op jit(solution)/shard_map/all_gather | solution.py:466
  91.4 2.0 copy-start.34
  91.5 4.0 copy-start.33
  174.1 12.0 %all-to-all-start.5 = ((bf16[8,64,512]{2,1,0:T(8,128)(2,1)}), bf16[8,64,512]{2,1,0:T(8,128)(2,1)S(1)}, u32[]{:S(2)}, u32[]{:S(2)}) async-start(bf16[8,64,512]{2,1,0:T(8,128)(2,1)} %bitcast.174), calls=%async_computation.5 | async-start | bytes 1048576 | tf_op jit(solution)/shard_map/all_to_all | solution.py:31
  187.1 14.7 %all-to-all-start.6 = ((bf16[8,64,512]{2,1,0:T(8,128)(2,1)}), bf16[8,64,512]{2,1,0:T(8,128)(2,1)S(1)}, u32[]{:S(2)}, u32[]{:S(2)}) async-start(bf16[8,64,512]{2,1,0:T(8,128)(2,1)} %tile.5), calls=%async_computation.6 | async-start | bytes 1048576 | tf_op jit(solution)/shard_map/all_to_all | solution.py:31
  202.6 18.4 %all-to-all-start.4 = ((bf16[8,32,1536]{2,1,0:T(8,128)(2,1)}), bf16[8,32,1536]{2,1,0:T(8,128)(2,1)S(1)}, u32[]{:S(2)}, u32[]{:S(2)}) async-start(bf16[8,32,1536]{2,1,0:T(8,128)(2,1)} %bitcast.165), calls=%async_computation.4 | async-start | bytes 1572864 | tf_op jit(solution)/shard_map/all_to_all | solution.py:31
  209.0 107.6 %all-gather.11.cloned.1.call-start = ((), (), s32[]{:S(2)}) async-start(), calls=%async_computation.21 | async-start | bytes 6684672 | tf_op jit(solution)/shard_map/all_gather | solution.py:470
  209.1 1.0 copy-start.10
  233.6 24.5 %all-to-all-start.7 = ((bf16[8,32,2048]{2,1,0:T(8,128)(2,1)}), bf16[8,32,2048]{2,1,0:T(8,128)(2,1)}, u32[]{:S(2)}, u32[]{:S(2)}) async-start(bf16[8,32,2048]{2,1,0:T(8,128)(2,1)} %bitcast.154), calls=%async_computation.7 | async-start | bytes 2097152 | tf_op jit(solution)/shard_map/all_to_all | solution.py:31
  262.6 10.5 %copy-start.7 = (bf16[256,640]{1,0:T(8,128)(2,1)S(1)}, bf16[256,640]{1,0:T(8,128)(2,1)}, u32[]{:S(2)}) copy-start(bf16[256,640]{1,0:T(8,128)(2,1)} %copy-done.6) | copy-start | bytes 983044
  265.3 22.2 %all-to-all-start.9 = ((bf16[8,32,2048]{2,1,0:T(8,128)(2,1)}), bf16[8,32,2048]{2,1,0:T(8,128)(2,1)}, u32[]{:S(2)}, u32[]{:S(2)}) async-start(bf16[8,32,2048]{2,1,0:T(8,128)(2,1)} %bitcast.27), calls=%async_computation.9 | async-start | bytes 2097152 | tf_op jit(solution)/shard_map/all_to_all | solution.py:31
  316.6 1.5 copy-start.3
  324.5 1.3 copy-start.2
  325.8 33.1 %all-to-all-start.10 = ((bf16[8,32,4224]{2,1,0:T(8,128)(2,1)}), bf16[8,32,4224]{2,1,0:T(8,128)(2,1)S(1)}, u32[]{:S(2)}, u32[]{:S(2)}) async-start(bf16[8,32,4224]{2,1,0:T(8,128)(2,1)} %bitcast.148), calls=%async_computation.10 | async-start | bytes 4325376 | tf_op jit(solution)/shard_map/all_to_all | solution.py:31
  358.9 1.1 copy-start.18
  369.5 6.6 %copy-start.12 = (bf16[4,256,640]{2,1,0:T(8,128)(2,1)}, bf16[4,256,640]{2,1,0:T(8,128)(2,1)S(1)}, u32[]{:S(2)}) copy-start(bf16[4,256,640]{2,1,0:T(8,128)(2,1)S(1)} %get-tuple-element.53) | copy-start | bytes 3932164
  369.5 30.9 %copy-start.21 = (f32[256,640]{1,0:T(8,128)}, f32[256,640]{1,0:T(8,128)S(1)}, u32[]{:S(2)}) copy-start(f32[256,640]{1,0:T(8,128)S(1)} %get-tuple-element.51.refs_3_) | copy-start | bytes 1966084
  369.5 25.7 %copy-start.24 = (f32[6,32,512]{2,1,0:T(8,128)S(1)}, f32[6,32,512]{2,1,0:T(8,128)}, u32[]{:S(2)}) copy-start(f32[6,32,512]{2,1,0:T(8,128)} %copy-done.23) | copy-start | bytes 1179652
  369.5 25.7 %copy-start.27 = (f32[4,32,512]{2,1,0:T(8,128)S(1)}, f32[4,32,512]{2,1,0:T(8,128)}, u32[]{:S(2)}) copy-start(f32[4,32,512]{2,1,0:T(8,128)} %copy-done.26) | copy-start | bytes 786436
  373.7 66.2 %collective-permute-start.2 = (bf16[8,1280,128]{2,1,0:T(8,128)(2,1)}, bf16[8,1280,128]{2,1,0:T(8,128)(2,1)}, u32[]{:S(2)}, u32[]{:S(2)}) collective-permute-start(bf16[8,1280,128]{2,1,0:T(8,128)(2,1)} %dynamic-slice_bitcast_fusion), channel_id=1, source_target_pairs={{0,1},{1,0},{2,3},{3,2},{4,5},{5,4},{6,7},{7,6},{8,9},{9,8},{10,11... | collective-permute-start | bytes 7864328 | tf_op jit(solution)/shard_map/ppermute | solution.py:365
  400.4 20.0 %all-to-all-start.12 = ((bf16[8,32,2176]{2,1,0:T(8,128)(2,1)}), bf16[8,32,2176]{2,1,0:T(8,128)(2,1)S(1)}, u32[]{:S(2)}, u32[]{:S(2)}) async-start(bf16[8,32,2176]{2,1,0:T(8,128)(2,1)} %bitcast.31), calls=%async_computation.12 | async-start | bytes 2228224 | tf_op jit(solution)/shard_map/all_to_all | solution.py:31
  403.9 157.4 %reduce-scatter.2.cloned.1.call-start = ((), (), s32[]{:S(2)}) async-start(), calls=%async_computation.22 | async-start | bytes 2949120 | tf_op jit(solution)/shard_map/reduce_scatter | solution.py:376
  421.4 1.2 copy-start.5
  422.6 1.1 copy-start.22
  433.8 1.1 copy-start.14
  438.3 6.3 %copy-start.13 = (bf16[4,256,640]{2,1,0:T(8,128)(2,1)S(1)}, bf16[4,256,640]{2,1,0:T(8,128)(2,1)}, u32[]{:S(2)}) copy-start(bf16[4,256,640]{2,1,0:T(8,128)(2,1)} %copy-done.12) | copy-start | bytes 3932164
  438.3 6.3 %copy-start.15 = (bf16[4,256,640]{2,1,0:T(8,128)(2,1)S(1)}, bf16[4,256,640]{2,1,0:T(8,128)(2,1)}, u32[]{:S(2)}) copy-start(bf16[4,256,640]{2,1,0:T(8,128)(2,1)} %copy-done.14) | copy-start | bytes 3932164
  438.3 11.7 %collective-permute-start.1 = (bf16[8,1280,128]{2,1,0:T(8,128)(2,1)}, bf16[8,1280,128]{2,1,0:T(8,128)(2,1)}, u32[]{:S(2)}, u32[]{:S(2)}) collective-permute-start(bf16[8,1280,128]{2,1,0:T(8,128)(2,1)} %dynamic-slice_bitcast_fusion.1), channel_id=1, source_target_pairs={{0,1},{1,0},{2,3},{3,2},{4,5},{5,4},{6,7},{7,6},{8,9},{9,8},{10,11... | collective-permute-start | bytes 7864328 | tf_op jit(solution)/shard_map/ppermute | solution.py:365
  446.4 52.7 %all-to-all-start.13 = ((bf16[8,256,640]{2,1,0:T(8,128)(2,1)}), bf16[8,256,640]{2,1,0:T(8,128)(2,1)S(1)}, u32[]{:S(2)}, u32[]{:S(2)}) async-start(bf16[8,256,640]{2,1,0:T(8,128)(2,1)} %pad_maximum_fusion), calls=%async_computation.13 | async-start | bytes 5242880 | tf_op jit(solution)/shard_map/all_to_all | solution.py:31
  454.9 119.5 %copy-start.30 = (f32[1,320,512]{2,1,0:T(8,128)S(1)}, f32[1,320,512]{2,1,0:T(8,128)}, u32[]{:S(2)}) copy-start(f32[1,320,512]{2,1,0:T(8,128)} %param.10) | copy-start | bytes 1966084
  499.1 1.5 copy-start.28
  549.4 33.1 %copy-start.8 = (f32[1,32,5120]{2,1,0:T(8,128)S(1)}, f32[1,32,5120]{2,1,0:T(8,128)}, u32[]{:S(2)}) copy-start(f32[1,32,5120]{2,1,0:T(8,128)} %param.11) | copy-start | bytes 1966084
  549.4 33.1 %copy-start.19 = (f32[1,32,5120]{2,1,0:T(8,128)S(1)}, f32[1,32,5120]{2,1,0:T(8,128)}, u32[]{:S(2)}) copy-start(f32[1,32,5120]{2,1,0:T(8,128)} %param.13) | copy-start | bytes 1966084
  549.4 33.1 %copy-start.20 = (f32[1,32,5120]{2,1,0:T(8,128)S(1)}, f32[1,32,5120]{2,1,0:T(8,128)}, u32[]{:S(2)}) copy-start(f32[1,32,5120]{2,1,0:T(8,128)} %param.15) | copy-start | bytes 1966084
  549.7 24.7 %collective-permute-start.6 = (bf16[160,512]{1,0:T(8,128)(2,1)S(1)}, bf16[160,512]{1,0:T(8,128)(2,1)S(1)}, u32[]{:S(2)}, u32[]{:S(2)}) collective-permute-start(bf16[160,512]{1,0:T(8,128)(2,1)S(1)} %get-tuple-element.59), channel_id=1, source_target_pairs={{1,0},{3,1},{5,16},{7,17},{9,32},{11,33},{13,48},{15,49},{17,2},{1... | collective-permute-start | bytes 491528 | tf_op jit(solution)/shard_map/ppermute | solution.py:402
  553.8 20.6 %collective-permute-start.5 = (bf16[160,512]{1,0:T(8,128)(2,1)S(1)}, bf16[160,512]{1,0:T(8,128)(2,1)}, u32[]{:S(2)}, u32[]{:S(2)}) collective-permute-start(bf16[160,512]{1,0:T(8,128)(2,1)S(1)} %get-tuple-element.59), channel_id=1, source_target_pairs={{0,0},{2,1},{4,16},{6,17},{8,32},{10,33},{12,48},{14,49},{16,2},{1... | collective-permute-start | bytes 491528 | tf_op jit(solution)/shard_map/ppermute | solution.py:402
  562.4 12.0 %collective-permute-start.4 = (bf16[160,512]{1,0:T(8,128)(2,1)S(1)}, bf16[160,512]{1,0:T(8,128)(2,1)}, u32[]{:S(2)}, u32[]{:S(2)}) collective-permute-start(bf16[160,512]{1,0:T(8,128)(2,1)S(1)} %get-tuple-element.57), channel_id=1, source_target_pairs={{1,64},{3,65},{5,80},{7,81},{9,96},{11,97},{13,112},{15,113},{17,6... | collective-permute-start | bytes 491528 | tf_op jit(solution)/shard_map/ppermute | solution.py:402
  567.0 7.5 %collective-permute-start.3 = (bf16[160,512]{1,0:T(8,128)(2,1)S(1)}, bf16[160,512]{1,0:T(8,128)(2,1)}, u32[]{:S(2)}, u32[]{:S(2)}) collective-permute-start(bf16[160,512]{1,0:T(8,128)(2,1)S(1)} %get-tuple-element.57), channel_id=1, source_target_pairs={{0,64},{2,65},{4,80},{6,81},{8,96},{10,97},{12,112},{14,113},{16,6... | collective-permute-start | bytes 491528 | tf_op jit(solution)/shard_map/ppermute | solution.py:402
  569.0 13.5 %all-to-all-start.15 = ((bf16[8,160,128]{2,1,0:T(8,128)(2,1)}), bf16[8,160,128]{2,1,0:T(8,128)(2,1)S(1)}, u32[]{:S(2)}, u32[]{:S(2)}) async-start(bf16[8,160,128]{2,1,0:T(8,128)(2,1)} %pad_maximum_fusion.4), calls=%async_computation.16 | async-start | bytes 655360 | tf_op jit(solution)/shard_map/all_to_all | solution.py:31
  584.0 13.9 %copy-start.29 = (bf16[8,256,640]{2,1,0:T(8,128)(2,1)S(1)}, bf16[8,256,640]{2,1,0:T(8,128)(2,1)}, u32[]{:S(2)}) copy-start(bf16[8,256,640]{2,1,0:T(8,128)(2,1)} %copy-done.28) | copy-start | bytes 7864324
  591.4 19.3 %all-to-all-start.16 = ((bf16[16,2,32,320]{3,2,1,0:T(8,128)(2,1)}), bf16[16,2,32,320]{3,2,1,0:T(8,128)(2,1)}, u32[]{:S(2)}, u32[]{:S(2)}) async-start(bf16[16,2,32,320]{3,2,1,0:T(8,128)(2,1)} %copy.69), calls=%async_computation.17 | async-start | bytes 1572864 | tf_op jit(solution)/shard_map/all_to_all | solution.py:31
  600.6 13.4 %copy-start.1 = (bf16[256,5120]{1,0:T(8,128)(2,1)S(1)}, bf16[256,5120]{1,0:T(8,128)(2,1)}, u32[]{:S(2)}) copy-start(bf16[256,5120]{1,0:T(8,128)(2,1)} %param.9) | copy-start | bytes 7864324
  (10 other events, 8.3 us)
Sparse Core Ops, SparseCore 0:
  10.3 63.0 all-gather.6
  75.7 50.8 all-gather.4
  165.2 60.7 all-gather.8
  228.1 65.3 all-gather.10
  444.7 116.6 reduce-scatter.1

commit v4 on v3

--- a/solution.py
+++ b/solution.py
@@ -58,12 +58,23 @@
     return (master_new, moment_new, second_new)
 
 
-def run(kernel, shapes, *operands):
+def run(kernel, shapes, *operands, specs=None):
+    more = {}
+    if specs is not None:
+        whole = [pl.BlockSpec(x.shape, zeros_map(x.ndim)) for x in operands]
+        outs = [pl.BlockSpec(shape, zeros_map(len(shape))) for shape, _ in shapes]
+        given = [specs.get(at, spec) for at, spec in enumerate(whole)]
+        more = {"grid": (1,), "in_specs": given, "out_specs": outs}
     return pl.pallas_call(
         kernel,
         out_shape=[jax.ShapeDtypeStruct(shape, kind) for shape, kind in shapes],
         compiler_params=pltpu.CompilerParams(vmem_limit_bytes=VMEM_BYTES),
+        **more,
     )(*operands)
+
+
+def zeros_map(ndim):
+    return lambda step: (0,) * ndim
 
 
 def part(ref, at, inner):
@@ -87,16 +98,28 @@
     return total
 
 
-def order_of(first, last):
-    units = []
-    for j in range(first, last - 1):
-        units += [(j, t, False) for t in range(j, last - 1)]
-        units += [(j, t, True) for t in range(j + 1, last)]
-    return units
-
-
-def forward_chain(first, last, width, inner, down_ref, up_ref, up_start, gram_ref):
-    where = {unit: at for at, unit in enumerate(order_of(first, last))}
+def down_units(first, last):
+    return [(j, t, True) for j in range(first, last) for t in range(j + 1, last)]
+
+
+def up_units(first, last):
+    return [(j, t, False) for j in range(first, last - 1) for t in range(j, last - 1)]
+
+
+def finder(first, last, inner, down_ref, up_ref, up_start):
+    places = {unit: (down_ref, at) for at, unit in enumerate(down_units(first, last))}
+    if up_ref is not None:
+        for at, unit in enumerate(up_units(first, last)):
+            places[unit] = (up_ref, up_start + at)
+
+    def find(unit):
+        ref, at = places[unit]
+        return part(ref, at, inner)
+
+    return find
+
+
+def forward_chain(first, last, width, inner, down_ref, up_ref, up_start, find):
     count = last - first
     raw = {s: summed_part(down_ref, (s - first) * inner, inner) for s in range(first, last)}
     cross = {
@@ -117,20 +140,19 @@
         added = {}
         for k in range(first, last - 1):
             if k >= s:
-                added[k] = dot(act, part(gram_ref, where[(s, k, False)], inner), ROWS)
+                added[k] = dot(act, find((s, k, False)), ROWS)
             else:
-                added[k] = dot(act, part(gram_ref, where[(k, s, False)], inner), LAST)
+                added[k] = dot(act, find((k, s, False)), LAST)
         wide = act.astype(jnp.float32)
         square = square + jnp.sum(wide * (2.0 * cross[s] + added[s]), axis=1, keepdims=True)
         cross = {k: cross[k] + added[k] for k in cross}
         for t in range(s + 1, last):
-            raw[t] = raw[t] + dot(act, part(gram_ref, where[(s, t, True)], inner), ROWS)
+            raw[t] = raw[t] + dot(act, find((s, t, True)), ROWS)
         crosses[s + 1] = cross
     return state, crosses
 
 
-def backward_chain(first, last, width, inner, grad_ref, hidden_of, scale_of, cross_of, gram_ref):
-    where = {unit: at for at, unit in enumerate(order_of(first, last))}
+def backward_chain(first, last, width, inner, grad_ref, hidden_of, scale_of, cross_of, find):
     grad_act = {s: summed_part(grad_ref, (s - first) * inner, inner) for s in range(first, last)}
     packs, pulls = {}, {}
     for s in reversed(range(first, last)):
@@ -143,7 +165,7 @@
         for t in range(first, s):
             grad_act[t] = (
                 grad_act[t]
-                + dot(packs[s], part(gram_ref, where[(t, s, True)], inner), LAST)
+                + dot(packs[s], find((t, s, True)), LAST)
                 - pulls[s] * cross_of(s, t)
             )
     return packs, pulls
@@ -154,10 +176,11 @@
 
 
 def forward_kernel(first, last, width, inner, copies):
-    def kernel(down_ref, up_ref, gram_ref, acts_ref, hidden_ref, scale_ref, cross_ref):
-        state, crosses = forward_chain(
-            first, last, width, inner, down_ref, up_ref, 0, gram_ref
-        )
+    def kernel(
+        down_ref, up_ref, gram_in_ref, gram_out_ref, acts_ref, hidden_ref, scale_ref, cross_ref
+    ):
+        find = finder(first, last, inner, gram_in_ref, gram_out_ref, 0)
+        state, crosses = forward_chain(first, last, width, inner, down_ref, up_ref, 0, find)
         rows = down_ref.shape[1]
         for s in range(first, last):
             hidden, scale, act = state[s]
@@ -195,7 +218,7 @@
             lambda s: hidden_ref[s - first],
             lambda s: scale_ref[s - first][:, 0:1],
             lambda s, t: cross_ref[kept[(s, t)]],
-            gram_ref,
+            finder(first, last, inner, gram_ref, None, 0),
         )
         store_packs(out_ref, packs, pulls, first, last, inner, grad_ref.shape[1], copies)
 
@@ -205,8 +228,9 @@
 def turning_kernel(first, last, width, inner, copies):
     def kernel(sums_ref, grad_ref, gram_ref, out_ref):
         count = last - first
+        find = finder(first, last, inner, gram_ref, gram_ref, len(down_units(first, last)))
         state, crosses = forward_chain(
-            first, last, width, inner, sums_ref, sums_ref, count * inner + LANES, gram_ref
+            first, last, width, inner, sums_ref, sums_ref, count * inner + LANES, find
         )
         packs, pulls = backward_chain(
             first,
@@ -217,7 +241,7 @@
             lambda s: state[s][0],
             lambda s: state[s][1],
             lambda s, t: crosses[s][t],
-            gram_ref,
+            find,
         )
         rows = sums_ref.shape[1]
         store_packs(out_ref, packs, pulls, first, last, inner, rows, copies)
@@ -262,8 +286,8 @@
     lanes_out = chunk // LANES
 
     def kernel(*refs):
-        exact_ref, packs_ref, acts_ref, up_ref, in_ref, out_ref = refs[:6]
-        grads_ref, packed_ref, up_new_ref = refs[6:9]
+        core_ref, exact_ref, packs_ref, acts_ref, up_ref, in_ref, out_ref = refs[:7]
+        grads_ref, mine_ref, other_ref, up_new_ref = refs[7:11]
         exact = exact_ref[...].astype(jnp.float32)
         rows = {first: exact.astype(jnp.bfloat16)}
 
@@ -283,20 +307,35 @@
             at = 2 * (s - first)
             pull = pull[:, at : at + 1] + pull[:, at + 1 : at + 2]
             into = dot(rows[s], pack, FIRST).astype(jnp.bfloat16)
-            for piece in range(chunk // share_in):
-                device = (s - first) * (chunk // share_in) + piece
-                for c in range(lanes_in):
-                    packed_ref[device % 2, device // 2, c * share_in : (c + 1) * share_in] = into[
-                        piece * share_in : (piece + 1) * share_in, c * LANES : (c + 1) * LANES
-                    ]
             onto = dot(act_of(s), narrow, FIRST).astype(jnp.bfloat16)
             base = lanes_in * share_in + (s - first) * lanes_out * share_out
-            for device in range(n_dp):
-                for c in range(lanes_out):
-                    row = base + c * share_out
-                    packed_ref[device % 2, device // 2, row : row + share_out] = onto[
-                        device * share_out : (device + 1) * share_out, c * LANES : (c + 1) * LANES
-                    ]
+
+            def store(refs_of, into=into, onto=onto, base=base, s=s):
+                for piece in range(chunk // share_in):
+                    device = (s - first) * (chunk // share_in) + piece
+                    ref = refs_of[device % 2]
+                    for c in range(lanes_in):
+                        ref[device // 2, c * share_in : (c + 1) * share_in] = into[
+                            piece * share_in : (piece + 1) * share_in,
+                            c * LANES : (c + 1) * LANES,
+                        ]
+                for device in range(n_dp):
+                    ref = refs_of[device % 2]
+                    for c in range(lanes_out):
+                        row = base + c * share_out
+                        ref[device // 2, row : row + share_out] = onto[
+                            device * share_out : (device + 1) * share_out,
+                            c * LANES : (c + 1) * LANES,
+                        ]
+
+            @pl.when(core_ref[0] == 0)
+            def _():
+                store((mine_ref, other_ref))
+
+            @pl.when(core_ref[0] == 1)
+            def _():
+                store((other_ref, mine_ref))
+
             weight = in_ref[s * chunk : (s + 1) * chunk]
             upstream = (
                 upstream + dot(pack, weight, LAST) - pull * rows[s].astype(jnp.float32)
@@ -307,7 +346,7 @@
         if before < first:
             for s in range(before, first):
                 columns = dot(narrow, part(out_ref, s, chunk), LAST).astype(jnp.bfloat16)
-                refs[9][:, (s - before) * inner : (s - before + 1) * inner] = columns
+                refs[11][:, (s - before) * inner : (s - before + 1) * inner] = columns
 
     return kernel
 
@@ -331,37 +370,65 @@
     return kernel
 
 
-def adam_out_kernel(share, lanes):
-    def kernel(grad_ref, master_ref, moment_ref, second_ref, master_new, moment_new, second_new):
-        for device in range(grad_ref.shape[0]):
+def adam_kernel(share, lanes, share_in):
+    def kernel(*refs):
+        into_ref, onto_ref = refs[:2]
+        state_in, state_out = refs[2:5], refs[5:8]
+        new_in, new_out, pieces_ref = refs[8:11], refs[11:14], refs[14]
+        per = LANES // share
+        for c in range(into_ref.shape[1] // LANES):
+            there = slice(c * LANES, (c + 1) * LANES)
+            grad = into_ref[:, there].astype(jnp.float32)
+            results = adam_update(*(ref[:, there] for ref in state_in), grad)
+            for ref, value in zip(new_in, results):
+                ref[:, there] = value
+            turned = results[0].T.astype(jnp.bfloat16)
+            for q in range(per):
+                pieces_ref[c * per + q, 0] = turned[q * share : (q + 1) * share]
+        for device in range(onto_ref.shape[0]):
             for c in range(lanes):
                 at = (device * lanes + c) * LANES
-                grad = grad_ref[device, c * share : (c + 1) * share].astype(jnp.float32)
-                results = adam_update(
-                    master_ref[:, at : at + LANES],
-                    moment_ref[:, at : at + LANES],
-                    second_ref[:, at : at + LANES],
-                    grad,
-                )
-                for ref, value in zip((master_new, moment_new, second_new), results):
+                grad = onto_ref[device, c * share : (c + 1) * share].astype(jnp.float32)
+                results = adam_update(*(ref[:, at : at + LANES] for ref in state_out), grad)
+                for ref, value in zip(new_out, results):
                     ref[:, at : at + LANES] = value
-
-    return kernel
-
-
-def columns_kernel(order):
-    def kernel(every_ref, out_ref):
+        for device in range(pieces_ref.shape[0]):
+            at = device * share_in
+            start = at // LANES * LANES
+            stop = -(-(at + share_in) // LANES) * LANES
+            values = new_out[0][:, start:stop][:, at - start : at - start + share_in]
+            pieces_ref[device, 1] = values.astype(jnp.bfloat16)
+
+    return kernel
+
+
+def rollout_kernel(share, share_in):
+    def kernel(pieces_ref, in_ref, out_ref):
+        per = LANES // share
+        for pair in range(pieces_ref.shape[0] // 2):
+            both = [pieces_ref[2 * pair + h, 0].astype(jnp.float32) for h in range(2)]
+            at = 2 * pair * share_in
+            in_ref[:, at : at + 2 * share_in] = jnp.concatenate(both, axis=1).astype(jnp.bfloat16)
+        for c in range(pieces_ref.shape[0] // per):
+            rows = [pieces_ref[c * per + q, 1].astype(jnp.float32) for q in range(per)]
+            out_ref[:, c * LANES : (c + 1) * LANES] = jnp.concatenate(rows, axis=0).T.astype(
+                jnp.bfloat16
+            )
+
+    return kernel
+
+
+def columns_kernel(orders):
+    def kernel(every_ref, *out_refs):
         size = every_ref.shape[2]
-        for at, unit in enumerate(order):
-            out_ref[:, at * size : (at + 1) * size] = every_ref[unit]
-
-    return kernel
-
-
-def core_halves(packed, n_dp):
-    core = lax.axis_index("dp") % 2
-    mine = lax.dynamic_index_in_dim(packed, core, 0, keepdims=False)
-    other = lax.dynamic_index_in_dim(packed, 1 - core, 0, keepdims=False)
+        for out_ref, order in zip(out_refs, orders):
+            for at, unit in enumerate(order):
+                out_ref[:, at * size : (at + 1) * size] = every_ref[unit]
+
+    return kernel
+
+
+def core_halves(mine, other, n_dp):
     other = lax.ppermute(other, "dp", [(j, j + 1 - 2 * (j % 2)) for j in range(n_dp)])
     return (mine.astype(jnp.float32) + other.astype(jnp.float32)).astype(jnp.bfloat16)
 
@@ -370,8 +437,8 @@
     return [list(range(c, n_dp, 2)) for c in range(2)]
 
 
-def reduce_apart(packed, n_dp):
-    mine = core_halves(packed, n_dp)
+def reduce_apart(mine, other, n_dp):
+    mine = core_halves(mine, other, n_dp)
     rows = mine.shape[1]
     summed = lax.psum_scatter(
         mine.reshape(-1, LANES),
@@ -383,9 +450,9 @@
     return summed.reshape(1, rows, LANES)
 
 
-def reduce_now(packed, n_dp):
+def reduce_now(mine, other, n_dp):
     return lax.all_to_all(
-        core_halves(packed, n_dp), "dp", 0, 0, tiled=True, axis_index_groups=chips_of(n_dp)
+        core_halves(mine, other, n_dp), "dp", 0, 0, tiled=True, axis_index_groups=chips_of(n_dp)
     )
 
 
@@ -431,26 +498,34 @@
     all_out = lax.all_gather(flat_out, "dp", axis=0, tiled=True)
     weight_in = [all_in[s * chunk : (s + 1) * chunk] for s in range(n_pipe)]
 
-    def products(first, last):
-        units, partial = [], []
-        for t in range(first + 1, last):
-            left = piece_out[first:t].reshape(-1, chunk)
-            partial.append(dot(left, weight_in[t], ROWS))
-            units += [(k, t, True) for k in range(first, t)]
-        for t in range(first, last - 1):
-            left = piece_out[first : t + 1].reshape(-1, chunk)
-            partial.append(dot(left, weight_out[t], LAST))
-            units += [(k, t, False) for k in range(first, t + 1)]
+    def products(down, blocks):
+        units, partial, orders = [], [], []
+        for first, last in blocks:
+            wanted = (down_units if down else up_units)(first, last)
+            for t in sorted({t for _, t, _ in wanted}):
+                ks = [k for k, other, _ in wanted if other == t]
+                left = piece_out[ks[0] : ks[-1] + 1].reshape(-1, chunk)
+                if down:
+                    partial.append(dot(left, weight_in[t], ROWS))
+                else:
+                    partial.append(dot(left, weight_out[t], LAST))
+                units += [(k, t, down) for k in ks]
+        for first, last in blocks:
+            wanted = (down_units if down else up_units)(first, last)
+            orders.append([units.index(unit) for unit in wanted])
         padded = -(-len(units) // n_pipe) * n_pipe
         partial = [p.astype(jnp.bfloat16) for p in partial]
-        partial.append(jnp.zeros(((padded - len(units)) * share_out, inner), jnp.bfloat16))
+        if padded > len(units):
+            partial.append(jnp.zeros(((padded - len(units)) * share_out, inner), jnp.bfloat16))
         arrived = swap(jnp.concatenate(partial, axis=0), "pipe")
         arrived = arrived.reshape(n_pipe, -1, inner)
         mine = jnp.sum(arrived.astype(jnp.float32), axis=0).astype(jnp.bfloat16)
         every = swap(jnp.tile(mine, (n_pipe, 1)), "pipe").reshape(padded, share_out, inner)
-        order = [units.index(unit) for unit in order_of(first, last)]
-        shape = (share_out, len(units) * inner)
-        return run(columns_kernel(order), [(shape, jnp.bfloat16)], every)[0]
+        shapes = [((share_out, len(order) * inner), jnp.bfloat16) for order in orders]
+        return run(columns_kernel(orders), shapes, every)
+
+    def over_dp(columns):
+        return lax.all_gather(columns, "dp", axis=0, tiled=True)
 
     rows = lax.dynamic_slice_in_dim(inputs_x, me * chunk, chunk, 1)
     seed = lax.dynamic_slice_in_dim(cotangent, me * chunk, chunk, 1)
@@ -461,13 +536,20 @@
     down = [dot(rows, weight_in[s], ROWS) for s in range(first, middle)]
     down += split_scalars([jnp.sum(wide * wide, axis=1, keepdims=True)])
     down = exchanged(down, n_pipe)
-    all_out, down = lax.optimization_barrier((all_out, down))
+    (down_low,) = products(True, BLOCKS[:1])
+    all_out, down, down_low = lax.optimization_barrier((all_out, down, down_low))
     weight_out = [all_out[:, s * chunk : (s + 1) * chunk] for s in range(n_pipe)]
-    gram_low = lax.all_gather(products(first, middle), "dp", axis=0, tiled=True)
+    gram_in_low = over_dp(down_low)
+    up_low, up_high = products(False, BLOCKS)
+    gram_out_low = over_dp(up_low)
+    held_in, up_low = lax.optimization_barrier((all_in, up_low))
+    weight_in = [held_in[s * chunk : (s + 1) * chunk] for s in range(n_pipe)]
+    (down_high,) = products(True, BLOCKS[1:])
     up = exchanged([dot(rows, weight_out[s], LAST) for s in range(first, middle - 1)], n_pipe)
-    columns = products(middle, last)
-    gram_low, up, columns = lax.optimization_barrier((gram_low, up, columns))
-    gram_high = lax.all_gather(columns, "dp", axis=0, tiled=True)
+    gram_in_low, gram_out_low, up, columns = lax.optimization_barrier(
+        (gram_in_low, gram_out_low, up, jnp.concatenate([down_high, up_high], axis=1))
+    )
+    gram_high = over_dp(columns)
 
     kept = len(kept_crosses(first, middle))
     acts, hidden, scale, cross = run(
@@ -480,10 +562,11 @@
         ],
         down,
         up,
-        gram_low,
-    )
+        gram_in_low,
+        gram_out_low,
+    )
+    late, acts = lax.optimization_barrier((seed, acts))
     acts = swap(acts, "pipe")
-    late, acts = lax.optimization_barrier((seed, acts))
     exact, columns = run(
         next_rows_kernel(first, middle, last, inner, chunk),
         [
@@ -492,8 +575,13 @@
         ],
         rows,
         acts,
-        all_in[middle * chunk : last * chunk],
+        all_in,
         all_out,
+        specs={
+            2: pl.BlockSpec(
+                ((last - middle) * chunk, inner), lambda step: (middle // (last - middle), 0)
+            )
+        },
     )
     sums = exchanged(columns, n_pipe)
     grad_high = exchanged([dot(late, weight_out[s], LAST) for s in range(middle, last)], n_pipe)
@@ -509,25 +597,31 @@
 
     def packed_shape(group):
         rows_packed = 2 * group * chunk * inner // (n_dp * LANES)
-        return (2, n_dp // 2, rows_packed, LANES)
-
-    grads_high, packed_high, upstream, columns = run(
+        return (n_dp // 2, rows_packed, LANES)
+
+    core = (lax.axis_index("dp") % 2).astype(jnp.int32).reshape(1)
+    in_smem = {0: pl.BlockSpec(memory_space=pltpu.SMEM)}
+
+    grads_high, mine, other, upstream, columns = run(
         grads_kernel(middle, last, first, inner, chunk, n_dp, (last - middle) * inner + LANES),
         [
             ((last - middle, tok_rows, chunk), jnp.bfloat16),
             (packed_shape(last - middle), jnp.bfloat16),
+            (packed_shape(last - middle), jnp.bfloat16),
             ((tok_rows, chunk), jnp.float32),
             ((tok_rows, count * inner), jnp.bfloat16),
         ],
+        core,
         exact,
         turned,
         turned,
         seed,
         all_in,
         all_out,
+        specs=in_smem,
     )
     grad_low = exchanged(columns, n_pipe)
-    summed_high = reduce_apart(packed_high, n_dp)
+    summed_high = reduce_apart(mine, other, n_dp)
 
     packs = run(
         backward_kernel(first, middle, width, inner, n_pipe),
@@ -536,24 +630,27 @@
         hidden,
         scale,
         cross,
-        gram_low,
+        gram_in_low,
     )[0]
     packs = swap(packs, "pipe")
-    grads_low, packed_low, _ = run(
+    grads_low, mine, other, _ = run(
         grads_kernel(first, middle, first, inner, chunk, n_dp, 0),
         [
             ((count, tok_rows, chunk), jnp.bfloat16),
             (packed_shape(count), jnp.bfloat16),
+            (packed_shape(count), jnp.bfloat16),
             ((tok_rows, chunk), jnp.float32),
         ],
+        core,
         rows,
         packs,
         acts,
         upstream,
         all_in,
         all_out,
-    )
-    arrived_low = reduce_now(packed_low, n_dp)
+        specs=in_smem,
+    )
+    arrived_low = reduce_now(mine, other, n_dp)
 
     input_grads = swap(jnp.concatenate([grads_low, grads_high], axis=0), "pipe")
     input_grads, arrived_low = lax.optimization_barrier((input_grads, arrived_low))
@@ -577,23 +674,27 @@
         outs.append(sum_out.reshape(group, -1, LANES))
     grad_out = swap(jnp.concatenate(outs, axis=0), "pipe")
 
-    new_in, new_moment_in, new_second_in = adam_update(
-        master_in[0], moment_in[0], second_in[0], grad_in.astype(jnp.float32)
-    )
-    shape_out = (share_out, width)
-    new_out, new_moment_out, new_second_out = run(
-        adam_out_kernel(share_out, chunk // LANES),
-        [(shape_out, jnp.float32)] * 3,
+    shape_in, shape_out = (share_in, inner), (share_out, width)
+    *updated, pieces = run(
+        adam_kernel(share_out, chunk // LANES, share_in),
+        [(shape_in, jnp.float32)] * 3
+        + [(shape_out, jnp.float32)] * 3
+        + [((n_dp, 2, share_out, share_in), jnp.bfloat16)],
+        grad_in,
         grad_out,
+        master_in[0],
+        moment_in[0],
+        second_in[0],
         master_out[0],
         moment_out[0],
         second_out[0],
     )
-    cast_in = new_in.astype(jnp.bfloat16).T.reshape(n_dp, share_out, share_in)
-    cast_out = new_out.astype(jnp.bfloat16).reshape(share_out, n_dp, share_in).transpose(1, 0, 2)
-    swapped = swap(jnp.stack([cast_in, cast_out], axis=1), "dp")
-    roll_in = swapped[:, 0].transpose(1, 0, 2).reshape(share_out, width)
-    roll_out = swapped[:, 1].reshape(inner, share_in).T
+    new_in, new_moment_in, new_second_in, new_out, new_moment_out, new_second_out = updated
+    roll_in, roll_out = run(
+        rollout_kernel(share_out, share_in),
+        [(shape_out, jnp.bfloat16), (shape_in, jnp.bfloat16)],
+        swap(pieces, "dp"),
+    )
     return (
         input_grads,
         new_in[None],

time: 624 us -> 611 us (0.979)
  waiting for transfers between devices: 204 us -> 180 us
  blocking collectives: 164 us -> 184 us
  local copies, waits for them, and re-layouts: 52.2 us -> 38.3 us
  starting transfers between devices: 71.5 us -> 79.7 us
  other arithmetic: 28.9 us -> 22.3 us
    all_to_all x5 -> x6, blocking collectives: 116 us -> 135 us  [swap(): return lax.all_to_all(x, axis, 0, 0, tiled=True)]
    all_to_all x11 -> x12, waiting for transfers between devices: 143 us -> 124 us  [swap(): return lax.all_to_all(x, axis, 0, 0, tiled=True)]
    all_gather x1, waiting for transfers between devices: 29.2 us -> 15.7 us  [on_device(): all_out = lax.all_gather(flat_out, 'dp', axis=0, tiled=True)]
    ppermute x4, waiting for transfers between devices: 0.01 us -> 10.8 us  [move_in(): moved.append(lax.ppermute(summed, ('pipe', 'dp'), pairs))]
    all_to_all x11 -> x12, starting transfers between devices: 55.5 us -> 63.9 us  [swap(): return lax.all_to_all(x, axis, 0, 0, tiled=True)]
    squeeze x2 -> x0, local copies, waits for them, and re-layouts: 7.64 us -> none  [core_halves(): other = lax.dynamic_index_in_dim(packed, 1 - core, 0, keepdims=False)]
    pallas_call x11 -> x13, Pallas kernels: 44.9 us -> 47.1 us  [run(): pl.pallas_call(kernel, out_shape=[jax.ShapeDtypeStruct(shape, kind) for s...]
    unnamed x73 -> x84, local copies, waits for them, and re-layouts: 23.7 us -> 23.6 us
  transfers between devices with their start and end apart: 23 -> 25, of which waited for: 14 -> 16; matrix products, arithmetic and copies ran while one was open for 13% -> 13% of each run, Pallas kernels for 4% -> 4%
where the time goes in v4:
time: 611 us; the launch traced here: 604 us
  blocking collectives  184 us (30%)
  waiting for transfers between devices  180 us (29%)
  starting transfers between devices  79.7 us (13%)
  Pallas kernels  47.1 us (8%)
  local copies, waits for them, and re-layouts  38.3 us (6%)
  matrix products  37.8 us (6%)
  other arithmetic  22.3 us (4%)
  between operations  14.6 us (2%)
    all_to_all x6, blocking collectives, swap(): return lax.all_to_all(x, axis, 0, 0, tiled=True)  135 us
    all_to_all x12, waiting for transfers between devices, swap(): return lax.all_to_all(x, axis, 0, 0, tiled=True)  124 us
    all_to_all x12, starting transfers between devices, swap(): return lax.all_to_all(x, axis, 0, 0, tiled=True)  63.9 us
    all_to_all x1, blocking collectives, reduce_now(): lax.all_to_all(core_halves(mine, other, n_dp), 'dp', 0, 0, tiled=True, ax...  49.2 us
    pallas_call x13, Pallas kernels, run(): pl.pallas_call(kernel, out_shape=[jax.ShapeDtypeStruct(shape, kind) for s...  47.1 us
    dot_general x23, matrix products, dot(): lax.dot_general(left, right, (dims, ((), ())), preferred_element_type=jnp...  37.8 us
    unnamed x84, local copies, waits for them, and re-layouts  23.6 us
    all_gather x1, waiting for transfers between devices, on_device(): all_in = lax.all_gather(piece_in, 'dp', axis=0, tiled=True)  19.6 us
  transfers between devices with their start and end apart: 25, of which 16 were waited for; matrix products, arithmetic and copies ran while one was open for 13% of the time, Pallas kernels for 4%

profile of v4, /device:TPU:1, one launch (start us, length us, event | category | flops | bytes accessed | tf_op | source)
XLA Modules:
  0.0 604.0 jit_solution(13897679052065693456)
XLA Ops:
  11.2 37.5 %all_to_all.145 = bf16[8,32,640]{2,1,0:T(8,128)(2,1)S(1)} all-to-all(bf16[8,32,640]{2,1,0:T(8,128)(2,1)S(1)} %copy.42), channel_id=1, replica_groups=mesh['pipe'=8,'dp'=16] {'pipe'}, dimensions={0} | all-to-all | bytes 655360 | tf_op jit(solution)/shard_map/all_to_all | solution.py:31
  53.9 19.6 %all-gather.8.cloned.1.call-done.in_ref.refs_5_ = bf16[5120,512]{1,0:T(8,128)(2,1)} async-done(((bf16[320,512]{1,0:T(8,128)(2,1)}), bf16[5120,512]{1,0:T(8,128)(2,1)}) %all-gather.8.cloned.1.call-update) | async-done | bytes 5242896 | tf_op jit(solution)/shard_map/all_gather | solution.py:497
  78.3 6.1 %all-to-all-start.2 = ((bf16[8,32,512]{2,1,0:T(8,128)(2,1)}), bf16[8,32,512]{2,1,0:T(8,128)(2,1)S(1)}, u32[]{:S(2)}, u32[]{:S(2)}) async-start(bf16[8,32,512]{2,1,0:T(8,128)(2,1)} %bitcast.135), calls=%async_computation.2 | async-start | bytes 524288 | tf_op jit(solution)/shard_map/all_to_all | solution.py:31
  88.7 2.2 convolution_convert_fusion.8
  94.1 5.7 all-to-all-start.3
  102.5 3.3 concatenate.46
  107.0 5.4 all-to-all-start.1
  113.1 15.7 %all-gather.6.cloned.1.call-done.out_ref.refs_6_ = bf16[512,5120]{1,0:T(8,128)(2,1)} async-done(((bf16[32,5120]{1,0:T(8,128)(2,1)}), bf16[512,5120]{1,0:T(8,128)(2,1)}) %all-gather.6.cloned.1.call-update) | async-done | bytes 5242896 | tf_op jit(solution)/shard_map/all_gather | solution.py:498
  138.7 15.6 %all_to_all.146 = bf16[8,64,512]{2,1,0:T(8,128)(2,1)} all-to-all(bf16[8,64,512]{2,1,0:T(8,128)(2,1)S(1)} %bitcast.136), channel_id=1, replica_groups=mesh['pipe'=8,'dp'=16] {'pipe'}, dimensions={0} | all-to-all | bytes 1048576 | tf_op jit(solution)/shard_map/all_to_all | solution.py:31
  155.4 14.7 %all_to_all.147 = bf16[8,64,512]{2,1,0:T(8,128)(2,1)S(1)} all-to-all(bf16[8,64,512]{2,1,0:T(8,128)(2,1)S(1)} %tile.7), channel_id=1, replica_groups=mesh['pipe'=8,'dp'=16] {'pipe'}, dimensions={0} | all-to-all | bytes 1048576 | tf_op jit(solution)/shard_map/all_to_all | solution.py:31
  171.5 2.2 convolution_convert_fusion.4
  180.7 5.6 all-to-all-start.7
  188.5 5.2 all-to-all-done.7
  194.5 3.4 all-to-all-start.8
  199.9 5.3 all-to-all-done.8.every_ref
  205.9 3.6 all-to-all-start.6
  212.2 7.3 %all-to-all-done.6.up_ref = bf16[8,32,1536]{2,1,0:T(8,128)(2,1)S(1)} async-done(((bf16[8,32,1536]{2,1,0:T(8,128)(2,1)}), bf16[8,32,1536]{2,1,0:T(8,128)(2,1)S(1)}, u32[]{:S(2)}, u32[]{:S(2)}) %all-to-all-start.6) | async-done | bytes 786464 | tf_op jit(solution)/shard_map/all_to_all | solution.py:31
  219.5 2.6 all-gather.12.cloned.1.call-done.gram_out_ref
  223.0 6.2 %shard_map.154 = (bf16[256,2048]{1,0:T(8,128)(2,1)}, f32[4,32,512]{2,1,0:T(8,128)S(1)}, f32[4,32,128]{2,1,0:T(8,128)S(1)}, f32[6,32,512]{2,1,0:T(8,128)S(1)}) custom-call(bf16[8,32,2176]{2,1,0:T(8,128)(2,1)} %all-to-all-done.1.down_ref, bf16[8,32,1536]{2,1,0:T(8,128)(2,1)S(1)} %all-to-all-done.6.up_ref, ...), custom_call_target="tpu_custom_call" | custom-call | tf_op jit(solution)/shard_map/pallas_call | solution.py:68
  231.2 7.8 %all-to-all-start.9 = ((bf16[8,32,2048]{2,1,0:T(8,128)(2,1)}), bf16[8,32,2048]{2,1,0:T(8,128)(2,1)S(1)}, u32[]{:S(2)}, u32[]{:S(2)}) async-start(bf16[8,32,2048]{2,1,0:T(8,128)(2,1)} %bitcast.28), calls=%async_computation.9 | async-start | bytes 2097152 | tf_op jit(solution)/shard_map/all_to_all | solution.py:31
  246.2 10.5 %all-to-all-done.9 = bf16[8,32,2048]{2,1,0:T(8,128)(2,1)S(1)} async-done(((bf16[8,32,2048]{2,1,0:T(8,128)(2,1)}), bf16[8,32,2048]{2,1,0:T(8,128)(2,1)S(1)}, u32[]{:S(2)}, u32[]{:S(2)}) %all-to-all-start.9) | async-done | bytes 1048608 | tf_op jit(solution)/shard_map/all_to_all | solution.py:31
  256.7 4.3 all-to-all-start.11
  261.0 5.9 shard_map.155
  268.9 9.9 %all-to-all-done.11.grad_ref = bf16[8,32,2048]{2,1,0:T(8,128)(2,1)S(1)} async-done(((bf16[8,32,2048]{2,1,0:T(8,128)(2,1)}), bf16[8,32,2048]{2,1,0:T(8,128)(2,1)S(1)}, u32[]{:S(2)}, u32[]{:S(2)}) %all-to-all-start.11) | async-done | bytes 1048608 | tf_op jit(solution)/shard_map/all_to_all | solution.py:31
  279.8 29.1 %all_to_all.148.sums_ref = bf16[8,32,3712]{2,1,0:T(8,128)(2,1)S(1)} all-to-all(bf16[8,32,3712]{2,1,0:T(8,128)(2,1)} %bitcast.119), channel_id=1, replica_groups=mesh['pipe'=8,'dp'=16] {'pipe'}, dimensions={0} | all-to-all | bytes 3801088 | tf_op jit(solution)/shard_map/all_to_all | solution.py:31
  310.1 6.0 shard_map.156
  317.5 5.5 all-to-all-start.12
  323.0 31.5 %all-to-all-done.12 = bf16[8,32,4224]{2,1,0:T(8,128)(2,1)S(1)} async-done(((bf16[8,32,4224]{2,1,0:T(8,128)(2,1)}), bf16[8,32,4224]{2,1,0:T(8,128)(2,1)S(1)}, u32[]{:S(2)}, u32[]{:S(2)}) %all-to-all-start.12) | async-done | bytes 2162720 | tf_op jit(solution)/shard_map/all_to_all | solution.py:31
  356.6 10.8 %shard_map.157 = (bf16[4,256,640]{2,1,0:T(8,128)(2,1)S(1)}, bf16[8,1280,128]{2,1,0:T(8,128)(2,1)}, bf16[8,1280,128]{2,1,0:T(8,128)(2,1)}, f32[256,640]{1,0:T(8,128)S(1)}, bf16[256,2048]{1,0:T(8,128)(2,1)S(1)}) custom-call(s32[1]{0:T(128)} %bitcast.refs_0_, f32[256,640]{1,0:T(8,128)S(1)} %copy-done.21, bf16[256,4224]{1,0:T(8,128)(2,1)S(1)} %bitcast.109, ...), custom_call_target="tpu_custom_call" | custom-call | tf_op jit(solution)/shard_map/pallas_call | solution.py:68
  370.1 19.2 %all_to_all.149.grad_ref = bf16[8,32,2048]{2,1,0:T(8,128)(2,1)S(1)} all-to-all(bf16[8,32,2048]{2,1,0:T(8,128)(2,1)S(1)} %bitcast.120), channel_id=1, replica_groups=mesh['pipe'=8,'dp'=16] {'pipe'}, dimensions={0} | all-to-all | bytes 2097152 | tf_op jit(solution)/shard_map/all_to_all | solution.py:31
  390.7 18.8 %all_to_all.150 = bf16[8,32,2176]{2,1,0:T(8,128)(2,1)S(1)} all-to-all(bf16[8,32,2176]{2,1,0:T(8,128)(2,1)S(1)} %bitcast.114), channel_id=1, replica_groups=mesh['pipe'=8,'dp'=16] {'pipe'}, dimensions={0} | all-to-all | bytes 2228224 | tf_op jit(solution)/shard_map/all_to_all | solution.py:31
  409.4 11.3 %shard_map.159 = (bf16[4,256,640]{2,1,0:T(8,128)(2,1)S(1)}, bf16[8,1280,128]{2,1,0:T(8,128)(2,1)}, bf16[8,1280,128]{2,1,0:T(8,128)(2,1)}, f32[256,640]{1,0:T(8,128)}) custom-call(s32[1]{0:T(128)} %bitcast.refs_0_, bf16[256,640]{1,0:T(8,128)(2,1)S(1)} %copy-done.7, bf16[256,2176]{1,0:T(8,128)(2,1)S(1)} %bitcast.115, bf16[256,2048]{1,0:T(8,128)(2,1)S(1)} %bitcast.112, ...), custom_call_target="tpu_custom_call" | custom-call | tf_op jit(solution)/shard_map/pallas_call | solution.py:68
  421.9 2.8 collective-permute-start.1
  424.6 2.2 add_convert_fusion
  428.7 4.7 all-to-all-start.15
  433.4 3.9 add_convert_fusion.1
  437.3 47.0 %all-to-all-done.15 = bf16[8,256,640]{2,1,0:T(8,128)(2,1)} async-done(((bf16[8,256,640]{2,1,0:T(8,128)(2,1)}), bf16[8,256,640]{2,1,0:T(8,128)(2,1)}, u32[]{:S(2)}, u32[]{:S(2)}) %all-to-all-start.15) | async-done | bytes 2621472 | tf_op jit(solution)/shard_map/all_to_all | solution.py:31
  484.3 49.2 %all_to_all.151.arrived_ref = bf16[8,1280,128]{2,1,0:T(8,128)(2,1)S(1)} all-to-all(bf16[8,1280,128]{2,1,0:T(8,128)(2,1)} %add_convert_fusion.1), channel_id=1, replica_groups={{0,2,4,6,8,10,12,14},{1,3,5,7,9,11,13,15},{16,18,20,22,24,26,28,30},{17..., dimensions={0} | all-to-all | bytes 5242880 | tf_op jit(solution)/shard_map/all_to_all | solution.py:454
  533.8 7.3 %reduce-scatter.2.cloned.1.call-done = bf16[1280,128]{1,0:T(8,128)(2,1)} async-done(((bf16[10240,128]{1,0:T(8,128)(2,1)}), bf16[1280,128]{1,0:T(8,128)(2,1)}) %reduce-scatter.2.cloned.1.call-update) | async-done | bytes 327696 | tf_op jit(solution)/shard_map/reduce_scatter | solution.py:443
  542.9 8.1 %all-to-all-start.17 = ((bf16[8,160,128]{2,1,0:T(8,128)(2,1)}), bf16[8,160,128]{2,1,0:T(8,128)(2,1)S(1)}, u32[]{:S(2)}, u32[]{:S(2)}) async-start(bf16[8,160,128]{2,1,0:T(8,128)(2,1)} %pad_maximum_fusion.4), calls=%async_computation.18 | async-start | bytes 655360 | tf_op jit(solution)/shard_map/all_to_all | solution.py:31
  551.0 2.8 collective-permute-start.6
  555.2 5.1 collective-permute-start.4
  561.6 10.8 %collective-permute-done.4 = bf16[160,512]{1,0:T(8,128)(2,1)} collective-permute-done((bf16[160,512]{1,0:T(8,128)(2,1)S(1)}, bf16[160,512]{1,0:T(8,128)(2,1)}, u32[]{:S(2)}, u32[]{:S(2)}) %collective-permute-start.4) | collective-permute-done | bytes 163872 | tf_op jit(solution)/shard_map/ppermute | solution.py:469
  575.8 2.8 shard_map.162
  579.5 3.9 all-to-all-start.18
  583.4 4.6 copy.47
  588.0 4.4 copy.48
  592.4 3.8 all-to-all-done.18.pieces_ref
  (171 shorter events, 88.5 us)
Async XLA Ops:
  7.2 215.0 %copy-start = (bf16[256,5120]{1,0:T(8,128)(2,1)S(1)}, bf16[256,5120]{1,0:T(8,128)(2,1)}, u32[]{:S(2)}) copy-start(bf16[256,5120]{1,0:T(8,128)(2,1)} %param.9) | copy-start | bytes 7864324
  7.2 66.3 %all-gather.8.cloned.1.call-start = ((), (), s32[]{:S(2)}) async-start(), calls=%async_computation.21 | async-start | bytes 5570560 | tf_op jit(solution)/shard_map/all_gather | solution.py:497
  8.5 0.7 collective-permute-start
  10.0 118.9 %all-gather.6.cloned.1.call-start = ((), (), s32[]{:S(2)}) async-start(), calls=%async_computation.20 | async-start | bytes 5570560 | tf_op jit(solution)/shard_map/all_gather | solution.py:498
  50.7 135.6 %copy-start.6 = (bf16[256,640]{1,0:T(8,128)(2,1)}, bf16[256,640]{1,0:T(8,128)(2,1)S(1)}, u32[]{:S(2)}) copy-start(bf16[256,640]{1,0:T(8,128)(2,1)S(1)} %get-tuple-element.137.rows_ref.refs_1_) | copy-start | bytes 983044
  53.2 22.9 %copy-start.40 = (bf16[2,32,640]{2,1,0:T(8,128)(2,1)}, bf16[2,32,640]{2,1,0:T(8,128)(2,1)S(1)}, u32[]{:S(2)}) copy-start(bf16[2,32,640]{2,1,0:T(8,128)(2,1)S(1)} %get-tuple-element.141) | copy-start | bytes 245764
  53.9 24.4 %copy-start.39 = (bf16[3,32,640]{2,1,0:T(8,128)(2,1)}, bf16[3,32,640]{2,1,0:T(8,128)(2,1)S(1)}, u32[]{:S(2)}) copy-start(bf16[3,32,640]{2,1,0:T(8,128)(2,1)S(1)} %get-tuple-element.139) | copy-start | bytes 368644
  78.3 13.7 %all-to-all-start.2 = ((bf16[8,32,512]{2,1,0:T(8,128)(2,1)}), bf16[8,32,512]{2,1,0:T(8,128)(2,1)S(1)}, u32[]{:S(2)}, u32[]{:S(2)}) async-start(bf16[8,32,512]{2,1,0:T(8,128)(2,1)} %bitcast.135), calls=%async_computation.2 | async-start | bytes 524288 | tf_op jit(solution)/shard_map/all_to_all | solution.py:31
  94.1 13.0 %all-to-all-start.3 = ((bf16[8,32,512]{2,1,0:T(8,128)(2,1)}), bf16[8,32,512]{2,1,0:T(8,128)(2,1)S(1)}, u32[]{:S(2)}, u32[]{:S(2)}) async-start(bf16[8,32,512]{2,1,0:T(8,128)(2,1)} %tile.6), calls=%async_computation.3 | async-start | bytes 524288 | tf_op jit(solution)/shard_map/all_to_all | solution.py:31
  107.0 23.0 %all-to-all-start.1 = ((bf16[8,32,2176]{2,1,0:T(8,128)(2,1)}), bf16[8,32,2176]{2,1,0:T(8,128)(2,1)}, u32[]{:S(2)}, u32[]{:S(2)}) async-start(bf16[8,32,2176]{2,1,0:T(8,128)(2,1)} %concatenate.46), calls=%async_computation.1 | async-start | bytes 2228224 | tf_op jit(solution)/shard_map/all_to_all | solution.py:31
  112.4 107.1 %all-gather.10.cloned.1.call-start = ((), (), s32[]{:S(2)}) async-start(), calls=%async_computation.22 | async-start | bytes 3342336 | tf_op jit(solution)/shard_map/all_gather | solution.py:528
  130.1 92.1 %all-gather.12.cloned.1.call-start = ((), (), s32[]{:S(2)}) async-start(), calls=%async_computation.23 | async-start | bytes 3342336 | tf_op jit(solution)/shard_map/all_gather | solution.py:528
  135.7 42.9 %copy-start.38 = (bf16[3,32,640]{2,1,0:T(8,128)(2,1)S(1)}, bf16[3,32,640]{2,1,0:T(8,128)(2,1)}, u32[]{:S(2)}) copy-start(bf16[3,32,640]{2,1,0:T(8,128)(2,1)} %get-tuple-element.138) | copy-start | bytes 368644
  177.1 20.8 %copy-start.37 = (bf16[256,512]{1,0:T(8,128)(2,1)S(1)}, bf16[256,512]{1,0:T(8,128)(2,1)}, u32[]{:S(2)}) copy-start(bf16[256,512]{1,0:T(8,128)(2,1)} %convolution_convert_fusion.4) | copy-start | bytes 786436
  180.7 13.0 %all-to-all-start.7 = ((bf16[8,32,512]{2,1,0:T(8,128)(2,1)}), bf16[8,32,512]{2,1,0:T(8,128)(2,1)S(1)}, u32[]{:S(2)}, u32[]{:S(2)}) async-start(bf16[8,32,512]{2,1,0:T(8,128)(2,1)} %bitcast.27), calls=%async_computation.7 | async-start | bytes 524288 | tf_op jit(solution)/shard_map/all_to_all | solution.py:31
  194.5 10.7 %all-to-all-start.8 = ((bf16[8,32,512]{2,1,0:T(8,128)(2,1)}), bf16[8,32,512]{2,1,0:T(8,128)(2,1)S(1)}, u32[]{:S(2)}, u32[]{:S(2)}) async-start(bf16[8,32,512]{2,1,0:T(8,128)(2,1)} %tile.8), calls=%async_computation.8 | async-start | bytes 524288 | tf_op jit(solution)/shard_map/all_to_all | solution.py:31
  205.9 13.6 %all-to-all-start.6 = ((bf16[8,32,1536]{2,1,0:T(8,128)(2,1)}), bf16[8,32,1536]{2,1,0:T(8,128)(2,1)S(1)}, u32[]{:S(2)}, u32[]{:S(2)}) async-start(bf16[8,32,1536]{2,1,0:T(8,128)(2,1)} %bitcast.131), calls=%async_computation.6 | async-start | bytes 1572864 | tf_op jit(solution)/shard_map/all_to_all | solution.py:31
  209.5 99.5 %all-gather.14.cloned.1.call-start = ((), (), s32[]{:S(2)}) async-start(), calls=%async_computation.24 | async-start | bytes 6684672 | tf_op jit(solution)/shard_map/all_gather | solution.py:528
  223.0 16.0 %copy-start.15 = (bf16[256,640]{1,0:T(8,128)(2,1)S(1)}, bf16[256,640]{1,0:T(8,128)(2,1)}, u32[]{:S(2)}) copy-start(bf16[256,640]{1,0:T(8,128)(2,1)} %constant_dynamic-slice_fusion.refs_4_) | copy-start | bytes 983044
  231.2 25.5 %all-to-all-start.9 = ((bf16[8,32,2048]{2,1,0:T(8,128)(2,1)}), bf16[8,32,2048]{2,1,0:T(8,128)(2,1)S(1)}, u32[]{:S(2)}, u32[]{:S(2)}) async-start(bf16[8,32,2048]{2,1,0:T(8,128)(2,1)} %bitcast.28), calls=%async_computation.9 | async-start | bytes 2097152 | tf_op jit(solution)/shard_map/all_to_all | solution.py:31
  239.0 22.0 %copy-start.7 = (bf16[256,640]{1,0:T(8,128)(2,1)S(1)}, bf16[256,640]{1,0:T(8,128)(2,1)}, u32[]{:S(2)}) copy-start(bf16[256,640]{1,0:T(8,128)(2,1)} %copy-done.6) | copy-start | bytes 983044
  256.7 22.1 %all-to-all-start.11 = ((bf16[8,32,2048]{2,1,0:T(8,128)(2,1)}), bf16[8,32,2048]{2,1,0:T(8,128)(2,1)S(1)}, u32[]{:S(2)}, u32[]{:S(2)}) async-start(bf16[8,32,2048]{2,1,0:T(8,128)(2,1)} %bitcast.31), calls=%async_computation.11 | async-start | bytes 2097152 | tf_op jit(solution)/shard_map/all_to_all | solution.py:31
  266.8 1.3 copy-start.10
  316.2 1.3 copy-start.3
  317.5 37.0 %all-to-all-start.12 = ((bf16[8,32,4224]{2,1,0:T(8,128)(2,1)}), bf16[8,32,4224]{2,1,0:T(8,128)(2,1)S(1)}, u32[]{:S(2)}, u32[]{:S(2)}) async-start(bf16[8,32,4224]{2,1,0:T(8,128)(2,1)} %bitcast.113), calls=%async_computation.12 | async-start | bytes 4325376 | tf_op jit(solution)/shard_map/all_to_all | solution.py:31
  323.0 218.1 %reduce-scatter.2.cloned.1.call-start = ((), (), s32[]{:S(2)}) async-start(), calls=%async_computation.25 | async-start | bytes 2949120 | tf_op jit(solution)/shard_map/reduce_scatter | solution.py:443
  356.6 32.7 %copy-start.2 = (bf16[512,3072]{1,0:T(8,128)(2,1)S(1)}, bf16[512,3072]{1,0:T(8,128)(2,1)}, u32[]{:S(2)}) copy-start(bf16[512,3072]{1,0:T(8,128)(2,1)} %all-gather.10.cloned.1.call-done.gram_in_ref.gram_ref) | copy-start | bytes 9437188
  356.6 32.7 %copy-start.27 = (f32[6,32,512]{2,1,0:T(8,128)S(1)}, f32[6,32,512]{2,1,0:T(8,128)}, u32[]{:S(2)}) copy-start(f32[6,32,512]{2,1,0:T(8,128)} %copy-done.26) | copy-start | bytes 1179652
  356.6 32.7 %copy-start.30 = (f32[4,32,512]{2,1,0:T(8,128)S(1)}, f32[4,32,512]{2,1,0:T(8,128)}, u32[]{:S(2)}) copy-start(f32[4,32,512]{2,1,0:T(8,128)} %copy-done.29) | copy-start | bytes 786436
  356.6 32.7 %copy-start.33 = (f32[4,32,128]{2,1,0:T(8,128)S(1)}, f32[4,32,128]{2,1,0:T(8,128)}, u32[]{:S(2)}) copy-start(f32[4,32,128]{2,1,0:T(8,128)} %copy-done.32) | copy-start | bytes 196612
  368.5 56.1 %collective-permute-start.2 = (bf16[8,1280,128]{2,1,0:T(8,128)(2,1)}, bf16[8,1280,128]{2,1,0:T(8,128)(2,1)S(1)}, u32[]{:S(2)}, u32[]{:S(2)}) collective-permute-start(bf16[8,1280,128]{2,1,0:T(8,128)(2,1)} %get-tuple-element.76), channel_id=1, source_target_pairs={{0,1},{1,0},{2,3},{3,2},{4,5},{5,4},{6,7},{7,6},{8,9},{9,8},{10,11... | collective-permute-start | bytes 7864328 | tf_op jit(solution)/shard_map/ppermute | solution.py:432
  409.4 15.2 %copy-start.34 = (bf16[8,1280,128]{2,1,0:T(8,128)(2,1)S(1)}, bf16[8,1280,128]{2,1,0:T(8,128)(2,1)}, u32[]{:S(2)}) copy-start(bf16[8,1280,128]{2,1,0:T(8,128)(2,1)} %get-tuple-element.75) | copy-start | bytes 7864324
  421.9 11.5 %collective-permute-start.1 = (bf16[8,1280,128]{2,1,0:T(8,128)(2,1)}, bf16[8,1280,128]{2,1,0:T(8,128)(2,1)}, u32[]{:S(2)}, u32[]{:S(2)}) collective-permute-start(bf16[8,1280,128]{2,1,0:T(8,128)(2,1)} %get-tuple-element.73), channel_id=1, source_target_pairs={{0,1},{1,0},{2,3},{3,2},{4,5},{5,4},{6,7},{7,6},{8,9},{9,8},{10,11... | collective-permute-start | bytes 7864328 | tf_op jit(solution)/shard_map/ppermute | solution.py:432
  424.6 2.3 copy-start.12
  424.6 2.3 copy-start.14
  428.7 4.7 copy-start.35
  428.7 55.6 %all-to-all-start.15 = ((bf16[8,256,640]{2,1,0:T(8,128)(2,1)}), bf16[8,256,640]{2,1,0:T(8,128)(2,1)}, u32[]{:S(2)}, u32[]{:S(2)}) async-start(bf16[8,256,640]{2,1,0:T(8,128)(2,1)} %pad_maximum_fusion), calls=%async_computation.15 | async-start | bytes 5242880 | tf_op jit(solution)/shard_map/all_to_all | solution.py:31
  437.3 136.3 %copy-start.8 = (f32[1,320,512]{2,1,0:T(8,128)S(1)}, f32[1,320,512]{2,1,0:T(8,128)}, u32[]{:S(2)}) copy-start(f32[1,320,512]{2,1,0:T(8,128)} %param.10) | copy-start | bytes 1966084
  437.3 136.3 %copy-start.9 = (f32[1,32,5120]{2,1,0:T(8,128)S(1)}, f32[1,32,5120]{2,1,0:T(8,128)}, u32[]{:S(2)}) copy-start(f32[1,32,5120]{2,1,0:T(8,128)} %param.11) | copy-start | bytes 1966084
  437.3 136.3 %copy-start.22 = (f32[1,320,512]{2,1,0:T(8,128)S(1)}, f32[1,320,512]{2,1,0:T(8,128)}, u32[]{:S(2)}) copy-start(f32[1,320,512]{2,1,0:T(8,128)} %param.12) | copy-start | bytes 1966084
  437.3 136.3 %copy-start.23 = (f32[1,320,512]{2,1,0:T(8,128)S(1)}, f32[1,320,512]{2,1,0:T(8,128)}, u32[]{:S(2)}) copy-start(f32[1,320,512]{2,1,0:T(8,128)} %param.14) | copy-start | bytes 1966084
  542.9 30.6 %all-to-all-start.17 = ((bf16[8,160,128]{2,1,0:T(8,128)(2,1)}), bf16[8,160,128]{2,1,0:T(8,128)(2,1)S(1)}, u32[]{:S(2)}, u32[]{:S(2)}) async-start(bf16[8,160,128]{2,1,0:T(8,128)(2,1)} %pad_maximum_fusion.4), calls=%async_computation.18 | async-start | bytes 655360 | tf_op jit(solution)/shard_map/all_to_all | solution.py:31
  551.0 10.5 %collective-permute-start.6 = (bf16[160,512]{1,0:T(8,128)(2,1)S(1)}, bf16[160,512]{1,0:T(8,128)(2,1)S(1)}, u32[]{:S(2)}, u32[]{:S(2)}) collective-permute-start(bf16[160,512]{1,0:T(8,128)(2,1)S(1)} %get-tuple-element.79), channel_id=1, source_target_pairs={{1,0},{3,1},{5,16},{7,17},{9,32},{11,33},{13,48},{15,49},{17,2},{1... | collective-permute-start | bytes 491528 | tf_op jit(solution)/shard_map/ppermute | solution.py:469
  553.9 7.7 %collective-permute-start.5 = (bf16[160,512]{1,0:T(8,128)(2,1)S(1)}, bf16[160,512]{1,0:T(8,128)(2,1)}, u32[]{:S(2)}, u32[]{:S(2)}) collective-permute-start(bf16[160,512]{1,0:T(8,128)(2,1)S(1)} %get-tuple-element.79), channel_id=1, source_target_pairs={{0,0},{2,1},{4,16},{6,17},{8,32},{10,33},{12,48},{14,49},{16,2},{1... | collective-permute-start | bytes 491528 | tf_op jit(solution)/shard_map/ppermute | solution.py:469
  555.2 17.2 %collective-permute-start.4 = (bf16[160,512]{1,0:T(8,128)(2,1)S(1)}, bf16[160,512]{1,0:T(8,128)(2,1)}, u32[]{:S(2)}, u32[]{:S(2)}) collective-permute-start(bf16[160,512]{1,0:T(8,128)(2,1)S(1)} %get-tuple-element.77), channel_id=1, source_target_pairs={{1,64},{3,65},{5,80},{7,81},{9,96},{11,97},{13,112},{15,113},{17,6... | collective-permute-start | bytes 491528 | tf_op jit(solution)/shard_map/ppermute | solution.py:469
  560.3 12.1 %collective-permute-start.3 = (bf16[160,512]{1,0:T(8,128)(2,1)S(1)}, bf16[160,512]{1,0:T(8,128)(2,1)}, u32[]{:S(2)}, u32[]{:S(2)}) collective-permute-start(bf16[160,512]{1,0:T(8,128)(2,1)S(1)} %get-tuple-element.77), channel_id=1, source_target_pairs={{0,64},{2,65},{4,80},{6,81},{8,96},{10,97},{12,112},{14,113},{16,6... | collective-permute-start | bytes 491528 | tf_op jit(solution)/shard_map/ppermute | solution.py:469
  579.5 16.7 %all-to-all-start.18 = ((bf16[16,2,32,320]{3,2,1,0:T(8,128)(2,1)}), bf16[16,2,32,320]{3,2,1,0:T(8,128)(2,1)S(1)}, u32[]{:S(2)}, u32[]{:S(2)}) async-start(bf16[16,2,32,320]{3,2,1,0:T(8,128)(2,1)} %copy-done.19), calls=%async_computation.19 | async-start | bytes 1572864 | tf_op jit(solution)/shard_map/all_to_all | solution.py:31
  583.4 13.8 %copy-start.1 = (bf16[256,5120]{1,0:T(8,128)(2,1)S(1)}, bf16[256,5120]{1,0:T(8,128)(2,1)}, u32[]{:S(2)}) copy-start(bf16[256,5120]{1,0:T(8,128)(2,1)} %param.9) | copy-start | bytes 7864324
  (18 other events, 16.5 us)
Sparse Core Ops, SparseCore 0:
  10.3 63.1 all-gather.7
  75.7 53.0 all-gather.5
  131.2 44.9 all-gather.9
  178.3 43.8 all-gather.11
  224.3 76.5 all-gather.13
  427.0 114.0 reduce-scatter.1

commit v5 on v4

--- a/solution.py
+++ b/solution.py
@@ -286,7 +286,7 @@
     lanes_out = chunk // LANES
 
     def kernel(*refs):
-        core_ref, exact_ref, packs_ref, acts_ref, up_ref, in_ref, out_ref = refs[:7]
+        place_ref, exact_ref, packs_ref, acts_ref, up_ref, in_ref, out_ref = refs[:7]
         grads_ref, mine_ref, other_ref, up_new_ref = refs[7:11]
         exact = exact_ref[...].astype(jnp.float32)
         rows = {first: exact.astype(jnp.bfloat16)}
@@ -315,7 +315,7 @@
                     device = (s - first) * (chunk // share_in) + piece
                     ref = refs_of[device % 2]
                     for c in range(lanes_in):
-                        ref[device // 2, c * share_in : (c + 1) * share_in] = into[
+                        ref[place_ref[device // 2], c * share_in : (c + 1) * share_in] = into[
                             piece * share_in : (piece + 1) * share_in,
                             c * LANES : (c + 1) * LANES,
                         ]
@@ -323,16 +323,16 @@
                     ref = refs_of[device % 2]
                     for c in range(lanes_out):
                         row = base + c * share_out
-                        ref[device // 2, row : row + share_out] = onto[
+                        ref[place_ref[device // 2], row : row + share_out] = onto[
                             device * share_out : (device + 1) * share_out,
                             c * LANES : (c + 1) * LANES,
                         ]
 
-            @pl.when(core_ref[0] == 0)
+            @pl.when(place_ref[n_dp // 2] == 0)
             def _():
                 store((mine_ref, other_ref))
 
-            @pl.when(core_ref[0] == 1)
+            @pl.when(place_ref[n_dp // 2] == 1)
             def _():
                 store((other_ref, mine_ref))
 
@@ -351,34 +351,38 @@
     return kernel
 
 
-def unpack_kernel(inner, share_in):
-    def kernel(arrived_ref, in_ref, out_ref):
+def unpack_kernel(inner, share_in, sources):
+    def kernel(*refs):
+        in_ref, out_ref = refs[sources:]
         lanes = inner // LANES
+
+        def total_of(start, stop):
+            total = refs[0][start:stop].astype(jnp.float32)
+            for ref in refs[1:sources]:
+                total = total + ref[start:stop].astype(jnp.float32)
+            return total.astype(jnp.bfloat16)
+
         for c in range(lanes):
-            total = arrived_ref[0, c * share_in : (c + 1) * share_in].astype(jnp.float32)
-            for source in range(1, arrived_ref.shape[0]):
-                total = total + arrived_ref[source, c * share_in : (c + 1) * share_in].astype(
-                    jnp.float32
-                )
-            in_ref[:, c * LANES : (c + 1) * LANES] = total.astype(jnp.bfloat16)
-        start = lanes * share_in
-        total = arrived_ref[0, start:].astype(jnp.float32)
-        for source in range(1, arrived_ref.shape[0]):
-            total = total + arrived_ref[source, start:].astype(jnp.float32)
-        out_ref[...] = total.astype(jnp.bfloat16)
+            in_ref[:, c * LANES : (c + 1) * LANES] = total_of(c * share_in, (c + 1) * share_in)
+        out_ref[...] = total_of(lanes * share_in, refs[0].shape[0])
 
     return kernel
 
 
 def adam_kernel(share, lanes, share_in):
     def kernel(*refs):
-        into_ref, onto_ref = refs[:2]
-        state_in, state_out = refs[2:5], refs[5:8]
-        new_in, new_out, pieces_ref = refs[8:11], refs[11:14], refs[14]
+        swapped_ref, one_ref, two_ref, onto_ref = refs[:4]
+        state_in, state_out = refs[4:7], refs[7:10]
+        new_in, new_out, pieces_ref = refs[10:13], refs[13:16], refs[16]
         per = LANES // share
-        for c in range(into_ref.shape[1] // LANES):
+        for c in range(one_ref.shape[1] // LANES):
             there = slice(c * LANES, (c + 1) * LANES)
-            grad = into_ref[:, there].astype(jnp.float32)
+            one = one_ref[:, there].astype(jnp.float32)
+            two = two_ref[:, there].astype(jnp.float32)
+            swapped = swapped_ref[0] == 1
+            grad = jnp.concatenate(
+                [jnp.where(swapped, two, one), jnp.where(swapped, one, two)], axis=0
+            )
             results = adam_update(*(ref[:, there] for ref in state_in), grad)
             for ref, value in zip(new_in, results):
                 ref[:, there] = value
@@ -428,46 +432,55 @@
     return kernel
 
 
-def core_halves(mine, other, n_dp):
-    other = lax.ppermute(other, "dp", [(j, j + 1 - 2 * (j % 2)) for j in range(n_dp)])
-    return (mine.astype(jnp.float32) + other.astype(jnp.float32)).astype(jnp.bfloat16)
-
-
-def chips_of(n_dp):
-    return [list(range(c, n_dp, 2)) for c in range(2)]
-
-
-def reduce_apart(mine, other, n_dp):
-    mine = core_halves(mine, other, n_dp)
-    rows = mine.shape[1]
+def other_core(x, n_dp):
+    return lax.ppermute(x, "dp", [(j, j + 1 - 2 * (j % 2)) for j in range(n_dp)])
+
+
+def add_kernel(mine_ref, other_ref, *out_refs):
+    for at, out_ref in enumerate(out_refs):
+        total = mine_ref[at].astype(jnp.float32) + other_ref[at].astype(jnp.float32)
+        out_ref[...] = total.astype(jnp.bfloat16)
+
+
+def chip_steps(n_dp):
+    return [(dx, dz) for dx in range(n_dp // 4) for dz in range(2)]
+
+
+def between_chips(blocks, n_dp):
+    arrived = [blocks[0]]
+    for (dx, dz), block in list(zip(chip_steps(n_dp), blocks))[1:]:
+        pairs = []
+        for j in range(n_dp):
+            x, z, core = j // 4, j // 2 % 2, j % 2
+            pairs.append((j, (x + dx) % (n_dp // 4) * 4 + (z ^ dz) * 2 + core))
+        arrived.append(lax.ppermute(block, "dp", pairs))
+    return arrived
+
+
+def reduce_apart(mine, n_dp):
     summed = lax.psum_scatter(
         mine.reshape(-1, LANES),
         "dp",
         scatter_dimension=0,
         tiled=True,
-        axis_index_groups=chips_of(n_dp),
-    )
-    return summed.reshape(1, rows, LANES)
-
-
-def reduce_now(mine, other, n_dp):
-    return lax.all_to_all(
-        core_halves(mine, other, n_dp), "dp", 0, 0, tiled=True, axis_index_groups=chips_of(n_dp)
-    )
-
-
-def move_in(summed, first, group, n_pipe, n_dp):
-    per = n_pipe // group
+        axis_index_groups=[list(range(c, n_dp, 2)) for c in range(2)],
+    )
+    return [summed]
+
+
+def move_in(low, high, n_pipe, n_dp):
+    odd = lax.axis_index("dp") % 2 == 1
+    group = n_pipe // 2
     moved = []
-    for q in range(per):
+    for q in range(2):
         pairs = []
         for i in range(n_pipe):
-            for j in range(q, n_dp, per):
-                section = j * group // n_dp
-                half = j // per % 2
-                pairs.append((i * n_dp + j, (first + section) * n_dp + 2 * i + half))
-        moved.append(lax.ppermute(summed, ("pipe", "dp"), pairs))
-    return jnp.concatenate(moved, axis=0)
+            for j in range(n_dp):
+                section = j * group // n_dp + (0 if j % 2 == q else group)
+                pairs.append((i * n_dp + j, section * n_dp + 2 * i + j // 2 % 2))
+        payload = jnp.where(odd, low, high) if q == 1 else jnp.where(odd, high, low)
+        moved.append(lax.ppermute(payload, ("pipe", "dp"), pairs))
+    return moved
 
 
 def on_device(
@@ -599,7 +612,13 @@
         rows_packed = 2 * group * chunk * inner // (n_dp * LANES)
         return (n_dp // 2, rows_packed, LANES)
 
-    core = (lax.axis_index("dp") % 2).astype(jnp.int32).reshape(1)
+    dp = lax.axis_index("dp")
+    core, chip = dp % 2, dp // 2
+    chips = jnp.arange(n_dp // 2)
+    xs = n_dp // 4
+    away = (chips // 2 - chip // 2 + xs) % xs * 2 + (chips % 2 + chip % 2) % 2
+    fixed = jnp.concatenate([chips, core[None]]).astype(jnp.int32)
+    place = jnp.concatenate([away, core[None]]).astype(jnp.int32)
     in_smem = {0: pl.BlockSpec(memory_space=pltpu.SMEM)}
 
     grads_high, mine, other, upstream, columns = run(
@@ -611,7 +630,7 @@
             ((tok_rows, chunk), jnp.float32),
             ((tok_rows, count * inner), jnp.bfloat16),
         ],
-        core,
+        fixed,
         exact,
         turned,
         turned,
@@ -621,7 +640,10 @@
         specs=in_smem,
     )
     grad_low = exchanged(columns, n_pipe)
-    summed_high = reduce_apart(mine, other, n_dp)
+    other = other_core(other, n_dp)
+    mine = (mine.astype(jnp.float32) + other.astype(jnp.float32)).astype(jnp.bfloat16)
+    grad_low, mine = lax.optimization_barrier((grad_low, mine))
+    arrived_high = reduce_apart(mine, n_dp)
 
     packs = run(
         backward_kernel(first, middle, width, inner, n_pipe),
@@ -641,7 +663,7 @@
             (packed_shape(count), jnp.bfloat16),
             ((tok_rows, chunk), jnp.float32),
         ],
-        core,
+        place,
         rows,
         packs,
         acts,
@@ -650,29 +672,34 @@
         all_out,
         specs=in_smem,
     )
-    arrived_low = reduce_now(mine, other, n_dp)
+    blocks = run(
+        add_kernel,
+        [(mine.shape[1:], jnp.bfloat16)] * mine.shape[0],
+        mine,
+        other_core(other, n_dp),
+    )
+    arrived_low = between_chips(blocks, n_dp)
 
     input_grads = swap(jnp.concatenate([grads_low, grads_high], axis=0), "pipe")
     input_grads, arrived_low = lax.optimization_barrier((input_grads, arrived_low))
     input_grads = input_grads.transpose(1, 0, 2).reshape(1, tok_rows, width)
 
-    grad_in = jnp.zeros((share_in, inner), jnp.bfloat16)
-    outs = []
-    for (low, high), arrived in zip(BLOCKS, (arrived_low, summed_high)):
-        group = high - low
-        share = group * chunk // n_dp
+    ins, outs = [], []
+    for (low, high), arrived in zip(BLOCKS, (arrived_low, arrived_high)):
+        share = (high - low) * chunk // n_dp
         sum_in, sum_out = run(
-            unpack_kernel(inner, share),
+            unpack_kernel(inner, share, len(arrived)),
             [
                 ((share, inner), jnp.bfloat16),
-                ((arrived.shape[1] - share * inner // LANES, LANES), jnp.bfloat16),
+                ((arrived[0].shape[0] - share * inner // LANES, LANES), jnp.bfloat16),
             ],
-            arrived,
+            *arrived,
         )
-        moved = move_in(sum_in, low, group, n_pipe, n_dp)
-        grad_in = jnp.where((me >= low) & (me < high), moved, grad_in)
-        outs.append(sum_out.reshape(group, -1, LANES))
+        ins.append(sum_in)
+        outs.append(sum_out.reshape(high - low, -1, LANES))
     grad_out = swap(jnp.concatenate(outs, axis=0), "pipe")
+    grad_in = move_in(*ins, n_pipe, n_dp)
+    is_high = (me >= middle).astype(jnp.int32).reshape(1)
 
     shape_in, shape_out = (share_in, inner), (share_out, width)
     *updated, pieces = run(
@@ -680,7 +707,8 @@
         [(shape_in, jnp.float32)] * 3
         + [(shape_out, jnp.float32)] * 3
         + [((n_dp, 2, share_out, share_in), jnp.bfloat16)],
-        grad_in,
+        is_high,
+        *grad_in,
         grad_out,
         master_in[0],
         moment_in[0],
@@ -688,6 +716,7 @@
         master_out[0],
         moment_out[0],
         second_out[0],
+        specs=in_smem,
     )
     new_in, new_moment_in, new_second_in, new_out, new_moment_out, new_second_out = updated
     roll_in, roll_out = run(

time: 611 us -> 603 us (0.987)
  blocking collectives: 184 us -> 99.2 us
  waiting for transfers between devices: 180 us -> 231 us
  starting transfers between devices: 79.7 us -> 102 us
    ppermute x6 -> x11, waiting for transfers between devices: 10.8 us -> 81.7 us  [the longest x7 69.8 us: between_chips(): arrived.append(lax.ppermute(block, 'dp', pairs))]
    all_to_all x1 -> x0, blocking collectives: 49.2 us -> none  [reduce_now(): lax.all_to_all(core_halves(mine, other, n_dp), 'dp', 0, 0, tiled=True, ax...]
    all_to_all x6 -> x4, blocking collectives: 135 us -> 99.2 us  [swap(): return lax.all_to_all(x, axis, 0, 0, tiled=True)]
    all_to_all x12 -> x14, starting transfers between devices: 63.9 us -> 82.6 us  [swap(): return lax.all_to_all(x, axis, 0, 0, tiled=True)]
    all_to_all x12 -> x14, waiting for transfers between devices: 124 us -> 114 us  [swap(): return lax.all_to_all(x, axis, 0, 0, tiled=True)]
    reduce_scatter x1, waiting for transfers between devices: 7.29 us -> 0.02 us  [reduce_apart(): lax.psum_scatter(mine.reshape(-1, LANES), 'dp', scatter_dimension=0, tile...]
    pallas_call x13 -> x14, Pallas kernels: 47.1 us -> 51.6 us  [run(): pl.pallas_call(kernel, out_shape=[jax.ShapeDtypeStruct(shape, kind) for s...]
    ppermute x6 -> x11, starting transfers between devices: 14.9 us -> 18.2 us  [the longest x7 9.86 us: between_chips(): arrived.append(lax.ppermute(block, 'dp', pairs))]
  transfers between devices with their start and end apart: 25 -> 32, of which waited for: 16 -> 19; matrix products, arithmetic and copies ran while one was open for 13% -> 12% of each run, Pallas kernels for 4% -> 5%
where the time goes in v5:
time: 603 us; the launch traced here: 599 us
  waiting for transfers between devices  231 us (38%)
  starting transfers between devices  102 us (17%)
  blocking collectives  99.2 us (16%)
  Pallas kernels  51.6 us (9%)
  local copies, waits for them, and re-layouts  43.7 us (7%)
  matrix products  37.8 us (6%)
  other arithmetic  20 us (3%)
  between operations  14.7 us (2%)
    all_to_all x14, waiting for transfers between devices, swap(): return lax.all_to_all(x, axis, 0, 0, tiled=True)  114 us
    all_to_all x4, blocking collectives, swap(): return lax.all_to_all(x, axis, 0, 0, tiled=True)  99.2 us
    all_to_all x14, starting transfers between devices, swap(): return lax.all_to_all(x, axis, 0, 0, tiled=True)  82.6 us
    ppermute x7, waiting for transfers between devices, between_chips(): arrived.append(lax.ppermute(block, 'dp', pairs))  69.8 us
    pallas_call x14, Pallas kernels, run(): pl.pallas_call(kernel, out_shape=[jax.ShapeDtypeStruct(shape, kind) for s...  51.6 us
    dot_general x23, matrix products, dot(): lax.dot_general(left, right, (dims, ((), ())), preferred_element_type=jnp...  37.8 us
    unnamed x84, local copies, waits for them, and re-layouts  28.9 us
    all_gather x1, waiting for transfers between devices, on_device(): all_in = lax.all_gather(piece_in, 'dp', axis=0, tiled=True)  19.6 us
  transfers between devices with their start and end apart: 32, of which 19 were waited for; matrix products, arithmetic and copies ran while one was open for 12% of the time, Pallas kernels for 5%

profile of v5, /device:TPU:1, one launch (start us, length us, event | category | flops | bytes accessed | tf_op | source)
XLA Modules:
  0.0 599.5 jit_solution(13670915753118392145)
XLA Ops:
  11.2 37.5 %all_to_all.140 = bf16[8,32,640]{2,1,0:T(8,128)(2,1)S(1)} all-to-all(bf16[8,32,640]{2,1,0:T(8,128)(2,1)S(1)} %copy.42), channel_id=1, replica_groups=mesh['pipe'=8,'dp'=16] {'pipe'}, dimensions={0} | all-to-all | bytes 655360 | tf_op jit(solution)/shard_map/all_to_all | solution.py:31
  53.9 19.6 %all-gather.8.cloned.1.call-done.in_ref.refs_5_ = bf16[5120,512]{1,0:T(8,128)(2,1)} async-done(((bf16[320,512]{1,0:T(8,128)(2,1)}), bf16[5120,512]{1,0:T(8,128)(2,1)}) %all-gather.8.cloned.1.call-update) | async-done | bytes 5242896 | tf_op jit(solution)/shard_map/all_gather | solution.py:510
  78.3 6.1 %all-to-all-start.2 = ((bf16[8,32,512]{2,1,0:T(8,128)(2,1)}), bf16[8,32,512]{2,1,0:T(8,128)(2,1)S(1)}, u32[]{:S(2)}, u32[]{:S(2)}) async-start(bf16[8,32,512]{2,1,0:T(8,128)(2,1)} %bitcast.135), calls=%async_computation.2 | async-start | bytes 524288 | tf_op jit(solution)/shard_map/all_to_all | solution.py:31
  94.0 5.7 all-to-all-start.3
  102.5 3.3 concatenate.48
  107.0 5.4 all-to-all-start.1
  113.1 15.7 %all-gather.6.cloned.1.call-done.out_ref.refs_6_ = bf16[512,5120]{1,0:T(8,128)(2,1)} async-done(((bf16[32,5120]{1,0:T(8,128)(2,1)}), bf16[512,5120]{1,0:T(8,128)(2,1)}) %all-gather.6.cloned.1.call-update) | async-done | bytes 5242896 | tf_op jit(solution)/shard_map/all_gather | solution.py:511
  138.6 15.6 %all_to_all.141 = bf16[8,64,512]{2,1,0:T(8,128)(2,1)} all-to-all(bf16[8,64,512]{2,1,0:T(8,128)(2,1)S(1)} %bitcast.136), channel_id=1, replica_groups=mesh['pipe'=8,'dp'=16] {'pipe'}, dimensions={0} | all-to-all | bytes 1048576 | tf_op jit(solution)/shard_map/all_to_all | solution.py:31
  155.4 14.6 %all_to_all.142 = bf16[8,64,512]{2,1,0:T(8,128)(2,1)S(1)} all-to-all(bf16[8,64,512]{2,1,0:T(8,128)(2,1)S(1)} %tile.7), channel_id=1, replica_groups=mesh['pipe'=8,'dp'=16] {'pipe'}, dimensions={0} | all-to-all | bytes 1048576 | tf_op jit(solution)/shard_map/all_to_all | solution.py:31
  180.7 5.6 all-to-all-start.7
  188.5 5.2 all-to-all-done.7
  194.5 3.4 all-to-all-start.8
  199.9 5.3 all-to-all-done.8.every_ref
  205.9 3.5 all-to-all-start.6
  212.2 7.0 %all-to-all-done.6.up_ref = bf16[8,32,1536]{2,1,0:T(8,128)(2,1)S(1)} async-done(((bf16[8,32,1536]{2,1,0:T(8,128)(2,1)}), bf16[8,32,1536]{2,1,0:T(8,128)(2,1)S(1)}, u32[]{:S(2)}, u32[]{:S(2)}) %all-to-all-start.6) | async-done | bytes 786464 | tf_op jit(solution)/shard_map/all_to_all | solution.py:31
  220.0 6.2 %shard_map.154 = (bf16[256,2048]{1,0:T(8,128)(2,1)}, f32[4,32,512]{2,1,0:T(8,128)S(1)}, f32[4,32,128]{2,1,0:T(8,128)S(1)}, f32[6,32,512]{2,1,0:T(8,128)S(1)}) custom-call(bf16[8,32,2176]{2,1,0:T(8,128)(2,1)} %all-to-all-done.1.down_ref, bf16[8,32,1536]{2,1,0:T(8,128)(2,1)S(1)} %all-to-all-done.6.up_ref, ...), custom_call_target="tpu_custom_call" | custom-call | tf_op jit(solution)/shard_map/pallas_call | solution.py:68
  227.6 10.9 %all-to-all-start.9 = ((bf16[8,32,2048]{2,1,0:T(8,128)(2,1)}), bf16[8,32,2048]{2,1,0:T(8,128)(2,1)S(1)}, u32[]{:S(2)}, u32[]{:S(2)}) async-start(bf16[8,32,2048]{2,1,0:T(8,128)(2,1)} %bitcast.28), calls=%async_computation.9 | async-start | bytes 2097152 | tf_op jit(solution)/shard_map/all_to_all | solution.py:31
  245.8 10.8 %all-to-all-done.9 = bf16[8,32,2048]{2,1,0:T(8,128)(2,1)S(1)} async-done(((bf16[8,32,2048]{2,1,0:T(8,128)(2,1)}), bf16[8,32,2048]{2,1,0:T(8,128)(2,1)S(1)}, u32[]{:S(2)}, u32[]{:S(2)}) %all-to-all-start.9) | async-done | bytes 1048608 | tf_op jit(solution)/shard_map/all_to_all | solution.py:31
  256.6 4.2 all-to-all-start.11
  260.9 5.9 shard_map.155
  268.8 10.0 %all-to-all-done.11.grad_ref = bf16[8,32,2048]{2,1,0:T(8,128)(2,1)S(1)} async-done(((bf16[8,32,2048]{2,1,0:T(8,128)(2,1)}), bf16[8,32,2048]{2,1,0:T(8,128)(2,1)S(1)}, u32[]{:S(2)}, u32[]{:S(2)}) %all-to-all-start.11) | async-done | bytes 1048608 | tf_op jit(solution)/shard_map/all_to_all | solution.py:31
  278.9 31.4 %all_to_all.143.sums_ref = bf16[8,32,3712]{2,1,0:T(8,128)(2,1)S(1)} all-to-all(bf16[8,32,3712]{2,1,0:T(8,128)(2,1)} %bitcast.119), channel_id=1, replica_groups=mesh['pipe'=8,'dp'=16] {'pipe'}, dimensions={0} | all-to-all | bytes 3801088 | tf_op jit(solution)/shard_map/all_to_all | solution.py:31
  310.2 6.0 %shard_map.156 = bf16[256,4224]{1,0:T(8,128)(2,1)S(1)} custom-call(bf16[8,32,3712]{2,1,0:T(8,128)(2,1)S(1)} %all_to_all.143.sums_ref, bf16[8,32,2048]{2,1,0:T(8,128)(2,1)S(1)} %all-to-all-done.11.grad_ref, bf16[512,6144]{1,0:T(8,128)(2,1)} %all-gather.14.cloned.1.call-done.gram_ref), custom_call_target="tpu_custom_call" | custom-call | tf_op jit(solution)/shard_map/pallas_call | solution.py:68
  317.6 5.1 all-to-all-start.12
  322.8 31.8 %all-to-all-done.12 = bf16[8,32,4224]{2,1,0:T(8,128)(2,1)S(1)} async-done(((bf16[8,32,4224]{2,1,0:T(8,128)(2,1)}), bf16[8,32,4224]{2,1,0:T(8,128)(2,1)S(1)}, u32[]{:S(2)}, u32[]{:S(2)}) %all-to-all-start.12) | async-done | bytes 2162720 | tf_op jit(solution)/shard_map/all_to_all | solution.py:31
  356.6 10.7 %shard_map.157 = (bf16[4,256,640]{2,1,0:T(8,128)(2,1)S(1)}, bf16[8,1280,128]{2,1,0:T(8,128)(2,1)}, bf16[8,1280,128]{2,1,0:T(8,128)(2,1)}, f32[256,640]{1,0:T(8,128)S(1)}, bf16[256,2048]{1,0:T(8,128)(2,1)S(1)}) custom-call(s32[9]{0:T(128)S(1)} %pad_add_fusion.1.refs_0_, f32[256,640]{1,0:T(8,128)S(1)} %copy-done.21, bf16[256,4224]{1,0:T(8,128)(2,1)S(1)} %bitcast.109, ...), custom_call_target="tpu_custom_call" | custom-call | tf_op jit(solution)/shard_map/pallas_call | solution.py:68
  369.8 4.3 all-to-all-start.13
  374.7 4.8 add_convert_fusion
  379.5 10.1 %all-to-all-done.13.grad_ref = bf16[8,32,2048]{2,1,0:T(8,128)(2,1)} async-done(((bf16[8,32,2048]{2,1,0:T(8,128)(2,1)}), bf16[8,32,2048]{2,1,0:T(8,128)(2,1)}, u32[]{:S(2)}, u32[]{:S(2)}) %all-to-all-start.13) | async-done | bytes 1048608 | tf_op jit(solution)/shard_map/all_to_all | solution.py:31
  391.6 2.6 shard_map.158
  395.2 3.9 all-to-all-start.14
  399.2 26.3 %all-to-all-done.14 = bf16[8,32,2176]{2,1,0:T(8,128)(2,1)S(1)} async-done(((bf16[8,32,2176]{2,1,0:T(8,128)(2,1)}), bf16[8,32,2176]{2,1,0:T(8,128)(2,1)S(1)}, u32[]{:S(2)}, u32[]{:S(2)}) %all-to-all-start.14) | async-done | bytes 1114144 | tf_op jit(solution)/shard_map/all_to_all | solution.py:31
  427.8 11.3 %shard_map.159 = (bf16[4,256,640]{2,1,0:T(8,128)(2,1)S(1)}, bf16[8,1280,128]{2,1,0:T(8,128)(2,1)}, bf16[8,1280,128]{2,1,0:T(8,128)(2,1)}, f32[256,640]{1,0:T(8,128)}) custom-call(s32[9]{0:T(128)S(1)} %pad_add_fusion.refs_0_, bf16[256,640]{1,0:T(8,128)(2,1)S(1)} %copy-done.8, bf16[256,2176]{1,0:T(8,128)(2,1)S(1)} %bitcast.115, ...), custom_call_target="tpu_custom_call" | custom-call | tf_op jit(solution)/shard_map/pallas_call | solution.py:68
  441.2 4.5 all-to-all-start.15
  445.8 3.0 shard_map.160
  449.5 5.0 collective-permute-start.6
  454.6 56.5 %collective-permute-done.3.refs_1_ = bf16[1280,128]{1,0:T(8,128)(2,1)S(1)} collective-permute-done((bf16[1280,128]{1,0:T(8,128)(2,1)S(1)}, bf16[1280,128]{1,0:T(8,128)(2,1)S(1)}, u32[]{:S(2)}, u32[]{:S(2)}) %collective-permute-start.3) | collective-permute-done | bytes 327712 | tf_op jit(solution)/shard_map/ppermute | solution.py:456
  511.1 4.8 collective-permute-start.8
  515.9 6.3 %collective-permute-done.8.refs_6_ = bf16[1280,128]{1,0:T(8,128)(2,1)S(1)} collective-permute-done((bf16[1280,128]{1,0:T(8,128)(2,1)}, bf16[1280,128]{1,0:T(8,128)(2,1)S(1)}, u32[]{:S(2)}, u32[]{:S(2)}) %collective-permute-start.8) | collective-permute-done | bytes 327712 | tf_op jit(solution)/shard_map/ppermute | solution.py:456
  522.2 7.0 %collective-permute-done.9.refs_7_ = bf16[1280,128]{1,0:T(8,128)(2,1)S(1)} collective-permute-done((bf16[1280,128]{1,0:T(8,128)(2,1)}, bf16[1280,128]{1,0:T(8,128)(2,1)S(1)}, u32[]{:S(2)}, u32[]{:S(2)}) %collective-permute-start.9) | collective-permute-done | bytes 327712 | tf_op jit(solution)/shard_map/ppermute | solution.py:456
  532.4 8.0 %all-to-all-start.16 = ((bf16[8,160,128]{2,1,0:T(8,128)(2,1)}), bf16[8,160,128]{2,1,0:T(8,128)(2,1)S(1)}, u32[]{:S(2)}, u32[]{:S(2)}) async-start(bf16[8,160,128]{2,1,0:T(8,128)(2,1)} %pad_maximum_fusion.4), calls=%async_computation.17 | async-start | bytes 655360 | tf_op jit(solution)/shard_map/all_to_all | solution.py:31
  540.4 6.6 %collective-permute-start.10 = (bf16[160,512]{1,0:T(8,128)(2,1)S(1)}, bf16[160,512]{1,0:T(8,128)(2,1)S(1)}, u32[]{:S(2)}, u32[]{:S(2)}) collective-permute-start(bf16[160,512]{1,0:T(8,128)(2,1)S(1)} %get-tuple-element.173), channel_id=1, source_target_pairs={{0,0},{1,64},{2,1},{3,65},{4,16},{5,80},{6,17},{7,81},{8,32},{9,96... | collective-permute-start | bytes 491528 | tf_op jit(solution)/shard_map/ppermute | solution.py:482
  547.1 11.3 %collective-permute-done.10.refs_1_ = bf16[160,512]{1,0:T(8,128)(2,1)S(1)} collective-permute-done((bf16[160,512]{1,0:T(8,128)(2,1)S(1)}, bf16[160,512]{1,0:T(8,128)(2,1)S(1)}, u32[]{:S(2)}, u32[]{:S(2)}) %collective-permute-start.10) | collective-permute-done | bytes 163872 | tf_op jit(solution)/shard_map/ppermute | solution.py:482
  563.8 3.2 shard_map.163
  567.0 12.0 %all-to-all-start.17 = ((bf16[16,2,32,320]{3,2,1,0:T(8,128)(2,1)}), bf16[16,2,32,320]{3,2,1,0:T(8,128)(2,1)S(1)}, u32[]{:S(2)}, u32[]{:S(2)}) async-start(bf16[16,2,32,320]{3,2,1,0:T(8,128)(2,1)} %get-tuple-element.122), calls=%async_computation.18 | async-start | bytes 1572864 | tf_op jit(solution)/shard_map/all_to_all | solution.py:31
  579.0 4.5 copy.47
  583.5 4.4 copy.48
  587.9 3.7 all-to-all-done.17.pieces_ref
  (186 shorter events, 94.2 us)
Async XLA Ops:
  7.2 212.1 %copy-start = (bf16[256,5120]{1,0:T(8,128)(2,1)S(1)}, bf16[256,5120]{1,0:T(8,128)(2,1)}, u32[]{:S(2)}) copy-start(bf16[256,5120]{1,0:T(8,128)(2,1)} %param.9) | copy-start | bytes 7864324
  7.2 66.3 %all-gather.8.cloned.1.call-start = ((), (), s32[]{:S(2)}) async-start(), calls=%async_computation.20 | async-start | bytes 5570560 | tf_op jit(solution)/shard_map/all_gather | solution.py:510
  8.5 0.7 collective-permute-start
  10.0 118.8 %all-gather.6.cloned.1.call-start = ((), (), s32[]{:S(2)}) async-start(), calls=%async_computation.19 | async-start | bytes 5570560 | tf_op jit(solution)/shard_map/all_gather | solution.py:511
  50.7 135.6 %copy-start.7 = (bf16[256,640]{1,0:T(8,128)(2,1)}, bf16[256,640]{1,0:T(8,128)(2,1)S(1)}, u32[]{:S(2)}) copy-start(bf16[256,640]{1,0:T(8,128)(2,1)S(1)} %get-tuple-element.171.rows_ref.refs_1_) | copy-start | bytes 983044
  53.2 22.9 %copy-start.40 = (bf16[2,32,640]{2,1,0:T(8,128)(2,1)}, bf16[2,32,640]{2,1,0:T(8,128)(2,1)S(1)}, u32[]{:S(2)}) copy-start(bf16[2,32,640]{2,1,0:T(8,128)(2,1)S(1)} %get-tuple-element.177) | copy-start | bytes 245764
  53.9 24.4 %copy-start.39 = (bf16[3,32,640]{2,1,0:T(8,128)(2,1)}, bf16[3,32,640]{2,1,0:T(8,128)(2,1)S(1)}, u32[]{:S(2)}) copy-start(bf16[3,32,640]{2,1,0:T(8,128)(2,1)S(1)} %get-tuple-element.175) | copy-start | bytes 368644
  78.3 13.6 %all-to-all-start.2 = ((bf16[8,32,512]{2,1,0:T(8,128)(2,1)}), bf16[8,32,512]{2,1,0:T(8,128)(2,1)S(1)}, u32[]{:S(2)}, u32[]{:S(2)}) async-start(bf16[8,32,512]{2,1,0:T(8,128)(2,1)} %bitcast.135), calls=%async_computation.2 | async-start | bytes 524288 | tf_op jit(solution)/shard_map/all_to_all | solution.py:31
  94.0 13.0 %all-to-all-start.3 = ((bf16[8,32,512]{2,1,0:T(8,128)(2,1)}), bf16[8,32,512]{2,1,0:T(8,128)(2,1)S(1)}, u32[]{:S(2)}, u32[]{:S(2)}) async-start(bf16[8,32,512]{2,1,0:T(8,128)(2,1)} %tile.6), calls=%async_computation.3 | async-start | bytes 524288 | tf_op jit(solution)/shard_map/all_to_all | solution.py:31
  107.0 23.0 %all-to-all-start.1 = ((bf16[8,32,2176]{2,1,0:T(8,128)(2,1)}), bf16[8,32,2176]{2,1,0:T(8,128)(2,1)}, u32[]{:S(2)}, u32[]{:S(2)}) async-start(bf16[8,32,2176]{2,1,0:T(8,128)(2,1)} %concatenate.48), calls=%async_computation.1 | async-start | bytes 2228224 | tf_op jit(solution)/shard_map/all_to_all | solution.py:31
  112.4 106.8 %all-gather.10.cloned.1.call-start = ((), (), s32[]{:S(2)}) async-start(), calls=%async_computation.21 | async-start | bytes 3342336 | tf_op jit(solution)/shard_map/all_gather | solution.py:541
  130.0 89.2 %all-gather.12.cloned.1.call-start = ((), (), s32[]{:S(2)}) async-start(), calls=%async_computation.22 | async-start | bytes 3342336 | tf_op jit(solution)/shard_map/all_gather | solution.py:541
  135.7 42.9 %copy-start.38 = (bf16[3,32,640]{2,1,0:T(8,128)(2,1)S(1)}, bf16[3,32,640]{2,1,0:T(8,128)(2,1)}, u32[]{:S(2)}) copy-start(bf16[3,32,640]{2,1,0:T(8,128)(2,1)} %get-tuple-element.174) | copy-start | bytes 368644
  177.1 20.8 %copy-start.37 = (bf16[256,512]{1,0:T(8,128)(2,1)S(1)}, bf16[256,512]{1,0:T(8,128)(2,1)}, u32[]{:S(2)}) copy-start(bf16[256,512]{1,0:T(8,128)(2,1)} %convolution_convert_fusion.4) | copy-start | bytes 786436
  180.7 13.0 %all-to-all-start.7 = ((bf16[8,32,512]{2,1,0:T(8,128)(2,1)}), bf16[8,32,512]{2,1,0:T(8,128)(2,1)S(1)}, u32[]{:S(2)}, u32[]{:S(2)}) async-start(bf16[8,32,512]{2,1,0:T(8,128)(2,1)} %bitcast.27), calls=%async_computation.7 | async-start | bytes 524288 | tf_op jit(solution)/shard_map/all_to_all | solution.py:31
  194.5 10.7 %all-to-all-start.8 = ((bf16[8,32,512]{2,1,0:T(8,128)(2,1)}), bf16[8,32,512]{2,1,0:T(8,128)(2,1)S(1)}, u32[]{:S(2)}, u32[]{:S(2)}) async-start(bf16[8,32,512]{2,1,0:T(8,128)(2,1)} %tile.8), calls=%async_computation.8 | async-start | bytes 524288 | tf_op jit(solution)/shard_map/all_to_all | solution.py:31
  205.9 13.3 %all-to-all-start.6 = ((bf16[8,32,1536]{2,1,0:T(8,128)(2,1)}), bf16[8,32,1536]{2,1,0:T(8,128)(2,1)S(1)}, u32[]{:S(2)}, u32[]{:S(2)}) async-start(bf16[8,32,1536]{2,1,0:T(8,128)(2,1)} %bitcast.131), calls=%async_computation.6 | async-start | bytes 1572864 | tf_op jit(solution)/shard_map/all_to_all | solution.py:31
  209.5 100.8 %all-gather.14.cloned.1.call-start = ((), (), s32[]{:S(2)}) async-start(), calls=%async_computation.23 | async-start | bytes 6684672 | tf_op jit(solution)/shard_map/all_gather | solution.py:541
  220.0 18.5 %copy-start.15 = (bf16[256,640]{1,0:T(8,128)(2,1)S(1)}, bf16[256,640]{1,0:T(8,128)(2,1)}, u32[]{:S(2)}) copy-start(bf16[256,640]{1,0:T(8,128)(2,1)} %constant_dynamic-slice_fusion.refs_4_) | copy-start | bytes 983044
  227.6 29.0 %all-to-all-start.9 = ((bf16[8,32,2048]{2,1,0:T(8,128)(2,1)}), bf16[8,32,2048]{2,1,0:T(8,128)(2,1)S(1)}, u32[]{:S(2)}, u32[]{:S(2)}) async-start(bf16[8,32,2048]{2,1,0:T(8,128)(2,1)} %bitcast.28), calls=%async_computation.9 | async-start | bytes 2097152 | tf_op jit(solution)/shard_map/all_to_all | solution.py:31
  238.5 22.4 %copy-start.8 = (bf16[256,640]{1,0:T(8,128)(2,1)S(1)}, bf16[256,640]{1,0:T(8,128)(2,1)}, u32[]{:S(2)}) copy-start(bf16[256,640]{1,0:T(8,128)(2,1)} %copy-done.7) | copy-start | bytes 983044
  256.6 10.1 %copy-start.3 = (bf16[8,32,2048]{2,1,0:T(8,128)(2,1)}, bf16[8,32,2048]{2,1,0:T(8,128)(2,1)S(1)}, u32[]{:S(2)}) copy-start(bf16[8,32,2048]{2,1,0:T(8,128)(2,1)S(1)} %all-to-all-done.9) | copy-start | bytes 3145732
  256.6 22.2 %all-to-all-start.11 = ((bf16[8,32,2048]{2,1,0:T(8,128)(2,1)}), bf16[8,32,2048]{2,1,0:T(8,128)(2,1)S(1)}, u32[]{:S(2)}, u32[]{:S(2)}) async-start(bf16[8,32,2048]{2,1,0:T(8,128)(2,1)} %bitcast.129), calls=%async_computation.11 | async-start | bytes 2097152 | tf_op jit(solution)/shard_map/all_to_all | solution.py:31
  317.6 37.0 %all-to-all-start.12 = ((bf16[8,32,4224]{2,1,0:T(8,128)(2,1)}), bf16[8,32,4224]{2,1,0:T(8,128)(2,1)S(1)}, u32[]{:S(2)}, u32[]{:S(2)}) async-start(bf16[8,32,4224]{2,1,0:T(8,128)(2,1)} %bitcast.113), calls=%async_computation.12 | async-start | bytes 4325376 | tf_op jit(solution)/shard_map/all_to_all | solution.py:31
  368.4 1.4 copy-start.19
  368.5 6.2 %copy-start.26 = (f32[256,640]{1,0:T(8,128)}, f32[256,640]{1,0:T(8,128)S(1)}, u32[]{:S(2)}) copy-start(f32[256,640]{1,0:T(8,128)S(1)} %get-tuple-element.89.refs_4_) | copy-start | bytes 1966084
  368.5 6.2 %collective-permute-start.1 = (bf16[8,1280,128]{2,1,0:T(8,128)(2,1)}, bf16[8,1280,128]{2,1,0:T(8,128)(2,1)}, u32[]{:S(2)}, u32[]{:S(2)}) collective-permute-start(bf16[8,1280,128]{2,1,0:T(8,128)(2,1)} %get-tuple-element.84), channel_id=1, source_target_pairs={{0,1},{1,0},{2,3},{3,2},{4,5},{5,4},{6,7},{7,6},{8,9},{9,8},{10,11... | collective-permute-start | bytes 7864328 | tf_op jit(solution)/shard_map/ppermute | solution.py:436
  369.8 19.8 %all-to-all-start.13 = ((bf16[8,32,2048]{2,1,0:T(8,128)(2,1)}), bf16[8,32,2048]{2,1,0:T(8,128)(2,1)}, u32[]{:S(2)}, u32[]{:S(2)}) async-start(bf16[8,32,2048]{2,1,0:T(8,128)(2,1)} %bitcast.120), calls=%async_computation.13 | async-start | bytes 2097152 | tf_op jit(solution)/shard_map/all_to_all | solution.py:31
  374.1 156.5 %reduce-scatter.2.cloned.1.call-start = ((), (), s32[]{:S(2)}) async-start(), calls=%async_computation.24 | async-start | bytes 2949120 | tf_op jit(solution)/shard_map/reduce_scatter | solution.py:461
  374.7 15.0 %copy-start.2 = (bf16[512,3072]{1,0:T(8,128)(2,1)S(1)}, bf16[512,3072]{1,0:T(8,128)(2,1)}, u32[]{:S(2)}) copy-start(bf16[512,3072]{1,0:T(8,128)(2,1)} %all-gather.10.cloned.1.call-done.gram_in_ref.gram_ref) | copy-start | bytes 9437188
  395.2 30.3 %all-to-all-start.14 = ((bf16[8,32,2176]{2,1,0:T(8,128)(2,1)}), bf16[8,32,2176]{2,1,0:T(8,128)(2,1)S(1)}, u32[]{:S(2)}, u32[]{:S(2)}) async-start(bf16[8,32,2176]{2,1,0:T(8,128)(2,1)} %bitcast.114), calls=%async_computation.14 | async-start | bytes 2228224 | tf_op jit(solution)/shard_map/all_to_all | solution.py:31
  427.8 11.7 %copy-start.14 = (bf16[4,256,640]{2,1,0:T(8,128)(2,1)S(1)}, bf16[4,256,640]{2,1,0:T(8,128)(2,1)}, u32[]{:S(2)}) copy-start(bf16[4,256,640]{2,1,0:T(8,128)(2,1)} %copy-done.13) | copy-start | bytes 3932164
  439.1 6.7 %collective-permute-start.2 = (bf16[8,1280,128]{2,1,0:T(8,128)(2,1)}, bf16[8,1280,128]{2,1,0:T(8,128)(2,1)}, u32[]{:S(2)}, u32[]{:S(2)}) collective-permute-start(bf16[8,1280,128]{2,1,0:T(8,128)(2,1)} %get-tuple-element.93), channel_id=1, source_target_pairs={{0,1},{1,0},{2,3},{3,2},{4,5},{5,4},{6,7},{7,6},{8,9},{9,8},{10,11... | collective-permute-start | bytes 7864328 | tf_op jit(solution)/shard_map/ppermute | solution.py:436
  439.5 6.3 %copy-start.9 = (bf16[8,1280,128]{2,1,0:T(8,128)(2,1)S(1)}, bf16[8,1280,128]{2,1,0:T(8,128)(2,1)}, u32[]{:S(2)}) copy-start(bf16[8,1280,128]{2,1,0:T(8,128)(2,1)} %get-tuple-element.92.mine_ref) | copy-start | bytes 7864324
  441.2 74.7 %all-to-all-start.15 = ((bf16[8,256,640]{2,1,0:T(8,128)(2,1)}), bf16[8,256,640]{2,1,0:T(8,128)(2,1)}, u32[]{:S(2)}, u32[]{:S(2)}) async-start(bf16[8,256,640]{2,1,0:T(8,128)(2,1)} %pad_maximum_fusion), calls=%async_computation.15 | async-start | bytes 5242880 | tf_op jit(solution)/shard_map/all_to_all | solution.py:31
  445.7 112.6 %copy-start.10 = (f32[1,320,512]{2,1,0:T(8,128)S(1)}, f32[1,320,512]{2,1,0:T(8,128)}, u32[]{:S(2)}) copy-start(f32[1,320,512]{2,1,0:T(8,128)} %param.10) | copy-start | bytes 1966084
  449.5 61.5 %collective-permute-start.3 = (bf16[1280,128]{1,0:T(8,128)(2,1)S(1)}, bf16[1280,128]{1,0:T(8,128)(2,1)S(1)}, u32[]{:S(2)}, u32[]{:S(2)}) collective-permute-start(bf16[1280,128]{1,0:T(8,128)(2,1)S(1)} %get-tuple-element.95), channel_id=1, source_target_pairs={{0,2},{1,3},{2,0},{3,1},{4,6},{5,7},{6,4},{7,5},{8,10},{9,11},{10,... | collective-permute-start | bytes 983048 | tf_op jit(solution)/shard_map/ppermute | solution.py:456
  449.5 66.3 %collective-permute-start.4 = (bf16[1280,128]{1,0:T(8,128)(2,1)S(1)}, bf16[1280,128]{1,0:T(8,128)(2,1)S(1)}, u32[]{:S(2)}, u32[]{:S(2)}) collective-permute-start(bf16[1280,128]{1,0:T(8,128)(2,1)S(1)} %get-tuple-element.96), channel_id=1, source_target_pairs={{0,4},{1,5},{2,6},{3,7},{4,8},{5,9},{6,10},{7,11},{8,12},{9,13},{1... | collective-permute-start | bytes 983048 | tf_op jit(solution)/shard_map/ppermute | solution.py:456
  449.5 66.4 %collective-permute-start.5 = (bf16[1280,128]{1,0:T(8,128)(2,1)}, bf16[1280,128]{1,0:T(8,128)(2,1)S(1)}, u32[]{:S(2)}, u32[]{:S(2)}) collective-permute-start(bf16[1280,128]{1,0:T(8,128)(2,1)} %get-tuple-element.97), channel_id=1, source_target_pairs={{0,6},{1,7},{2,4},{3,5},{4,10},{5,11},{6,8},{7,9},{8,14},{9,15},{1... | collective-permute-start | bytes 983048 | tf_op jit(solution)/shard_map/ppermute | solution.py:456
  449.5 66.4 %collective-permute-start.6 = (bf16[1280,128]{1,0:T(8,128)(2,1)}, bf16[1280,128]{1,0:T(8,128)(2,1)S(1)}, u32[]{:S(2)}, u32[]{:S(2)}) collective-permute-start(bf16[1280,128]{1,0:T(8,128)(2,1)} %get-tuple-element.98), channel_id=1, source_target_pairs={{0,8},{1,9},{2,10},{3,11},{4,12},{5,13},{6,14},{7,15},{8,0},{9,1},... | collective-permute-start | bytes 983048 | tf_op jit(solution)/shard_map/ppermute | solution.py:456
  454.6 61.3 %collective-permute-start.7 = (bf16[1280,128]{1,0:T(8,128)(2,1)}, bf16[1280,128]{1,0:T(8,128)(2,1)S(1)}, u32[]{:S(2)}, u32[]{:S(2)}) collective-permute-start(bf16[1280,128]{1,0:T(8,128)(2,1)} %get-tuple-element.99), channel_id=1, source_target_pairs={{0,10},{1,11},{2,8},{3,9},{4,14},{5,15},{6,12},{7,13},{8,2},{9,3},... | collective-permute-start | bytes 983048 | tf_op jit(solution)/shard_map/ppermute | solution.py:456
  511.1 11.2 %collective-permute-start.8 = (bf16[1280,128]{1,0:T(8,128)(2,1)}, bf16[1280,128]{1,0:T(8,128)(2,1)S(1)}, u32[]{:S(2)}, u32[]{:S(2)}) collective-permute-start(bf16[1280,128]{1,0:T(8,128)(2,1)} %get-tuple-element.100), channel_id=1, source_target_pairs={{0,12},{1,13},{2,14},{3,15},{4,0},{5,1},{6,2},{7,3},{8,4},{9,5},{1... | collective-permute-start | bytes 983048 | tf_op jit(solution)/shard_map/ppermute | solution.py:456
  515.9 13.4 %collective-permute-start.9 = (bf16[1280,128]{1,0:T(8,128)(2,1)}, bf16[1280,128]{1,0:T(8,128)(2,1)S(1)}, u32[]{:S(2)}, u32[]{:S(2)}) collective-permute-start(bf16[1280,128]{1,0:T(8,128)(2,1)} %get-tuple-element.101), channel_id=1, source_target_pairs={{0,14},{1,15},{2,12},{3,13},{4,2},{5,3},{6,0},{7,1},{8,6},{9,7},{1... | collective-permute-start | bytes 983048 | tf_op jit(solution)/shard_map/ppermute | solution.py:456
  532.4 26.0 %all-to-all-start.16 = ((bf16[8,160,128]{2,1,0:T(8,128)(2,1)}), bf16[8,160,128]{2,1,0:T(8,128)(2,1)S(1)}, u32[]{:S(2)}, u32[]{:S(2)}) async-start(bf16[8,160,128]{2,1,0:T(8,128)(2,1)} %pad_maximum_fusion.4), calls=%async_computation.17 | async-start | bytes 655360 | tf_op jit(solution)/shard_map/all_to_all | solution.py:31
  540.4 17.9 %collective-permute-start.10 = (bf16[160,512]{1,0:T(8,128)(2,1)S(1)}, bf16[160,512]{1,0:T(8,128)(2,1)S(1)}, u32[]{:S(2)}, u32[]{:S(2)}) collective-permute-start(bf16[160,512]{1,0:T(8,128)(2,1)S(1)} %get-tuple-element.173), channel_id=1, source_target_pairs={{0,0},{1,64},{2,1},{3,65},{4,16},{5,80},{6,17},{7,81},{8,32},{9,96... | collective-permute-start | bytes 491528 | tf_op jit(solution)/shard_map/ppermute | solution.py:482
  547.0 11.4 %collective-permute-start.11 = (bf16[160,512]{1,0:T(8,128)(2,1)S(1)}, bf16[160,512]{1,0:T(8,128)(2,1)S(1)}, u32[]{:S(2)}, u32[]{:S(2)}) collective-permute-start(bf16[160,512]{1,0:T(8,128)(2,1)S(1)} %get-tuple-element.172), channel_id=1, source_target_pairs={{0,64},{1,0},{2,65},{3,1},{4,80},{5,16},{6,81},{7,17},{8,96},{9,32... | collective-permute-start | bytes 491528 | tf_op jit(solution)/shard_map/ppermute | solution.py:482
  567.0 24.6 %all-to-all-start.17 = ((bf16[16,2,32,320]{3,2,1,0:T(8,128)(2,1)}), bf16[16,2,32,320]{3,2,1,0:T(8,128)(2,1)S(1)}, u32[]{:S(2)}, u32[]{:S(2)}) async-start(bf16[16,2,32,320]{3,2,1,0:T(8,128)(2,1)} %get-tuple-element.122), calls=%async_computation.18 | async-start | bytes 1572864 | tf_op jit(solution)/shard_map/all_to_all | solution.py:31
  579.0 13.7 %copy-start.1 = (bf16[256,5120]{1,0:T(8,128)(2,1)S(1)}, bf16[256,5120]{1,0:T(8,128)(2,1)}, u32[]{:S(2)}) copy-start(bf16[256,5120]{1,0:T(8,128)(2,1)} %param.9) | copy-start | bytes 7864324
  (25 other events, 24.5 us)
Sparse Core Ops, SparseCore 0:
  10.3 63.1 all-gather.7
  75.8 53.0 all-gather.5
  131.1 45.0 all-gather.9
  178.3 40.2 all-gather.11
  220.7 89.0 all-gather.13
  389.8 122.3 reduce-scatter.1

commit v6 on v5

--- a/solution.py
+++ b/solution.py
@@ -354,17 +354,20 @@
 def unpack_kernel(inner, share_in, sources):
     def kernel(*refs):
         in_ref, out_ref = refs[sources:]
+        given = refs[:sources]
+        if sources == 1:
+            given = [refs[0].at[k] for k in range(refs[0].shape[0])]
         lanes = inner // LANES
 
         def total_of(start, stop):
-            total = refs[0][start:stop].astype(jnp.float32)
-            for ref in refs[1:sources]:
+            total = given[0][start:stop].astype(jnp.float32)
+            for ref in given[1:]:
                 total = total + ref[start:stop].astype(jnp.float32)
             return total.astype(jnp.bfloat16)
 
         for c in range(lanes):
             in_ref[:, c * LANES : (c + 1) * LANES] = total_of(c * share_in, (c + 1) * share_in)
-        out_ref[...] = total_of(lanes * share_in, refs[0].shape[0])
+        out_ref[...] = total_of(lanes * share_in, given[0].shape[0])
 
     return kernel
 
@@ -437,9 +440,17 @@
 
 
 def add_kernel(mine_ref, other_ref, *out_refs):
-    for at, out_ref in enumerate(out_refs):
+    for at in range(mine_ref.shape[0]):
         total = mine_ref[at].astype(jnp.float32) + other_ref[at].astype(jnp.float32)
-        out_ref[...] = total.astype(jnp.bfloat16)
+        if len(out_refs) == 1:
+            out_refs[0][at] = total.astype(jnp.bfloat16)
+        else:
+            out_refs[at][...] = total.astype(jnp.bfloat16)
+
+
+def added(mine, other, count):
+    shape = mine.shape if count == 1 else mine.shape[1:]
+    return run(add_kernel, [(shape, jnp.bfloat16)] * count, mine, other)
 
 
 def chip_steps(n_dp):
@@ -455,17 +466,6 @@
             pairs.append((j, (x + dx) % (n_dp // 4) * 4 + (z ^ dz) * 2 + core))
         arrived.append(lax.ppermute(block, "dp", pairs))
     return arrived
-
-
-def reduce_apart(mine, n_dp):
-    summed = lax.psum_scatter(
-        mine.reshape(-1, LANES),
-        "dp",
-        scatter_dimension=0,
-        tiled=True,
-        axis_index_groups=[list(range(c, n_dp, 2)) for c in range(2)],
-    )
-    return [summed]
 
 
 def move_in(low, high, n_pipe, n_dp):
@@ -630,7 +630,7 @@
             ((tok_rows, chunk), jnp.float32),
             ((tok_rows, count * inner), jnp.bfloat16),
         ],
-        fixed,
+        place,
         exact,
         turned,
         turned,
@@ -641,9 +641,8 @@
     )
     grad_low = exchanged(columns, n_pipe)
     other = other_core(other, n_dp)
-    mine = (mine.astype(jnp.float32) + other.astype(jnp.float32)).astype(jnp.bfloat16)
-    grad_low, mine = lax.optimization_barrier((grad_low, mine))
-    arrived_high = reduce_apart(mine, n_dp)
+    grad_low, mine, other = lax.optimization_barrier((grad_low, mine, other))
+    arrived_high = between_chips(added(mine, other, mine.shape[0]), n_dp)
 
     packs = run(
         backward_kernel(first, middle, width, inner, n_pipe),
@@ -663,7 +662,7 @@
             (packed_shape(count), jnp.bfloat16),
             ((tok_rows, chunk), jnp.float32),
         ],
-        place,
+        fixed,
         rows,
         packs,
         acts,
@@ -672,32 +671,34 @@
         all_out,
         specs=in_smem,
     )
-    blocks = run(
-        add_kernel,
-        [(mine.shape[1:], jnp.bfloat16)] * mine.shape[0],
-        mine,
-        other_core(other, n_dp),
-    )
-    arrived_low = between_chips(blocks, n_dp)
-
-    input_grads = swap(jnp.concatenate([grads_low, grads_high], axis=0), "pipe")
-    input_grads, arrived_low = lax.optimization_barrier((input_grads, arrived_low))
-    input_grads = input_grads.transpose(1, 0, 2).reshape(1, tok_rows, width)
+    mine, other, arrived_high = lax.optimization_barrier((mine, other, arrived_high))
+    arrived_low = lax.all_to_all(
+        added(mine, other_core(other, n_dp), 1)[0],
+        "dp",
+        0,
+        0,
+        tiled=True,
+        axis_index_groups=[list(range(c, n_dp, 2)) for c in range(2)],
+    )
 
     ins, outs = [], []
-    for (low, high), arrived in zip(BLOCKS, (arrived_low, arrived_high)):
+    for (low, high), arrived in zip(BLOCKS, ([arrived_low], arrived_high)):
         share = (high - low) * chunk // n_dp
         sum_in, sum_out = run(
             unpack_kernel(inner, share, len(arrived)),
             [
                 ((share, inner), jnp.bfloat16),
-                ((arrived[0].shape[0] - share * inner // LANES, LANES), jnp.bfloat16),
+                ((arrived[0].shape[-2] - share * inner // LANES, LANES), jnp.bfloat16),
             ],
             *arrived,
         )
         ins.append(sum_in)
         outs.append(sum_out.reshape(high - low, -1, LANES))
     grad_out = swap(jnp.concatenate(outs, axis=0), "pipe")
+    grads = jnp.concatenate([grads_low, grads_high], axis=0)
+    grads, grad_out = lax.optimization_barrier((grads, grad_out))
+    input_grads = swap(grads, "pipe")
+    input_grads = input_grads.transpose(1, 0, 2).reshape(1, tok_rows, width)
     grad_in = move_in(*ins, n_pipe, n_dp)
     is_high = (me >= middle).astype(jnp.int32).reshape(1)
 

time: 603 us -> 622 us (1.032)
  blocking collectives: 99.2 us -> 141 us
  waiting for transfers between devices: 231 us -> 208 us
    ppermute x7, waiting for transfers between devices: 69.8 us -> 15.5 us  [between_chips(): arrived.append(lax.ppermute(block, 'dp', pairs))]
    all_to_all x4 -> x6, blocking collectives: 99.2 us -> 141 us  [swap(): return lax.all_to_all(x, axis, 0, 0, tiled=True)]
    all_to_all x0 -> x1, waiting for transfers between devices: none -> 34.5 us  [on_device(): lax.all_to_all(added(mine, other_core(other, n_dp), 1)[0], 'dp', 0, 0, ti...]
    all_to_all x14 -> x12, starting transfers between devices: 82.6 us -> 64.7 us  [swap(): return lax.all_to_all(x, axis, 0, 0, tiled=True)]
    ppermute x7, starting transfers between devices: 9.86 us -> 17.6 us  [between_chips(): arrived.append(lax.ppermute(block, 'dp', pairs))]
    pallas_call x14 -> x15, Pallas kernels: 51.6 us -> 55.4 us  [run(): pl.pallas_call(kernel, out_shape=[jax.ShapeDtypeStruct(shape, kind) for s...]
    all_to_all x14 -> x12, waiting for transfers between devices: 114 us -> 111 us  [swap(): return lax.all_to_all(x, axis, 0, 0, tiled=True)]
    unnamed x84 -> x98, local copies, waits for them, and re-layouts: 28.9 us -> 31.9 us
  transfers between devices with their start and end apart: 32 -> 30, of which waited for: 19 -> 16; matrix products, arithmetic and copies ran while one was open for 12% -> 10% of each run, Pallas kernels for 5% -> 5%
where the time goes in v6:
time: 622 us; the launch traced here: 618 us
  waiting for transfers between devices  208 us (33%)
  blocking collectives  141 us (23%)
  starting transfers between devices  96.9 us (16%)
  Pallas kernels  55.4 us (9%)
  local copies, waits for them, and re-layouts  46.6 us (7%)
  matrix products  38.2 us (6%)
  other arithmetic  17.8 us (3%)
  between operations  14.3 us (2%)
    all_to_all x6, blocking collectives, swap(): return lax.all_to_all(x, axis, 0, 0, tiled=True)  141 us
    all_to_all x12, waiting for transfers between devices, swap(): return lax.all_to_all(x, axis, 0, 0, tiled=True)  111 us
    all_to_all x12, starting transfers between devices, swap(): return lax.all_to_all(x, axis, 0, 0, tiled=True)  64.7 us
    pallas_call x15, Pallas kernels, run(): pl.pallas_call(kernel, out_shape=[jax.ShapeDtypeStruct(shape, kind) for s...  55.4 us
    dot_general x23, matrix products, dot(): lax.dot_general(left, right, (dims, ((), ())), preferred_element_type=jnp...  38.2 us
    all_to_all x1, waiting for transfers between devices, on_device(): lax.all_to_all(added(mine, other_core(other, n_dp), 1)[0], 'dp', 0, 0, ti...  34.5 us
    unnamed x98, local copies, waits for them, and re-layouts  31.9 us
    all_gather x1, waiting for transfers between devices, on_device(): all_in = lax.all_gather(piece_in, 'dp', axis=0, tiled=True)  19.6 us
  transfers between devices with their start and end apart: 30, of which 16 were waited for; matrix products, arithmetic and copies ran while one was open for 10% of the time, Pallas kernels for 5%

profile of v6, /device:TPU:1, one launch (start us, length us, event | category | flops | bytes accessed | tf_op | source)
XLA Modules:
  0.0 618.4 jit_solution(11259404366989619693)
XLA Ops:
  11.2 37.5 %all_to_all.145 = bf16[8,32,640]{2,1,0:T(8,128)(2,1)S(1)} all-to-all(bf16[8,32,640]{2,1,0:T(8,128)(2,1)S(1)} %copy.42), channel_id=1, replica_groups=mesh['pipe'=8,'dp'=16] {'pipe'}, dimensions={0} | all-to-all | bytes 655360 | tf_op jit(solution)/shard_map/all_to_all | solution.py:31
  53.9 19.6 %all-gather.8.cloned.1.call-done.in_ref.refs_5_ = bf16[5120,512]{1,0:T(8,128)(2,1)} async-done(((bf16[320,512]{1,0:T(8,128)(2,1)}), bf16[5120,512]{1,0:T(8,128)(2,1)}) %all-gather.8.cloned.1.call-update) | async-done | bytes 5242896 | tf_op jit(solution)/shard_map/all_gather | solution.py:510
  78.3 6.0 all-to-all-start.2
  94.0 5.7 all-to-all-start.3
  102.4 3.3 concatenate.48
  107.0 5.3 all-to-all-start.1
  113.1 16.0 %all-gather.6.cloned.1.call-done.out_ref.refs_6_ = bf16[512,5120]{1,0:T(8,128)(2,1)} async-done(((bf16[32,5120]{1,0:T(8,128)(2,1)}), bf16[512,5120]{1,0:T(8,128)(2,1)}) %all-gather.6.cloned.1.call-update) | async-done | bytes 5242896 | tf_op jit(solution)/shard_map/all_gather | solution.py:511
  138.6 15.7 %all_to_all.146 = bf16[8,64,512]{2,1,0:T(8,128)(2,1)} all-to-all(bf16[8,64,512]{2,1,0:T(8,128)(2,1)S(1)} %bitcast.131), channel_id=1, replica_groups=mesh['pipe'=8,'dp'=16] {'pipe'}, dimensions={0} | all-to-all | bytes 1048576 | tf_op jit(solution)/shard_map/all_to_all | solution.py:31
  155.5 14.8 %all_to_all.147 = bf16[8,64,512]{2,1,0:T(8,128)(2,1)S(1)} all-to-all(bf16[8,64,512]{2,1,0:T(8,128)(2,1)S(1)} %tile.7), channel_id=1, replica_groups=mesh['pipe'=8,'dp'=16] {'pipe'}, dimensions={0} | all-to-all | bytes 1048576 | tf_op jit(solution)/shard_map/all_to_all | solution.py:31
  181.0 5.6 all-to-all-start.7
  188.8 5.3 all-to-all-done.7
  194.9 3.8 all-to-all-start.8
  200.6 5.4 all-to-all-done.8.every_ref
  206.7 3.5 all-to-all-start.6
  213.0 7.0 %all-to-all-done.6.up_ref = bf16[8,32,1536]{2,1,0:T(8,128)(2,1)S(1)} async-done(((bf16[8,32,1536]{2,1,0:T(8,128)(2,1)}), bf16[8,32,1536]{2,1,0:T(8,128)(2,1)S(1)}, u32[]{:S(2)}, u32[]{:S(2)}) %all-to-all-start.6) | async-done | bytes 786464 | tf_op jit(solution)/shard_map/all_to_all | solution.py:31
  220.8 6.1 shard_map.154
  227.6 9.6 %all-to-all-start.9 = ((bf16[8,32,2048]{2,1,0:T(8,128)(2,1)}), bf16[8,32,2048]{2,1,0:T(8,128)(2,1)S(1)}, u32[]{:S(2)}, u32[]{:S(2)}) async-start(bf16[8,32,2048]{2,1,0:T(8,128)(2,1)} %bitcast.28), calls=%async_computation.9 | async-start | bytes 2097152 | tf_op jit(solution)/shard_map/all_to_all | solution.py:31
  244.9 10.5 %all-to-all-done.9 = bf16[8,32,2048]{2,1,0:T(8,128)(2,1)S(1)} async-done(((bf16[8,32,2048]{2,1,0:T(8,128)(2,1)}), bf16[8,32,2048]{2,1,0:T(8,128)(2,1)S(1)}, u32[]{:S(2)}, u32[]{:S(2)}) %all-to-all-start.9) | async-done | bytes 1048608 | tf_op jit(solution)/shard_map/all_to_all | solution.py:31
  256.3 4.3 all-to-all-start.11
  261.9 5.8 shard_map.155
  267.7 10.4 %all-to-all-done.11.grad_ref = bf16[8,32,2048]{2,1,0:T(8,128)(2,1)} async-done(((bf16[8,32,2048]{2,1,0:T(8,128)(2,1)}), bf16[8,32,2048]{2,1,0:T(8,128)(2,1)}, u32[]{:S(2)}, u32[]{:S(2)}) %all-to-all-start.11) | async-done | bytes 1048608 | tf_op jit(solution)/shard_map/all_to_all | solution.py:31
  278.1 32.1 %all_to_all.148.sums_ref = bf16[8,32,3712]{2,1,0:T(8,128)(2,1)} all-to-all(bf16[8,32,3712]{2,1,0:T(8,128)(2,1)S(1)} %bitcast.116), channel_id=1, replica_groups=mesh['pipe'=8,'dp'=16] {'pipe'}, dimensions={0} | all-to-all | bytes 3801088 | tf_op jit(solution)/shard_map/all_to_all | solution.py:31
  311.7 6.3 %shard_map.156 = bf16[256,4224]{1,0:T(8,128)(2,1)S(1)} custom-call(bf16[8,32,3712]{2,1,0:T(8,128)(2,1)S(1)} %copy-done.8, bf16[8,32,2048]{2,1,0:T(8,128)(2,1)} %all-to-all-done.11.grad_ref, bf16[512,6144]{1,0:T(8,128)(2,1)} %all-gather.14.cloned.1.call-done.gram_ref), custom_call_target="tpu_custom_call" | custom-call | tf_op jit(solution)/shard_map/pallas_call | solution.py:68
  319.4 5.2 all-to-all-start.12
  324.7 31.8 %all-to-all-done.12 = bf16[8,32,4224]{2,1,0:T(8,128)(2,1)S(1)} async-done(((bf16[8,32,4224]{2,1,0:T(8,128)(2,1)}), bf16[8,32,4224]{2,1,0:T(8,128)(2,1)S(1)}, u32[]{:S(2)}, u32[]{:S(2)}) %all-to-all-start.12) | async-done | bytes 2162720 | tf_op jit(solution)/shard_map/all_to_all | solution.py:31
  357.6 10.8 %shard_map.157 = (bf16[4,256,640]{2,1,0:T(8,128)(2,1)S(1)}, bf16[8,1280,128]{2,1,0:T(8,128)(2,1)}, bf16[8,1280,128]{2,1,0:T(8,128)(2,1)}, f32[256,640]{1,0:T(8,128)S(1)}, bf16[256,2048]{1,0:T(8,128)(2,1)S(1)}) custom-call(s32[9]{0:T(128)S(1)} %pad_add_fusion.1.refs_0_, f32[256,640]{1,0:T(8,128)S(1)} %copy-done.23, bf16[256,4224]{1,0:T(8,128)(2,1)S(1)} %bitcast.108, ...), custom_call_target="tpu_custom_call" | custom-call | tf_op jit(solution)/shard_map/pallas_call | solution.py:68
  369.8 18.2 %all_to_all.149.grad_ref = bf16[8,32,2048]{2,1,0:T(8,128)(2,1)S(1)} all-to-all(bf16[8,32,2048]{2,1,0:T(8,128)(2,1)S(1)} %bitcast.117), channel_id=1, replica_groups=mesh['pipe'=8,'dp'=16] {'pipe'}, dimensions={0} | all-to-all | bytes 2097152 | tf_op jit(solution)/shard_map/all_to_all | solution.py:31
  388.0 2.3 shard_map.158
  390.3 4.2 all-to-all-start.14
  396.3 3.0 shard_map.160
  399.4 5.7 collective-permute-start.5
  405.0 15.4 %collective-permute-done.2.refs_1_ = bf16[1280,128]{1,0:T(8,128)(2,1)S(1)} collective-permute-done((bf16[1280,128]{1,0:T(8,128)(2,1)S(1)}, bf16[1280,128]{1,0:T(8,128)(2,1)S(1)}, u32[]{:S(2)}, u32[]{:S(2)}) %collective-permute-start.2) | collective-permute-done | bytes 327712 | tf_op jit(solution)/shard_map/ppermute | solution.py:467
  421.2 9.9 %collective-permute-start.7 = (bf16[1280,128]{1,0:T(8,128)(2,1)}, bf16[1280,128]{1,0:T(8,128)(2,1)}, u32[]{:S(2)}, u32[]{:S(2)}) collective-permute-start(bf16[1280,128]{1,0:T(8,128)(2,1)} %get-tuple-element.106), channel_id=1, source_target_pairs={{0,12},{1,13},{2,14},{3,15},{4,0},{5,1},{6,2},{7,3},{8,4},{9,5},{1... | collective-permute-start | bytes 983048 | tf_op jit(solution)/shard_map/ppermute | solution.py:467
  436.2 11.3 %shard_map.159 = (bf16[4,256,640]{2,1,0:T(8,128)(2,1)S(1)}, bf16[8,1280,128]{2,1,0:T(8,128)(2,1)}, bf16[8,1280,128]{2,1,0:T(8,128)(2,1)}, f32[256,640]{1,0:T(8,128)}) custom-call(s32[9]{0:T(128)S(1)} %pad_add_fusion.refs_0_, bf16[256,640]{1,0:T(8,128)(2,1)S(1)} %copy-done.10, bf16[256,2176]{1,0:T(8,128)(2,1)} %bitcast.36.refs_2_, ...), custom_call_target="tpu_custom_call" | custom-call | tf_op jit(solution)/shard_map/pallas_call | solution.py:68
  449.5 4.7 collective-permute-done.9.other_ref
  457.4 2.4 shard_map.161
  461.3 3.6 all-to-all-start.15
  468.3 34.5 %all-to-all-done.15.refs_0_ = bf16[8,1280,128]{2,1,0:T(8,128)(2,1)S(1)} async-done(((bf16[8,1280,128]{2,1,0:T(8,128)(2,1)}), bf16[8,1280,128]{2,1,0:T(8,128)(2,1)S(1)}, u32[]{:S(2)}, u32[]{:S(2)}) %all-to-all-start.15) | async-done | bytes 2621472 | tf_op jit(solution)/shard_map/all_to_all | solution.py:675
  504.6 6.6 %all-to-all-start.16 = ((bf16[8,160,128]{2,1,0:T(8,128)(2,1)}), bf16[8,160,128]{2,1,0:T(8,128)(2,1)S(1)}, u32[]{:S(2)}, u32[]{:S(2)}) async-start(bf16[8,160,128]{2,1,0:T(8,128)(2,1)} %pad_maximum_fusion.4), calls=%async_computation.16 | async-start | bytes 655360 | tf_op jit(solution)/shard_map/all_to_all | solution.py:31
  512.3 6.7 %collective-permute-start.10 = (bf16[160,512]{1,0:T(8,128)(2,1)S(1)}, bf16[160,512]{1,0:T(8,128)(2,1)S(1)}, u32[]{:S(2)}, u32[]{:S(2)}) collective-permute-start(bf16[160,512]{1,0:T(8,128)(2,1)S(1)} %get-tuple-element.181), channel_id=1, source_target_pairs={{0,0},{1,64},{2,1},{3,65},{4,16},{5,80},{6,17},{7,81},{8,32},{9,96... | collective-permute-start | bytes 491528 | tf_op jit(solution)/shard_map/ppermute | solution.py:482
  519.0 3.5 pad_maximum_fusion
  523.2 7.1 %collective-permute-done.10.refs_1_ = bf16[160,512]{1,0:T(8,128)(2,1)S(1)} collective-permute-done((bf16[160,512]{1,0:T(8,128)(2,1)S(1)}, bf16[160,512]{1,0:T(8,128)(2,1)S(1)}, u32[]{:S(2)}, u32[]{:S(2)}) %collective-permute-start.10) | collective-permute-done | bytes 163872 | tf_op jit(solution)/shard_map/ppermute | solution.py:482
  534.5 2.9 shard_map.164
  537.4 22.8 %all_to_all.150.pieces_ref = bf16[16,2,32,320]{3,2,1,0:T(8,128)(2,1)S(1)} all-to-all(bf16[16,2,32,320]{3,2,1,0:T(8,128)(2,1)S(1)} %get-tuple-element.130), channel_id=1, replica_groups=mesh['pipe'=8,'dp'=16] {'dp'}, dimensions={0} | all-to-all | bytes 1310720 | tf_op jit(solution)/shard_map/all_to_all | solution.py:31
  560.2 4.8 all-to-all-start.17
  566.0 37.0 %all-to-all-done.17 = bf16[8,256,640]{2,1,0:T(8,128)(2,1)} async-done(((bf16[8,256,640]{2,1,0:T(8,128)(2,1)}), bf16[8,256,640]{2,1,0:T(8,128)(2,1)}, u32[]{:S(2)}, u32[]{:S(2)}) %all-to-all-start.17) | async-done | bytes 2621472 | tf_op jit(solution)/shard_map/all_to_all | solution.py:31
  603.0 4.5 copy.47
  607.5 4.4 copy.48
  (197 shorter events, 101.0 us)
Async XLA Ops:
  7.2 212.8 %copy-start = (bf16[256,5120]{1,0:T(8,128)(2,1)S(1)}, bf16[256,5120]{1,0:T(8,128)(2,1)}, u32[]{:S(2)}) copy-start(bf16[256,5120]{1,0:T(8,128)(2,1)} %param.9) | copy-start | bytes 7864324
  7.2 66.3 %all-gather.8.cloned.1.call-start = ((), (), s32[]{:S(2)}) async-start(), calls=%async_computation.20 | async-start | bytes 5570560 | tf_op jit(solution)/shard_map/all_gather | solution.py:510
  8.5 0.7 collective-permute-start
  10.0 119.1 %all-gather.6.cloned.1.call-start = ((), (), s32[]{:S(2)}) async-start(), calls=%async_computation.19 | async-start | bytes 5570560 | tf_op jit(solution)/shard_map/all_gather | solution.py:511
  50.7 135.9 %copy-start.9 = (bf16[256,640]{1,0:T(8,128)(2,1)}, bf16[256,640]{1,0:T(8,128)(2,1)S(1)}, u32[]{:S(2)}) copy-start(bf16[256,640]{1,0:T(8,128)(2,1)S(1)} %get-tuple-element.179.rows_ref.refs_1_) | copy-start | bytes 983044
  53.2 22.9 %copy-start.47 = (bf16[2,32,640]{2,1,0:T(8,128)(2,1)}, bf16[2,32,640]{2,1,0:T(8,128)(2,1)S(1)}, u32[]{:S(2)}) copy-start(bf16[2,32,640]{2,1,0:T(8,128)(2,1)S(1)} %get-tuple-element.185) | copy-start | bytes 245764
  53.9 24.4 %copy-start.46 = (bf16[3,32,640]{2,1,0:T(8,128)(2,1)}, bf16[3,32,640]{2,1,0:T(8,128)(2,1)S(1)}, u32[]{:S(2)}) copy-start(bf16[3,32,640]{2,1,0:T(8,128)(2,1)S(1)} %get-tuple-element.183) | copy-start | bytes 368644
  78.3 13.6 %all-to-all-start.2 = ((bf16[8,32,512]{2,1,0:T(8,128)(2,1)}), bf16[8,32,512]{2,1,0:T(8,128)(2,1)S(1)}, u32[]{:S(2)}, u32[]{:S(2)}) async-start(bf16[8,32,512]{2,1,0:T(8,128)(2,1)} %bitcast.130), calls=%async_computation.2 | async-start | bytes 524288 | tf_op jit(solution)/shard_map/all_to_all | solution.py:31
  94.0 13.0 %all-to-all-start.3 = ((bf16[8,32,512]{2,1,0:T(8,128)(2,1)}), bf16[8,32,512]{2,1,0:T(8,128)(2,1)S(1)}, u32[]{:S(2)}, u32[]{:S(2)}) async-start(bf16[8,32,512]{2,1,0:T(8,128)(2,1)} %tile.6), calls=%async_computation.3 | async-start | bytes 524288 | tf_op jit(solution)/shard_map/all_to_all | solution.py:31
  107.0 22.9 %all-to-all-start.1 = ((bf16[8,32,2176]{2,1,0:T(8,128)(2,1)}), bf16[8,32,2176]{2,1,0:T(8,128)(2,1)}, u32[]{:S(2)}, u32[]{:S(2)}) async-start(bf16[8,32,2176]{2,1,0:T(8,128)(2,1)} %concatenate.48), calls=%async_computation.1 | async-start | bytes 2228224 | tf_op jit(solution)/shard_map/all_to_all | solution.py:31
  112.4 107.6 %all-gather.10.cloned.1.call-start = ((), (), s32[]{:S(2)}) async-start(), calls=%async_computation.21 | async-start | bytes 3342336 | tf_op jit(solution)/shard_map/all_gather | solution.py:541
  130.0 90.0 %all-gather.12.cloned.1.call-start = ((), (), s32[]{:S(2)}) async-start(), calls=%async_computation.22 | async-start | bytes 3342336 | tf_op jit(solution)/shard_map/all_gather | solution.py:541
  135.6 43.2 %copy-start.45 = (bf16[3,32,640]{2,1,0:T(8,128)(2,1)S(1)}, bf16[3,32,640]{2,1,0:T(8,128)(2,1)}, u32[]{:S(2)}) copy-start(bf16[3,32,640]{2,1,0:T(8,128)(2,1)} %get-tuple-element.182) | copy-start | bytes 368644
  177.4 21.2 %copy-start.44 = (bf16[256,512]{1,0:T(8,128)(2,1)S(1)}, bf16[256,512]{1,0:T(8,128)(2,1)}, u32[]{:S(2)}) copy-start(bf16[256,512]{1,0:T(8,128)(2,1)} %convolution_convert_fusion.4) | copy-start | bytes 786436
  181.0 13.1 %all-to-all-start.7 = ((bf16[8,32,512]{2,1,0:T(8,128)(2,1)}), bf16[8,32,512]{2,1,0:T(8,128)(2,1)S(1)}, u32[]{:S(2)}, u32[]{:S(2)}) async-start(bf16[8,32,512]{2,1,0:T(8,128)(2,1)} %bitcast.27), calls=%async_computation.7 | async-start | bytes 524288 | tf_op jit(solution)/shard_map/all_to_all | solution.py:31
  194.9 11.1 %all-to-all-start.8 = ((bf16[8,32,512]{2,1,0:T(8,128)(2,1)}), bf16[8,32,512]{2,1,0:T(8,128)(2,1)S(1)}, u32[]{:S(2)}, u32[]{:S(2)}) async-start(bf16[8,32,512]{2,1,0:T(8,128)(2,1)} %tile.8), calls=%async_computation.8 | async-start | bytes 524288 | tf_op jit(solution)/shard_map/all_to_all | solution.py:31
  206.7 13.3 %all-to-all-start.6 = ((bf16[8,32,1536]{2,1,0:T(8,128)(2,1)}), bf16[8,32,1536]{2,1,0:T(8,128)(2,1)S(1)}, u32[]{:S(2)}, u32[]{:S(2)}) async-start(bf16[8,32,1536]{2,1,0:T(8,128)(2,1)} %bitcast.126), calls=%async_computation.6 | async-start | bytes 1572864 | tf_op jit(solution)/shard_map/all_to_all | solution.py:31
  210.2 100.0 %all-gather.14.cloned.1.call-start = ((), (), s32[]{:S(2)}) async-start(), calls=%async_computation.23 | async-start | bytes 6684672 | tf_op jit(solution)/shard_map/all_gather | solution.py:541
  227.6 28.7 %copy-start.30 = (f32[6,32,512]{2,1,0:T(8,128)}, f32[6,32,512]{2,1,0:T(8,128)S(1)}, u32[]{:S(2)}) copy-start(f32[6,32,512]{2,1,0:T(8,128)S(1)} %get-tuple-element.92.cross_ref) | copy-start | bytes 1179652
  227.6 14.6 %copy-start.19 = (bf16[256,640]{1,0:T(8,128)(2,1)S(1)}, bf16[256,640]{1,0:T(8,128)(2,1)}, u32[]{:S(2)}) copy-start(bf16[256,640]{1,0:T(8,128)(2,1)} %constant_dynamic-slice_fusion.refs_4_) | copy-start | bytes 983044
  227.6 27.7 %all-to-all-start.9 = ((bf16[8,32,2048]{2,1,0:T(8,128)(2,1)}), bf16[8,32,2048]{2,1,0:T(8,128)(2,1)S(1)}, u32[]{:S(2)}, u32[]{:S(2)}) async-start(bf16[8,32,2048]{2,1,0:T(8,128)(2,1)} %bitcast.28), calls=%async_computation.9 | async-start | bytes 2097152 | tf_op jit(solution)/shard_map/all_to_all | solution.py:31
  237.3 23.3 %copy-start.10 = (bf16[256,640]{1,0:T(8,128)(2,1)S(1)}, bf16[256,640]{1,0:T(8,128)(2,1)}, u32[]{:S(2)}) copy-start(bf16[256,640]{1,0:T(8,128)(2,1)} %copy-done.9) | copy-start | bytes 983044
  256.3 21.8 %all-to-all-start.11 = ((bf16[8,32,2048]{2,1,0:T(8,128)(2,1)}), bf16[8,32,2048]{2,1,0:T(8,128)(2,1)}, u32[]{:S(2)}, u32[]{:S(2)}) async-start(bf16[8,32,2048]{2,1,0:T(8,128)(2,1)} %bitcast.31), calls=%async_computation.11 | async-start | bytes 2097152 | tf_op jit(solution)/shard_map/all_to_all | solution.py:31
  267.7 42.5 %copy-start.22 = (f32[256,640]{1,0:T(8,128)}, f32[256,640]{1,0:T(8,128)S(1)}, u32[]{:S(2)}) copy-start(f32[256,640]{1,0:T(8,128)S(1)} %get-tuple-element.82.refs_1_) | copy-start | bytes 1966084
  319.4 37.0 %all-to-all-start.12 = ((bf16[8,32,4224]{2,1,0:T(8,128)(2,1)}), bf16[8,32,4224]{2,1,0:T(8,128)(2,1)S(1)}, u32[]{:S(2)}, u32[]{:S(2)}) async-start(bf16[8,32,4224]{2,1,0:T(8,128)(2,1)} %bitcast.112), calls=%async_computation.12 | async-start | bytes 4325376 | tf_op jit(solution)/shard_map/all_to_all | solution.py:31
  357.6 30.4 %copy-start.2 = (bf16[512,3072]{1,0:T(8,128)(2,1)S(1)}, bf16[512,3072]{1,0:T(8,128)(2,1)}, u32[]{:S(2)}) copy-start(bf16[512,3072]{1,0:T(8,128)(2,1)} %all-gather.10.cloned.1.call-done.gram_in_ref.gram_ref) | copy-start | bytes 9437188
  357.6 30.4 %copy-start.31 = (f32[6,32,512]{2,1,0:T(8,128)S(1)}, f32[6,32,512]{2,1,0:T(8,128)}, u32[]{:S(2)}) copy-start(f32[6,32,512]{2,1,0:T(8,128)} %copy-done.30) | copy-start | bytes 1179652
  357.6 30.4 %copy-start.37 = (f32[4,32,512]{2,1,0:T(8,128)S(1)}, f32[4,32,512]{2,1,0:T(8,128)}, u32[]{:S(2)}) copy-start(f32[4,32,512]{2,1,0:T(8,128)} %copy-done.36) | copy-start | bytes 786436
  368.4 21.9 %copy-start.28 = (f32[256,640]{1,0:T(8,128)}, f32[256,640]{1,0:T(8,128)S(1)}, u32[]{:S(2)}) copy-start(f32[256,640]{1,0:T(8,128)S(1)} %get-tuple-element.93.refs_4_) | copy-start | bytes 1966084
  368.4 19.5 %collective-permute-start.1 = (bf16[8,1280,128]{2,1,0:T(8,128)(2,1)}, bf16[8,1280,128]{2,1,0:T(8,128)(2,1)S(1)}, u32[]{:S(2)}, u32[]{:S(2)}) collective-permute-start(bf16[8,1280,128]{2,1,0:T(8,128)(2,1)} %get-tuple-element.88), channel_id=1, source_target_pairs={{0,1},{1,0},{2,3},{3,2},{4,5},{5,4},{6,7},{7,6},{8,9},{9,8},{10,11... | collective-permute-start | bytes 7864328 | tf_op jit(solution)/shard_map/ppermute | solution.py:439
  390.3 43.6 %all-to-all-start.14 = ((bf16[8,32,2176]{2,1,0:T(8,128)(2,1)}), bf16[8,32,2176]{2,1,0:T(8,128)(2,1)}, u32[]{:S(2)}, u32[]{:S(2)}) async-start(bf16[8,32,2176]{2,1,0:T(8,128)(2,1)} %bitcast.35), calls=%async_computation.14 | async-start | bytes 2228224 | tf_op jit(solution)/shard_map/all_to_all | solution.py:31
  399.3 21.2 %collective-permute-start.2 = (bf16[1280,128]{1,0:T(8,128)(2,1)S(1)}, bf16[1280,128]{1,0:T(8,128)(2,1)S(1)}, u32[]{:S(2)}, u32[]{:S(2)}) collective-permute-start(bf16[1280,128]{1,0:T(8,128)(2,1)S(1)} %get-tuple-element.101), channel_id=1, source_target_pairs={{0,2},{1,3},{2,0},{3,1},{4,6},{5,7},{6,4},{7,5},{8,10},{9,11},{10,... | collective-permute-start | bytes 983048 | tf_op jit(solution)/shard_map/ppermute | solution.py:467
  399.3 31.9 %collective-permute-start.3 = (bf16[1280,128]{1,0:T(8,128)(2,1)S(1)}, bf16[1280,128]{1,0:T(8,128)(2,1)S(1)}, u32[]{:S(2)}, u32[]{:S(2)}) collective-permute-start(bf16[1280,128]{1,0:T(8,128)(2,1)S(1)} %get-tuple-element.102), channel_id=1, source_target_pairs={{0,4},{1,5},{2,6},{3,7},{4,8},{5,9},{6,10},{7,11},{8,12},{9,13},{1... | collective-permute-start | bytes 983048 | tf_op jit(solution)/shard_map/ppermute | solution.py:467
  399.3 48.2 %collective-permute-start.4 = (bf16[1280,128]{1,0:T(8,128)(2,1)}, bf16[1280,128]{1,0:T(8,128)(2,1)}, u32[]{:S(2)}, u32[]{:S(2)}) collective-permute-start(bf16[1280,128]{1,0:T(8,128)(2,1)} %get-tuple-element.103), channel_id=1, source_target_pairs={{0,6},{1,7},{2,4},{3,5},{4,10},{5,11},{6,8},{7,9},{8,14},{9,15},{1... | collective-permute-start | bytes 983048 | tf_op jit(solution)/shard_map/ppermute | solution.py:467
  399.4 48.1 %collective-permute-start.5 = (bf16[1280,128]{1,0:T(8,128)(2,1)}, bf16[1280,128]{1,0:T(8,128)(2,1)}, u32[]{:S(2)}, u32[]{:S(2)}) collective-permute-start(bf16[1280,128]{1,0:T(8,128)(2,1)} %get-tuple-element.104), channel_id=1, source_target_pairs={{0,8},{1,9},{2,10},{3,11},{4,12},{5,13},{6,14},{7,15},{8,0},{9,1},... | collective-permute-start | bytes 983048 | tf_op jit(solution)/shard_map/ppermute | solution.py:467
  405.0 42.4 %collective-permute-start.6 = (bf16[1280,128]{1,0:T(8,128)(2,1)}, bf16[1280,128]{1,0:T(8,128)(2,1)}, u32[]{:S(2)}, u32[]{:S(2)}) collective-permute-start(bf16[1280,128]{1,0:T(8,128)(2,1)} %get-tuple-element.105), channel_id=1, source_target_pairs={{0,10},{1,11},{2,8},{3,9},{4,14},{5,15},{6,12},{7,13},{8,2},{9,3},... | collective-permute-start | bytes 983048 | tf_op jit(solution)/shard_map/ppermute | solution.py:467
  421.2 26.3 %collective-permute-start.7 = (bf16[1280,128]{1,0:T(8,128)(2,1)}, bf16[1280,128]{1,0:T(8,128)(2,1)}, u32[]{:S(2)}, u32[]{:S(2)}) collective-permute-start(bf16[1280,128]{1,0:T(8,128)(2,1)} %get-tuple-element.106), channel_id=1, source_target_pairs={{0,12},{1,13},{2,14},{3,15},{4,0},{5,1},{6,2},{7,3},{8,4},{9,5},{1... | collective-permute-start | bytes 983048 | tf_op jit(solution)/shard_map/ppermute | solution.py:467
  431.9 15.6 %collective-permute-start.8 = (bf16[1280,128]{1,0:T(8,128)(2,1)}, bf16[1280,128]{1,0:T(8,128)(2,1)}, u32[]{:S(2)}, u32[]{:S(2)}) collective-permute-start(bf16[1280,128]{1,0:T(8,128)(2,1)} %get-tuple-element.107), channel_id=1, source_target_pairs={{0,14},{1,15},{2,12},{3,13},{4,2},{5,3},{6,0},{7,1},{8,6},{9,7},{1... | collective-permute-start | bytes 983048 | tf_op jit(solution)/shard_map/ppermute | solution.py:467
  447.5 6.7 %collective-permute-start.9 = (bf16[8,1280,128]{2,1,0:T(8,128)(2,1)}, bf16[8,1280,128]{2,1,0:T(8,128)(2,1)S(1)}, u32[]{:S(2)}, u32[]{:S(2)}) collective-permute-start(bf16[8,1280,128]{2,1,0:T(8,128)(2,1)} %get-tuple-element.109), channel_id=1, source_target_pairs={{0,1},{1,0},{2,3},{3,2},{4,5},{5,4},{6,7},{7,6},{8,9},{9,8},{10,11... | collective-permute-start | bytes 7864328 | tf_op jit(solution)/shard_map/ppermute | solution.py:439
  461.3 41.5 %all-to-all-start.15 = ((bf16[8,1280,128]{2,1,0:T(8,128)(2,1)}), bf16[8,1280,128]{2,1,0:T(8,128)(2,1)S(1)}, u32[]{:S(2)}, u32[]{:S(2)}) async-start(bf16[8,1280,128]{2,1,0:T(8,128)(2,1)} %copy-done.3), calls=%async_computation.15 | async-start | bytes 5242880 | tf_op jit(solution)/shard_map/all_to_all | solution.py:675
  468.3 62.0 %copy-start.12 = (f32[1,320,512]{2,1,0:T(8,128)S(1)}, f32[1,320,512]{2,1,0:T(8,128)}, u32[]{:S(2)}) copy-start(f32[1,320,512]{2,1,0:T(8,128)} %param.10) | copy-start | bytes 1966084
  503.8 26.5 %copy-start.13 = (f32[1,32,5120]{2,1,0:T(8,128)S(1)}, f32[1,32,5120]{2,1,0:T(8,128)}, u32[]{:S(2)}) copy-start(f32[1,32,5120]{2,1,0:T(8,128)} %param.11) | copy-start | bytes 1966084
  503.8 26.5 %copy-start.24 = (f32[1,320,512]{2,1,0:T(8,128)S(1)}, f32[1,320,512]{2,1,0:T(8,128)}, u32[]{:S(2)}) copy-start(f32[1,320,512]{2,1,0:T(8,128)} %param.12) | copy-start | bytes 1966084
  504.6 17.9 %all-to-all-start.16 = ((bf16[8,160,128]{2,1,0:T(8,128)(2,1)}), bf16[8,160,128]{2,1,0:T(8,128)(2,1)S(1)}, u32[]{:S(2)}, u32[]{:S(2)}) async-start(bf16[8,160,128]{2,1,0:T(8,128)(2,1)} %pad_maximum_fusion.4), calls=%async_computation.16 | async-start | bytes 655360 | tf_op jit(solution)/shard_map/all_to_all | solution.py:31
  512.3 18.0 %collective-permute-start.10 = (bf16[160,512]{1,0:T(8,128)(2,1)S(1)}, bf16[160,512]{1,0:T(8,128)(2,1)S(1)}, u32[]{:S(2)}, u32[]{:S(2)}) collective-permute-start(bf16[160,512]{1,0:T(8,128)(2,1)S(1)} %get-tuple-element.181), channel_id=1, source_target_pairs={{0,0},{1,64},{2,1},{3,65},{4,16},{5,80},{6,17},{7,81},{8,32},{9,96... | collective-permute-start | bytes 491528 | tf_op jit(solution)/shard_map/ppermute | solution.py:482
  518.9 11.4 %collective-permute-start.11 = (bf16[160,512]{1,0:T(8,128)(2,1)S(1)}, bf16[160,512]{1,0:T(8,128)(2,1)S(1)}, u32[]{:S(2)}, u32[]{:S(2)}) collective-permute-start(bf16[160,512]{1,0:T(8,128)(2,1)S(1)} %get-tuple-element.180), channel_id=1, source_target_pairs={{0,64},{1,0},{2,65},{3,1},{4,80},{5,16},{6,81},{7,17},{8,96},{9,32... | collective-permute-start | bytes 491528 | tf_op jit(solution)/shard_map/ppermute | solution.py:482
  560.2 42.8 %all-to-all-start.17 = ((bf16[8,256,640]{2,1,0:T(8,128)(2,1)}), bf16[8,256,640]{2,1,0:T(8,128)(2,1)}, u32[]{:S(2)}, u32[]{:S(2)}) async-start(bf16[8,256,640]{2,1,0:T(8,128)(2,1)} %pad_maximum_fusion), calls=%async_computation.17 | async-start | bytes 5242880 | tf_op jit(solution)/shard_map/all_to_all | solution.py:31
  603.0 8.9 %copy-start.1 = (bf16[256,5120]{1,0:T(8,128)(2,1)S(1)}, bf16[256,5120]{1,0:T(8,128)(2,1)}, u32[]{:S(2)}) copy-start(bf16[256,5120]{1,0:T(8,128)(2,1)} %param.9) | copy-start | bytes 7864324
  (30 other events, 40.7 us)
Sparse Core Ops, SparseCore 0:
  10.3 63.1 all-gather.7
  75.7 53.3 all-gather.5
  131.4 44.4 all-gather.9
  178.0 40.4 all-gather.11
  220.6 89.1 all-gather.13

commit v7 on v6

--- a/solution.py
+++ b/solution.py
@@ -15,7 +15,7 @@
 
 BLOCKS = ((0, 4), (4, 8))
 LANES = 128
-VMEM_BYTES = 48 * 1024 * 1024
+VMEM_BYTES = 34 * 1024 * 1024
 
 
 def dot(left, right, dims):
@@ -58,19 +58,38 @@
     return (master_new, moment_new, second_new)
 
 
-def run(kernel, shapes, *operands, specs=None):
+def run(kernel, shapes, *operands, specs=None, smem=False):
     more = {}
     if specs is not None:
         whole = [pl.BlockSpec(x.shape, zeros_map(x.ndim)) for x in operands]
         outs = [pl.BlockSpec(shape, zeros_map(len(shape))) for shape, _ in shapes]
         given = [specs.get(at, spec) for at, spec in enumerate(whole)]
         more = {"grid": (1,), "in_specs": given, "out_specs": outs}
+    if smem:
+        rest = [pl.BlockSpec(memory_space=pltpu.VMEM)] * (len(operands) - 1)
+        more = {"in_specs": [pl.BlockSpec(memory_space=pltpu.SMEM)] + rest}
     return pl.pallas_call(
         kernel,
         out_shape=[jax.ShapeDtypeStruct(shape, kind) for shape, kind in shapes],
         compiler_params=pltpu.CompilerParams(vmem_limit_bytes=VMEM_BYTES),
         **more,
     )(*operands)
+
+
+def columns_in_place(x):
+    count, rows, columns = x.shape
+
+    def kernel(x_ref, out_ref):
+        out_ref[...] = x_ref[0]
+
+    return pl.pallas_call(
+        kernel,
+        out_shape=jax.ShapeDtypeStruct((rows, count * columns), x.dtype),
+        grid=(count,),
+        in_specs=[pl.BlockSpec((1, rows, columns), lambda at: (at, 0, 0))],
+        out_specs=pl.BlockSpec((rows, columns), lambda at: (0, at)),
+        compiler_params=pltpu.CompilerParams(vmem_limit_bytes=VMEM_BYTES),
+    )(x)
 
 
 def zeros_map(ndim):
@@ -287,7 +306,11 @@
 
     def kernel(*refs):
         place_ref, exact_ref, packs_ref, acts_ref, up_ref, in_ref, out_ref = refs[:7]
-        grads_ref, mine_ref, other_ref, up_new_ref = refs[7:11]
+        refs = refs[7:]
+        if first == 0:
+            refs[1][last:] = refs[0][...]
+            refs = refs[1:]
+        grads_ref, mine_ref, other_ref, up_new_ref = refs[:4]
         exact = exact_ref[...].astype(jnp.float32)
         rows = {first: exact.astype(jnp.bfloat16)}
 
@@ -346,7 +369,7 @@
         if before < first:
             for s in range(before, first):
                 columns = dot(narrow, part(out_ref, s, chunk), LAST).astype(jnp.bfloat16)
-                refs[11][:, (s - before) * inner : (s - before + 1) * inner] = columns
+                refs[4][:, (s - before) * inner : (s - before + 1) * inner] = columns
 
     return kernel
 
@@ -526,14 +549,11 @@
         for first, last in blocks:
             wanted = (down_units if down else up_units)(first, last)
             orders.append([units.index(unit) for unit in wanted])
-        padded = -(-len(units) // n_pipe) * n_pipe
         partial = [p.astype(jnp.bfloat16) for p in partial]
-        if padded > len(units):
-            partial.append(jnp.zeros(((padded - len(units)) * share_out, inner), jnp.bfloat16))
         arrived = swap(jnp.concatenate(partial, axis=0), "pipe")
         arrived = arrived.reshape(n_pipe, -1, inner)
         mine = jnp.sum(arrived.astype(jnp.float32), axis=0).astype(jnp.bfloat16)
-        every = swap(jnp.tile(mine, (n_pipe, 1)), "pipe").reshape(padded, share_out, inner)
+        every = swap(jnp.tile(mine, (n_pipe, 1)), "pipe").reshape(-1, share_out, inner)
         shapes = [((share_out, len(order) * inner), jnp.bfloat16) for order in orders]
         return run(columns_kernel(orders), shapes, every)
 
@@ -619,7 +639,6 @@
     away = (chips // 2 - chip // 2 + xs) % xs * 2 + (chips % 2 + chip % 2) % 2
     fixed = jnp.concatenate([chips, core[None]]).astype(jnp.int32)
     place = jnp.concatenate([away, core[None]]).astype(jnp.int32)
-    in_smem = {0: pl.BlockSpec(memory_space=pltpu.SMEM)}
 
     grads_high, mine, other, upstream, columns = run(
         grads_kernel(middle, last, first, inner, chunk, n_dp, (last - middle) * inner + LANES),
@@ -637,7 +656,7 @@
         seed,
         all_in,
         all_out,
-        specs=in_smem,
+        smem=True,
     )
     grad_low = exchanged(columns, n_pipe)
     other = other_core(other, n_dp)
@@ -654,10 +673,10 @@
         gram_in_low,
     )[0]
     packs = swap(packs, "pipe")
-    grads_low, mine, other, _ = run(
+    grads, mine, other, _ = run(
         grads_kernel(first, middle, first, inner, chunk, n_dp, 0),
         [
-            ((count, tok_rows, chunk), jnp.bfloat16),
+            ((n_pipe, tok_rows, chunk), jnp.bfloat16),
             (packed_shape(count), jnp.bfloat16),
             (packed_shape(count), jnp.bfloat16),
             ((tok_rows, chunk), jnp.float32),
@@ -669,7 +688,8 @@
         upstream,
         all_in,
         all_out,
-        specs=in_smem,
+        grads_high,
+        smem=True,
     )
     mine, other, arrived_high = lax.optimization_barrier((mine, other, arrived_high))
     arrived_low = lax.all_to_all(
@@ -695,10 +715,8 @@
         ins.append(sum_in)
         outs.append(sum_out.reshape(high - low, -1, LANES))
     grad_out = swap(jnp.concatenate(outs, axis=0), "pipe")
-    grads = jnp.concatenate([grads_low, grads_high], axis=0)
     grads, grad_out = lax.optimization_barrier((grads, grad_out))
     input_grads = swap(grads, "pipe")
-    input_grads = input_grads.transpose(1, 0, 2).reshape(1, tok_rows, width)
     grad_in = move_in(*ins, n_pipe, n_dp)
     is_high = (me >= middle).astype(jnp.int32).reshape(1)
 
@@ -717,9 +735,11 @@
         master_out[0],
         moment_out[0],
         second_out[0],
-        specs=in_smem,
+        smem=True,
     )
     new_in, new_moment_in, new_second_in, new_out, new_moment_out, new_second_out = updated
+    pieces, input_grads = lax.optimization_barrier((pieces, input_grads))
+    input_grads = columns_in_place(input_grads)[None]
     roll_in, roll_out = run(
         rollout_kernel(share_out, share_in),
         [(shape_out, jnp.bfloat16), (shape_in, jnp.bfloat16)],

time: 622 us -> 615 us (0.989)
  local copies, waits for them, and re-layouts: 46.6 us -> 65.2 us
  blocking collectives: 141 us -> 129 us
  Pallas kernels: 55.4 us -> 47.2 us
    ppermute x2, waiting for transfers between devices: 7.06 us -> 35.7 us  [move_in(): moved.append(lax.ppermute(payload, ('pipe', 'dp'), pairs))]
    all_to_all x12, waiting for transfers between devices: 111 us -> 82 us  [swap(): return lax.all_to_all(x, axis, 0, 0, tiled=True)]
    unnamed x98 -> x123, local copies, waits for them, and re-layouts: 31.9 us -> 54.4 us
    pallas_call x15, Pallas kernels: 55.4 us -> 41.3 us  [run(): pl.pallas_call(kernel, out_shape=[jax.ShapeDtypeStruct(shape, kind) for s...]
    all_to_all x6, blocking collectives: 141 us -> 129 us  [swap(): return lax.all_to_all(x, axis, 0, 0, tiled=True)]
  transfers between devices with their start and end apart: 30 -> 30, of which waited for: 16 -> 17; matrix products, arithmetic and copies ran while one was open for 10% -> 10% of each run, Pallas kernels for 5% -> 5%
where the time goes in v7:
time: 615 us; the launch traced here: 607 us
  waiting for transfers between devices  207 us (34%)
  blocking collectives  129 us (21%)
  starting transfers between devices  94.2 us (15%)
  local copies, waits for them, and re-layouts  65.2 us (11%)
  Pallas kernels  47.2 us (8%)
  matrix products  37.5 us (6%)
  between operations  14.4 us (2%)
  other arithmetic  12.6 us (2%)
    all_to_all x6, blocking collectives, swap(): return lax.all_to_all(x, axis, 0, 0, tiled=True)  129 us
    all_to_all x12, waiting for transfers between devices, swap(): return lax.all_to_all(x, axis, 0, 0, tiled=True)  82 us
    all_to_all x12, starting transfers between devices, swap(): return lax.all_to_all(x, axis, 0, 0, tiled=True)  60.5 us
    unnamed x123, local copies, waits for them, and re-layouts  54.4 us
    pallas_call x15, Pallas kernels, run(): pl.pallas_call(kernel, out_shape=[jax.ShapeDtypeStruct(shape, kind) for s...  41.3 us
    dot_general x23, matrix products, dot(): lax.dot_general(left, right, (dims, ((), ())), preferred_element_type=jnp...  37.5 us
    ppermute x2, waiting for transfers between devices, move_in(): moved.append(lax.ppermute(payload, ('pipe', 'dp'), pairs))  35.7 us
    all_to_all x1, waiting for transfers between devices, on_device(): lax.all_to_all(added(mine, other_core(other, n_dp), 1)[0], 'dp', 0, 0, ti...  34.9 us
  transfers between devices with their start and end apart: 30, of which 17 were waited for; matrix products, arithmetic and copies ran while one was open for 10% of the time, Pallas kernels for 5%

profile of v7, /device:TPU:1, one launch (start us, length us, event | category | flops | bytes accessed | tf_op | source)
XLA Modules:
  0.0 606.7 jit_solution(15986248629860834704)
XLA Ops:
  11.2 37.5 %all_to_all.145 = bf16[8,32,640]{2,1,0:T(8,128)(2,1)S(1)} all-to-all(bf16[8,32,640]{2,1,0:T(8,128)(2,1)S(1)} %copy.30), channel_id=1, replica_groups=mesh['pipe'=8,'dp'=16] {'pipe'}, dimensions={0} | all-to-all | bytes 655360 | tf_op jit(solution)/shard_map/all_to_all | solution.py:31
  54.8 18.6 %all-gather.8.cloned.1.call-done.in_ref.refs_5_ = bf16[5120,512]{1,0:T(8,128)(2,1)} async-done(((bf16[320,512]{1,0:T(8,128)(2,1)}), bf16[5120,512]{1,0:T(8,128)(2,1)}) %all-gather.8.cloned.1.call-update) | async-done | bytes 5242896 | tf_op jit(solution)/shard_map/all_gather | solution.py:533
  78.1 6.2 %all-to-all-start.2 = ((bf16[8,24,512]{2,1,0:T(8,128)(2,1)}), bf16[8,24,512]{2,1,0:T(8,128)(2,1)S(1)}, u32[]{:S(2)}, u32[]{:S(2)}) async-start(bf16[8,24,512]{2,1,0:T(8,128)(2,1)} %bitcast.133), calls=%async_computation.2 | async-start | bytes 393216 | tf_op jit(solution)/shard_map/all_to_all | solution.py:31
  93.8 5.9 all-to-all-start.3
  102.5 3.3 concatenate.45
  106.8 5.7 all-to-all-start.1
  113.3 10.7 %all-gather.6.cloned.1.call-done.out_ref.refs_6_ = bf16[512,5120]{1,0:T(8,128)(2,1)} async-done(((bf16[32,5120]{1,0:T(8,128)(2,1)}), bf16[512,5120]{1,0:T(8,128)(2,1)}) %all-gather.6.cloned.1.call-update) | async-done | bytes 5242896 | tf_op jit(solution)/shard_map/all_gather | solution.py:534
  123.9 4.8 all-to-all-done.1.down_ref
  137.4 13.3 %all_to_all.146 = bf16[8,48,512]{2,1,0:T(8,128)(2,1)} all-to-all(bf16[8,48,512]{2,1,0:T(8,128)(2,1)S(1)} %bitcast.134), channel_id=1, replica_groups=mesh['pipe'=8,'dp'=16] {'pipe'}, dimensions={0} | all-to-all | bytes 786432 | tf_op jit(solution)/shard_map/all_to_all | solution.py:31
  151.7 13.2 %all_to_all.147 = bf16[8,48,512]{2,1,0:T(8,128)(2,1)S(1)} all-to-all(bf16[8,48,512]{2,1,0:T(8,128)(2,1)S(1)} %tile.7), channel_id=1, replica_groups=mesh['pipe'=8,'dp'=16] {'pipe'}, dimensions={0} | all-to-all | bytes 786432 | tf_op jit(solution)/shard_map/all_to_all | solution.py:31
  175.4 5.0 all-to-all-start.7
  182.0 5.6 all-to-all-done.7
  188.3 3.4 all-to-all-start.8
  193.7 5.0 all-to-all-done.8
  199.4 3.5 all-to-all-start.6
  205.6 7.1 %all-to-all-done.6.up_ref = bf16[8,32,1536]{2,1,0:T(8,128)(2,1)S(1)} async-done(((bf16[8,32,1536]{2,1,0:T(8,128)(2,1)}), bf16[8,32,1536]{2,1,0:T(8,128)(2,1)S(1)}, u32[]{:S(2)}, u32[]{:S(2)}) %all-to-all-start.6) | async-done | bytes 786464 | tf_op jit(solution)/shard_map/all_to_all | solution.py:31
  212.7 4.4 all-gather.12.cloned.1.call-done.gram_out_ref
  221.6 4.2 shard_map.154
  226.5 7.0 %all-to-all-start.9 = ((bf16[8,32,2048]{2,1,0:T(8,128)(2,1)}), bf16[8,32,2048]{2,1,0:T(8,128)(2,1)S(1)}, u32[]{:S(2)}, u32[]{:S(2)}) async-start(bf16[8,32,2048]{2,1,0:T(8,128)(2,1)} %bitcast.31), calls=%async_computation.9 | async-start | bytes 2097152 | tf_op jit(solution)/shard_map/all_to_all | solution.py:31
  241.1 10.2 %all-to-all-done.9 = bf16[8,32,2048]{2,1,0:T(8,128)(2,1)S(1)} async-done(((bf16[8,32,2048]{2,1,0:T(8,128)(2,1)}), bf16[8,32,2048]{2,1,0:T(8,128)(2,1)S(1)}, u32[]{:S(2)}, u32[]{:S(2)}) %all-to-all-start.9) | async-done | bytes 1048608 | tf_op jit(solution)/shard_map/all_to_all | solution.py:31
  251.3 4.3 all-to-all-start.11
  255.6 2.6 copy-done.2
  258.2 2.5 copy-done.5
  264.4 9.1 %all-to-all-done.11.grad_ref = bf16[8,32,2048]{2,1,0:T(8,128)(2,1)} async-done(((bf16[8,32,2048]{2,1,0:T(8,128)(2,1)}), bf16[8,32,2048]{2,1,0:T(8,128)(2,1)}, u32[]{:S(2)}, u32[]{:S(2)}) %all-to-all-start.11) | async-done | bytes 1048608 | tf_op jit(solution)/shard_map/all_to_all | solution.py:31
  273.5 30.9 %all_to_all.148.sums_ref = bf16[8,32,3712]{2,1,0:T(8,128)(2,1)} all-to-all(bf16[8,32,3712]{2,1,0:T(8,128)(2,1)S(1)} %bitcast.116), channel_id=1, replica_groups=mesh['pipe'=8,'dp'=16] {'pipe'}, dimensions={0} | all-to-all | bytes 3801088 | tf_op jit(solution)/shard_map/all_to_all | solution.py:31
  305.9 2.8 copy-done.16
  308.7 4.5 shard_map.156
  314.5 4.4 all-to-all-start.12
  319.0 31.5 %all-to-all-done.12 = bf16[8,32,4224]{2,1,0:T(8,128)(2,1)S(1)} async-done(((bf16[8,32,4224]{2,1,0:T(8,128)(2,1)}), bf16[8,32,4224]{2,1,0:T(8,128)(2,1)S(1)}, u32[]{:S(2)}, u32[]{:S(2)}) %all-to-all-start.12) | async-done | bytes 2162720 | tf_op jit(solution)/shard_map/all_to_all | solution.py:31
  357.0 8.2 %shard_map.157 = (bf16[4,256,640]{2,1,0:T(8,128)(2,1)S(1)}, bf16[8,1280,128]{2,1,0:T(8,128)(2,1)S(1)}, bf16[8,1280,128]{2,1,0:T(8,128)(2,1)S(1)}, f32[256,640]{1,0:T(8,128)S(1)}, bf16[256,2048]{1,0:T(8,128)(2,1)S(1)}) custom-call(s32[9]{0:T(128)S(1)} %pad_add_fusion.1.refs_0_, f32[256,640]{1,0:T(8,128)S(1)} %copy-done.35, bf16[256,4224]{1,0:T(8,128)(2,1)S(1)} %bitcast.109, ...), custom_call_target="tpu_custom_call" | custom-call | tf_op jit(solution)/shard_map/pallas_call | solution.py:71
  368.3 19.2 %all_to_all.149.grad_ref = bf16[8,32,2048]{2,1,0:T(8,128)(2,1)S(1)} all-to-all(bf16[8,32,2048]{2,1,0:T(8,128)(2,1)S(1)} %bitcast.118), channel_id=1, replica_groups=mesh['pipe'=8,'dp'=16] {'pipe'}, dimensions={0} | all-to-all | bytes 2097152 | tf_op jit(solution)/shard_map/all_to_all | solution.py:31
  391.4 4.3 all-to-all-start.14
  401.9 5.1 collective-permute-start.5
  407.0 16.1 %collective-permute-done.2.refs_1_ = bf16[1280,128]{1,0:T(8,128)(2,1)S(1)} collective-permute-done((bf16[1280,128]{1,0:T(8,128)(2,1)S(1)}, bf16[1280,128]{1,0:T(8,128)(2,1)S(1)}, u32[]{:S(2)}, u32[]{:S(2)}) %collective-permute-start.2) | collective-permute-done | bytes 327712 | tf_op jit(solution)/shard_map/ppermute | solution.py:490
  423.9 9.4 %collective-permute-start.7 = (bf16[1280,128]{1,0:T(8,128)(2,1)}, bf16[1280,128]{1,0:T(8,128)(2,1)}, u32[]{:S(2)}, u32[]{:S(2)}) collective-permute-start(bf16[1280,128]{1,0:T(8,128)(2,1)} %get-tuple-element.107), channel_id=1, source_target_pairs={{0,12},{1,13},{2,14},{3,15},{4,0},{5,1},{6,2},{7,3},{8,4},{9,5},{1... | collective-permute-start | bytes 983048 | tf_op jit(solution)/shard_map/ppermute | solution.py:490
  435.7 2.5 copy-done.4
  441.8 8.6 %shard_map.159 = (bf16[8,256,640]{2,1,0:T(8,128)(2,1)S(1)}, bf16[8,1280,128]{2,1,0:T(8,128)(2,1)S(1)}, bf16[8,1280,128]{2,1,0:T(8,128)(2,1)S(1)}, f32[256,640]{1,0:T(8,128)}) custom-call(s32[9]{0:T(128)S(1)} %pad_add_fusion.refs_0_, bf16[256,640]{1,0:T(8,128)(2,1)S(1)} %copy-done.19, bf16[256,2176]{1,0:T(8,128)(2,1)} %bitcast.39.refs_2_, ...), custom_call_target="tpu_custom_call" | custom-call | tf_op jit(solution)/shard_map/pallas_call | solution.py:71
  453.8 4.5 collective-permute-done.9.other_ref
  460.5 4.4 all-to-all-start.15
  468.3 34.9 %all-to-all-done.15.refs_0_ = bf16[8,1280,128]{2,1,0:T(8,128)(2,1)} async-done(((bf16[8,1280,128]{2,1,0:T(8,128)(2,1)}), bf16[8,1280,128]{2,1,0:T(8,128)(2,1)}, u32[]{:S(2)}, u32[]{:S(2)}) %all-to-all-start.15) | async-done | bytes 2621472 | tf_op jit(solution)/shard_map/all_to_all | solution.py:695
  505.9 14.5 %all_to_all.150.refs_3_ = bf16[8,160,128]{2,1,0:T(8,128)(2,1)} all-to-all(bf16[8,160,128]{2,1,0:T(8,128)(2,1)S(1)} %pad_maximum_fusion.3), channel_id=1, replica_groups=mesh['pipe'=8,'dp'=16] {'pipe'}, dimensions={0} | all-to-all | bytes 655360 | tf_op jit(solution)/shard_map/all_to_all | solution.py:31
  520.4 4.5 all-to-all-start.17
  525.0 7.5 %collective-permute-start.10 = (bf16[160,512]{1,0:T(8,128)(2,1)S(1)}, bf16[160,512]{1,0:T(8,128)(2,1)S(1)}, u32[]{:S(2)}, u32[]{:S(2)}) collective-permute-start(bf16[160,512]{1,0:T(8,128)(2,1)S(1)} %get-tuple-element.140), channel_id=1, source_target_pairs={{0,0},{1,64},{2,1},{3,65},{4,16},{5,80},{6,17},{7,81},{8,32},{9,96... | collective-permute-start | bytes 491528 | tf_op jit(solution)/shard_map/ppermute | solution.py:505
  532.6 35.6 %collective-permute-done.10.refs_1_ = bf16[160,512]{1,0:T(8,128)(2,1)S(1)} collective-permute-done((bf16[160,512]{1,0:T(8,128)(2,1)S(1)}, bf16[160,512]{1,0:T(8,128)(2,1)S(1)}, u32[]{:S(2)}, u32[]{:S(2)}) %collective-permute-start.10) | collective-permute-done | bytes 163872 | tf_op jit(solution)/shard_map/ppermute | solution.py:505
  576.4 2.9 shard_map.164
  580.2 6.2 %all-to-all-start.18 = ((bf16[16,2,32,320]{3,2,1,0:T(8,128)(2,1)}), bf16[16,2,32,320]{3,2,1,0:T(8,128)(2,1)S(1)}, u32[]{:S(2)}, u32[]{:S(2)}) async-start(bf16[16,2,32,320]{3,2,1,0:T(8,128)(2,1)} %copy-done.31), calls=%async_computation.18 | async-start | bytes 1572864 | tf_op jit(solution)/shard_map/all_to_all | solution.py:31
  586.4 5.9 shard_map.165
  592.3 6.9 %all-to-all-done.18.pieces_ref = bf16[16,2,32,320]{3,2,1,0:T(8,128)(2,1)S(1)} async-done(((bf16[16,2,32,320]{3,2,1,0:T(8,128)(2,1)}), bf16[16,2,32,320]{3,2,1,0:T(8,128)(2,1)S(1)}, u32[]{:S(2)}, u32[]{:S(2)}) %all-to-all-start.18) | async-done | bytes 655392 | tf_op jit(solution)/shard_map/all_to_all | solution.py:31
  (218 shorter events, 123.9 us)
Async XLA Ops:
  7.2 209.9 %copy-start = (bf16[256,5120]{1,0:T(8,128)(2,1)S(1)}, bf16[256,5120]{1,0:T(8,128)(2,1)}, u32[]{:S(2)}) copy-start(bf16[256,5120]{1,0:T(8,128)(2,1)} %param.9) | copy-start | bytes 7864324
  7.2 66.2 %all-gather.8.cloned.1.call-start = ((), (), s32[]{:S(2)}) async-start(), calls=%async_computation.20 | async-start | bytes 5570560 | tf_op jit(solution)/shard_map/all_gather | solution.py:533
  8.5 0.7 collective-permute-start
  10.0 114.0 %all-gather.6.cloned.1.call-start = ((), (), s32[]{:S(2)}) async-start(), calls=%async_computation.19 | async-start | bytes 5570560 | tf_op jit(solution)/shard_map/all_gather | solution.py:534
  50.7 129.8 %copy-start.18 = (bf16[256,640]{1,0:T(8,128)(2,1)}, bf16[256,640]{1,0:T(8,128)(2,1)S(1)}, u32[]{:S(2)}) copy-start(bf16[256,640]{1,0:T(8,128)(2,1)S(1)} %get-tuple-element.138.rows_ref.refs_1_) | copy-start | bytes 983044
  54.8 23.4 %copy-start.59 = (bf16[3,32,640]{2,1,0:T(8,128)(2,1)}, bf16[3,32,640]{2,1,0:T(8,128)(2,1)S(1)}, u32[]{:S(2)}) copy-start(bf16[3,32,640]{2,1,0:T(8,128)(2,1)S(1)} %get-tuple-element.142) | copy-start | bytes 368644
  78.1 13.6 %all-to-all-start.2 = ((bf16[8,24,512]{2,1,0:T(8,128)(2,1)}), bf16[8,24,512]{2,1,0:T(8,128)(2,1)S(1)}, u32[]{:S(2)}, u32[]{:S(2)}) async-start(bf16[8,24,512]{2,1,0:T(8,128)(2,1)} %bitcast.133), calls=%async_computation.2 | async-start | bytes 393216 | tf_op jit(solution)/shard_map/all_to_all | solution.py:31
  93.8 13.0 %all-to-all-start.3 = ((bf16[8,24,512]{2,1,0:T(8,128)(2,1)}), bf16[8,24,512]{2,1,0:T(8,128)(2,1)S(1)}, u32[]{:S(2)}, u32[]{:S(2)}) async-start(bf16[8,24,512]{2,1,0:T(8,128)(2,1)} %tile.6), calls=%async_computation.3 | async-start | bytes 393216 | tf_op jit(solution)/shard_map/all_to_all | solution.py:31
  105.8 28.7 %copy-start.60 = (bf16[2,32,640]{2,1,0:T(8,128)(2,1)S(1)}, bf16[2,32,640]{2,1,0:T(8,128)(2,1)}, u32[]{:S(2)}) copy-start(bf16[2,32,640]{2,1,0:T(8,128)(2,1)} %get-tuple-element.143) | copy-start | bytes 245764
  106.8 22.0 %all-to-all-start.1 = ((bf16[8,32,2176]{2,1,0:T(8,128)(2,1)}), bf16[8,32,2176]{2,1,0:T(8,128)(2,1)}, u32[]{:S(2)}, u32[]{:S(2)}) async-start(bf16[8,32,2176]{2,1,0:T(8,128)(2,1)} %concatenate.45), calls=%async_computation.1 | async-start | bytes 2228224 | tf_op jit(solution)/shard_map/all_to_all | solution.py:31
  112.5 100.1 %all-gather.10.cloned.1.call-start = ((), (), s32[]{:S(2)}) async-start(), calls=%async_computation.21 | async-start | bytes 3342336 | tf_op jit(solution)/shard_map/all_gather | solution.py:561
  128.8 88.3 %all-gather.12.cloned.1.call-start = ((), (), s32[]{:S(2)}) async-start(), calls=%async_computation.22 | async-start | bytes 3342336 | tf_op jit(solution)/shard_map/all_gather | solution.py:561
  133.1 40.3 %copy-start.58 = (bf16[3,32,640]{2,1,0:T(8,128)(2,1)S(1)}, bf16[3,32,640]{2,1,0:T(8,128)(2,1)}, u32[]{:S(2)}) copy-start(bf16[3,32,640]{2,1,0:T(8,128)(2,1)} %get-tuple-element.141) | copy-start | bytes 368644
  175.4 12.1 %all-to-all-start.7 = ((bf16[8,24,512]{2,1,0:T(8,128)(2,1)}), bf16[8,24,512]{2,1,0:T(8,128)(2,1)S(1)}, u32[]{:S(2)}, u32[]{:S(2)}) async-start(bf16[8,24,512]{2,1,0:T(8,128)(2,1)} %bitcast.29), calls=%async_computation.7 | async-start | bytes 393216 | tf_op jit(solution)/shard_map/all_to_all | solution.py:31
  188.3 10.4 %all-to-all-start.8 = ((bf16[8,24,512]{2,1,0:T(8,128)(2,1)}), bf16[8,24,512]{2,1,0:T(8,128)(2,1)S(1)}, u32[]{:S(2)}, u32[]{:S(2)}) async-start(bf16[8,24,512]{2,1,0:T(8,128)(2,1)} %tile.8), calls=%async_computation.8 | async-start | bytes 393216 | tf_op jit(solution)/shard_map/all_to_all | solution.py:31
  199.4 13.3 %all-to-all-start.6 = ((bf16[8,32,1536]{2,1,0:T(8,128)(2,1)}), bf16[8,32,1536]{2,1,0:T(8,128)(2,1)S(1)}, u32[]{:S(2)}, u32[]{:S(2)}) async-start(bf16[8,32,1536]{2,1,0:T(8,128)(2,1)} %bitcast.128), calls=%async_computation.6 | async-start | bytes 1572864 | tf_op jit(solution)/shard_map/all_to_all | solution.py:31
  202.9 101.5 %all-gather.14.cloned.1.call-start = ((), (), s32[]{:S(2)}) async-start(), calls=%async_computation.23 | async-start | bytes 6684672 | tf_op jit(solution)/shard_map/all_gather | solution.py:561
  226.5 24.8 %copy-start.42 = (f32[6,32,512]{2,1,0:T(8,128)}, f32[6,32,512]{2,1,0:T(8,128)S(1)}, u32[]{:S(2)}) copy-start(f32[6,32,512]{2,1,0:T(8,128)S(1)} %get-tuple-element.94.cross_ref) | copy-start | bytes 1179652
  226.5 11.9 %copy-start.30 = (bf16[256,640]{1,0:T(8,128)(2,1)S(1)}, bf16[256,640]{1,0:T(8,128)(2,1)}, u32[]{:S(2)}) copy-start(bf16[256,640]{1,0:T(8,128)(2,1)} %constant_dynamic-slice_fusion.refs_4_) | copy-start | bytes 983044
  226.5 24.8 %all-to-all-start.9 = ((bf16[8,32,2048]{2,1,0:T(8,128)(2,1)}), bf16[8,32,2048]{2,1,0:T(8,128)(2,1)S(1)}, u32[]{:S(2)}, u32[]{:S(2)}) async-start(bf16[8,32,2048]{2,1,0:T(8,128)(2,1)} %bitcast.31), calls=%async_computation.9 | async-start | bytes 2097152 | tf_op jit(solution)/shard_map/all_to_all | solution.py:31
  233.5 22.1 %copy-start.19 = (bf16[256,640]{1,0:T(8,128)(2,1)S(1)}, bf16[256,640]{1,0:T(8,128)(2,1)}, u32[]{:S(2)}) copy-start(bf16[256,640]{1,0:T(8,128)(2,1)} %copy-done.18) | copy-start | bytes 983044
  251.3 22.1 %all-to-all-start.11 = ((bf16[8,32,2048]{2,1,0:T(8,128)(2,1)}), bf16[8,32,2048]{2,1,0:T(8,128)(2,1)}, u32[]{:S(2)}, u32[]{:S(2)}) async-start(bf16[8,32,2048]{2,1,0:T(8,128)(2,1)} %bitcast.34), calls=%async_computation.11 | async-start | bytes 2097152 | tf_op jit(solution)/shard_map/all_to_all | solution.py:31
  264.4 40.0 %copy-start.34 = (f32[256,640]{1,0:T(8,128)}, f32[256,640]{1,0:T(8,128)S(1)}, u32[]{:S(2)}) copy-start(f32[256,640]{1,0:T(8,128)S(1)} %get-tuple-element.84.refs_1_) | copy-start | bytes 1966084
  314.5 36.0 %all-to-all-start.12 = ((bf16[8,32,4224]{2,1,0:T(8,128)(2,1)}), bf16[8,32,4224]{2,1,0:T(8,128)(2,1)S(1)}, u32[]{:S(2)}, u32[]{:S(2)}) async-start(bf16[8,32,4224]{2,1,0:T(8,128)(2,1)} %bitcast.113), calls=%async_computation.12 | async-start | bytes 4325376 | tf_op jit(solution)/shard_map/all_to_all | solution.py:31
  357.0 32.0 %copy-start.9 = (bf16[512,3072]{1,0:T(8,128)(2,1)S(1)}, bf16[512,3072]{1,0:T(8,128)(2,1)}, u32[]{:S(2)}) copy-start(bf16[512,3072]{1,0:T(8,128)(2,1)} %all-gather.10.cloned.1.call-done.gram_in_ref.gram_ref) | copy-start | bytes 9437188
  357.0 32.0 %copy-start.43 = (f32[6,32,512]{2,1,0:T(8,128)S(1)}, f32[6,32,512]{2,1,0:T(8,128)}, u32[]{:S(2)}) copy-start(f32[6,32,512]{2,1,0:T(8,128)} %copy-done.42) | copy-start | bytes 1179652
  357.0 32.0 %copy-start.49 = (f32[4,32,512]{2,1,0:T(8,128)S(1)}, f32[4,32,512]{2,1,0:T(8,128)}, u32[]{:S(2)}) copy-start(f32[4,32,512]{2,1,0:T(8,128)} %copy-done.48) | copy-start | bytes 786436
  366.7 24.6 %copy-start.28 = (bf16[4,256,640]{2,1,0:T(8,128)(2,1)}, bf16[4,256,640]{2,1,0:T(8,128)(2,1)S(1)}, u32[]{:S(2)}) copy-start(bf16[4,256,640]{2,1,0:T(8,128)(2,1)S(1)} %get-tuple-element.96.refs_7_) | copy-start | bytes 3932164
  366.7 24.6 %copy-start.36 = (f32[256,640]{1,0:T(8,128)}, f32[256,640]{1,0:T(8,128)S(1)}, u32[]{:S(2)}) copy-start(f32[256,640]{1,0:T(8,128)S(1)} %get-tuple-element.95.refs_4_) | copy-start | bytes 1966084
  366.7 20.8 %collective-permute-start.1 = (bf16[8,1280,128]{2,1,0:T(8,128)(2,1)S(1)}, bf16[8,1280,128]{2,1,0:T(8,128)(2,1)S(1)}, u32[]{:S(2)}, u32[]{:S(2)}) collective-permute-start(bf16[8,1280,128]{2,1,0:T(8,128)(2,1)S(1)} %get-tuple-element.90), channel_id=1, source_target_pairs={{0,1},{1,0},{2,3},{3,2},{4,5},{5,4},{6,7},{7,6},{8,9},{9,8},{10,11... | collective-permute-start | bytes 7864328 | tf_op jit(solution)/shard_map/ppermute | solution.py:462
  391.4 44.3 %all-to-all-start.14 = ((bf16[8,32,2176]{2,1,0:T(8,128)(2,1)}), bf16[8,32,2176]{2,1,0:T(8,128)(2,1)}, u32[]{:S(2)}, u32[]{:S(2)}) async-start(bf16[8,32,2176]{2,1,0:T(8,128)(2,1)} %bitcast.38), calls=%async_computation.14 | async-start | bytes 2228224 | tf_op jit(solution)/shard_map/all_to_all | solution.py:31
  400.6 22.6 %collective-permute-start.2 = (bf16[1280,128]{1,0:T(8,128)(2,1)S(1)}, bf16[1280,128]{1,0:T(8,128)(2,1)S(1)}, u32[]{:S(2)}, u32[]{:S(2)}) collective-permute-start(bf16[1280,128]{1,0:T(8,128)(2,1)S(1)} %get-tuple-element.102), channel_id=1, source_target_pairs={{0,2},{1,3},{2,0},{3,1},{4,6},{5,7},{6,4},{7,5},{8,10},{9,11},{10,... | collective-permute-start | bytes 983048 | tf_op jit(solution)/shard_map/ppermute | solution.py:490
  401.9 31.4 %collective-permute-start.3 = (bf16[1280,128]{1,0:T(8,128)(2,1)S(1)}, bf16[1280,128]{1,0:T(8,128)(2,1)S(1)}, u32[]{:S(2)}, u32[]{:S(2)}) collective-permute-start(bf16[1280,128]{1,0:T(8,128)(2,1)S(1)} %get-tuple-element.103), channel_id=1, source_target_pairs={{0,4},{1,5},{2,6},{3,7},{4,8},{5,9},{6,10},{7,11},{8,12},{9,13},{1... | collective-permute-start | bytes 983048 | tf_op jit(solution)/shard_map/ppermute | solution.py:490
  401.9 49.9 %collective-permute-start.4 = (bf16[1280,128]{1,0:T(8,128)(2,1)}, bf16[1280,128]{1,0:T(8,128)(2,1)}, u32[]{:S(2)}, u32[]{:S(2)}) collective-permute-start(bf16[1280,128]{1,0:T(8,128)(2,1)} %get-tuple-element.104), channel_id=1, source_target_pairs={{0,6},{1,7},{2,4},{3,5},{4,10},{5,11},{6,8},{7,9},{8,14},{9,15},{1... | collective-permute-start | bytes 983048 | tf_op jit(solution)/shard_map/ppermute | solution.py:490
  401.9 49.9 %collective-permute-start.5 = (bf16[1280,128]{1,0:T(8,128)(2,1)}, bf16[1280,128]{1,0:T(8,128)(2,1)}, u32[]{:S(2)}, u32[]{:S(2)}) collective-permute-start(bf16[1280,128]{1,0:T(8,128)(2,1)} %get-tuple-element.105), channel_id=1, source_target_pairs={{0,8},{1,9},{2,10},{3,11},{4,12},{5,13},{6,14},{7,15},{8,0},{9,1},... | collective-permute-start | bytes 983048 | tf_op jit(solution)/shard_map/ppermute | solution.py:490
  407.0 44.8 %collective-permute-start.6 = (bf16[1280,128]{1,0:T(8,128)(2,1)}, bf16[1280,128]{1,0:T(8,128)(2,1)}, u32[]{:S(2)}, u32[]{:S(2)}) collective-permute-start(bf16[1280,128]{1,0:T(8,128)(2,1)} %get-tuple-element.106), channel_id=1, source_target_pairs={{0,10},{1,11},{2,8},{3,9},{4,14},{5,15},{6,12},{7,13},{8,2},{9,3},... | collective-permute-start | bytes 983048 | tf_op jit(solution)/shard_map/ppermute | solution.py:490
  423.9 28.0 %collective-permute-start.7 = (bf16[1280,128]{1,0:T(8,128)(2,1)}, bf16[1280,128]{1,0:T(8,128)(2,1)}, u32[]{:S(2)}, u32[]{:S(2)}) collective-permute-start(bf16[1280,128]{1,0:T(8,128)(2,1)} %get-tuple-element.107), channel_id=1, source_target_pairs={{0,12},{1,13},{2,14},{3,15},{4,0},{5,1},{6,2},{7,3},{8,4},{9,5},{1... | collective-permute-start | bytes 983048 | tf_op jit(solution)/shard_map/ppermute | solution.py:490
  434.1 17.8 %collective-permute-start.8 = (bf16[1280,128]{1,0:T(8,128)(2,1)}, bf16[1280,128]{1,0:T(8,128)(2,1)}, u32[]{:S(2)}, u32[]{:S(2)}) collective-permute-start(bf16[1280,128]{1,0:T(8,128)(2,1)} %get-tuple-element.108), channel_id=1, source_target_pairs={{0,14},{1,15},{2,12},{3,13},{4,2},{5,3},{6,0},{7,1},{8,6},{9,7},{1... | collective-permute-start | bytes 983048 | tf_op jit(solution)/shard_map/ppermute | solution.py:490
  451.9 13.0 %copy-start.45 = (bf16[1280,128]{1,0:T(8,128)(2,1)S(1)}, bf16[1280,128]{1,0:T(8,128)(2,1)}, u32[]{:S(2)}) copy-start(bf16[1280,128]{1,0:T(8,128)(2,1)} %copy-done.44) | copy-start | bytes 983044
  451.9 6.5 %collective-permute-start.9 = (bf16[8,1280,128]{2,1,0:T(8,128)(2,1)S(1)}, bf16[8,1280,128]{2,1,0:T(8,128)(2,1)S(1)}, u32[]{:S(2)}, u32[]{:S(2)}) collective-permute-start(bf16[8,1280,128]{2,1,0:T(8,128)(2,1)S(1)} %get-tuple-element.119), channel_id=1, source_target_pairs={{0,1},{1,0},{2,3},{3,2},{4,5},{5,4},{6,7},{7,6},{8,9},{9,8},{10,11... | collective-permute-start | bytes 7864328 | tf_op jit(solution)/shard_map/ppermute | solution.py:462
  460.5 42.6 %all-to-all-start.15 = ((bf16[8,1280,128]{2,1,0:T(8,128)(2,1)}), bf16[8,1280,128]{2,1,0:T(8,128)(2,1)}, u32[]{:S(2)}, u32[]{:S(2)}) async-start(bf16[8,1280,128]{2,1,0:T(8,128)(2,1)} %copy-done.10), calls=%async_computation.15 | async-start | bytes 5242880 | tf_op jit(solution)/shard_map/all_to_all | solution.py:695
  468.3 100.6 %copy-start.25 = (f32[1,320,512]{2,1,0:T(8,128)S(1)}, f32[1,320,512]{2,1,0:T(8,128)}, u32[]{:S(2)}) copy-start(f32[1,320,512]{2,1,0:T(8,128)} %param.10) | copy-start | bytes 1966084
  505.2 19.7 %copy-start.54 = (bf16[160,512]{1,0:T(8,128)(2,1)S(1)}, bf16[160,512]{1,0:T(8,128)(2,1)}, u32[]{:S(2)}) copy-start(bf16[160,512]{1,0:T(8,128)(2,1)} %copy-done.53) | copy-start | bytes 491524
  520.4 59.8 %all-to-all-start.17 = ((bf16[8,256,640]{2,1,0:T(8,128)(2,1)}), bf16[8,256,640]{2,1,0:T(8,128)(2,1)}, u32[]{:S(2)}, u32[]{:S(2)}) async-start(bf16[8,256,640]{2,1,0:T(8,128)(2,1)} %copy-done.20), calls=%async_computation.17 | async-start | bytes 5242880 | tf_op jit(solution)/shard_map/all_to_all | solution.py:31
  525.0 43.2 %collective-permute-start.10 = (bf16[160,512]{1,0:T(8,128)(2,1)S(1)}, bf16[160,512]{1,0:T(8,128)(2,1)S(1)}, u32[]{:S(2)}, u32[]{:S(2)}) collective-permute-start(bf16[160,512]{1,0:T(8,128)(2,1)S(1)} %get-tuple-element.140), channel_id=1, source_target_pairs={{0,0},{1,64},{2,1},{3,65},{4,16},{5,80},{6,17},{7,81},{8,32},{9,96... | collective-permute-start | bytes 491528 | tf_op jit(solution)/shard_map/ppermute | solution.py:505
  532.5 35.8 %collective-permute-start.11 = (bf16[160,512]{1,0:T(8,128)(2,1)S(1)}, bf16[160,512]{1,0:T(8,128)(2,1)S(1)}, u32[]{:S(2)}, u32[]{:S(2)}) collective-permute-start(bf16[160,512]{1,0:T(8,128)(2,1)S(1)} %get-tuple-element.139), channel_id=1, source_target_pairs={{0,64},{1,0},{2,65},{3,1},{4,80},{5,16},{6,81},{7,17},{8,96},{9,32... | collective-permute-start | bytes 491528 | tf_op jit(solution)/shard_map/ppermute | solution.py:505
  568.9 31.3 %copy-start.1 = (bf16[256,5120]{1,0:T(8,128)(2,1)S(1)}, bf16[256,5120]{1,0:T(8,128)(2,1)}, u32[]{:S(2)}) copy-start(bf16[256,5120]{1,0:T(8,128)(2,1)} %param.9) | copy-start | bytes 7864324
  580.2 19.0 %all-to-all-start.18 = ((bf16[16,2,32,320]{3,2,1,0:T(8,128)(2,1)}), bf16[16,2,32,320]{3,2,1,0:T(8,128)(2,1)S(1)}, u32[]{:S(2)}, u32[]{:S(2)}) async-start(bf16[16,2,32,320]{3,2,1,0:T(8,128)(2,1)} %copy-done.31), calls=%async_computation.18 | async-start | bytes 1572864 | tf_op jit(solution)/shard_map/all_to_all | solution.py:31
  (43 other events, 63.2 us)
Sparse Core Ops, SparseCore 0:
  10.3 63.0 all-gather.7
  75.7 48.2 all-gather.5
  128.9 41.7 all-gather.9
  172.8 44.1 all-gather.11
  219.2 81.1 all-gather.13

commit v8 on v7

--- a/solution.py
+++ b/solution.py
@@ -196,11 +196,14 @@
 
 def forward_kernel(first, last, width, inner, copies):
     def kernel(
-        down_ref, up_ref, gram_in_ref, gram_out_ref, acts_ref, hidden_ref, scale_ref, cross_ref
+        sums_ref, gram_in_ref, gram_out_ref, acts_ref, hidden_ref, scale_ref, cross_ref
     ):
         find = finder(first, last, inner, gram_in_ref, gram_out_ref, 0)
-        state, crosses = forward_chain(first, last, width, inner, down_ref, up_ref, 0, find)
-        rows = down_ref.shape[1]
+        up_start = (last - first) * inner + LANES
+        state, crosses = forward_chain(
+            first, last, width, inner, sums_ref, sums_ref, up_start, find
+        )
+        rows = sums_ref.shape[1]
         for s in range(first, last):
             hidden, scale, act = state[s]
             at = s - first
@@ -566,21 +569,23 @@
     (first, middle), (_, last) = BLOCKS
     count = middle - first
     wide = rows.astype(jnp.float32)
-    down = [dot(rows, weight_in[s], ROWS) for s in range(first, middle)]
-    down += split_scalars([jnp.sum(wide * wide, axis=1, keepdims=True)])
-    down = exchanged(down, n_pipe)
-    (down_low,) = products(True, BLOCKS[:1])
-    all_out, down, down_low = lax.optimization_barrier((all_out, down, down_low))
+    down_low, down_high = products(True, BLOCKS)
+    all_out, down_low = lax.optimization_barrier((all_out, down_low))
     weight_out = [all_out[:, s * chunk : (s + 1) * chunk] for s in range(n_pipe)]
     gram_in_low = over_dp(down_low)
     up_low, up_high = products(False, BLOCKS)
     gram_out_low = over_dp(up_low)
-    held_in, up_low = lax.optimization_barrier((all_in, up_low))
-    weight_in = [held_in[s * chunk : (s + 1) * chunk] for s in range(n_pipe)]
-    (down_high,) = products(True, BLOCKS[1:])
-    up = exchanged([dot(rows, weight_out[s], LAST) for s in range(first, middle - 1)], n_pipe)
-    gram_in_low, gram_out_low, up, columns = lax.optimization_barrier(
-        (gram_in_low, gram_out_low, up, jnp.concatenate([down_high, up_high], axis=1))
+    columns = [dot(rows, weight_in[s], ROWS) for s in range(first, middle)]
+    columns += split_scalars([jnp.sum(wide * wide, axis=1, keepdims=True)])
+    columns += [dot(rows, weight_out[s], LAST) for s in range(first, middle - 1)]
+    columns, up_low = lax.optimization_barrier((columns, up_low))
+    sums_low = exchanged(columns, n_pipe)
+    columns = [dot(seed, weight_out[s], LAST) for s in range(middle, last)]
+    columns, sums_low = lax.optimization_barrier((columns, sums_low))
+    grad_high = exchanged(columns, n_pipe)
+    columns = jnp.concatenate([down_high, up_high], axis=1)
+    gram_in_low, gram_out_low, sums_low, grad_high, columns = lax.optimization_barrier(
+        (gram_in_low, gram_out_low, sums_low, grad_high, columns)
     )
     gram_high = over_dp(columns)
 
@@ -593,12 +598,10 @@
             ((count, block, LANES), jnp.float32),
             ((kept, block, inner), jnp.float32),
         ],
-        down,
-        up,
+        sums_low,
         gram_in_low,
         gram_out_low,
     )
-    late, acts = lax.optimization_barrier((seed, acts))
     acts = swap(acts, "pipe")
     exact, columns = run(
         next_rows_kernel(first, middle, last, inner, chunk),
@@ -617,7 +620,6 @@
         },
     )
     sums = exchanged(columns, n_pipe)
-    grad_high = exchanged([dot(late, weight_out[s], LAST) for s in range(middle, last)], n_pipe)
 
     turned = run(
         turning_kernel(middle, last, width, inner, n_pipe),
@@ -637,7 +639,6 @@
     chips = jnp.arange(n_dp // 2)
     xs = n_dp // 4
     away = (chips // 2 - chip // 2 + xs) % xs * 2 + (chips % 2 + chip % 2) % 2
-    fixed = jnp.concatenate([chips, core[None]]).astype(jnp.int32)
     place = jnp.concatenate([away, core[None]]).astype(jnp.int32)
 
     grads_high, mine, other, upstream, columns = run(
@@ -681,7 +682,7 @@
             (packed_shape(count), jnp.bfloat16),
             ((tok_rows, chunk), jnp.float32),
         ],
-        fixed,
+        place,
         rows,
         packs,
         acts,
@@ -692,17 +693,13 @@
         smem=True,
     )
     mine, other, arrived_high = lax.optimization_barrier((mine, other, arrived_high))
-    arrived_low = lax.all_to_all(
-        added(mine, other_core(other, n_dp), 1)[0],
-        "dp",
-        0,
-        0,
-        tiled=True,
-        axis_index_groups=[list(range(c, n_dp, 2)) for c in range(2)],
-    )
+    blocks = added(mine, other_core(other, n_dp), mine.shape[0])
+    arrived_low = between_chips(blocks, n_dp)
+    input_grads = swap(grads, "pipe")
+    input_grads, arrived_low = lax.optimization_barrier((input_grads, arrived_low))
 
     ins, outs = [], []
-    for (low, high), arrived in zip(BLOCKS, ([arrived_low], arrived_high)):
+    for (low, high), arrived in zip(BLOCKS, (arrived_low, arrived_high)):
         share = (high - low) * chunk // n_dp
         sum_in, sum_out = run(
             unpack_kernel(inner, share, len(arrived)),
@@ -715,8 +712,6 @@
         ins.append(sum_in)
         outs.append(sum_out.reshape(high - low, -1, LANES))
     grad_out = swap(jnp.concatenate(outs, axis=0), "pipe")
-    grads, grad_out = lax.optimization_barrier((grads, grad_out))
-    input_grads = swap(grads, "pipe")
     grad_in = move_in(*ins, n_pipe, n_dp)
     is_high = (me >= middle).astype(jnp.int32).reshape(1)
 
@@ -738,7 +733,6 @@
         smem=True,
     )
     new_in, new_moment_in, new_second_in, new_out, new_moment_out, new_second_out = updated
-    pieces, input_grads = lax.optimization_barrier((pieces, input_grads))
     input_grads = columns_in_place(input_grads)[None]
     roll_in, roll_out = run(
         rollout_kernel(share_out, share_in),

time: 615 us -> 616 us (level)
  blocking collectives: 129 us -> 169 us
  waiting for transfers between devices: 207 us -> 188 us
  starting transfers between devices: 94.2 us -> 80.4 us
    ppermute x7 -> x14, waiting for transfers between devices: 16.2 us -> 63.8 us  [between_chips(): arrived.append(lax.ppermute(block, 'dp', pairs))]
    all_to_all x6 -> x8, blocking collectives: 129 us -> 169 us  [swap(): return lax.all_to_all(x, axis, 0, 0, tiled=True)]
    all_to_all x1 -> x0, waiting for transfers between devices: 34.9 us -> none  [on_device(): lax.all_to_all(added(mine, other_core(other, n_dp), 1)[0], 'dp', 0, 0, ti...]
    ppermute x2, waiting for transfers between devices: 35.7 us -> 10.9 us  [move_in(): moved.append(lax.ppermute(payload, ('pipe', 'dp'), pairs))]
    all_to_all x12 -> x7, starting transfers between devices: 60.5 us -> 47.2 us  [swap(): return lax.all_to_all(x, axis, 0, 0, tiled=True)]
    unnamed x123 -> x137, local copies, waits for them, and re-layouts: 54.4 us -> 62.3 us
    all_to_all x12 -> x7, waiting for transfers between devices: 82 us -> 75 us  [swap(): return lax.all_to_all(x, axis, 0, 0, tiled=True)]
    ppermute x7 -> x14, starting transfers between devices: 17.4 us -> 22.6 us  [between_chips(): arrived.append(lax.ppermute(block, 'dp', pairs))]
  transfers between devices with their start and end apart: 30 -> 31, of which waited for: 17 -> 12; matrix products, arithmetic and copies ran while one was open for 10% -> 8% of each run, Pallas kernels for 5% -> 5%
where the time goes in v8:
time: 616 us; the launch traced here: 613 us
  waiting for transfers between devices  188 us (31%)
  blocking collectives  169 us (27%)
  starting transfers between devices  80.4 us (13%)
  local copies, waits for them, and re-layouts  67.3 us (11%)
  Pallas kernels  48.8 us (8%)
  matrix products  37.6 us (6%)
  between operations  14.4 us (2%)
  other arithmetic  7.39 us (1%)
    all_to_all x8, blocking collectives, swap(): return lax.all_to_all(x, axis, 0, 0, tiled=True)  169 us
    all_to_all x7, waiting for transfers between devices, swap(): return lax.all_to_all(x, axis, 0, 0, tiled=True)  75 us
    ppermute x14, waiting for transfers between devices, between_chips(): arrived.append(lax.ppermute(block, 'dp', pairs))  63.8 us
    unnamed x137, local copies, waits for them, and re-layouts  62.3 us
    all_to_all x7, starting transfers between devices, swap(): return lax.all_to_all(x, axis, 0, 0, tiled=True)  47.2 us
    pallas_call x14, Pallas kernels, run(): pl.pallas_call(kernel, out_shape=[jax.ShapeDtypeStruct(shape, kind) for s...  42.9 us
    dot_general x23, matrix products, dot(): lax.dot_general(left, right, (dims, ((), ())), preferred_element_type=jnp...  37.6 us
    all_gather x1, waiting for transfers between devices, on_device(): all_in = lax.all_gather(piece_in, 'dp', axis=0, tiled=True)  23.7 us
  transfers between devices with their start and end apart: 31, of which 12 were waited for; matrix products, arithmetic and copies ran while one was open for 8% of the time, Pallas kernels for 5%

profile of v8, /device:TPU:1, one launch (start us, length us, event | category | flops | bytes accessed | tf_op | source)
XLA Modules:
  0.0 612.6 jit_solution(16127316971258227081)
XLA Ops:
  11.2 37.5 %all_to_all.119 = bf16[8,32,640]{2,1,0:T(8,128)(2,1)S(1)} all-to-all(bf16[8,32,640]{2,1,0:T(8,128)(2,1)S(1)} %copy.30), channel_id=1, replica_groups=mesh['pipe'=8,'dp'=16] {'pipe'}, dimensions={0} | all-to-all | bytes 655360 | tf_op jit(solution)/shard_map/all_to_all | solution.py:31
  49.7 23.7 %all-gather.8.cloned.1.call-done.in_ref.refs_5_ = bf16[5120,512]{1,0:T(8,128)(2,1)} async-done(((bf16[320,512]{1,0:T(8,128)(2,1)}), bf16[5120,512]{1,0:T(8,128)(2,1)}) %all-gather.8.cloned.1.call-update) | async-done | bytes 5242896 | tf_op jit(solution)/shard_map/all_gather | solution.py:536
  81.4 15.2 %all_to_all.120 = bf16[8,48,512]{2,1,0:T(8,128)(2,1)S(1)} all-to-all(bf16[8,48,512]{2,1,0:T(8,128)(2,1)S(1)} %bitcast.123), channel_id=1, replica_groups=mesh['pipe'=8,'dp'=16] {'pipe'}, dimensions={0} | all-to-all | bytes 786432 | tf_op jit(solution)/shard_map/all_to_all | solution.py:31
  96.7 13.1 %all_to_all.121 = bf16[8,48,512]{2,1,0:T(8,128)(2,1)S(1)} all-to-all(bf16[8,48,512]{2,1,0:T(8,128)(2,1)S(1)} %tile.4), channel_id=1, replica_groups=mesh['pipe'=8,'dp'=16] {'pipe'}, dimensions={0} | all-to-all | bytes 786432 | tf_op jit(solution)/shard_map/all_to_all | solution.py:31
  110.5 12.6 %all-gather.6.cloned.1.call-done.out_ref.refs_6_ = bf16[512,5120]{1,0:T(8,128)(2,1)} async-done(((bf16[32,5120]{1,0:T(8,128)(2,1)}), bf16[512,5120]{1,0:T(8,128)(2,1)}) %all-gather.6.cloned.1.call-update) | async-done | bytes 5242896 | tf_op jit(solution)/shard_map/all_gather | solution.py:537
  131.6 15.3 %all_to_all.122 = bf16[8,48,512]{2,1,0:T(8,128)(2,1)S(1)} all-to-all(bf16[8,48,512]{2,1,0:T(8,128)(2,1)S(1)} %bitcast.122), channel_id=1, replica_groups=mesh['pipe'=8,'dp'=16] {'pipe'}, dimensions={0} | all-to-all | bytes 786432 | tf_op jit(solution)/shard_map/all_to_all | solution.py:31
  147.0 12.7 %all_to_all.123 = bf16[8,48,512]{2,1,0:T(8,128)(2,1)S(1)} all-to-all(bf16[8,48,512]{2,1,0:T(8,128)(2,1)S(1)} %tile.5), channel_id=1, replica_groups=mesh['pipe'=8,'dp'=16] {'pipe'}, dimensions={0} | all-to-all | bytes 786432 | tf_op jit(solution)/shard_map/all_to_all | solution.py:31
  162.2 2.2 fusion.18
  166.6 2.2 fusion.28
  170.9 2.2 fusion.43
  173.1 2.2 fusion.46
  175.3 2.2 fusion.49
  177.8 3.8 concatenate.24
  181.5 4.9 all-to-all-start.5
  192.5 21.6 %all-to-all-done.5.sums_ref = bf16[8,32,3712]{2,1,0:T(8,128)(2,1)} async-done(((bf16[8,32,3712]{2,1,0:T(8,128)(2,1)}), bf16[8,32,3712]{2,1,0:T(8,128)(2,1)}, u32[]{:S(2)}, u32[]{:S(2)}) %all-to-all-start.5) | async-done | bytes 1900576 | tf_op jit(solution)/shard_map/all_to_all | solution.py:31
  215.3 5.8 all-to-all-start.6
  221.9 14.8 %all-to-all-done.6.grad_ref = bf16[8,32,2048]{2,1,0:T(8,128)(2,1)S(1)} async-done(((bf16[8,32,2048]{2,1,0:T(8,128)(2,1)}), bf16[8,32,2048]{2,1,0:T(8,128)(2,1)S(1)}, u32[]{:S(2)}, u32[]{:S(2)}) %all-to-all-start.6) | async-done | bytes 1048608 | tf_op jit(solution)/shard_map/all_to_all | solution.py:31
  241.5 3.5 shard_map.153
  245.0 21.5 %all_to_all.124 = bf16[8,32,2048]{2,1,0:T(8,128)(2,1)S(1)} all-to-all(bf16[8,32,2048]{2,1,0:T(8,128)(2,1)S(1)} %bitcast.109), channel_id=1, replica_groups=mesh['pipe'=8,'dp'=16] {'pipe'}, dimensions={0} | all-to-all | bytes 2097152 | tf_op jit(solution)/shard_map/all_to_all | solution.py:31
  266.5 3.0 copy-done.2
  269.4 2.6 copy-done.5
  272.0 2.4 shard_map.154
  274.5 33.6 %all_to_all.125.sums_ref = bf16[8,32,3712]{2,1,0:T(8,128)(2,1)} all-to-all(bf16[8,32,3712]{2,1,0:T(8,128)(2,1)S(1)} %bitcast.105), channel_id=1, replica_groups=mesh['pipe'=8,'dp'=16] {'pipe'}, dimensions={0} | all-to-all | bytes 3801088 | tf_op jit(solution)/shard_map/all_to_all | solution.py:31
  311.5 2.8 copy-done.14
  315.5 3.2 shard_map.155
  320.1 6.3 %all-to-all-start.9 = ((bf16[8,32,4224]{2,1,0:T(8,128)(2,1)}), bf16[8,32,4224]{2,1,0:T(8,128)(2,1)S(1)}, u32[]{:S(2)}, u32[]{:S(2)}) async-start(bf16[8,32,4224]{2,1,0:T(8,128)(2,1)} %bitcast.102), calls=%async_computation.9 | async-start | bytes 4325376 | tf_op jit(solution)/shard_map/all_to_all | solution.py:31
  326.5 31.8 %all-to-all-done.9 = bf16[8,32,4224]{2,1,0:T(8,128)(2,1)S(1)} async-done(((bf16[8,32,4224]{2,1,0:T(8,128)(2,1)}), bf16[8,32,4224]{2,1,0:T(8,128)(2,1)S(1)}, u32[]{:S(2)}, u32[]{:S(2)}) %all-to-all-start.9) | async-done | bytes 2162720 | tf_op jit(solution)/shard_map/all_to_all | solution.py:31
  359.6 2.5 copy-done.3
  364.8 8.2 %shard_map.156 = (bf16[4,256,640]{2,1,0:T(8,128)(2,1)S(1)}, bf16[8,1280,128]{2,1,0:T(8,128)(2,1)S(1)}, bf16[8,1280,128]{2,1,0:T(8,128)(2,1)S(1)}, f32[256,640]{1,0:T(8,128)S(1)}, bf16[256,2048]{1,0:T(8,128)(2,1)S(1)}) custom-call(s32[9]{0:T(128)S(1)} %pad_add_fusion.refs_0_, f32[256,640]{1,0:T(8,128)S(1)} %copy-done.32, bf16[256,4224]{1,0:T(8,128)(2,1)S(1)} %bitcast.98, ...), custom_call_target="tpu_custom_call" | custom-call | tf_op jit(solution)/shard_map/pallas_call | solution.py:71
  376.7 19.8 %all_to_all.126.grad_ref = bf16[8,32,2048]{2,1,0:T(8,128)(2,1)S(1)} all-to-all(bf16[8,32,2048]{2,1,0:T(8,128)(2,1)S(1)} %bitcast.108), channel_id=1, replica_groups=mesh['pipe'=8,'dp'=16] {'pipe'}, dimensions={0} | all-to-all | bytes 2097152 | tf_op jit(solution)/shard_map/all_to_all | solution.py:31
  398.0 2.3 shard_map.157
  400.3 4.2 all-to-all-start.11
  411.5 3.8 collective-permute-start.5
  415.3 15.3 %collective-permute-done.2.refs_1_ = bf16[1280,128]{1,0:T(8,128)(2,1)S(1)} collective-permute-done((bf16[1280,128]{1,0:T(8,128)(2,1)S(1)}, bf16[1280,128]{1,0:T(8,128)(2,1)S(1)}, u32[]{:S(2)}, u32[]{:S(2)}) %collective-permute-start.2) | collective-permute-done | bytes 327712 | tf_op jit(solution)/shard_map/ppermute | solution.py:493
  431.3 9.5 %collective-permute-start.7 = (bf16[1280,128]{1,0:T(8,128)(2,1)}, bf16[1280,128]{1,0:T(8,128)(2,1)}, u32[]{:S(2)}, u32[]{:S(2)}) collective-permute-start(bf16[1280,128]{1,0:T(8,128)(2,1)} %get-tuple-element.149), channel_id=1, source_target_pairs={{0,12},{1,13},{2,14},{3,15},{4,0},{5,1},{6,2},{7,3},{8,4},{9,5},{1... | collective-permute-start | bytes 983048 | tf_op jit(solution)/shard_map/ppermute | solution.py:493
  442.8 2.5 copy-done.4
  448.9 10.1 %shard_map.158 = (bf16[8,256,640]{2,1,0:T(8,128)(2,1)}, bf16[8,1280,128]{2,1,0:T(8,128)(2,1)S(1)}, bf16[8,1280,128]{2,1,0:T(8,128)(2,1)}, f32[256,640]{1,0:T(8,128)}) custom-call(s32[9]{0:T(128)S(1)} %pad_add_fusion.refs_0_, bf16[256,640]{1,0:T(8,128)(2,1)S(1)} %get-tuple-element.192.rows_ref.refs_1_, bf16[256,2176]{1,0:T(8,128)(2,1)} %bitcast.30.refs_2_, ...), custom_call_target="tpu_custom_call" | custom-call | tf_op jit(solution)/shard_map/pallas_call | solution.py:71
  462.6 6.5 %all-to-all-start.12 = ((bf16[8,256,640]{2,1,0:T(8,128)(2,1)}), bf16[8,256,640]{2,1,0:T(8,128)(2,1)}, u32[]{:S(2)}, u32[]{:S(2)}) async-start(bf16[8,256,640]{2,1,0:T(8,128)(2,1)} %get-tuple-element.138), calls=%async_computation.12 | async-start | bytes 5242880 | tf_op jit(solution)/shard_map/all_to_all | solution.py:31
  469.1 3.0 shard_map.160
  478.8 39.7 %collective-permute-done.10.refs_1_ = bf16[1280,128]{1,0:T(8,128)(2,1)S(1)} collective-permute-done((bf16[1280,128]{1,0:T(8,128)(2,1)S(1)}, bf16[1280,128]{1,0:T(8,128)(2,1)S(1)}, u32[]{:S(2)}, u32[]{:S(2)}) %collective-permute-start.10) | collective-permute-done | bytes 327712 | tf_op jit(solution)/shard_map/ppermute | solution.py:493
  527.6 8.3 %collective-permute-done.16.refs_7_ = bf16[1280,128]{1,0:T(8,128)(2,1)} collective-permute-done((bf16[1280,128]{1,0:T(8,128)(2,1)}, bf16[1280,128]{1,0:T(8,128)(2,1)}, u32[]{:S(2)}, u32[]{:S(2)}) %collective-permute-start.16) | collective-permute-done | bytes 327712 | tf_op jit(solution)/shard_map/ppermute | solution.py:493
  541.9 9.0 %all-to-all-start.13 = ((bf16[8,160,128]{2,1,0:T(8,128)(2,1)}), bf16[8,160,128]{2,1,0:T(8,128)(2,1)S(1)}, u32[]{:S(2)}, u32[]{:S(2)}) async-start(bf16[8,160,128]{2,1,0:T(8,128)(2,1)} %pad_maximum_fusion.2), calls=%async_computation.13 | async-start | bytes 655360 | tf_op jit(solution)/shard_map/all_to_all | solution.py:31
  551.9 6.3 %collective-permute-start.17 = (bf16[160,512]{1,0:T(8,128)(2,1)S(1)}, bf16[160,512]{1,0:T(8,128)(2,1)S(1)}, u32[]{:S(2)}, u32[]{:S(2)}) collective-permute-start(bf16[160,512]{1,0:T(8,128)(2,1)S(1)} %get-tuple-element.194), channel_id=1, source_target_pairs={{0,0},{1,64},{2,1},{3,65},{4,16},{5,80},{6,17},{7,81},{8,32},{9,96... | collective-permute-start | bytes 491528 | tf_op jit(solution)/shard_map/ppermute | solution.py:508
  558.4 10.9 %collective-permute-done.17.refs_1_ = bf16[160,512]{1,0:T(8,128)(2,1)S(1)} collective-permute-done((bf16[160,512]{1,0:T(8,128)(2,1)S(1)}, bf16[160,512]{1,0:T(8,128)(2,1)S(1)}, u32[]{:S(2)}, u32[]{:S(2)}) %collective-permute-start.17) | collective-permute-done | bytes 163872 | tf_op jit(solution)/shard_map/ppermute | solution.py:508
  578.2 2.9 shard_map.164
  582.0 10.4 %all-to-all-start.14 = ((bf16[16,2,32,320]{3,2,1,0:T(8,128)(2,1)}), bf16[16,2,32,320]{3,2,1,0:T(8,128)(2,1)S(1)}, u32[]{:S(2)}, u32[]{:S(2)}) async-start(bf16[16,2,32,320]{3,2,1,0:T(8,128)(2,1)} %copy-done.30), calls=%async_computation.14 | async-start | bytes 1572864 | tf_op jit(solution)/shard_map/all_to_all | solution.py:31
  592.4 5.9 shard_map.161
  598.3 6.8 %all-to-all-done.14.pieces_ref = bf16[16,2,32,320]{3,2,1,0:T(8,128)(2,1)S(1)} async-done(((bf16[16,2,32,320]{3,2,1,0:T(8,128)(2,1)}), bf16[16,2,32,320]{3,2,1,0:T(8,128)(2,1)S(1)}, u32[]{:S(2)}, u32[]{:S(2)}) %all-to-all-start.14) | async-done | bytes 655392 | tf_op jit(solution)/shard_map/all_to_all | solution.py:31
  (226 shorter events, 107.7 us)
Async XLA Ops:
  7.2 179.2 %copy-start = (bf16[256,5120]{1,0:T(8,128)(2,1)S(1)}, bf16[256,5120]{1,0:T(8,128)(2,1)}, u32[]{:S(2)}) copy-start(bf16[256,5120]{1,0:T(8,128)(2,1)} %param.9) | copy-start | bytes 7864324
  7.2 66.3 %all-gather.8.cloned.1.call-start = ((), (), s32[]{:S(2)}) async-start(), calls=%async_computation.16 | async-start | bytes 5570560 | tf_op jit(solution)/shard_map/all_gather | solution.py:536
  8.5 0.7 collective-permute-start
  10.0 113.1 %all-gather.6.cloned.1.call-start = ((), (), s32[]{:S(2)}) async-start(), calls=%async_computation.15 | async-start | bytes 5570560 | tf_op jit(solution)/shard_map/all_gather | solution.py:537
  49.6 188.1 %all-gather.10.cloned.1.call-start = ((), (), s32[]{:S(2)}) async-start(), calls=%async_computation.17 | async-start | bytes 3342336 | tf_op jit(solution)/shard_map/all_gather | solution.py:564
  49.6 31.8 %copy-start.67 = (bf16[2,32,640]{2,1,0:T(8,128)(2,1)}, bf16[2,32,640]{2,1,0:T(8,128)(2,1)S(1)}, u32[]{:S(2)}) copy-start(bf16[2,32,640]{2,1,0:T(8,128)(2,1)S(1)} %get-tuple-element.198) | copy-start | bytes 245764
  49.7 31.7 %copy-start.64 = (bf16[3,32,640]{2,1,0:T(8,128)(2,1)}, bf16[3,32,640]{2,1,0:T(8,128)(2,1)S(1)}, u32[]{:S(2)}) copy-start(bf16[3,32,640]{2,1,0:T(8,128)(2,1)S(1)} %get-tuple-element.195) | copy-start | bytes 368644
  49.7 31.7 %copy-start.66 = (bf16[3,32,640]{2,1,0:T(8,128)(2,1)}, bf16[3,32,640]{2,1,0:T(8,128)(2,1)S(1)}, u32[]{:S(2)}) copy-start(bf16[3,32,640]{2,1,0:T(8,128)(2,1)S(1)} %get-tuple-element.196) | copy-start | bytes 368644
  96.6 33.5 %copy-start.65 = (bf16[3,32,640]{2,1,0:T(8,128)(2,1)S(1)}, bf16[3,32,640]{2,1,0:T(8,128)(2,1)}, u32[]{:S(2)}) copy-start(bf16[3,32,640]{2,1,0:T(8,128)(2,1)} %copy-done.64) | copy-start | bytes 368644
  123.1 114.6 %all-gather.12.cloned.1.call-start = ((), (), s32[]{:S(2)}) async-start(), calls=%async_computation.18 | async-start | bytes 3342336 | tf_op jit(solution)/shard_map/all_gather | solution.py:564
  181.5 32.6 %all-to-all-start.5 = ((bf16[8,32,3712]{2,1,0:T(8,128)(2,1)}), bf16[8,32,3712]{2,1,0:T(8,128)(2,1)}, u32[]{:S(2)}, u32[]{:S(2)}) async-start(bf16[8,32,3712]{2,1,0:T(8,128)(2,1)} %bitcast.116), calls=%async_computation.5 | async-start | bytes 3801088 | tf_op jit(solution)/shard_map/all_to_all | solution.py:31
  186.5 34.7 %copy-start.56 = (bf16[32,3072]{1,0:T(8,128)(2,1)S(1)}, bf16[32,3072]{1,0:T(8,128)(2,1)}, u32[]{:S(2)}) copy-start(bf16[32,3072]{1,0:T(8,128)(2,1)} %copy-done.55) | copy-start | bytes 589828
  215.3 21.4 %all-to-all-start.6 = ((bf16[8,32,2048]{2,1,0:T(8,128)(2,1)}), bf16[8,32,2048]{2,1,0:T(8,128)(2,1)S(1)}, u32[]{:S(2)}, u32[]{:S(2)}) async-start(bf16[8,32,2048]{2,1,0:T(8,128)(2,1)} %bitcast.22), calls=%async_computation.6 | async-start | bytes 2097152 | tf_op jit(solution)/shard_map/all_to_all | solution.py:31
  221.1 88.9 %all-gather.14.cloned.1.call-start = ((), (), s32[]{:S(2)}) async-start(), calls=%async_computation.19 | async-start | bytes 6684672 | tf_op jit(solution)/shard_map/all_gather | solution.py:564
  245.0 21.5 %copy-start.39 = (f32[6,32,512]{2,1,0:T(8,128)}, f32[6,32,512]{2,1,0:T(8,128)S(1)}, u32[]{:S(2)}) copy-start(f32[6,32,512]{2,1,0:T(8,128)S(1)} %get-tuple-element.135.cross_ref) | copy-start | bytes 1179652
  245.0 21.5 %copy-start.61 = (f32[4,32,128]{2,1,0:T(8,128)}, f32[4,32,128]{2,1,0:T(8,128)S(1)}, u32[]{:S(2)}) copy-start(f32[4,32,128]{2,1,0:T(8,128)S(1)} %get-tuple-element.134.scale_ref) | copy-start | bytes 196612
  266.5 8.0 %copy-start.10 = (bf16[8,32,2048]{2,1,0:T(8,128)(2,1)}, bf16[8,32,2048]{2,1,0:T(8,128)(2,1)S(1)}, u32[]{:S(2)}) copy-start(bf16[8,32,2048]{2,1,0:T(8,128)(2,1)S(1)} %all_to_all.124) | copy-start | bytes 3145732
  274.4 33.6 %copy-start.31 = (f32[256,640]{1,0:T(8,128)}, f32[256,640]{1,0:T(8,128)S(1)}, u32[]{:S(2)}) copy-start(f32[256,640]{1,0:T(8,128)S(1)} %get-tuple-element.125.refs_1_) | copy-start | bytes 1966084
  320.1 38.2 %all-to-all-start.9 = ((bf16[8,32,4224]{2,1,0:T(8,128)(2,1)}), bf16[8,32,4224]{2,1,0:T(8,128)(2,1)S(1)}, u32[]{:S(2)}, u32[]{:S(2)}) async-start(bf16[8,32,4224]{2,1,0:T(8,128)(2,1)} %bitcast.102), calls=%async_computation.9 | async-start | bytes 4325376 | tf_op jit(solution)/shard_map/all_to_all | solution.py:31
  364.8 33.2 %copy-start.9 = (bf16[512,3072]{1,0:T(8,128)(2,1)S(1)}, bf16[512,3072]{1,0:T(8,128)(2,1)}, u32[]{:S(2)}) copy-start(bf16[512,3072]{1,0:T(8,128)(2,1)} %all-gather.10.cloned.1.call-done.gram_in_ref.gram_ref) | copy-start | bytes 9437188
  364.8 33.2 %copy-start.40 = (f32[6,32,512]{2,1,0:T(8,128)S(1)}, f32[6,32,512]{2,1,0:T(8,128)}, u32[]{:S(2)}) copy-start(f32[6,32,512]{2,1,0:T(8,128)} %copy-done.39) | copy-start | bytes 1179652
  364.8 33.2 %copy-start.62 = (f32[4,32,128]{2,1,0:T(8,128)S(1)}, f32[4,32,128]{2,1,0:T(8,128)}, u32[]{:S(2)}) copy-start(f32[4,32,128]{2,1,0:T(8,128)} %copy-done.61) | copy-start | bytes 196612
  375.3 25.0 %copy-start.28 = (bf16[4,256,640]{2,1,0:T(8,128)(2,1)}, bf16[4,256,640]{2,1,0:T(8,128)(2,1)S(1)}, u32[]{:S(2)}) copy-start(bf16[4,256,640]{2,1,0:T(8,128)(2,1)S(1)} %get-tuple-element.137.refs_7_) | copy-start | bytes 3932164
  375.3 21.2 %collective-permute-start.1 = (bf16[8,1280,128]{2,1,0:T(8,128)(2,1)S(1)}, bf16[8,1280,128]{2,1,0:T(8,128)(2,1)S(1)}, u32[]{:S(2)}, u32[]{:S(2)}) collective-permute-start(bf16[8,1280,128]{2,1,0:T(8,128)(2,1)S(1)} %get-tuple-element.131), channel_id=1, source_target_pairs={{0,1},{1,0},{2,3},{3,2},{4,5},{5,4},{6,7},{7,6},{8,9},{9,8},{10,11... | collective-permute-start | bytes 7864328 | tf_op jit(solution)/shard_map/ppermute | solution.py:465
  400.3 42.5 %all-to-all-start.11 = ((bf16[8,32,2176]{2,1,0:T(8,128)(2,1)}), bf16[8,32,2176]{2,1,0:T(8,128)(2,1)}, u32[]{:S(2)}, u32[]{:S(2)}) async-start(bf16[8,32,2176]{2,1,0:T(8,128)(2,1)} %bitcast.29), calls=%async_computation.11 | async-start | bytes 2228224 | tf_op jit(solution)/shard_map/all_to_all | solution.py:31
  410.3 20.3 %collective-permute-start.2 = (bf16[1280,128]{1,0:T(8,128)(2,1)S(1)}, bf16[1280,128]{1,0:T(8,128)(2,1)S(1)}, u32[]{:S(2)}, u32[]{:S(2)}) collective-permute-start(bf16[1280,128]{1,0:T(8,128)(2,1)S(1)} %get-tuple-element.144), channel_id=1, source_target_pairs={{0,2},{1,3},{2,0},{3,1},{4,6},{5,7},{6,4},{7,5},{8,10},{9,11},{10,... | collective-permute-start | bytes 983048 | tf_op jit(solution)/shard_map/ppermute | solution.py:493
  410.3 30.6 %collective-permute-start.3 = (bf16[1280,128]{1,0:T(8,128)(2,1)S(1)}, bf16[1280,128]{1,0:T(8,128)(2,1)S(1)}, u32[]{:S(2)}, u32[]{:S(2)}) collective-permute-start(bf16[1280,128]{1,0:T(8,128)(2,1)S(1)} %get-tuple-element.145), channel_id=1, source_target_pairs={{0,4},{1,5},{2,6},{3,7},{4,8},{5,9},{6,10},{7,11},{8,12},{9,13},{1... | collective-permute-start | bytes 983048 | tf_op jit(solution)/shard_map/ppermute | solution.py:493
  410.3 50.3 %collective-permute-start.4 = (bf16[1280,128]{1,0:T(8,128)(2,1)}, bf16[1280,128]{1,0:T(8,128)(2,1)S(1)}, u32[]{:S(2)}, u32[]{:S(2)}) collective-permute-start(bf16[1280,128]{1,0:T(8,128)(2,1)} %get-tuple-element.146), channel_id=1, source_target_pairs={{0,6},{1,7},{2,4},{3,5},{4,10},{5,11},{6,8},{7,9},{8,14},{9,15},{1... | collective-permute-start | bytes 983048 | tf_op jit(solution)/shard_map/ppermute | solution.py:493
  411.5 49.1 %collective-permute-start.5 = (bf16[1280,128]{1,0:T(8,128)(2,1)}, bf16[1280,128]{1,0:T(8,128)(2,1)}, u32[]{:S(2)}, u32[]{:S(2)}) collective-permute-start(bf16[1280,128]{1,0:T(8,128)(2,1)} %get-tuple-element.147), channel_id=1, source_target_pairs={{0,8},{1,9},{2,10},{3,11},{4,12},{5,13},{6,14},{7,15},{8,0},{9,1},... | collective-permute-start | bytes 983048 | tf_op jit(solution)/shard_map/ppermute | solution.py:493
  415.3 45.3 %collective-permute-start.6 = (bf16[1280,128]{1,0:T(8,128)(2,1)}, bf16[1280,128]{1,0:T(8,128)(2,1)}, u32[]{:S(2)}, u32[]{:S(2)}) collective-permute-start(bf16[1280,128]{1,0:T(8,128)(2,1)} %get-tuple-element.148), channel_id=1, source_target_pairs={{0,10},{1,11},{2,8},{3,9},{4,14},{5,15},{6,12},{7,13},{8,2},{9,3},... | collective-permute-start | bytes 983048 | tf_op jit(solution)/shard_map/ppermute | solution.py:493
  431.3 29.2 %collective-permute-start.7 = (bf16[1280,128]{1,0:T(8,128)(2,1)}, bf16[1280,128]{1,0:T(8,128)(2,1)}, u32[]{:S(2)}, u32[]{:S(2)}) collective-permute-start(bf16[1280,128]{1,0:T(8,128)(2,1)} %get-tuple-element.149), channel_id=1, source_target_pairs={{0,12},{1,13},{2,14},{3,15},{4,0},{5,1},{6,2},{7,3},{8,4},{9,5},{1... | collective-permute-start | bytes 983048 | tf_op jit(solution)/shard_map/ppermute | solution.py:493
  441.6 19.0 %collective-permute-start.8 = (bf16[1280,128]{1,0:T(8,128)(2,1)}, bf16[1280,128]{1,0:T(8,128)(2,1)}, u32[]{:S(2)}, u32[]{:S(2)}) collective-permute-start(bf16[1280,128]{1,0:T(8,128)(2,1)} %get-tuple-element.150), channel_id=1, source_target_pairs={{0,14},{1,15},{2,12},{3,13},{4,2},{5,3},{6,0},{7,1},{8,6},{9,7},{1... | collective-permute-start | bytes 983048 | tf_op jit(solution)/shard_map/ppermute | solution.py:493
  460.6 8.5 %copy-start.19 = (bf16[8,1280,128]{2,1,0:T(8,128)(2,1)S(1)}, bf16[8,1280,128]{2,1,0:T(8,128)(2,1)}, u32[]{:S(2)}) copy-start(bf16[8,1280,128]{2,1,0:T(8,128)(2,1)} %copy-done.18) | copy-start | bytes 7864324
  460.6 8.5 %collective-permute-start.9 = (bf16[8,1280,128]{2,1,0:T(8,128)(2,1)}, bf16[8,1280,128]{2,1,0:T(8,128)(2,1)}, u32[]{:S(2)}, u32[]{:S(2)}) collective-permute-start(bf16[8,1280,128]{2,1,0:T(8,128)(2,1)} %get-tuple-element.152), channel_id=1, source_target_pairs={{0,1},{1,0},{2,3},{3,2},{4,5},{5,4},{6,7},{7,6},{8,9},{9,8},{10,11... | collective-permute-start | bytes 7864328 | tf_op jit(solution)/shard_map/ppermute | solution.py:465
  462.6 64.5 %all-to-all-start.12 = ((bf16[8,256,640]{2,1,0:T(8,128)(2,1)}), bf16[8,256,640]{2,1,0:T(8,128)(2,1)}, u32[]{:S(2)}, u32[]{:S(2)}) async-start(bf16[8,256,640]{2,1,0:T(8,128)(2,1)} %get-tuple-element.138), calls=%async_computation.12 | async-start | bytes 5242880 | tf_op jit(solution)/shard_map/all_to_all | solution.py:31
  469.1 101.6 %copy-start.24 = (f32[1,320,512]{2,1,0:T(8,128)S(1)}, f32[1,320,512]{2,1,0:T(8,128)}, u32[]{:S(2)}) copy-start(f32[1,320,512]{2,1,0:T(8,128)} %param.10) | copy-start | bytes 1966084
  472.9 45.6 %collective-permute-start.10 = (bf16[1280,128]{1,0:T(8,128)(2,1)S(1)}, bf16[1280,128]{1,0:T(8,128)(2,1)S(1)}, u32[]{:S(2)}, u32[]{:S(2)}) collective-permute-start(bf16[1280,128]{1,0:T(8,128)(2,1)S(1)} %get-tuple-element.154), channel_id=1, source_target_pairs={{0,2},{1,3},{2,0},{3,1},{4,6},{5,7},{6,4},{7,5},{8,10},{9,11},{10,... | collective-permute-start | bytes 983048 | tf_op jit(solution)/shard_map/ppermute | solution.py:493
  472.9 46.3 %collective-permute-start.11 = (bf16[1280,128]{1,0:T(8,128)(2,1)S(1)}, bf16[1280,128]{1,0:T(8,128)(2,1)S(1)}, u32[]{:S(2)}, u32[]{:S(2)}) collective-permute-start(bf16[1280,128]{1,0:T(8,128)(2,1)S(1)} %get-tuple-element.155), channel_id=1, source_target_pairs={{0,4},{1,5},{2,6},{3,7},{4,8},{5,9},{6,10},{7,11},{8,12},{9,13},{1... | collective-permute-start | bytes 983048 | tf_op jit(solution)/shard_map/ppermute | solution.py:493
  474.6 52.4 %collective-permute-start.12 = (bf16[1280,128]{1,0:T(8,128)(2,1)}, bf16[1280,128]{1,0:T(8,128)(2,1)}, u32[]{:S(2)}, u32[]{:S(2)}) collective-permute-start(bf16[1280,128]{1,0:T(8,128)(2,1)} %get-tuple-element.156), channel_id=1, source_target_pairs={{0,6},{1,7},{2,4},{3,5},{4,10},{5,11},{6,8},{7,9},{8,14},{9,15},{1... | collective-permute-start | bytes 983048 | tf_op jit(solution)/shard_map/ppermute | solution.py:493
  475.8 51.2 %collective-permute-start.13 = (bf16[1280,128]{1,0:T(8,128)(2,1)}, bf16[1280,128]{1,0:T(8,128)(2,1)}, u32[]{:S(2)}, u32[]{:S(2)}) collective-permute-start(bf16[1280,128]{1,0:T(8,128)(2,1)} %get-tuple-element.157), channel_id=1, source_target_pairs={{0,8},{1,9},{2,10},{3,11},{4,12},{5,13},{6,14},{7,15},{8,0},{9,1},... | collective-permute-start | bytes 983048 | tf_op jit(solution)/shard_map/ppermute | solution.py:493
  477.9 49.1 %collective-permute-start.14 = (bf16[1280,128]{1,0:T(8,128)(2,1)}, bf16[1280,128]{1,0:T(8,128)(2,1)}, u32[]{:S(2)}, u32[]{:S(2)}) collective-permute-start(bf16[1280,128]{1,0:T(8,128)(2,1)} %get-tuple-element.158), channel_id=1, source_target_pairs={{0,10},{1,11},{2,8},{3,9},{4,14},{5,15},{6,12},{7,13},{8,2},{9,3},... | collective-permute-start | bytes 983048 | tf_op jit(solution)/shard_map/ppermute | solution.py:493
  519.2 8.5 %collective-permute-start.15 = (bf16[1280,128]{1,0:T(8,128)(2,1)}, bf16[1280,128]{1,0:T(8,128)(2,1)}, u32[]{:S(2)}, u32[]{:S(2)}) collective-permute-start(bf16[1280,128]{1,0:T(8,128)(2,1)} %get-tuple-element.159), channel_id=1, source_target_pairs={{0,12},{1,13},{2,14},{3,15},{4,0},{5,1},{6,2},{7,3},{8,4},{9,5},{1... | collective-permute-start | bytes 983048 | tf_op jit(solution)/shard_map/ppermute | solution.py:493
  519.9 16.0 %collective-permute-start.16 = (bf16[1280,128]{1,0:T(8,128)(2,1)}, bf16[1280,128]{1,0:T(8,128)(2,1)}, u32[]{:S(2)}, u32[]{:S(2)}) collective-permute-start(bf16[1280,128]{1,0:T(8,128)(2,1)} %get-tuple-element.160), channel_id=1, source_target_pairs={{0,14},{1,15},{2,12},{3,13},{4,2},{5,3},{6,0},{7,1},{8,6},{9,7},{1... | collective-permute-start | bytes 983048 | tf_op jit(solution)/shard_map/ppermute | solution.py:493
  541.9 28.1 %all-to-all-start.13 = ((bf16[8,160,128]{2,1,0:T(8,128)(2,1)}), bf16[8,160,128]{2,1,0:T(8,128)(2,1)S(1)}, u32[]{:S(2)}, u32[]{:S(2)}) async-start(bf16[8,160,128]{2,1,0:T(8,128)(2,1)} %pad_maximum_fusion.2), calls=%async_computation.13 | async-start | bytes 655360 | tf_op jit(solution)/shard_map/all_to_all | solution.py:31
  551.9 17.4 %collective-permute-start.17 = (bf16[160,512]{1,0:T(8,128)(2,1)S(1)}, bf16[160,512]{1,0:T(8,128)(2,1)S(1)}, u32[]{:S(2)}, u32[]{:S(2)}) collective-permute-start(bf16[160,512]{1,0:T(8,128)(2,1)S(1)} %get-tuple-element.194), channel_id=1, source_target_pairs={{0,0},{1,64},{2,1},{3,65},{4,16},{5,80},{6,17},{7,81},{8,32},{9,96... | collective-permute-start | bytes 491528 | tf_op jit(solution)/shard_map/ppermute | solution.py:508
  558.3 11.0 %collective-permute-start.18 = (bf16[160,512]{1,0:T(8,128)(2,1)S(1)}, bf16[160,512]{1,0:T(8,128)(2,1)S(1)}, u32[]{:S(2)}, u32[]{:S(2)}) collective-permute-start(bf16[160,512]{1,0:T(8,128)(2,1)S(1)} %get-tuple-element.193), channel_id=1, source_target_pairs={{0,64},{1,0},{2,65},{3,1},{4,80},{5,16},{6,81},{7,17},{8,96},{9,32... | collective-permute-start | bytes 491528 | tf_op jit(solution)/shard_map/ppermute | solution.py:508
  570.7 35.3 %copy-start.1 = (bf16[256,5120]{1,0:T(8,128)(2,1)S(1)}, bf16[256,5120]{1,0:T(8,128)(2,1)}, u32[]{:S(2)}) copy-start(bf16[256,5120]{1,0:T(8,128)(2,1)} %param.9) | copy-start | bytes 7864324
  582.0 23.1 %all-to-all-start.14 = ((bf16[16,2,32,320]{3,2,1,0:T(8,128)(2,1)}), bf16[16,2,32,320]{3,2,1,0:T(8,128)(2,1)S(1)}, u32[]{:S(2)}, u32[]{:S(2)}) async-start(bf16[16,2,32,320]{3,2,1,0:T(8,128)(2,1)} %copy-done.30), calls=%async_computation.14 | async-start | bytes 1572864 | tf_op jit(solution)/shard_map/all_to_all | solution.py:31
  (51 other events, 64.3 us)
Sparse Core Ops, SparseCore 0:
  10.3 63.0 all-gather.7
  75.7 47.2 all-gather.5
  125.3 40.3 all-gather.9
  167.3 55.5 all-gather.11
  237.8 72.0 all-gather.13

commit v9 on v8

--- a/solution.py
+++ b/solution.py
@@ -15,7 +15,7 @@
 
 BLOCKS = ((0, 4), (4, 8))
 LANES = 128
-VMEM_BYTES = 34 * 1024 * 1024
+VMEM_BYTES = 60 * 1024 * 1024
 
 
 def dot(left, right, dims):
@@ -196,14 +196,11 @@
 
 def forward_kernel(first, last, width, inner, copies):
     def kernel(
-        sums_ref, gram_in_ref, gram_out_ref, acts_ref, hidden_ref, scale_ref, cross_ref
+        down_ref, up_ref, gram_in_ref, gram_out_ref, acts_ref, hidden_ref, scale_ref, cross_ref
     ):
         find = finder(first, last, inner, gram_in_ref, gram_out_ref, 0)
-        up_start = (last - first) * inner + LANES
-        state, crosses = forward_chain(
-            first, last, width, inner, sums_ref, sums_ref, up_start, find
-        )
-        rows = sums_ref.shape[1]
+        state, crosses = forward_chain(first, last, width, inner, down_ref, up_ref, 0, find)
+        rows = down_ref.shape[1]
         for s in range(first, last):
             hidden, scale, act = state[s]
             at = s - first
@@ -570,22 +567,23 @@
     count = middle - first
     wide = rows.astype(jnp.float32)
     down_low, down_high = products(True, BLOCKS)
-    all_out, down_low = lax.optimization_barrier((all_out, down_low))
+    columns = [dot(rows, weight_in[s], ROWS) for s in range(first, middle)]
+    columns += split_scalars([jnp.sum(wide * wide, axis=1, keepdims=True)])
+    down = exchanged(columns, n_pipe)
+    all_out, down_low, down = lax.optimization_barrier((all_out, down_low, down))
     weight_out = [all_out[:, s * chunk : (s + 1) * chunk] for s in range(n_pipe)]
     gram_in_low = over_dp(down_low)
     up_low, up_high = products(False, BLOCKS)
     gram_out_low = over_dp(up_low)
-    columns = [dot(rows, weight_in[s], ROWS) for s in range(first, middle)]
-    columns += split_scalars([jnp.sum(wide * wide, axis=1, keepdims=True)])
-    columns += [dot(rows, weight_out[s], LAST) for s in range(first, middle - 1)]
+    columns = [dot(rows, weight_out[s], LAST) for s in range(first, middle - 1)]
     columns, up_low = lax.optimization_barrier((columns, up_low))
-    sums_low = exchanged(columns, n_pipe)
+    up = exchanged(columns, n_pipe)
     columns = [dot(seed, weight_out[s], LAST) for s in range(middle, last)]
-    columns, sums_low = lax.optimization_barrier((columns, sums_low))
+    columns, up = lax.optimization_barrier((columns, up))
     grad_high = exchanged(columns, n_pipe)
     columns = jnp.concatenate([down_high, up_high], axis=1)
-    gram_in_low, gram_out_low, sums_low, grad_high, columns = lax.optimization_barrier(
-        (gram_in_low, gram_out_low, sums_low, grad_high, columns)
+    gram_in_low, gram_out_low, up, grad_high, columns = lax.optimization_barrier(
+        (gram_in_low, gram_out_low, up, grad_high, columns)
     )
     gram_high = over_dp(columns)
 
@@ -598,7 +596,8 @@
             ((count, block, LANES), jnp.float32),
             ((kept, block, inner), jnp.float32),
         ],
-        sums_low,
+        down,
+        up,
         gram_in_low,
         gram_out_low,
     )
@@ -692,25 +691,24 @@
         grads_high,
         smem=True,
     )
-    mine, other, arrived_high = lax.optimization_barrier((mine, other, arrived_high))
+
+    def unpacked(arrived, group):
+        share = group * chunk // n_dp
+        rows_out = arrived[0].shape[-2] - share * inner // LANES
+        sum_in, sum_out = run(
+            unpack_kernel(inner, share, len(arrived)),
+            [((share, inner), jnp.bfloat16), ((rows_out, LANES), jnp.bfloat16)],
+            *arrived,
+        )
+        return sum_in, sum_out.reshape(group, -1, LANES)
+
+    high = unpacked(arrived_high, last - middle)
+    mine, other, high = lax.optimization_barrier((mine, other, high))
     blocks = added(mine, other_core(other, n_dp), mine.shape[0])
     arrived_low = between_chips(blocks, n_dp)
     input_grads = swap(grads, "pipe")
     input_grads, arrived_low = lax.optimization_barrier((input_grads, arrived_low))
-
-    ins, outs = [], []
-    for (low, high), arrived in zip(BLOCKS, (arrived_low, arrived_high)):
-        share = (high - low) * chunk // n_dp
-        sum_in, sum_out = run(
-            unpack_kernel(inner, share, len(arrived)),
-            [
-                ((share, inner), jnp.bfloat16),
-                ((arrived[0].shape[-2] - share * inner // LANES, LANES), jnp.bfloat16),
-            ],
-            *arrived,
-        )
-        ins.append(sum_in)
-        outs.append(sum_out.reshape(high - low, -1, LANES))
+    ins, outs = zip(unpacked(arrived_low, count), high)
     grad_out = swap(jnp.concatenate(outs, axis=0), "pipe")
     grad_in = move_in(*ins, n_pipe, n_dp)
     is_high = (me >= middle).astype(jnp.int32).reshape(1)

time: 616 us -> 619 us (level)
  local copies, waits for them, and re-layouts: 67.3 us -> 16.6 us
  starting transfers between devices: 80.4 us -> 119 us
  Pallas kernels: 48.8 us -> 84.6 us
  blocking collectives: 169 us -> 142 us
    unnamed x137 -> x77, local copies, waits for them, and re-layouts: 62.3 us -> 8.55 us
    pallas_call x14, Pallas kernels: 42.9 us -> 78.7 us  [run(): pl.pallas_call(kernel, out_shape=[jax.ShapeDtypeStruct(shape, kind) for s...]
    all_to_all x8 -> x6, blocking collectives: 169 us -> 142 us  [swap(): return lax.all_to_all(x, axis, 0, 0, tiled=True)]
    all_to_all x7 -> x10, starting transfers between devices: 47.2 us -> 73.6 us  [swap(): return lax.all_to_all(x, axis, 0, 0, tiled=True)]
    all_gather x1, waiting for transfers between devices: 12.6 us -> 0.01 us  [on_device(): all_out = lax.all_gather(flat_out, 'dp', axis=0, tiled=True)]
    ppermute x14, starting transfers between devices: 22.6 us -> 34.3 us  [between_chips(): arrived.append(lax.ppermute(block, 'dp', pairs))]
    all_gather x3, waiting for transfers between devices: 1.88 us -> 11.2 us  [over_dp(): return lax.all_gather(columns, 'dp', axis=0, tiled=True)]
    all_to_all x7 -> x10, waiting for transfers between devices: 75 us -> 83.9 us  [swap(): return lax.all_to_all(x, axis, 0, 0, tiled=True)]
  transfers between devices with their start and end apart: 31 -> 34, of which waited for: 12 -> 18; matrix products, arithmetic and copies ran while one was open for 8% -> 9% of each run, Pallas kernels for 5% -> 6%
where the time goes in v9:
time: 619 us; the launch traced here: 616 us
  waiting for transfers between devices  192 us (31%)
  blocking collectives  142 us (23%)
  starting transfers between devices  119 us (19%)
  Pallas kernels  84.6 us (14%)
  matrix products  35.1 us (6%)
  local copies, waits for them, and re-layouts  16.6 us (3%)
  between operations  14.3 us (2%)
  other arithmetic  13.1 us (2%)
    all_to_all x6, blocking collectives, swap(): return lax.all_to_all(x, axis, 0, 0, tiled=True)  142 us
    all_to_all x10, waiting for transfers between devices, swap(): return lax.all_to_all(x, axis, 0, 0, tiled=True)  83.9 us
    pallas_call x14, Pallas kernels, run(): pl.pallas_call(kernel, out_shape=[jax.ShapeDtypeStruct(shape, kind) for s...  78.7 us
    all_to_all x10, starting transfers between devices, swap(): return lax.all_to_all(x, axis, 0, 0, tiled=True)  73.6 us
    ppermute x14, waiting for transfers between devices, between_chips(): arrived.append(lax.ppermute(block, 'dp', pairs))  72.2 us
    dot_general x23, matrix products, dot(): lax.dot_general(left, right, (dims, ((), ())), preferred_element_type=jnp...  35.1 us
    ppermute x14, starting transfers between devices, between_chips(): arrived.append(lax.ppermute(block, 'dp', pairs))  34.3 us
    all_gather x1, waiting for transfers between devices, on_device(): all_in = lax.all_gather(piece_in, 'dp', axis=0, tiled=True)  20.3 us
  transfers between devices with their start and end apart: 34, of which 18 were waited for; matrix products, arithmetic and copies ran while one was open for 9% of the time, Pallas kernels for 6%

profile of v9, /device:TPU:1, one launch (start us, length us, event | category | flops | bytes accessed | tf_op | source)
XLA Modules:
  0.0 616.4 jit_solution(5020123495800305077)
XLA Ops:
  11.2 37.5 %all_to_all.125 = bf16[8,32,640]{2,1,0:T(8,128)(2,1)S(1)} all-to-all(bf16[8,32,640]{2,1,0:T(8,128)(2,1)S(1)} %copy.30), channel_id=1, replica_groups=mesh['pipe'=8,'dp'=16] {'pipe'}, dimensions={0} | all-to-all | bytes 655360 | tf_op jit(solution)/shard_map/all_to_all | solution.py:31
  53.2 20.3 %all-gather.8.cloned.1.call-done.in_ref.refs_5_ = bf16[5120,512]{1,0:T(8,128)(2,1)} async-done(((bf16[320,512]{1,0:T(8,128)(2,1)}), bf16[5120,512]{1,0:T(8,128)(2,1)}) %all-gather.8.cloned.1.call-update) | async-done | bytes 5242896 | tf_op jit(solution)/shard_map/all_gather | solution.py:533
  82.2 6.2 all-to-all-start.1
  92.1 5.9 all-to-all-done.1
  101.2 4.2 all-to-all-start.2
  110.4 3.2 concatenate.39
  113.6 6.8 %all-to-all-start.3 = ((bf16[8,32,2176]{2,1,0:T(8,128)(2,1)}), bf16[8,32,2176]{2,1,0:T(8,128)(2,1)}, u32[]{:S(2)}, u32[]{:S(2)}) async-start(bf16[8,32,2176]{2,1,0:T(8,128)(2,1)} %concatenate.39), calls=%async_computation.3 | async-start | bytes 2228224 | tf_op jit(solution)/shard_map/all_to_all | solution.py:31
  122.2 14.3 %all-to-all-done.3.down_ref = bf16[8,32,2176]{2,1,0:T(8,128)(2,1)} async-done(((bf16[8,32,2176]{2,1,0:T(8,128)(2,1)}), bf16[8,32,2176]{2,1,0:T(8,128)(2,1)}, u32[]{:S(2)}, u32[]{:S(2)}) %all-to-all-start.3) | async-done | bytes 1114144 | tf_op jit(solution)/shard_map/all_to_all | solution.py:31
  145.2 12.4 %all_to_all.126 = bf16[8,48,512]{2,1,0:T(8,128)(2,1)} all-to-all(bf16[8,48,512]{2,1,0:T(8,128)(2,1)S(1)} %bitcast.123), channel_id=1, replica_groups=mesh['pipe'=8,'dp'=16] {'pipe'}, dimensions={0} | all-to-all | bytes 786432 | tf_op jit(solution)/shard_map/all_to_all | solution.py:31
  158.7 13.1 %all_to_all.127 = bf16[8,48,512]{2,1,0:T(8,128)(2,1)} all-to-all(bf16[8,48,512]{2,1,0:T(8,128)(2,1)S(1)} %tile.5), channel_id=1, replica_groups=mesh['pipe'=8,'dp'=16] {'pipe'}, dimensions={0} | all-to-all | bytes 786432 | tf_op jit(solution)/shard_map/all_to_all | solution.py:31
  180.7 5.2 all-to-all-start.6
  190.4 8.5 %all-to-all-done.6.up_ref = bf16[8,32,1536]{2,1,0:T(8,128)(2,1)S(1)} async-done(((bf16[8,32,1536]{2,1,0:T(8,128)(2,1)}), bf16[8,32,1536]{2,1,0:T(8,128)(2,1)S(1)}, u32[]{:S(2)}, u32[]{:S(2)}) %all-to-all-start.6) | async-done | bytes 786464 | tf_op jit(solution)/shard_map/all_to_all | solution.py:31
  200.1 5.7 all-to-all-start.7
  206.6 17.1 %all-to-all-done.7.grad_ref = bf16[8,32,2048]{2,1,0:T(8,128)(2,1)S(1)} async-done(((bf16[8,32,2048]{2,1,0:T(8,128)(2,1)}), bf16[8,32,2048]{2,1,0:T(8,128)(2,1)S(1)}, u32[]{:S(2)}, u32[]{:S(2)}) %all-to-all-start.7) | async-done | bytes 1048608 | tf_op jit(solution)/shard_map/all_to_all | solution.py:31
  223.7 5.2 all-gather.12.cloned.1.call-done.gram_out_ref
  229.0 6.5 %shard_map.153 = (bf16[256,2048]{1,0:T(8,128)(2,1)}, f32[4,32,512]{2,1,0:T(8,128)}, f32[4,32,128]{2,1,0:T(8,128)}, f32[6,32,512]{2,1,0:T(8,128)}) custom-call(bf16[8,32,2176]{2,1,0:T(8,128)(2,1)} %all-to-all-done.3.down_ref, bf16[8,32,1536]{2,1,0:T(8,128)(2,1)} %copy-done.6, bf16[512,3072]{1,0:T(8,128)(2,1)} %all-gather.10.cloned.1.call-done.gram_in_ref.gram_ref, ...), custom_call_target="tpu_custom_call" | custom-call | tf_op jit(solution)/shard_map/pallas_call | solution.py:71
  235.4 24.7 %all_to_all.128 = bf16[8,32,2048]{2,1,0:T(8,128)(2,1)} all-to-all(bf16[8,32,2048]{2,1,0:T(8,128)(2,1)} %bitcast.118), channel_id=1, replica_groups=mesh['pipe'=8,'dp'=16] {'pipe'}, dimensions={0} | all-to-all | bytes 2097152 | tf_op jit(solution)/shard_map/all_to_all | solution.py:31
  260.1 7.6 %shard_map.154 = (f32[256,640]{1,0:T(8,128)}, bf16[256,3712]{1,0:T(8,128)(2,1)}) custom-call(bf16[256,640]{1,0:T(8,128)(2,1)} %copy-done.7, bf16[256,2048]{1,0:T(8,128)(2,1)} %bitcast.103, bf16[5120,512]{1,0:T(8,128)(2,1)} %all-gather.8.cloned.1.call-done.in_ref.refs_5_, bf16[512,5120]{1,0:T(8,128)(2,1)} %all-gather.6.cloned.1.call-done.out_ref.refs_6_), custom_call_target="tpu_custom_call" | custom-call | tf_op jit(solution)/shard_map/pallas_call | solution.py:71
  267.6 33.3 %all_to_all.129.sums_ref = bf16[8,32,3712]{2,1,0:T(8,128)(2,1)} all-to-all(bf16[8,32,3712]{2,1,0:T(8,128)(2,1)} %bitcast.112), channel_id=1, replica_groups=mesh['pipe'=8,'dp'=16] {'pipe'}, dimensions={0} | all-to-all | bytes 3801088 | tf_op jit(solution)/shard_map/all_to_all | solution.py:31
  300.9 6.0 all-gather.14.cloned.1.call-done.gram_ref
  306.9 8.3 %shard_map.155 = bf16[256,4224]{1,0:T(8,128)(2,1)} custom-call(bf16[8,32,3712]{2,1,0:T(8,128)(2,1)} %all_to_all.129.sums_ref, bf16[8,32,2048]{2,1,0:T(8,128)(2,1)} %copy-done.4, bf16[512,6144]{1,0:T(8,128)(2,1)} %all-gather.14.cloned.1.call-done.gram_ref), custom_call_target="tpu_custom_call" | custom-call | tf_op jit(solution)/shard_map/pallas_call | solution.py:71
  315.2 6.3 %all-to-all-start.10 = ((bf16[8,32,4224]{2,1,0:T(8,128)(2,1)}), bf16[8,32,4224]{2,1,0:T(8,128)(2,1)S(1)}, u32[]{:S(2)}, u32[]{:S(2)}) async-start(bf16[8,32,4224]{2,1,0:T(8,128)(2,1)} %bitcast.105), calls=%async_computation.10 | async-start | bytes 4325376 | tf_op jit(solution)/shard_map/all_to_all | solution.py:31
  322.1 31.3 %all-to-all-done.10 = bf16[8,32,4224]{2,1,0:T(8,128)(2,1)S(1)} async-done(((bf16[8,32,4224]{2,1,0:T(8,128)(2,1)}), bf16[8,32,4224]{2,1,0:T(8,128)(2,1)S(1)}, u32[]{:S(2)}, u32[]{:S(2)}) %all-to-all-start.10) | async-done | bytes 2162720 | tf_op jit(solution)/shard_map/all_to_all | solution.py:31
  354.7 13.2 %shard_map.156 = (bf16[4,256,640]{2,1,0:T(8,128)(2,1)}, bf16[8,1280,128]{2,1,0:T(8,128)(2,1)}, bf16[8,1280,128]{2,1,0:T(8,128)(2,1)}, f32[256,640]{1,0:T(8,128)}, bf16[256,2048]{1,0:T(8,128)(2,1)}) custom-call(s32[9]{0:T(128)} %pad_add_fusion.refs_0_, f32[256,640]{1,0:T(8,128)} %get-tuple-element.107.refs_1_, bf16[256,4224]{1,0:T(8,128)(2,1)} %bitcast.101, ...), custom_call_target="tpu_custom_call" | custom-call | tf_op jit(solution)/shard_map/pallas_call | solution.py:71
  369.2 21.0 %all_to_all.130.grad_ref = bf16[8,32,2048]{2,1,0:T(8,128)(2,1)} all-to-all(bf16[8,32,2048]{2,1,0:T(8,128)(2,1)} %bitcast.117), channel_id=1, replica_groups=mesh['pipe'=8,'dp'=16] {'pipe'}, dimensions={0} | all-to-all | bytes 2097152 | tf_op jit(solution)/shard_map/all_to_all | solution.py:31
  390.2 5.7 shard_map.157
  395.9 3.6 all-to-all-start.12
  399.5 4.1 shard_map.159
  403.6 3.1 collective-permute-start.4
  409.4 16.4 %collective-permute-done.2.refs_1_ = bf16[1280,128]{1,0:T(8,128)(2,1)S(1)} collective-permute-done((bf16[1280,128]{1,0:T(8,128)(2,1)}, bf16[1280,128]{1,0:T(8,128)(2,1)S(1)}, u32[]{:S(2)}, u32[]{:S(2)}) %collective-permute-start.2) | collective-permute-done | bytes 327712 | tf_op jit(solution)/shard_map/ppermute | solution.py:490
  425.7 9.5 %collective-permute-start.7 = (bf16[1280,128]{1,0:T(8,128)(2,1)}, bf16[1280,128]{1,0:T(8,128)(2,1)S(1)}, u32[]{:S(2)}, u32[]{:S(2)}) collective-permute-start(bf16[1280,128]{1,0:T(8,128)(2,1)} %get-tuple-element.131), channel_id=1, source_target_pairs={{0,12},{1,13},{2,14},{3,15},{4,0},{5,1},{6,2},{7,3},{8,4},{9,5},{1... | collective-permute-start | bytes 983048 | tf_op jit(solution)/shard_map/ppermute | solution.py:490
  436.8 3.6 collective-permute-done.6.refs_5_
  441.2 7.0 %collective-permute-done.8.refs_7_ = bf16[1280,128]{1,0:T(8,128)(2,1)S(1)} collective-permute-done((bf16[1280,128]{1,0:T(8,128)(2,1)}, bf16[1280,128]{1,0:T(8,128)(2,1)S(1)}, u32[]{:S(2)}, u32[]{:S(2)}) %collective-permute-start.8) | collective-permute-done | bytes 327712 | tf_op jit(solution)/shard_map/ppermute | solution.py:490
  452.6 13.1 %shard_map.158 = (bf16[8,256,640]{2,1,0:T(8,128)(2,1)}, bf16[8,1280,128]{2,1,0:T(8,128)(2,1)}, bf16[8,1280,128]{2,1,0:T(8,128)(2,1)}, f32[256,640]{1,0:T(8,128)}) custom-call(s32[9]{0:T(128)} %pad_add_fusion.refs_0_, bf16[256,640]{1,0:T(8,128)(2,1)} %copy-done.7, bf16[256,2176]{1,0:T(8,128)(2,1)} %bitcast.106, bf16[256,2048]{1,0:T(8,128)(2,1)} %bitcast.104, ...), custom_call_target="tpu_custom_call" | custom-call | tf_op jit(solution)/shard_map/pallas_call | solution.py:71
  467.9 8.0 %all-to-all-start.13 = ((bf16[8,256,640]{2,1,0:T(8,128)(2,1)}), bf16[8,256,640]{2,1,0:T(8,128)(2,1)}, u32[]{:S(2)}, u32[]{:S(2)}) async-start(bf16[8,256,640]{2,1,0:T(8,128)(2,1)} %get-tuple-element.120), calls=%async_computation.13 | async-start | bytes 5242880 | tf_op jit(solution)/shard_map/all_to_all | solution.py:31
  477.5 4.1 shard_map.161
  482.1 2.9 collective-permute-start.12
  484.9 3.0 collective-permute-start.13
  487.9 32.3 %collective-permute-done.10.refs_1_ = bf16[1280,128]{1,0:T(8,128)(2,1)S(1)} collective-permute-done((bf16[1280,128]{1,0:T(8,128)(2,1)}, bf16[1280,128]{1,0:T(8,128)(2,1)S(1)}, u32[]{:S(2)}, u32[]{:S(2)}) %collective-permute-start.10) | collective-permute-done | bytes 327712 | tf_op jit(solution)/shard_map/ppermute | solution.py:490
  520.3 9.8 %collective-permute-start.15 = (bf16[1280,128]{1,0:T(8,128)(2,1)}, bf16[1280,128]{1,0:T(8,128)(2,1)S(1)}, u32[]{:S(2)}, u32[]{:S(2)}) collective-permute-start(bf16[1280,128]{1,0:T(8,128)(2,1)} %get-tuple-element.143), channel_id=1, source_target_pairs={{0,12},{1,13},{2,14},{3,15},{4,0},{5,1},{6,2},{7,3},{8,4},{9,5},{1... | collective-permute-start | bytes 983048 | tf_op jit(solution)/shard_map/ppermute | solution.py:490
  531.5 5.1 collective-permute-done.15.refs_6_
  536.6 7.0 %collective-permute-done.16.refs_7_ = bf16[1280,128]{1,0:T(8,128)(2,1)S(1)} collective-permute-done((bf16[1280,128]{1,0:T(8,128)(2,1)}, bf16[1280,128]{1,0:T(8,128)(2,1)S(1)}, u32[]{:S(2)}, u32[]{:S(2)}) %collective-permute-start.16) | collective-permute-done | bytes 327712 | tf_op jit(solution)/shard_map/ppermute | solution.py:490
  548.7 8.0 %all-to-all-start.14 = ((bf16[8,160,128]{2,1,0:T(8,128)(2,1)}), bf16[8,160,128]{2,1,0:T(8,128)(2,1)S(1)}, u32[]{:S(2)}, u32[]{:S(2)}) async-start(bf16[8,160,128]{2,1,0:T(8,128)(2,1)} %pad_maximum_fusion.3), calls=%async_computation.14 | async-start | bytes 655360 | tf_op jit(solution)/shard_map/all_to_all | solution.py:31
  557.6 6.6 %collective-permute-start.17 = (bf16[160,512]{1,0:T(8,128)(2,1)S(1)}, bf16[160,512]{1,0:T(8,128)(2,1)S(1)}, u32[]{:S(2)}, u32[]{:S(2)}) collective-permute-start(bf16[160,512]{1,0:T(8,128)(2,1)S(1)} %get-tuple-element.170), channel_id=1, source_target_pairs={{0,0},{1,64},{2,1},{3,65},{4,16},{5,80},{6,17},{7,81},{8,32},{9,96... | collective-permute-start | bytes 491528 | tf_op jit(solution)/shard_map/ppermute | solution.py:505
  569.2 5.2 shard_map.164
  574.5 19.7 %all-to-all-start.15 = ((bf16[16,2,32,320]{3,2,1,0:T(8,128)(2,1)}), bf16[16,2,32,320]{3,2,1,0:T(8,128)(2,1)S(1)}, u32[]{:S(2)}, u32[]{:S(2)}) async-start(bf16[16,2,32,320]{3,2,1,0:T(8,128)(2,1)} %get-tuple-element.164), calls=%async_computation.15 | async-start | bytes 1572864 | tf_op jit(solution)/shard_map/all_to_all | solution.py:31
  594.2 5.9 shard_map.162
  600.1 6.8 %all-to-all-done.15.pieces_ref = bf16[16,2,32,320]{3,2,1,0:T(8,128)(2,1)S(1)} async-done(((bf16[16,2,32,320]{3,2,1,0:T(8,128)(2,1)}), bf16[16,2,32,320]{3,2,1,0:T(8,128)(2,1)S(1)}, u32[]{:S(2)}, u32[]{:S(2)}) %all-to-all-start.15) | async-done | bytes 655392 | tf_op jit(solution)/shard_map/all_to_all | solution.py:31
  (173 shorter events, 88.1 us)
Async XLA Ops:
  7.2 166.4 %copy-start = (bf16[256,5120]{1,0:T(8,128)(2,1)S(1)}, bf16[256,5120]{1,0:T(8,128)(2,1)}, u32[]{:S(2)}) copy-start(bf16[256,5120]{1,0:T(8,128)(2,1)} %param.9) | copy-start | bytes 7864324
  7.2 66.3 %all-gather.8.cloned.1.call-start = ((), (), s32[]{:S(2)}) async-start(), calls=%async_computation.17 | async-start | bytes 5570560 | tf_op jit(solution)/shard_map/all_gather | solution.py:533
  8.5 0.7 collective-permute-start
  10.0 112.2 %all-gather.6.cloned.1.call-start = ((), (), s32[]{:S(2)}) async-start(), calls=%async_computation.16 | async-start | bytes 5570560 | tf_op jit(solution)/shard_map/all_gather | solution.py:534
  50.7 126.1 %copy-start.7 = (bf16[256,640]{1,0:T(8,128)(2,1)}, bf16[256,640]{1,0:T(8,128)(2,1)S(1)}, u32[]{:S(2)}) copy-start(bf16[256,640]{1,0:T(8,128)(2,1)S(1)} %get-tuple-element.168.rows_ref.refs_1_) | copy-start | bytes 983044
  53.1 35.3 %copy-start.34 = (bf16[3,32,640]{2,1,0:T(8,128)(2,1)}, bf16[3,32,640]{2,1,0:T(8,128)(2,1)S(1)}, u32[]{:S(2)}) copy-start(bf16[3,32,640]{2,1,0:T(8,128)(2,1)S(1)} %get-tuple-element.171) | copy-start | bytes 368644
  53.2 35.3 %copy-start.36 = (bf16[3,32,640]{2,1,0:T(8,128)(2,1)}, bf16[3,32,640]{2,1,0:T(8,128)(2,1)S(1)}, u32[]{:S(2)}) copy-start(bf16[3,32,640]{2,1,0:T(8,128)(2,1)S(1)} %get-tuple-element.172) | copy-start | bytes 368644
  82.2 15.7 %all-to-all-start.1 = ((bf16[8,48,512]{2,1,0:T(8,128)(2,1)}), bf16[8,48,512]{2,1,0:T(8,128)(2,1)}, u32[]{:S(2)}, u32[]{:S(2)}) async-start(bf16[8,48,512]{2,1,0:T(8,128)(2,1)} %bitcast.124), calls=%async_computation.1 | async-start | bytes 786432 | tf_op jit(solution)/shard_map/all_to_all | solution.py:31
  101.2 12.4 %all-to-all-start.2 = ((bf16[8,48,512]{2,1,0:T(8,128)(2,1)}), bf16[8,48,512]{2,1,0:T(8,128)(2,1)}, u32[]{:S(2)}, u32[]{:S(2)}) async-start(bf16[8,48,512]{2,1,0:T(8,128)(2,1)} %tile.4), calls=%async_computation.2 | async-start | bytes 786432 | tf_op jit(solution)/shard_map/all_to_all | solution.py:31
  113.6 28.7 %copy-start.37 = (bf16[2,32,640]{2,1,0:T(8,128)(2,1)S(1)}, bf16[2,32,640]{2,1,0:T(8,128)(2,1)}, u32[]{:S(2)}) copy-start(bf16[2,32,640]{2,1,0:T(8,128)(2,1)} %get-tuple-element.173) | copy-start | bytes 245764
  113.6 30.1 %copy-start.35 = (bf16[3,32,640]{2,1,0:T(8,128)(2,1)S(1)}, bf16[3,32,640]{2,1,0:T(8,128)(2,1)}, u32[]{:S(2)}) copy-start(bf16[3,32,640]{2,1,0:T(8,128)(2,1)} %copy-done.34) | copy-start | bytes 368644
  113.6 22.9 %all-to-all-start.3 = ((bf16[8,32,2176]{2,1,0:T(8,128)(2,1)}), bf16[8,32,2176]{2,1,0:T(8,128)(2,1)}, u32[]{:S(2)}, u32[]{:S(2)}) async-start(bf16[8,32,2176]{2,1,0:T(8,128)(2,1)} %concatenate.39), calls=%async_computation.3 | async-start | bytes 2228224 | tf_op jit(solution)/shard_map/all_to_all | solution.py:31
  120.4 103.3 %all-gather.10.cloned.1.call-start = ((), (), s32[]{:S(2)}) async-start(), calls=%async_computation.18 | async-start | bytes 3342336 | tf_op jit(solution)/shard_map/all_gather | solution.py:561
  136.5 92.4 %all-gather.12.cloned.1.call-start = ((), (), s32[]{:S(2)}) async-start(), calls=%async_computation.19 | async-start | bytes 3342336 | tf_op jit(solution)/shard_map/all_gather | solution.py:561
  180.7 25.1 %copy-start.28 = (bf16[32,3072]{1,0:T(8,128)(2,1)S(1)}, bf16[32,3072]{1,0:T(8,128)(2,1)}, u32[]{:S(2)}) copy-start(bf16[32,3072]{1,0:T(8,128)(2,1)} %get-tuple-element.101) | copy-start | bytes 589828
  180.7 25.1 %copy-start.29 = (bf16[32,3072]{1,0:T(8,128)(2,1)S(1)}, bf16[32,3072]{1,0:T(8,128)(2,1)}, u32[]{:S(2)}) copy-start(bf16[32,3072]{1,0:T(8,128)(2,1)} %get-tuple-element.102) | copy-start | bytes 589828
  180.7 18.2 %all-to-all-start.6 = ((bf16[8,32,1536]{2,1,0:T(8,128)(2,1)}), bf16[8,32,1536]{2,1,0:T(8,128)(2,1)S(1)}, u32[]{:S(2)}, u32[]{:S(2)}) async-start(bf16[8,32,1536]{2,1,0:T(8,128)(2,1)} %bitcast.24), calls=%async_computation.6 | async-start | bytes 1572864 | tf_op jit(solution)/shard_map/all_to_all | solution.py:31
  198.9 30.1 %copy-start.6 = (bf16[8,32,1536]{2,1,0:T(8,128)(2,1)}, bf16[8,32,1536]{2,1,0:T(8,128)(2,1)S(1)}, u32[]{:S(2)}) copy-start(bf16[8,32,1536]{2,1,0:T(8,128)(2,1)S(1)} %all-to-all-done.6.up_ref) | copy-start | bytes 2359300
  200.1 23.6 %all-to-all-start.7 = ((bf16[8,32,2048]{2,1,0:T(8,128)(2,1)}), bf16[8,32,2048]{2,1,0:T(8,128)(2,1)S(1)}, u32[]{:S(2)}, u32[]{:S(2)}) async-start(bf16[8,32,2048]{2,1,0:T(8,128)(2,1)} %bitcast.25), calls=%async_computation.7 | async-start | bytes 2097152 | tf_op jit(solution)/shard_map/all_to_all | solution.py:31
  205.8 101.1 %all-gather.14.cloned.1.call-start = ((), (), s32[]{:S(2)}) async-start(), calls=%async_computation.20 | async-start | bytes 6684672 | tf_op jit(solution)/shard_map/all_gather | solution.py:561
  223.7 36.4 %copy-start.4 = (bf16[8,32,2048]{2,1,0:T(8,128)(2,1)}, bf16[8,32,2048]{2,1,0:T(8,128)(2,1)S(1)}, u32[]{:S(2)}) copy-start(bf16[8,32,2048]{2,1,0:T(8,128)(2,1)S(1)} %all-to-all-done.7.grad_ref) | copy-start | bytes 3145732
  315.2 38.2 %all-to-all-start.10 = ((bf16[8,32,4224]{2,1,0:T(8,128)(2,1)}), bf16[8,32,4224]{2,1,0:T(8,128)(2,1)S(1)}, u32[]{:S(2)}, u32[]{:S(2)}) async-start(bf16[8,32,4224]{2,1,0:T(8,128)(2,1)} %bitcast.105), calls=%async_computation.10 | async-start | bytes 4325376 | tf_op jit(solution)/shard_map/all_to_all | solution.py:31
  367.9 22.3 %collective-permute-start.1 = (bf16[8,1280,128]{2,1,0:T(8,128)(2,1)}, bf16[8,1280,128]{2,1,0:T(8,128)(2,1)S(1)}, u32[]{:S(2)}, u32[]{:S(2)}) collective-permute-start(bf16[8,1280,128]{2,1,0:T(8,128)(2,1)} %get-tuple-element.113), channel_id=1, source_target_pairs={{0,1},{1,0},{2,3},{3,2},{4,5},{5,4},{6,7},{7,6},{8,9},{9,8},{10,11... | collective-permute-start | bytes 7864328 | tf_op jit(solution)/shard_map/ppermute | solution.py:462
  395.9 55.6 %all-to-all-start.12 = ((bf16[8,32,2176]{2,1,0:T(8,128)(2,1)}), bf16[8,32,2176]{2,1,0:T(8,128)(2,1)S(1)}, u32[]{:S(2)}, u32[]{:S(2)}) async-start(bf16[8,32,2176]{2,1,0:T(8,128)(2,1)} %bitcast.107), calls=%async_computation.12 | async-start | bytes 2228224 | tf_op jit(solution)/shard_map/all_to_all | solution.py:31
  403.6 22.2 %collective-permute-start.2 = (bf16[1280,128]{1,0:T(8,128)(2,1)}, bf16[1280,128]{1,0:T(8,128)(2,1)S(1)}, u32[]{:S(2)}, u32[]{:S(2)}) collective-permute-start(bf16[1280,128]{1,0:T(8,128)(2,1)} %get-tuple-element.126), channel_id=1, source_target_pairs={{0,2},{1,3},{2,0},{3,1},{4,6},{5,7},{6,4},{7,5},{8,10},{9,11},{10,... | collective-permute-start | bytes 983048 | tf_op jit(solution)/shard_map/ppermute | solution.py:490
  403.6 31.6 %collective-permute-start.3 = (bf16[1280,128]{1,0:T(8,128)(2,1)}, bf16[1280,128]{1,0:T(8,128)(2,1)S(1)}, u32[]{:S(2)}, u32[]{:S(2)}) collective-permute-start(bf16[1280,128]{1,0:T(8,128)(2,1)} %get-tuple-element.127), channel_id=1, source_target_pairs={{0,4},{1,5},{2,6},{3,7},{4,8},{5,9},{6,10},{7,11},{8,12},{9,13},{1... | collective-permute-start | bytes 983048 | tf_op jit(solution)/shard_map/ppermute | solution.py:490
  403.6 33.2 %collective-permute-start.4 = (bf16[1280,128]{1,0:T(8,128)(2,1)}, bf16[1280,128]{1,0:T(8,128)(2,1)S(1)}, u32[]{:S(2)}, u32[]{:S(2)}) collective-permute-start(bf16[1280,128]{1,0:T(8,128)(2,1)} %get-tuple-element.128), channel_id=1, source_target_pairs={{0,6},{1,7},{2,4},{3,5},{4,10},{5,11},{6,8},{7,9},{8,14},{9,15},{1... | collective-permute-start | bytes 983048 | tf_op jit(solution)/shard_map/ppermute | solution.py:490
  406.7 30.1 %collective-permute-start.5 = (bf16[1280,128]{1,0:T(8,128)(2,1)}, bf16[1280,128]{1,0:T(8,128)(2,1)S(1)}, u32[]{:S(2)}, u32[]{:S(2)}) collective-permute-start(bf16[1280,128]{1,0:T(8,128)(2,1)} %get-tuple-element.129), channel_id=1, source_target_pairs={{0,8},{1,9},{2,10},{3,11},{4,12},{5,13},{6,14},{7,15},{8,0},{9,1},... | collective-permute-start | bytes 983048 | tf_op jit(solution)/shard_map/ppermute | solution.py:490
  408.6 31.8 %collective-permute-start.6 = (bf16[1280,128]{1,0:T(8,128)(2,1)}, bf16[1280,128]{1,0:T(8,128)(2,1)S(1)}, u32[]{:S(2)}, u32[]{:S(2)}) collective-permute-start(bf16[1280,128]{1,0:T(8,128)(2,1)} %get-tuple-element.130), channel_id=1, source_target_pairs={{0,10},{1,11},{2,8},{3,9},{4,14},{5,15},{6,12},{7,13},{8,2},{9,3},... | collective-permute-start | bytes 983048 | tf_op jit(solution)/shard_map/ppermute | solution.py:490
  425.7 15.4 %collective-permute-start.7 = (bf16[1280,128]{1,0:T(8,128)(2,1)}, bf16[1280,128]{1,0:T(8,128)(2,1)S(1)}, u32[]{:S(2)}, u32[]{:S(2)}) collective-permute-start(bf16[1280,128]{1,0:T(8,128)(2,1)} %get-tuple-element.131), channel_id=1, source_target_pairs={{0,12},{1,13},{2,14},{3,15},{4,0},{5,1},{6,2},{7,3},{8,4},{9,5},{1... | collective-permute-start | bytes 983048 | tf_op jit(solution)/shard_map/ppermute | solution.py:490
  435.2 13.0 %collective-permute-start.8 = (bf16[1280,128]{1,0:T(8,128)(2,1)}, bf16[1280,128]{1,0:T(8,128)(2,1)S(1)}, u32[]{:S(2)}, u32[]{:S(2)}) collective-permute-start(bf16[1280,128]{1,0:T(8,128)(2,1)} %get-tuple-element.132), channel_id=1, source_target_pairs={{0,14},{1,15},{2,12},{3,13},{4,2},{5,3},{6,0},{7,1},{8,6},{9,7},{1... | collective-permute-start | bytes 983048 | tf_op jit(solution)/shard_map/ppermute | solution.py:490
  465.7 10.3 %collective-permute-start.9 = (bf16[8,1280,128]{2,1,0:T(8,128)(2,1)}, bf16[8,1280,128]{2,1,0:T(8,128)(2,1)S(1)}, u32[]{:S(2)}, u32[]{:S(2)}) collective-permute-start(bf16[8,1280,128]{2,1,0:T(8,128)(2,1)} %get-tuple-element.136), channel_id=1, source_target_pairs={{0,1},{1,0},{2,3},{3,2},{4,5},{5,4},{6,7},{7,6},{8,9},{9,8},{10,11... | collective-permute-start | bytes 7864328 | tf_op jit(solution)/shard_map/ppermute | solution.py:462
  467.9 63.5 %all-to-all-start.13 = ((bf16[8,256,640]{2,1,0:T(8,128)(2,1)}), bf16[8,256,640]{2,1,0:T(8,128)(2,1)}, u32[]{:S(2)}, u32[]{:S(2)}) async-start(bf16[8,256,640]{2,1,0:T(8,128)(2,1)} %get-tuple-element.120), calls=%async_computation.13 | async-start | bytes 5242880 | tf_op jit(solution)/shard_map/all_to_all | solution.py:31
  475.9 71.1 %copy-start.32 = (bf16[640,128]{1,0:T(8,128)(2,1)S(1)}, bf16[640,128]{1,0:T(8,128)(2,1)}, u32[]{:S(2)}) copy-start(bf16[640,128]{1,0:T(8,128)(2,1)} %get-tuple-element.134) | copy-start | bytes 491524
  475.9 80.7 %copy-start.33 = (bf16[160,512]{1,0:T(8,128)(2,1)S(1)}, bf16[160,512]{1,0:T(8,128)(2,1)}, u32[]{:S(2)}) copy-start(bf16[160,512]{1,0:T(8,128)(2,1)} %get-tuple-element.146) | copy-start | bytes 491524
  481.6 38.7 %collective-permute-start.10 = (bf16[1280,128]{1,0:T(8,128)(2,1)}, bf16[1280,128]{1,0:T(8,128)(2,1)S(1)}, u32[]{:S(2)}, u32[]{:S(2)}) collective-permute-start(bf16[1280,128]{1,0:T(8,128)(2,1)} %get-tuple-element.138), channel_id=1, source_target_pairs={{0,2},{1,3},{2,0},{3,1},{4,6},{5,7},{6,4},{7,5},{8,10},{9,11},{10,... | collective-permute-start | bytes 983048 | tf_op jit(solution)/shard_map/ppermute | solution.py:490
  481.9 48.1 %collective-permute-start.11 = (bf16[1280,128]{1,0:T(8,128)(2,1)}, bf16[1280,128]{1,0:T(8,128)(2,1)S(1)}, u32[]{:S(2)}, u32[]{:S(2)}) collective-permute-start(bf16[1280,128]{1,0:T(8,128)(2,1)} %get-tuple-element.139), channel_id=1, source_target_pairs={{0,4},{1,5},{2,6},{3,7},{4,8},{5,9},{6,10},{7,11},{8,12},{9,13},{1... | collective-permute-start | bytes 983048 | tf_op jit(solution)/shard_map/ppermute | solution.py:490
  482.1 49.4 %collective-permute-start.12 = (bf16[1280,128]{1,0:T(8,128)(2,1)}, bf16[1280,128]{1,0:T(8,128)(2,1)S(1)}, u32[]{:S(2)}, u32[]{:S(2)}) collective-permute-start(bf16[1280,128]{1,0:T(8,128)(2,1)} %get-tuple-element.140), channel_id=1, source_target_pairs={{0,6},{1,7},{2,4},{3,5},{4,10},{5,11},{6,8},{7,9},{8,14},{9,15},{1... | collective-permute-start | bytes 983048 | tf_op jit(solution)/shard_map/ppermute | solution.py:490
  484.9 46.5 %collective-permute-start.13 = (bf16[1280,128]{1,0:T(8,128)(2,1)}, bf16[1280,128]{1,0:T(8,128)(2,1)S(1)}, u32[]{:S(2)}, u32[]{:S(2)}) collective-permute-start(bf16[1280,128]{1,0:T(8,128)(2,1)} %get-tuple-element.141), channel_id=1, source_target_pairs={{0,8},{1,9},{2,10},{3,11},{4,12},{5,13},{6,14},{7,15},{8,0},{9,1},... | collective-permute-start | bytes 983048 | tf_op jit(solution)/shard_map/ppermute | solution.py:490
  487.9 43.5 %collective-permute-start.14 = (bf16[1280,128]{1,0:T(8,128)(2,1)}, bf16[1280,128]{1,0:T(8,128)(2,1)S(1)}, u32[]{:S(2)}, u32[]{:S(2)}) collective-permute-start(bf16[1280,128]{1,0:T(8,128)(2,1)} %get-tuple-element.142), channel_id=1, source_target_pairs={{0,10},{1,11},{2,8},{3,9},{4,14},{5,15},{6,12},{7,13},{8,2},{9,3},... | collective-permute-start | bytes 983048 | tf_op jit(solution)/shard_map/ppermute | solution.py:490
  520.3 23.3 %copy-start.13 = (bf16[1280,128]{1,0:T(8,128)(2,1)}, bf16[1280,128]{1,0:T(8,128)(2,1)S(1)}, u32[]{:S(2)}) copy-start(bf16[1280,128]{1,0:T(8,128)(2,1)S(1)} %collective-permute-done.10.refs_1_) | copy-start | bytes 983044
  520.3 16.3 %collective-permute-start.15 = (bf16[1280,128]{1,0:T(8,128)(2,1)}, bf16[1280,128]{1,0:T(8,128)(2,1)S(1)}, u32[]{:S(2)}, u32[]{:S(2)}) collective-permute-start(bf16[1280,128]{1,0:T(8,128)(2,1)} %get-tuple-element.143), channel_id=1, source_target_pairs={{0,12},{1,13},{2,14},{3,15},{4,0},{5,1},{6,2},{7,3},{8,4},{9,5},{1... | collective-permute-start | bytes 983048 | tf_op jit(solution)/shard_map/ppermute | solution.py:490
  530.0 13.6 %collective-permute-start.16 = (bf16[1280,128]{1,0:T(8,128)(2,1)}, bf16[1280,128]{1,0:T(8,128)(2,1)S(1)}, u32[]{:S(2)}, u32[]{:S(2)}) collective-permute-start(bf16[1280,128]{1,0:T(8,128)(2,1)} %get-tuple-element.144), channel_id=1, source_target_pairs={{0,14},{1,15},{2,12},{3,13},{4,2},{5,3},{6,0},{7,1},{8,6},{9,7},{1... | collective-permute-start | bytes 983048 | tf_op jit(solution)/shard_map/ppermute | solution.py:490
  548.7 19.8 %all-to-all-start.14 = ((bf16[8,160,128]{2,1,0:T(8,128)(2,1)}), bf16[8,160,128]{2,1,0:T(8,128)(2,1)S(1)}, u32[]{:S(2)}, u32[]{:S(2)}) async-start(bf16[8,160,128]{2,1,0:T(8,128)(2,1)} %pad_maximum_fusion.3), calls=%async_computation.14 | async-start | bytes 655360 | tf_op jit(solution)/shard_map/all_to_all | solution.py:31
  557.6 8.9 %collective-permute-start.17 = (bf16[160,512]{1,0:T(8,128)(2,1)S(1)}, bf16[160,512]{1,0:T(8,128)(2,1)S(1)}, u32[]{:S(2)}, u32[]{:S(2)}) collective-permute-start(bf16[160,512]{1,0:T(8,128)(2,1)S(1)} %get-tuple-element.170), channel_id=1, source_target_pairs={{0,0},{1,64},{2,1},{3,65},{4,16},{5,80},{6,17},{7,81},{8,32},{9,96... | collective-permute-start | bytes 491528 | tf_op jit(solution)/shard_map/ppermute | solution.py:505
  564.2 4.2 collective-permute-start.18
  568.5 41.4 %copy-start.1 = (bf16[256,5120]{1,0:T(8,128)(2,1)S(1)}, bf16[256,5120]{1,0:T(8,128)(2,1)}, u32[]{:S(2)}) copy-start(bf16[256,5120]{1,0:T(8,128)(2,1)} %param.9) | copy-start | bytes 7864324
  574.5 32.4 %all-to-all-start.15 = ((bf16[16,2,32,320]{3,2,1,0:T(8,128)(2,1)}), bf16[16,2,32,320]{3,2,1,0:T(8,128)(2,1)S(1)}, u32[]{:S(2)}, u32[]{:S(2)}) async-start(bf16[16,2,32,320]{3,2,1,0:T(8,128)(2,1)} %get-tuple-element.164), calls=%async_computation.15 | async-start | bytes 1572864 | tf_op jit(solution)/shard_map/all_to_all | solution.py:31
  (24 other events, 162.4 us)
Sparse Core Ops, SparseCore 0:
  10.3 63.0 all-gather.7
  75.7 45.9 all-gather.5
  136.7 40.1 all-gather.9
  179.0 49.8 all-gather.11
  231.1 75.8 all-gather.13

commit v10 on v9

--- a/solution.py
+++ b/solution.py
@@ -15,7 +15,7 @@
 
 BLOCKS = ((0, 4), (4, 8))
 LANES = 128
-VMEM_BYTES = 60 * 1024 * 1024
+VMEM_BYTES = 48 * 1024 * 1024
 
 
 def dot(left, right, dims):
@@ -297,7 +297,7 @@
     return kernel
 
 
-def grads_kernel(first, last, before, inner, chunk, n_dp, acts_start):
+def grads_kernel(first, last, before, inner, chunk, n_dp, acts_start, paired):
     group = last - first
     share_in = group * chunk // n_dp
     share_out = inner // n_dp
@@ -310,7 +310,8 @@
         if first == 0:
             refs[1][last:] = refs[0][...]
             refs = refs[1:]
-        grads_ref, mine_ref, other_ref, up_new_ref = refs[:4]
+        grads_ref, up_new_ref, mine_ref = refs[:3]
+        more = refs[3:]
         exact = exact_ref[...].astype(jnp.float32)
         rows = {first: exact.astype(jnp.bfloat16)}
 
@@ -333,31 +334,33 @@
             onto = dot(act_of(s), narrow, FIRST).astype(jnp.bfloat16)
             base = lanes_in * share_in + (s - first) * lanes_out * share_out
 
-            def store(refs_of, into=into, onto=onto, base=base, s=s):
+            def store(target, into=into, onto=onto, base=base, s=s):
                 for piece in range(chunk // share_in):
-                    device = (s - first) * (chunk // share_in) + piece
-                    ref = refs_of[device % 2]
+                    ref, at = target((s - first) * (chunk // share_in) + piece)
                     for c in range(lanes_in):
-                        ref[place_ref[device // 2], c * share_in : (c + 1) * share_in] = into[
+                        ref[at, c * share_in : (c + 1) * share_in] = into[
                             piece * share_in : (piece + 1) * share_in,
                             c * LANES : (c + 1) * LANES,
                         ]
                 for device in range(n_dp):
-                    ref = refs_of[device % 2]
+                    ref, at = target(device)
                     for c in range(lanes_out):
                         row = base + c * share_out
-                        ref[place_ref[device // 2], row : row + share_out] = onto[
+                        ref[at, row : row + share_out] = onto[
                             device * share_out : (device + 1) * share_out,
                             c * LANES : (c + 1) * LANES,
                         ]
 
-            @pl.when(place_ref[n_dp // 2] == 0)
-            def _():
-                store((mine_ref, other_ref))
-
-            @pl.when(place_ref[n_dp // 2] == 1)
-            def _():
-                store((other_ref, mine_ref))
+            if paired:
+                for core in range(2):
+
+                    @pl.when(place_ref[n_dp // 2] == core)
+                    def _(store=store, core=core):
+                        halves = (mine_ref, more[0]) if core == 0 else (more[0], mine_ref)
+                        store(lambda device: (halves[device % 2], place_ref[device // 2]))
+
+            else:
+                store(lambda device: (mine_ref, device))
 
             weight = in_ref[s * chunk : (s + 1) * chunk]
             upstream = (
@@ -369,7 +372,7 @@
         if before < first:
             for s in range(before, first):
                 columns = dot(narrow, part(out_ref, s, chunk), LAST).astype(jnp.bfloat16)
-                refs[4][:, (s - before) * inner : (s - before + 1) * inner] = columns
+                more[0][:, (s - before) * inner : (s - before + 1) * inner] = columns
 
     return kernel
 
@@ -378,8 +381,6 @@
     def kernel(*refs):
         in_ref, out_ref = refs[sources:]
         given = refs[:sources]
-        if sources == 1:
-            given = [refs[0].at[k] for k in range(refs[0].shape[0])]
         lanes = inner // LANES
 
         def total_of(start, stop):
@@ -629,9 +630,8 @@
     )[0]
     turned = swap(turned, "pipe")
 
-    def packed_shape(group):
-        rows_packed = 2 * group * chunk * inner // (n_dp * LANES)
-        return (n_dp // 2, rows_packed, LANES)
+    def packed_shape(group, parts):
+        return (parts, 2 * group * chunk * inner // (n_dp * LANES), LANES)
 
     dp = lax.axis_index("dp")
     core, chip = dp % 2, dp // 2
@@ -640,13 +640,14 @@
     away = (chips // 2 - chip // 2 + xs) % xs * 2 + (chips % 2 + chip % 2) % 2
     place = jnp.concatenate([away, core[None]]).astype(jnp.int32)
 
-    grads_high, mine, other, upstream, columns = run(
-        grads_kernel(middle, last, first, inner, chunk, n_dp, (last - middle) * inner + LANES),
+    grads_high, upstream, packed, columns = run(
+        grads_kernel(
+            middle, last, first, inner, chunk, n_dp, (last - middle) * inner + LANES, False
+        ),
         [
             ((last - middle, tok_rows, chunk), jnp.bfloat16),
-            (packed_shape(last - middle), jnp.bfloat16),
-            (packed_shape(last - middle), jnp.bfloat16),
             ((tok_rows, chunk), jnp.float32),
+            (packed_shape(last - middle, n_dp), jnp.bfloat16),
             ((tok_rows, count * inner), jnp.bfloat16),
         ],
         place,
@@ -658,10 +659,9 @@
         all_out,
         smem=True,
     )
+    packed = packed.reshape(-1, LANES)
+    packed = lax.psum_scatter(packed, "dp", scatter_dimension=0, tiled=True)
     grad_low = exchanged(columns, n_pipe)
-    other = other_core(other, n_dp)
-    grad_low, mine, other = lax.optimization_barrier((grad_low, mine, other))
-    arrived_high = between_chips(added(mine, other, mine.shape[0]), n_dp)
 
     packs = run(
         backward_kernel(first, middle, width, inner, n_pipe),
@@ -673,13 +673,13 @@
         gram_in_low,
     )[0]
     packs = swap(packs, "pipe")
-    grads, mine, other, _ = run(
-        grads_kernel(first, middle, first, inner, chunk, n_dp, 0),
+    grads, _, mine, other = run(
+        grads_kernel(first, middle, first, inner, chunk, n_dp, 0, True),
         [
             ((n_pipe, tok_rows, chunk), jnp.bfloat16),
-            (packed_shape(count), jnp.bfloat16),
-            (packed_shape(count), jnp.bfloat16),
             ((tok_rows, chunk), jnp.float32),
+            (packed_shape(count, n_dp // 2), jnp.bfloat16),
+            (packed_shape(count, n_dp // 2), jnp.bfloat16),
         ],
         place,
         rows,
@@ -702,13 +702,11 @@
         )
         return sum_in, sum_out.reshape(group, -1, LANES)
 
-    high = unpacked(arrived_high, last - middle)
-    mine, other, high = lax.optimization_barrier((mine, other, high))
     blocks = added(mine, other_core(other, n_dp), mine.shape[0])
     arrived_low = between_chips(blocks, n_dp)
     input_grads = swap(grads, "pipe")
     input_grads, arrived_low = lax.optimization_barrier((input_grads, arrived_low))
-    ins, outs = zip(unpacked(arrived_low, count), high)
+    ins, outs = zip(unpacked(arrived_low, count), unpacked([packed], last - middle))
     grad_out = swap(jnp.concatenate(outs, axis=0), "pipe")
     grad_in = move_in(*ins, n_pipe, n_dp)
     is_high = (me >= middle).astype(jnp.int32).reshape(1)

time: 619 us -> 592 us (0.956)
  starting transfers between devices: 119 us -> 74.7 us
  Pallas kernels: 84.6 us -> 53 us
  blocking collectives: 142 us -> 168 us
  local copies, waits for them, and re-layouts: 16.6 us -> 41.5 us
    pallas_call x14 -> x13, Pallas kernels: 78.7 us -> 49.9 us  [run(): pl.pallas_call(kernel, out_shape=[jax.ShapeDtypeStruct(shape, kind) for s...]
    all_to_all x6 -> x7, blocking collectives: 142 us -> 168 us  [swap(): return lax.all_to_all(x, axis, 0, 0, tiled=True)]
    unnamed x77 -> x103, local copies, waits for them, and re-layouts: 8.55 us -> 34.2 us
    ppermute x14 -> x7, starting transfers between devices: 34.3 us -> 9.4 us  [between_chips(): arrived.append(lax.ppermute(block, 'dp', pairs))]
    all_to_all x10 -> x9, starting transfers between devices: 73.6 us -> 53.6 us  [swap(): return lax.all_to_all(x, axis, 0, 0, tiled=True)]
    ppermute x14 -> x7, waiting for transfers between devices: 72.2 us -> 64 us  [between_chips(): arrived.append(lax.ppermute(block, 'dp', pairs))]
    all_to_all x10 -> x9, waiting for transfers between devices: 83.9 us -> 83.9 us  [swap(): return lax.all_to_all(x, axis, 0, 0, tiled=True)]
  transfers between devices with their start and end apart: 34 -> 26, of which waited for: 18 -> 16; matrix products, arithmetic and copies ran while one was open for 9% -> 9% of each run, Pallas kernels for 6% -> 6%
where the time goes in v10:
time: 592 us; the launch traced here: 589 us
  waiting for transfers between devices  192 us (32%)
  blocking collectives  168 us (28%)
  starting transfers between devices  74.7 us (13%)
  Pallas kernels  53 us (9%)
  local copies, waits for them, and re-layouts  41.5 us (7%)
  matrix products  35.7 us (6%)
  between operations  14.7 us (2%)
  other arithmetic  9.29 us (2%)
    all_to_all x7, blocking collectives, swap(): return lax.all_to_all(x, axis, 0, 0, tiled=True)  168 us
    all_to_all x9, waiting for transfers between devices, swap(): return lax.all_to_all(x, axis, 0, 0, tiled=True)  83.9 us
    ppermute x7, waiting for transfers between devices, between_chips(): arrived.append(lax.ppermute(block, 'dp', pairs))  64 us
    all_to_all x9, starting transfers between devices, swap(): return lax.all_to_all(x, axis, 0, 0, tiled=True)  53.6 us
    pallas_call x13, Pallas kernels, run(): pl.pallas_call(kernel, out_shape=[jax.ShapeDtypeStruct(shape, kind) for s...  49.9 us
    dot_general x23, matrix products, dot(): lax.dot_general(left, right, (dims, ((), ())), preferred_element_type=jnp...  35.7 us
    unnamed x103, local copies, waits for them, and re-layouts  34.2 us
    all_gather x1, waiting for transfers between devices, on_device(): all_in = lax.all_gather(piece_in, 'dp', axis=0, tiled=True)  19.1 us
  transfers between devices with their start and end apart: 26, of which 16 were waited for; matrix products, arithmetic and copies ran while one was open for 9% of the time, Pallas kernels for 6%

profile of v10, /device:TPU:1, one launch (start us, length us, event | category | flops | bytes accessed | tf_op | source)
XLA Modules:
  0.0 588.6 jit_solution(16113917509127933129)
XLA Ops:
  11.2 37.5 %all_to_all.125 = bf16[8,32,640]{2,1,0:T(8,128)(2,1)S(1)} all-to-all(bf16[8,32,640]{2,1,0:T(8,128)(2,1)S(1)} %copy.30), channel_id=1, replica_groups=mesh['pipe'=8,'dp'=16] {'pipe'}, dimensions={0} | all-to-all | bytes 655360 | tf_op jit(solution)/shard_map/all_to_all | solution.py:31
  54.2 19.1 %all-gather.8.cloned.1.call-done.in_ref.refs_5_ = bf16[5120,512]{1,0:T(8,128)(2,1)} async-done(((bf16[320,512]{1,0:T(8,128)(2,1)}), bf16[5120,512]{1,0:T(8,128)(2,1)}) %all-gather.8.cloned.1.call-update) | async-done | bytes 5242896 | tf_op jit(solution)/shard_map/all_gather | solution.py:534
  82.2 6.4 %all-to-all-start.1 = ((bf16[8,48,512]{2,1,0:T(8,128)(2,1)}), bf16[8,48,512]{2,1,0:T(8,128)(2,1)}, u32[]{:S(2)}, u32[]{:S(2)}) async-start(bf16[8,48,512]{2,1,0:T(8,128)(2,1)} %bitcast.130), calls=%async_computation.1 | async-start | bytes 786432 | tf_op jit(solution)/shard_map/all_to_all | solution.py:31
  88.6 2.2 convolution_convert_fusion.2
  90.7 2.2 convolution_convert_fusion.1
  92.9 5.2 all-to-all-done.1
  99.9 4.2 all-to-all-start.2
  104.1 2.2 convolution_convert_fusion
  106.3 2.2 convolution_convert_fusion.3
  108.4 3.1 concatenate.39
  113.2 5.1 all-to-all-start.3
  119.8 2.4 all-gather.6.cloned.1.call-done.out_ref.refs_6_
  122.2 12.5 %all-to-all-done.3.down_ref = bf16[8,32,2176]{2,1,0:T(8,128)(2,1)} async-done(((bf16[8,32,2176]{2,1,0:T(8,128)(2,1)}), bf16[8,32,2176]{2,1,0:T(8,128)(2,1)}, u32[]{:S(2)}, u32[]{:S(2)}) %all-to-all-start.3) | async-done | bytes 1114144 | tf_op jit(solution)/shard_map/all_to_all | solution.py:31
  143.3 12.2 %all_to_all.126 = bf16[8,48,512]{2,1,0:T(8,128)(2,1)S(1)} all-to-all(bf16[8,48,512]{2,1,0:T(8,128)(2,1)S(1)} %bitcast.129), channel_id=1, replica_groups=mesh['pipe'=8,'dp'=16] {'pipe'}, dimensions={0} | all-to-all | bytes 786432 | tf_op jit(solution)/shard_map/all_to_all | solution.py:31
  155.6 12.9 %all_to_all.127 = bf16[8,48,512]{2,1,0:T(8,128)(2,1)S(1)} all-to-all(bf16[8,48,512]{2,1,0:T(8,128)(2,1)S(1)} %tile.5), channel_id=1, replica_groups=mesh['pipe'=8,'dp'=16] {'pipe'}, dimensions={0} | all-to-all | bytes 786432 | tf_op jit(solution)/shard_map/all_to_all | solution.py:31
  177.0 4.9 all-to-all-start.6
  186.4 8.1 %all-to-all-done.6.up_ref = bf16[8,32,1536]{2,1,0:T(8,128)(2,1)S(1)} async-done(((bf16[8,32,1536]{2,1,0:T(8,128)(2,1)}), bf16[8,32,1536]{2,1,0:T(8,128)(2,1)S(1)}, u32[]{:S(2)}, u32[]{:S(2)}) %all-to-all-start.6) | async-done | bytes 786464 | tf_op jit(solution)/shard_map/all_to_all | solution.py:31
  195.6 6.0 %all-to-all-start.7 = ((bf16[8,32,2048]{2,1,0:T(8,128)(2,1)}), bf16[8,32,2048]{2,1,0:T(8,128)(2,1)S(1)}, u32[]{:S(2)}, u32[]{:S(2)}) async-start(bf16[8,32,2048]{2,1,0:T(8,128)(2,1)} %bitcast.123), calls=%async_computation.7 | async-start | bytes 2097152 | tf_op jit(solution)/shard_map/all_to_all | solution.py:31
  202.4 17.0 %all-to-all-done.7.grad_ref = bf16[8,32,2048]{2,1,0:T(8,128)(2,1)S(1)} async-done(((bf16[8,32,2048]{2,1,0:T(8,128)(2,1)}), bf16[8,32,2048]{2,1,0:T(8,128)(2,1)S(1)}, u32[]{:S(2)}, u32[]{:S(2)}) %all-to-all-start.7) | async-done | bytes 1048608 | tf_op jit(solution)/shard_map/all_to_all | solution.py:31
  219.4 4.9 all-gather.12.cloned.1.call-done.gram_out_ref
  224.4 5.1 shard_map.153
  230.3 25.1 %all_to_all.128 = bf16[8,32,2048]{2,1,0:T(8,128)(2,1)S(1)} all-to-all(bf16[8,32,2048]{2,1,0:T(8,128)(2,1)S(1)} %bitcast.115), channel_id=1, replica_groups=mesh['pipe'=8,'dp'=16] {'pipe'}, dimensions={0} | all-to-all | bytes 2097152 | tf_op jit(solution)/shard_map/all_to_all | solution.py:31
  255.4 6.2 %shard_map.154 = (f32[256,640]{1,0:T(8,128)S(1)}, bf16[256,3712]{1,0:T(8,128)(2,1)S(1)}) custom-call(bf16[256,640]{1,0:T(8,128)(2,1)S(1)} %get-tuple-element.136.rows_ref.refs_1_, bf16[256,2048]{1,0:T(8,128)(2,1)S(1)} %bitcast.104, bf16[5120,512]{1,0:T(8,128)(2,1)} %all-gather.8.cloned.1.call-done.in_ref.refs_5_, ...), custom_call_target="tpu_custom_call" | custom-call | tf_op jit(solution)/shard_map/pallas_call | solution.py:71
  262.5 33.5 %all_to_all.129.sums_ref = bf16[8,32,3712]{2,1,0:T(8,128)(2,1)S(1)} all-to-all(bf16[8,32,3712]{2,1,0:T(8,128)(2,1)S(1)} %bitcast.111), channel_id=1, replica_groups=mesh['pipe'=8,'dp'=16] {'pipe'}, dimensions={0} | all-to-all | bytes 3801088 | tf_op jit(solution)/shard_map/all_to_all | solution.py:31
  295.9 6.9 %all-gather.14.cloned.1.call-done.gram_ref = bf16[512,6144]{1,0:T(8,128)(2,1)} async-done(((bf16[32,6144]{1,0:T(8,128)(2,1)}), bf16[512,6144]{1,0:T(8,128)(2,1)}) %all-gather.14.cloned.1.call-update) | async-done | bytes 6291472 | tf_op jit(solution)/shard_map/all_gather | solution.py:562
  302.8 6.0 %shard_map.155 = bf16[256,4224]{1,0:T(8,128)(2,1)S(1)} custom-call(bf16[8,32,3712]{2,1,0:T(8,128)(2,1)S(1)} %all_to_all.129.sums_ref, bf16[8,32,2048]{2,1,0:T(8,128)(2,1)S(1)} %all-to-all-done.7.grad_ref, bf16[512,6144]{1,0:T(8,128)(2,1)} %all-gather.14.cloned.1.call-done.gram_ref), custom_call_target="tpu_custom_call" | custom-call | tf_op jit(solution)/shard_map/pallas_call | solution.py:71
  310.2 6.9 %all-to-all-start.10 = ((bf16[8,32,4224]{2,1,0:T(8,128)(2,1)}), bf16[8,32,4224]{2,1,0:T(8,128)(2,1)S(1)}, u32[]{:S(2)}, u32[]{:S(2)}) async-start(bf16[8,32,4224]{2,1,0:T(8,128)(2,1)} %bitcast.106), calls=%async_computation.10 | async-start | bytes 4325376 | tf_op jit(solution)/shard_map/all_to_all | solution.py:31
  317.3 31.7 %all-to-all-done.10 = bf16[8,32,4224]{2,1,0:T(8,128)(2,1)S(1)} async-done(((bf16[8,32,4224]{2,1,0:T(8,128)(2,1)}), bf16[8,32,4224]{2,1,0:T(8,128)(2,1)S(1)}, u32[]{:S(2)}, u32[]{:S(2)}) %all-to-all-start.10) | async-done | bytes 2162720 | tf_op jit(solution)/shard_map/all_to_all | solution.py:31
  351.0 9.5 %shard_map.156 = (bf16[4,256,640]{2,1,0:T(8,128)(2,1)S(1)}, f32[256,640]{1,0:T(8,128)S(1)}, bf16[16,1280,128]{2,1,0:T(8,128)(2,1)}, bf16[256,2048]{1,0:T(8,128)(2,1)S(1)}) custom-call(s32[9]{0:T(128)S(1)} %pad_add_fusion.refs_0_, f32[256,640]{1,0:T(8,128)S(1)} %copy-done.20, bf16[256,4224]{1,0:T(8,128)(2,1)S(1)} %bitcast.102, ...), custom_call_target="tpu_custom_call" | custom-call | tf_op jit(solution)/shard_map/pallas_call | solution.py:71
  363.5 20.9 %all_to_all.130.grad_ref = bf16[8,32,2048]{2,1,0:T(8,128)(2,1)S(1)} all-to-all(bf16[8,32,2048]{2,1,0:T(8,128)(2,1)} %bitcast.114), channel_id=1, replica_groups=mesh['pipe'=8,'dp'=16] {'pipe'}, dimensions={0} | all-to-all | bytes 2097152 | tf_op jit(solution)/shard_map/all_to_all | solution.py:31
  387.6 25.9 %all_to_all.131 = bf16[8,32,2176]{2,1,0:T(8,128)(2,1)S(1)} all-to-all(bf16[8,32,2176]{2,1,0:T(8,128)(2,1)S(1)} %bitcast.108), channel_id=1, replica_groups=mesh['pipe'=8,'dp'=16] {'pipe'}, dimensions={0} | all-to-all | bytes 2228224 | tf_op jit(solution)/shard_map/all_to_all | solution.py:31
  413.5 12.2 %shard_map.158 = (bf16[8,256,640]{2,1,0:T(8,128)(2,1)}, f32[256,640]{1,0:T(8,128)}, bf16[8,1280,128]{2,1,0:T(8,128)(2,1)}, bf16[8,1280,128]{2,1,0:T(8,128)(2,1)}) custom-call(s32[9]{0:T(128)S(1)} %pad_add_fusion.refs_0_, bf16[256,640]{1,0:T(8,128)(2,1)S(1)} %get-tuple-element.136.rows_ref.refs_1_, bf16[256,2176]{1,0:T(8,128)(2,1)S(1)} %bitcast.107, ...), custom_call_target="tpu_custom_call" | custom-call | tf_op jit(solution)/shard_map/pallas_call | solution.py:71
  426.9 3.9 all-to-all-start.13
  432.0 1.8 copy-done.8
  433.8 3.0 shard_map.159
  438.3 2.9 collective-permute-start.4
  443.9 53.2 %collective-permute-done.2.refs_1_ = bf16[1280,128]{1,0:T(8,128)(2,1)S(1)} collective-permute-done((bf16[1280,128]{1,0:T(8,128)(2,1)S(1)}, bf16[1280,128]{1,0:T(8,128)(2,1)S(1)}, u32[]{:S(2)}, u32[]{:S(2)}) %collective-permute-start.2) | collective-permute-done | bytes 327712 | tf_op jit(solution)/shard_map/ppermute | solution.py:491
  497.8 2.2 collective-permute-start.7
  503.1 3.8 collective-permute-done.7.refs_6_
  506.9 7.0 %collective-permute-done.8.refs_7_ = bf16[1280,128]{1,0:T(8,128)(2,1)} collective-permute-done((bf16[1280,128]{1,0:T(8,128)(2,1)}, bf16[1280,128]{1,0:T(8,128)(2,1)}, u32[]{:S(2)}, u32[]{:S(2)}) %collective-permute-start.8) | collective-permute-done | bytes 327712 | tf_op jit(solution)/shard_map/ppermute | solution.py:491
  520.4 6.9 %all-to-all-start.14 = ((bf16[8,160,128]{2,1,0:T(8,128)(2,1)}), bf16[8,160,128]{2,1,0:T(8,128)(2,1)S(1)}, u32[]{:S(2)}, u32[]{:S(2)}) async-start(bf16[8,160,128]{2,1,0:T(8,128)(2,1)} %pad_maximum_fusion.3), calls=%async_computation.15 | async-start | bytes 655360 | tf_op jit(solution)/shard_map/all_to_all | solution.py:31
  528.9 8.1 %collective-permute-start.9 = (bf16[160,512]{1,0:T(8,128)(2,1)S(1)}, bf16[160,512]{1,0:T(8,128)(2,1)S(1)}, u32[]{:S(2)}, u32[]{:S(2)}) collective-permute-start(bf16[160,512]{1,0:T(8,128)(2,1)S(1)} %get-tuple-element.138), channel_id=1, source_target_pairs={{0,0},{1,64},{2,1},{3,65},{4,16},{5,80},{6,17},{7,81},{8,32},{9,96... | collective-permute-start | bytes 491528 | tf_op jit(solution)/shard_map/ppermute | solution.py:506
  537.0 9.1 %collective-permute-done.9.refs_1_ = bf16[160,512]{1,0:T(8,128)(2,1)S(1)} collective-permute-done((bf16[160,512]{1,0:T(8,128)(2,1)S(1)}, bf16[160,512]{1,0:T(8,128)(2,1)S(1)}, u32[]{:S(2)}, u32[]{:S(2)}) %collective-permute-start.9) | collective-permute-done | bytes 163872 | tf_op jit(solution)/shard_map/ppermute | solution.py:506
  555.0 2.9 shard_map.163
  558.8 9.3 %all-to-all-start.15 = ((bf16[16,2,32,320]{3,2,1,0:T(8,128)(2,1)}), bf16[16,2,32,320]{3,2,1,0:T(8,128)(2,1)S(1)}, u32[]{:S(2)}, u32[]{:S(2)}) async-start(bf16[16,2,32,320]{3,2,1,0:T(8,128)(2,1)} %copy-done.18), calls=%async_computation.16 | async-start | bytes 1572864 | tf_op jit(solution)/shard_map/all_to_all | solution.py:31
  568.1 1.7 copy-done.4
  569.8 3.1 shard_map.160
  572.9 7.8 %all-to-all-done.15.pieces_ref = bf16[16,2,32,320]{3,2,1,0:T(8,128)(2,1)S(1)} async-done(((bf16[16,2,32,320]{3,2,1,0:T(8,128)(2,1)}), bf16[16,2,32,320]{3,2,1,0:T(8,128)(2,1)S(1)}, u32[]{:S(2)}, u32[]{:S(2)}) %all-to-all-start.15) | async-done | bytes 655392 | tf_op jit(solution)/shard_map/all_to_all | solution.py:31
  (184 shorter events, 87.0 us)
Async XLA Ops:
  7.2 162.7 %copy-start = (bf16[256,5120]{1,0:T(8,128)(2,1)S(1)}, bf16[256,5120]{1,0:T(8,128)(2,1)}, u32[]{:S(2)}) copy-start(bf16[256,5120]{1,0:T(8,128)(2,1)} %param.9) | copy-start | bytes 7864324
  7.2 66.1 %all-gather.8.cloned.1.call-start = ((), (), s32[]{:S(2)}) async-start(), calls=%async_computation.18 | async-start | bytes 5570560 | tf_op jit(solution)/shard_map/all_gather | solution.py:534
  8.5 0.7 collective-permute-start
  10.0 112.2 %all-gather.6.cloned.1.call-start = ((), (), s32[]{:S(2)}) async-start(), calls=%async_computation.17 | async-start | bytes 5570560 | tf_op jit(solution)/shard_map/all_gather | solution.py:535
  48.8 41.9 %copy-start.45 = (bf16[8,32,640]{2,1,0:T(8,128)(2,1)}, bf16[8,32,640]{2,1,0:T(8,128)(2,1)S(1)}, u32[]{:S(2)}) copy-start(bf16[8,32,640]{2,1,0:T(8,128)(2,1)S(1)} %all_to_all.125) | copy-start | bytes 983044
  54.2 45.7 %copy-start.48 = (bf16[3,32,640]{2,1,0:T(8,128)(2,1)}, bf16[3,32,640]{2,1,0:T(8,128)(2,1)S(1)}, u32[]{:S(2)}) copy-start(bf16[3,32,640]{2,1,0:T(8,128)(2,1)S(1)} %get-tuple-element.139) | copy-start | bytes 368644
  82.2 15.9 %all-to-all-start.1 = ((bf16[8,48,512]{2,1,0:T(8,128)(2,1)}), bf16[8,48,512]{2,1,0:T(8,128)(2,1)}, u32[]{:S(2)}, u32[]{:S(2)}) async-start(bf16[8,48,512]{2,1,0:T(8,128)(2,1)} %bitcast.130), calls=%async_computation.1 | async-start | bytes 786432 | tf_op jit(solution)/shard_map/all_to_all | solution.py:31
  99.9 13.3 %all-to-all-start.2 = ((bf16[8,48,512]{2,1,0:T(8,128)(2,1)}), bf16[8,48,512]{2,1,0:T(8,128)(2,1)S(1)}, u32[]{:S(2)}, u32[]{:S(2)}) async-start(bf16[8,48,512]{2,1,0:T(8,128)(2,1)} %tile.4), calls=%async_computation.2 | async-start | bytes 786432 | tf_op jit(solution)/shard_map/all_to_all | solution.py:31
  111.6 28.9 %copy-start.50 = (bf16[2,32,640]{2,1,0:T(8,128)(2,1)S(1)}, bf16[2,32,640]{2,1,0:T(8,128)(2,1)}, u32[]{:S(2)}) copy-start(bf16[2,32,640]{2,1,0:T(8,128)(2,1)} %get-tuple-element.141) | copy-start | bytes 245764
  111.6 30.3 %copy-start.49 = (bf16[3,32,640]{2,1,0:T(8,128)(2,1)S(1)}, bf16[3,32,640]{2,1,0:T(8,128)(2,1)}, u32[]{:S(2)}) copy-start(bf16[3,32,640]{2,1,0:T(8,128)(2,1)} %copy-done.48) | copy-start | bytes 368644
  113.2 21.5 %all-to-all-start.3 = ((bf16[8,32,2176]{2,1,0:T(8,128)(2,1)}), bf16[8,32,2176]{2,1,0:T(8,128)(2,1)}, u32[]{:S(2)}, u32[]{:S(2)}) async-start(bf16[8,32,2176]{2,1,0:T(8,128)(2,1)} %concatenate.39), calls=%async_computation.3 | async-start | bytes 2228224 | tf_op jit(solution)/shard_map/all_to_all | solution.py:31
  118.4 101.0 %all-gather.10.cloned.1.call-start = ((), (), s32[]{:S(2)}) async-start(), calls=%async_computation.19 | async-start | bytes 3342336 | tf_op jit(solution)/shard_map/all_gather | solution.py:562
  134.7 89.6 %all-gather.12.cloned.1.call-start = ((), (), s32[]{:S(2)}) async-start(), calls=%async_computation.20 | async-start | bytes 3342336 | tf_op jit(solution)/shard_map/all_gather | solution.py:562
  170.0 14.9 %copy-start.15 = (bf16[256,640]{1,0:T(8,128)(2,1)}, bf16[256,640]{1,0:T(8,128)(2,1)S(1)}, u32[]{:S(2)}) copy-start(bf16[256,640]{1,0:T(8,128)(2,1)S(1)} %constant_dynamic-slice_fusion.refs_4_) | copy-start | bytes 983044
  177.0 24.6 %copy-start.40 = (bf16[32,3072]{1,0:T(8,128)(2,1)S(1)}, bf16[32,3072]{1,0:T(8,128)(2,1)}, u32[]{:S(2)}) copy-start(bf16[32,3072]{1,0:T(8,128)(2,1)} %copy-done.39) | copy-start | bytes 589828
  177.0 24.7 %copy-start.42 = (bf16[32,3072]{1,0:T(8,128)(2,1)S(1)}, bf16[32,3072]{1,0:T(8,128)(2,1)}, u32[]{:S(2)}) copy-start(bf16[32,3072]{1,0:T(8,128)(2,1)} %copy-done.41) | copy-start | bytes 589828
  177.0 17.5 %all-to-all-start.6 = ((bf16[8,32,1536]{2,1,0:T(8,128)(2,1)}), bf16[8,32,1536]{2,1,0:T(8,128)(2,1)S(1)}, u32[]{:S(2)}, u32[]{:S(2)}) async-start(bf16[8,32,1536]{2,1,0:T(8,128)(2,1)} %bitcast.24), calls=%async_computation.6 | async-start | bytes 1572864 | tf_op jit(solution)/shard_map/all_to_all | solution.py:31
  195.6 23.8 %all-to-all-start.7 = ((bf16[8,32,2048]{2,1,0:T(8,128)(2,1)}), bf16[8,32,2048]{2,1,0:T(8,128)(2,1)S(1)}, u32[]{:S(2)}, u32[]{:S(2)}) async-start(bf16[8,32,2048]{2,1,0:T(8,128)(2,1)} %bitcast.123), calls=%async_computation.7 | async-start | bytes 2097152 | tf_op jit(solution)/shard_map/all_to_all | solution.py:31
  201.6 101.2 %all-gather.14.cloned.1.call-start = ((), (), s32[]{:S(2)}) async-start(), calls=%async_computation.21 | async-start | bytes 6684672 | tf_op jit(solution)/shard_map/all_gather | solution.py:562
  230.3 25.1 %copy-start.36 = (f32[4,32,512]{2,1,0:T(8,128)}, f32[4,32,512]{2,1,0:T(8,128)S(1)}, u32[]{:S(2)}) copy-start(f32[4,32,512]{2,1,0:T(8,128)S(1)} %get-tuple-element.96.hidden_ref) | copy-start | bytes 786436
  255.4 6.2 %copy-start.5 = (bf16[8,32,2048]{2,1,0:T(8,128)(2,1)}, bf16[8,32,2048]{2,1,0:T(8,128)(2,1)S(1)}, u32[]{:S(2)}) copy-start(bf16[8,32,2048]{2,1,0:T(8,128)(2,1)S(1)} %all_to_all.128) | copy-start | bytes 3145732
  308.8 1.3 copy-start.7
  310.2 38.8 %all-to-all-start.10 = ((bf16[8,32,4224]{2,1,0:T(8,128)(2,1)}), bf16[8,32,4224]{2,1,0:T(8,128)(2,1)S(1)}, u32[]{:S(2)}, u32[]{:S(2)}) async-start(bf16[8,32,4224]{2,1,0:T(8,128)(2,1)} %bitcast.106), calls=%async_computation.10 | async-start | bytes 4325376 | tf_op jit(solution)/shard_map/all_to_all | solution.py:31
  317.1 201.5 %reduce-scatter.2.cloned.1.call-start = ((), (), s32[]{:S(2)}) async-start(), calls=%async_computation.22 | async-start | bytes 5570560 | tf_op jit(solution)/shard_map/reduce_scatter | solution.py:663
  363.4 20.9 %copy-start.2 = (bf16[512,3072]{1,0:T(8,128)(2,1)S(1)}, bf16[512,3072]{1,0:T(8,128)(2,1)}, u32[]{:S(2)}) copy-start(bf16[512,3072]{1,0:T(8,128)(2,1)} %all-gather.10.cloned.1.call-done.gram_in_ref.gram_ref) | copy-start | bytes 9437188
  363.4 50.1 %copy-start.6 = (bf16[8,32,2048]{2,1,0:T(8,128)(2,1)S(1)}, bf16[8,32,2048]{2,1,0:T(8,128)(2,1)}, u32[]{:S(2)}) copy-start(bf16[8,32,2048]{2,1,0:T(8,128)(2,1)} %copy-done.5) | copy-start | bytes 3145732
  363.4 50.1 %copy-start.14 = (bf16[4,256,640]{2,1,0:T(8,128)(2,1)S(1)}, bf16[4,256,640]{2,1,0:T(8,128)(2,1)}, u32[]{:S(2)}) copy-start(bf16[4,256,640]{2,1,0:T(8,128)(2,1)} %copy-done.13) | copy-start | bytes 3932164
  363.4 50.1 %copy-start.22 = (f32[256,640]{1,0:T(8,128)S(1)}, f32[256,640]{1,0:T(8,128)}, u32[]{:S(2)}) copy-start(f32[256,640]{1,0:T(8,128)} %copy-done.21) | copy-start | bytes 1966084
  425.8 6.3 %collective-permute-start.1 = (bf16[8,1280,128]{2,1,0:T(8,128)(2,1)}, bf16[8,1280,128]{2,1,0:T(8,128)(2,1)}, u32[]{:S(2)}, u32[]{:S(2)}) collective-permute-start(bf16[8,1280,128]{2,1,0:T(8,128)(2,1)} %get-tuple-element.103), channel_id=1, source_target_pairs={{0,1},{1,0},{2,3},{3,2},{4,5},{5,4},{6,7},{7,6},{8,9},{9,8},{10,11... | collective-permute-start | bytes 7864328 | tf_op jit(solution)/shard_map/ppermute | solution.py:463
  426.9 120.6 %copy-start.9 = (f32[1,320,512]{2,1,0:T(8,128)S(1)}, f32[1,320,512]{2,1,0:T(8,128)}, u32[]{:S(2)}) copy-start(f32[1,320,512]{2,1,0:T(8,128)} %param.10) | copy-start | bytes 1966084
  426.9 74.6 %all-to-all-start.13 = ((bf16[8,256,640]{2,1,0:T(8,128)(2,1)}), bf16[8,256,640]{2,1,0:T(8,128)(2,1)S(1)}, u32[]{:S(2)}, u32[]{:S(2)}) async-start(bf16[8,256,640]{2,1,0:T(8,128)(2,1)} %get-tuple-element.101), calls=%async_computation.13 | async-start | bytes 5242880 | tf_op jit(solution)/shard_map/all_to_all | solution.py:31
  432.0 1.8 copy-start.8
  437.5 59.6 %collective-permute-start.2 = (bf16[1280,128]{1,0:T(8,128)(2,1)S(1)}, bf16[1280,128]{1,0:T(8,128)(2,1)S(1)}, u32[]{:S(2)}, u32[]{:S(2)}) collective-permute-start(bf16[1280,128]{1,0:T(8,128)(2,1)S(1)} %get-tuple-element.105), channel_id=1, source_target_pairs={{0,2},{1,3},{2,0},{3,1},{4,6},{5,7},{6,4},{7,5},{8,10},{9,11},{10,... | collective-permute-start | bytes 983048 | tf_op jit(solution)/shard_map/ppermute | solution.py:491
  437.8 62.2 %collective-permute-start.3 = (bf16[1280,128]{1,0:T(8,128)(2,1)S(1)}, bf16[1280,128]{1,0:T(8,128)(2,1)S(1)}, u32[]{:S(2)}, u32[]{:S(2)}) collective-permute-start(bf16[1280,128]{1,0:T(8,128)(2,1)S(1)} %get-tuple-element.106), channel_id=1, source_target_pairs={{0,4},{1,5},{2,6},{3,7},{4,8},{5,9},{6,10},{7,11},{8,12},{9,13},{1... | collective-permute-start | bytes 983048 | tf_op jit(solution)/shard_map/ppermute | solution.py:491
  438.3 64.8 %collective-permute-start.4 = (bf16[1280,128]{1,0:T(8,128)(2,1)}, bf16[1280,128]{1,0:T(8,128)(2,1)}, u32[]{:S(2)}, u32[]{:S(2)}) collective-permute-start(bf16[1280,128]{1,0:T(8,128)(2,1)} %get-tuple-element.107), channel_id=1, source_target_pairs={{0,6},{1,7},{2,4},{3,5},{4,10},{5,11},{6,8},{7,9},{8,14},{9,15},{1... | collective-permute-start | bytes 983048 | tf_op jit(solution)/shard_map/ppermute | solution.py:491
  441.2 61.8 %collective-permute-start.5 = (bf16[1280,128]{1,0:T(8,128)(2,1)}, bf16[1280,128]{1,0:T(8,128)(2,1)}, u32[]{:S(2)}, u32[]{:S(2)}) collective-permute-start(bf16[1280,128]{1,0:T(8,128)(2,1)} %get-tuple-element.108), channel_id=1, source_target_pairs={{0,8},{1,9},{2,10},{3,11},{4,12},{5,13},{6,14},{7,15},{8,0},{9,1},... | collective-permute-start | bytes 983048 | tf_op jit(solution)/shard_map/ppermute | solution.py:491
  442.7 60.3 %collective-permute-start.6 = (bf16[1280,128]{1,0:T(8,128)(2,1)}, bf16[1280,128]{1,0:T(8,128)(2,1)}, u32[]{:S(2)}, u32[]{:S(2)}) collective-permute-start(bf16[1280,128]{1,0:T(8,128)(2,1)} %get-tuple-element.109), channel_id=1, source_target_pairs={{0,10},{1,11},{2,8},{3,9},{4,14},{5,15},{6,12},{7,13},{8,2},{9,3},... | collective-permute-start | bytes 983048 | tf_op jit(solution)/shard_map/ppermute | solution.py:491
  497.8 9.1 %collective-permute-start.7 = (bf16[1280,128]{1,0:T(8,128)(2,1)}, bf16[1280,128]{1,0:T(8,128)(2,1)}, u32[]{:S(2)}, u32[]{:S(2)}) collective-permute-start(bf16[1280,128]{1,0:T(8,128)(2,1)} %get-tuple-element.110), channel_id=1, source_target_pairs={{0,12},{1,13},{2,14},{3,15},{4,0},{5,1},{6,2},{7,3},{8,4},{9,5},{1... | collective-permute-start | bytes 983048 | tf_op jit(solution)/shard_map/ppermute | solution.py:491
  500.7 13.2 %collective-permute-start.8 = (bf16[1280,128]{1,0:T(8,128)(2,1)}, bf16[1280,128]{1,0:T(8,128)(2,1)}, u32[]{:S(2)}, u32[]{:S(2)}) collective-permute-start(bf16[1280,128]{1,0:T(8,128)(2,1)} %get-tuple-element.111), channel_id=1, source_target_pairs={{0,14},{1,15},{2,12},{3,13},{4,2},{5,3},{6,0},{7,1},{8,6},{9,7},{1... | collective-permute-start | bytes 983048 | tf_op jit(solution)/shard_map/ppermute | solution.py:491
  501.6 1.5 copy-start.3
  520.4 26.5 %all-to-all-start.14 = ((bf16[8,160,128]{2,1,0:T(8,128)(2,1)}), bf16[8,160,128]{2,1,0:T(8,128)(2,1)S(1)}, u32[]{:S(2)}, u32[]{:S(2)}) async-start(bf16[8,160,128]{2,1,0:T(8,128)(2,1)} %pad_maximum_fusion.3), calls=%async_computation.15 | async-start | bytes 655360 | tf_op jit(solution)/shard_map/all_to_all | solution.py:31
  527.3 9.7 %collective-permute-start.10 = (bf16[160,512]{1,0:T(8,128)(2,1)S(1)}, bf16[160,512]{1,0:T(8,128)(2,1)S(1)}, u32[]{:S(2)}, u32[]{:S(2)}) collective-permute-start(bf16[160,512]{1,0:T(8,128)(2,1)S(1)} %get-tuple-element.137), channel_id=1, source_target_pairs={{0,64},{1,0},{2,65},{3,1},{4,80},{5,16},{6,81},{7,17},{8,96},{9,32... | collective-permute-start | bytes 491528 | tf_op jit(solution)/shard_map/ppermute | solution.py:506
  528.9 17.3 %collective-permute-start.9 = (bf16[160,512]{1,0:T(8,128)(2,1)S(1)}, bf16[160,512]{1,0:T(8,128)(2,1)S(1)}, u32[]{:S(2)}, u32[]{:S(2)}) collective-permute-start(bf16[160,512]{1,0:T(8,128)(2,1)S(1)} %get-tuple-element.138), channel_id=1, source_target_pairs={{0,0},{1,64},{2,1},{3,65},{4,16},{5,80},{6,17},{7,81},{8,32},{9,96... | collective-permute-start | bytes 491528 | tf_op jit(solution)/shard_map/ppermute | solution.py:506
  547.6 34.2 %copy-start.1 = (bf16[256,5120]{1,0:T(8,128)(2,1)S(1)}, bf16[256,5120]{1,0:T(8,128)(2,1)}, u32[]{:S(2)}) copy-start(bf16[256,5120]{1,0:T(8,128)(2,1)} %param.9) | copy-start | bytes 7864324
  547.6 1.2 copy-start.10
  549.8 1.1 copy-start.23
  558.8 21.9 %all-to-all-start.15 = ((bf16[16,2,32,320]{3,2,1,0:T(8,128)(2,1)}), bf16[16,2,32,320]{3,2,1,0:T(8,128)(2,1)S(1)}, u32[]{:S(2)}, u32[]{:S(2)}) async-start(bf16[16,2,32,320]{3,2,1,0:T(8,128)(2,1)} %copy-done.18), calls=%async_computation.16 | async-start | bytes 1572864 | tf_op jit(solution)/shard_map/all_to_all | solution.py:31
  568.1 1.7 copy-start.4
  (29 other events, 25.5 us)
Sparse Core Ops, SparseCore 0:
  10.3 62.9 all-gather.7
  75.6 46.5 all-gather.5
  134.8 38.6 all-gather.9
  175.6 48.6 all-gather.11
  226.5 76.2 all-gather.13
  363.5 136.5 reduce-scatter.1

commit v11 on v10

--- a/solution.py
+++ b/solution.py
@@ -16,6 +16,7 @@
 BLOCKS = ((0, 4), (4, 8))
 LANES = 128
 VMEM_BYTES = 48 * 1024 * 1024
+VMEM_ALMOST_ALL = 60 * 1024 * 1024
 
 
 def dot(left, right, dims):
@@ -58,7 +59,7 @@
     return (master_new, moment_new, second_new)
 
 
-def run(kernel, shapes, *operands, specs=None, smem=False):
+def run(kernel, shapes, *operands, specs=None, smem=False, vmem=VMEM_BYTES):
     more = {}
     if specs is not None:
         whole = [pl.BlockSpec(x.shape, zeros_map(x.ndim)) for x in operands]
@@ -71,7 +72,7 @@
     return pl.pallas_call(
         kernel,
         out_shape=[jax.ShapeDtypeStruct(shape, kind) for shape, kind in shapes],
-        compiler_params=pltpu.CompilerParams(vmem_limit_bytes=VMEM_BYTES),
+        compiler_params=pltpu.CompilerParams(vmem_limit_bytes=vmem),
         **more,
     )(*operands)
 
@@ -474,7 +475,8 @@
 
 def added(mine, other, count):
     shape = mine.shape if count == 1 else mine.shape[1:]
-    return run(add_kernel, [(shape, jnp.bfloat16)] * count, mine, other)
+    shapes = [(shape, jnp.bfloat16)] * count
+    return run(add_kernel, shapes, mine, other, vmem=VMEM_ALMOST_ALL)
 
 
 def chip_steps(n_dp):
@@ -699,6 +701,7 @@
             unpack_kernel(inner, share, len(arrived)),
             [((share, inner), jnp.bfloat16), ((rows_out, LANES), jnp.bfloat16)],
             *arrived,
+            vmem=VMEM_ALMOST_ALL,
         )
         return sum_in, sum_out.reshape(group, -1, LANES)
 
@@ -727,6 +730,7 @@
         moment_out[0],
         second_out[0],
         smem=True,
+        vmem=VMEM_ALMOST_ALL,
     )
     new_in, new_moment_in, new_second_in, new_out, new_moment_out, new_second_out = updated
     input_grads = columns_in_place(input_grads)[None]

time: 592 us -> 585 us (0.988)
  local copies, waits for them, and re-layouts: 41.5 us -> 24.7 us
  Pallas kernels: 53 us -> 59.2 us
    unnamed x103 -> x75, local copies, waits for them, and re-layouts: 34.2 us -> 17.4 us
    pallas_call x13, Pallas kernels: 49.9 us -> 56.1 us  [run(): pl.pallas_call(kernel, out_shape=[jax.ShapeDtypeStruct(shape, kind) for s...]
where the time goes in v11:
time: 585 us; the launch traced here: 582 us
  waiting for transfers between devices  193 us (33%)
  blocking collectives  168 us (29%)
  starting transfers between devices  75.9 us (13%)
  Pallas kernels  59.2 us (10%)
  matrix products  35.7 us (6%)
  local copies, waits for them, and re-layouts  24.7 us (4%)
  between operations  14.7 us (3%)
  other arithmetic  11.3 us (2%)
    all_to_all x7, blocking collectives, swap(): return lax.all_to_all(x, axis, 0, 0, tiled=True)  168 us
    all_to_all x9, waiting for transfers between devices, swap(): return lax.all_to_all(x, axis, 0, 0, tiled=True)  83.9 us
    ppermute x7, waiting for transfers between devices, between_chips(): arrived.append(lax.ppermute(block, 'dp', pairs))  65.1 us
    pallas_call x13, Pallas kernels, run(): pl.pallas_call(kernel, out_shape=[jax.ShapeDtypeStruct(shape, kind) for s...  56.1 us
    all_to_all x9, starting transfers between devices, swap(): return lax.all_to_all(x, axis, 0, 0, tiled=True)  53.6 us
    dot_general x23, matrix products, dot(): lax.dot_general(left, right, (dims, ((), ())), preferred_element_type=jnp...  35.7 us
    all_gather x1, waiting for transfers between devices, on_device(): all_in = lax.all_gather(piece_in, 'dp', axis=0, tiled=True)  19.1 us
    unnamed x75, local copies, waits for them, and re-layouts  17.4 us
  transfers between devices with their start and end apart: 26, of which 16 were waited for; matrix products, arithmetic and copies ran while one was open for 9% of the time, Pallas kernels for 6%

profile of v11, /device:TPU:1, one launch (start us, length us, event | category | flops | bytes accessed | tf_op | source)
XLA Modules:
  0.0 582.2 jit_solution(9787470139485288070)
XLA Ops:
  11.2 37.5 %all_to_all.125 = bf16[8,32,640]{2,1,0:T(8,128)(2,1)S(1)} all-to-all(bf16[8,32,640]{2,1,0:T(8,128)(2,1)S(1)} %copy.30), channel_id=1, replica_groups=mesh['pipe'=8,'dp'=16] {'pipe'}, dimensions={0} | all-to-all | bytes 655360 | tf_op jit(solution)/shard_map/all_to_all | solution.py:32
  54.2 19.1 %all-gather.8.cloned.1.call-done.in_ref.refs_5_ = bf16[5120,512]{1,0:T(8,128)(2,1)} async-done(((bf16[320,512]{1,0:T(8,128)(2,1)}), bf16[5120,512]{1,0:T(8,128)(2,1)}) %all-gather.8.cloned.1.call-update) | async-done | bytes 5242896 | tf_op jit(solution)/shard_map/all_gather | solution.py:536
  82.2 6.4 %all-to-all-start.1 = ((bf16[8,48,512]{2,1,0:T(8,128)(2,1)}), bf16[8,48,512]{2,1,0:T(8,128)(2,1)}, u32[]{:S(2)}, u32[]{:S(2)}) async-start(bf16[8,48,512]{2,1,0:T(8,128)(2,1)} %bitcast.128), calls=%async_computation.1 | async-start | bytes 786432 | tf_op jit(solution)/shard_map/all_to_all | solution.py:32
  88.6 2.2 convolution_convert_fusion.2
  90.7 2.2 convolution_convert_fusion.1
  92.9 5.2 all-to-all-done.1
  99.9 4.2 all-to-all-start.2
  104.1 2.2 convolution_convert_fusion
  106.3 2.2 convolution_convert_fusion.3
  108.4 3.1 concatenate.39
  113.2 5.1 all-to-all-start.3
  119.8 2.4 all-gather.6.cloned.1.call-done.out_ref.refs_6_
  122.2 12.5 %all-to-all-done.3.down_ref = bf16[8,32,2176]{2,1,0:T(8,128)(2,1)} async-done(((bf16[8,32,2176]{2,1,0:T(8,128)(2,1)}), bf16[8,32,2176]{2,1,0:T(8,128)(2,1)}, u32[]{:S(2)}, u32[]{:S(2)}) %all-to-all-start.3) | async-done | bytes 1114144 | tf_op jit(solution)/shard_map/all_to_all | solution.py:32
  143.3 12.2 %all_to_all.126 = bf16[8,48,512]{2,1,0:T(8,128)(2,1)S(1)} all-to-all(bf16[8,48,512]{2,1,0:T(8,128)(2,1)S(1)} %bitcast.127), channel_id=1, replica_groups=mesh['pipe'=8,'dp'=16] {'pipe'}, dimensions={0} | all-to-all | bytes 786432 | tf_op jit(solution)/shard_map/all_to_all | solution.py:32
  155.6 12.9 %all_to_all.127 = bf16[8,48,512]{2,1,0:T(8,128)(2,1)S(1)} all-to-all(bf16[8,48,512]{2,1,0:T(8,128)(2,1)S(1)} %tile.5), channel_id=1, replica_groups=mesh['pipe'=8,'dp'=16] {'pipe'}, dimensions={0} | all-to-all | bytes 786432 | tf_op jit(solution)/shard_map/all_to_all | solution.py:32
  177.0 4.9 all-to-all-start.6
  186.4 8.1 %all-to-all-done.6.up_ref = bf16[8,32,1536]{2,1,0:T(8,128)(2,1)S(1)} async-done(((bf16[8,32,1536]{2,1,0:T(8,128)(2,1)}), bf16[8,32,1536]{2,1,0:T(8,128)(2,1)S(1)}, u32[]{:S(2)}, u32[]{:S(2)}) %all-to-all-start.6) | async-done | bytes 786464 | tf_op jit(solution)/shard_map/all_to_all | solution.py:32
  195.6 6.0 %all-to-all-start.7 = ((bf16[8,32,2048]{2,1,0:T(8,128)(2,1)}), bf16[8,32,2048]{2,1,0:T(8,128)(2,1)S(1)}, u32[]{:S(2)}, u32[]{:S(2)}) async-start(bf16[8,32,2048]{2,1,0:T(8,128)(2,1)} %bitcast.115), calls=%async_computation.7 | async-start | bytes 2097152 | tf_op jit(solution)/shard_map/all_to_all | solution.py:32
  202.4 17.0 %all-to-all-done.7.grad_ref = bf16[8,32,2048]{2,1,0:T(8,128)(2,1)S(1)} async-done(((bf16[8,32,2048]{2,1,0:T(8,128)(2,1)}), bf16[8,32,2048]{2,1,0:T(8,128)(2,1)S(1)}, u32[]{:S(2)}, u32[]{:S(2)}) %all-to-all-start.7) | async-done | bytes 1048608 | tf_op jit(solution)/shard_map/all_to_all | solution.py:32
  219.4 4.9 all-gather.12.cloned.1.call-done.gram_out_ref
  224.4 5.1 shard_map.153
  230.3 25.1 %all_to_all.128 = bf16[8,32,2048]{2,1,0:T(8,128)(2,1)S(1)} all-to-all(bf16[8,32,2048]{2,1,0:T(8,128)(2,1)S(1)} %bitcast.113), channel_id=1, replica_groups=mesh['pipe'=8,'dp'=16] {'pipe'}, dimensions={0} | all-to-all | bytes 2097152 | tf_op jit(solution)/shard_map/all_to_all | solution.py:32
  255.4 6.2 %shard_map.154 = (f32[256,640]{1,0:T(8,128)S(1)}, bf16[256,3712]{1,0:T(8,128)(2,1)S(1)}) custom-call(bf16[256,640]{1,0:T(8,128)(2,1)S(1)} %get-tuple-element.136.rows_ref.refs_1_, bf16[256,2048]{1,0:T(8,128)(2,1)S(1)} %bitcast.104, bf16[5120,512]{1,0:T(8,128)(2,1)} %all-gather.8.cloned.1.call-done.in_ref.refs_5_, ...), custom_call_target="tpu_custom_call" | custom-call | tf_op jit(solution)/shard_map/pallas_call | solution.py:72
  262.5 33.5 %all_to_all.129.sums_ref = bf16[8,32,3712]{2,1,0:T(8,128)(2,1)S(1)} all-to-all(bf16[8,32,3712]{2,1,0:T(8,128)(2,1)S(1)} %bitcast.109), channel_id=1, replica_groups=mesh['pipe'=8,'dp'=16] {'pipe'}, dimensions={0} | all-to-all | bytes 3801088 | tf_op jit(solution)/shard_map/all_to_all | solution.py:32
  295.9 6.9 %all-gather.14.cloned.1.call-done.gram_ref = bf16[512,6144]{1,0:T(8,128)(2,1)} async-done(((bf16[32,6144]{1,0:T(8,128)(2,1)}), bf16[512,6144]{1,0:T(8,128)(2,1)}) %all-gather.14.cloned.1.call-update) | async-done | bytes 6291472 | tf_op jit(solution)/shard_map/all_gather | solution.py:564
  302.8 6.0 %shard_map.155 = bf16[256,4224]{1,0:T(8,128)(2,1)S(1)} custom-call(bf16[8,32,3712]{2,1,0:T(8,128)(2,1)S(1)} %all_to_all.129.sums_ref, bf16[8,32,2048]{2,1,0:T(8,128)(2,1)S(1)} %all-to-all-done.7.grad_ref, bf16[512,6144]{1,0:T(8,128)(2,1)} %all-gather.14.cloned.1.call-done.gram_ref), custom_call_target="tpu_custom_call" | custom-call | tf_op jit(solution)/shard_map/pallas_call | solution.py:72
  310.2 6.9 %all-to-all-start.10 = ((bf16[8,32,4224]{2,1,0:T(8,128)(2,1)}), bf16[8,32,4224]{2,1,0:T(8,128)(2,1)S(1)}, u32[]{:S(2)}, u32[]{:S(2)}) async-start(bf16[8,32,4224]{2,1,0:T(8,128)(2,1)} %bitcast.106), calls=%async_computation.10 | async-start | bytes 4325376 | tf_op jit(solution)/shard_map/all_to_all | solution.py:32
  317.3 31.7 %all-to-all-done.10 = bf16[8,32,4224]{2,1,0:T(8,128)(2,1)S(1)} async-done(((bf16[8,32,4224]{2,1,0:T(8,128)(2,1)}), bf16[8,32,4224]{2,1,0:T(8,128)(2,1)S(1)}, u32[]{:S(2)}, u32[]{:S(2)}) %all-to-all-start.10) | async-done | bytes 2162720 | tf_op jit(solution)/shard_map/all_to_all | solution.py:32
  351.0 9.6 %shard_map.156 = (bf16[4,256,640]{2,1,0:T(8,128)(2,1)S(1)}, f32[256,640]{1,0:T(8,128)S(1)}, bf16[16,1280,128]{2,1,0:T(8,128)(2,1)}, bf16[256,2048]{1,0:T(8,128)(2,1)S(1)}) custom-call(s32[9]{0:T(128)S(1)} %pad_add_fusion.refs_0_, f32[256,640]{1,0:T(8,128)S(1)} %copy-done.14, bf16[256,4224]{1,0:T(8,128)(2,1)S(1)} %bitcast.102, ...), custom_call_target="tpu_custom_call" | custom-call | tf_op jit(solution)/shard_map/pallas_call | solution.py:72
  363.5 20.9 %all_to_all.130.grad_ref = bf16[8,32,2048]{2,1,0:T(8,128)(2,1)S(1)} all-to-all(bf16[8,32,2048]{2,1,0:T(8,128)(2,1)} %bitcast.112), channel_id=1, replica_groups=mesh['pipe'=8,'dp'=16] {'pipe'}, dimensions={0} | all-to-all | bytes 2097152 | tf_op jit(solution)/shard_map/all_to_all | solution.py:32
  387.7 25.9 %all_to_all.131 = bf16[8,32,2176]{2,1,0:T(8,128)(2,1)S(1)} all-to-all(bf16[8,32,2176]{2,1,0:T(8,128)(2,1)S(1)} %bitcast.108), channel_id=1, replica_groups=mesh['pipe'=8,'dp'=16] {'pipe'}, dimensions={0} | all-to-all | bytes 2228224 | tf_op jit(solution)/shard_map/all_to_all | solution.py:32
  413.6 12.2 %shard_map.158 = (bf16[8,256,640]{2,1,0:T(8,128)(2,1)}, f32[256,640]{1,0:T(8,128)}, bf16[8,1280,128]{2,1,0:T(8,128)(2,1)}, bf16[8,1280,128]{2,1,0:T(8,128)(2,1)}) custom-call(s32[9]{0:T(128)S(1)} %pad_add_fusion.refs_0_, bf16[256,640]{1,0:T(8,128)(2,1)S(1)} %get-tuple-element.136.rows_ref.refs_1_, bf16[256,2176]{1,0:T(8,128)(2,1)S(1)} %bitcast.107, ...), custom_call_target="tpu_custom_call" | custom-call | tf_op jit(solution)/shard_map/pallas_call | solution.py:72
  427.0 3.7 all-to-all-start.13
  432.1 4.1 shard_map.159
  437.0 2.9 collective-permute-start.4
  442.6 54.2 %collective-permute-done.2.refs_1_ = bf16[1280,128]{1,0:T(8,128)(2,1)S(1)} collective-permute-done((bf16[1280,128]{1,0:T(8,128)(2,1)}, bf16[1280,128]{1,0:T(8,128)(2,1)S(1)}, u32[]{:S(2)}, u32[]{:S(2)}) %collective-permute-start.2) | collective-permute-done | bytes 327712 | tf_op jit(solution)/shard_map/ppermute | solution.py:493
  496.8 2.4 collective-permute-start.7
  502.0 3.9 collective-permute-done.7.refs_6_
  506.0 7.0 %collective-permute-done.8.refs_7_ = bf16[1280,128]{1,0:T(8,128)(2,1)} collective-permute-done((bf16[1280,128]{1,0:T(8,128)(2,1)}, bf16[1280,128]{1,0:T(8,128)(2,1)}, u32[]{:S(2)}, u32[]{:S(2)}) %collective-permute-start.8) | collective-permute-done | bytes 327712 | tf_op jit(solution)/shard_map/ppermute | solution.py:493
  513.0 2.7 shard_map.162
  515.7 1.7 shard_map.161
  519.2 7.3 %all-to-all-start.14 = ((bf16[8,160,128]{2,1,0:T(8,128)(2,1)}), bf16[8,160,128]{2,1,0:T(8,128)(2,1)S(1)}, u32[]{:S(2)}, u32[]{:S(2)}) async-start(bf16[8,160,128]{2,1,0:T(8,128)(2,1)} %pad_maximum_fusion.3), calls=%async_computation.15 | async-start | bytes 655360 | tf_op jit(solution)/shard_map/all_to_all | solution.py:32
  529.2 8.3 %collective-permute-start.9 = (bf16[160,512]{1,0:T(8,128)(2,1)S(1)}, bf16[160,512]{1,0:T(8,128)(2,1)S(1)}, u32[]{:S(2)}, u32[]{:S(2)}) collective-permute-start(bf16[160,512]{1,0:T(8,128)(2,1)S(1)} %get-tuple-element.138), channel_id=1, source_target_pairs={{0,0},{1,64},{2,1},{3,65},{4,16},{5,80},{6,17},{7,81},{8,32},{9,96... | collective-permute-start | bytes 491528 | tf_op jit(solution)/shard_map/ppermute | solution.py:508
  537.5 9.0 %collective-permute-done.9.refs_1_ = bf16[160,512]{1,0:T(8,128)(2,1)S(1)} collective-permute-done((bf16[160,512]{1,0:T(8,128)(2,1)S(1)}, bf16[160,512]{1,0:T(8,128)(2,1)S(1)}, u32[]{:S(2)}, u32[]{:S(2)}) %collective-permute-start.9) | collective-permute-done | bytes 163872 | tf_op jit(solution)/shard_map/ppermute | solution.py:508
  547.3 5.3 shard_map.163
  552.5 9.1 %all-to-all-start.15 = ((bf16[16,2,32,320]{3,2,1,0:T(8,128)(2,1)}), bf16[16,2,32,320]{3,2,1,0:T(8,128)(2,1)S(1)}, u32[]{:S(2)}, u32[]{:S(2)}) async-start(bf16[16,2,32,320]{3,2,1,0:T(8,128)(2,1)} %get-tuple-element.132), calls=%async_computation.16 | async-start | bytes 1572864 | tf_op jit(solution)/shard_map/all_to_all | solution.py:32
  563.4 3.1 shard_map.160
  566.5 7.8 %all-to-all-done.15.pieces_ref = bf16[16,2,32,320]{3,2,1,0:T(8,128)(2,1)S(1)} async-done(((bf16[16,2,32,320]{3,2,1,0:T(8,128)(2,1)}), bf16[16,2,32,320]{3,2,1,0:T(8,128)(2,1)S(1)}, u32[]{:S(2)}, u32[]{:S(2)}) %all-to-all-start.15) | async-done | bytes 655392 | tf_op jit(solution)/shard_map/all_to_all | solution.py:32
  (156 shorter events, 74.6 us)
Async XLA Ops:
  7.2 162.7 %copy-start = (bf16[256,5120]{1,0:T(8,128)(2,1)S(1)}, bf16[256,5120]{1,0:T(8,128)(2,1)}, u32[]{:S(2)}) copy-start(bf16[256,5120]{1,0:T(8,128)(2,1)} %param.9) | copy-start | bytes 7864324
  7.2 66.1 %all-gather.8.cloned.1.call-start = ((), (), s32[]{:S(2)}) async-start(), calls=%async_computation.18 | async-start | bytes 5570560 | tf_op jit(solution)/shard_map/all_gather | solution.py:536
  8.5 0.7 collective-permute-start
  10.0 112.2 %all-gather.6.cloned.1.call-start = ((), (), s32[]{:S(2)}) async-start(), calls=%async_computation.17 | async-start | bytes 5570560 | tf_op jit(solution)/shard_map/all_gather | solution.py:537
  48.8 41.9 %copy-start.26 = (bf16[8,32,640]{2,1,0:T(8,128)(2,1)}, bf16[8,32,640]{2,1,0:T(8,128)(2,1)S(1)}, u32[]{:S(2)}) copy-start(bf16[8,32,640]{2,1,0:T(8,128)(2,1)S(1)} %all_to_all.125) | copy-start | bytes 983044
  54.2 45.7 %copy-start.34 = (bf16[3,32,640]{2,1,0:T(8,128)(2,1)}, bf16[3,32,640]{2,1,0:T(8,128)(2,1)S(1)}, u32[]{:S(2)}) copy-start(bf16[3,32,640]{2,1,0:T(8,128)(2,1)S(1)} %get-tuple-element.139) | copy-start | bytes 368644
  82.2 15.9 %all-to-all-start.1 = ((bf16[8,48,512]{2,1,0:T(8,128)(2,1)}), bf16[8,48,512]{2,1,0:T(8,128)(2,1)}, u32[]{:S(2)}, u32[]{:S(2)}) async-start(bf16[8,48,512]{2,1,0:T(8,128)(2,1)} %bitcast.128), calls=%async_computation.1 | async-start | bytes 786432 | tf_op jit(solution)/shard_map/all_to_all | solution.py:32
  99.9 13.3 %all-to-all-start.2 = ((bf16[8,48,512]{2,1,0:T(8,128)(2,1)}), bf16[8,48,512]{2,1,0:T(8,128)(2,1)S(1)}, u32[]{:S(2)}, u32[]{:S(2)}) async-start(bf16[8,48,512]{2,1,0:T(8,128)(2,1)} %tile.4), calls=%async_computation.2 | async-start | bytes 786432 | tf_op jit(solution)/shard_map/all_to_all | solution.py:32
  111.6 28.9 %copy-start.36 = (bf16[2,32,640]{2,1,0:T(8,128)(2,1)S(1)}, bf16[2,32,640]{2,1,0:T(8,128)(2,1)}, u32[]{:S(2)}) copy-start(bf16[2,32,640]{2,1,0:T(8,128)(2,1)} %get-tuple-element.141) | copy-start | bytes 245764
  111.6 30.3 %copy-start.35 = (bf16[3,32,640]{2,1,0:T(8,128)(2,1)S(1)}, bf16[3,32,640]{2,1,0:T(8,128)(2,1)}, u32[]{:S(2)}) copy-start(bf16[3,32,640]{2,1,0:T(8,128)(2,1)} %copy-done.34) | copy-start | bytes 368644
  113.2 21.5 %all-to-all-start.3 = ((bf16[8,32,2176]{2,1,0:T(8,128)(2,1)}), bf16[8,32,2176]{2,1,0:T(8,128)(2,1)}, u32[]{:S(2)}, u32[]{:S(2)}) async-start(bf16[8,32,2176]{2,1,0:T(8,128)(2,1)} %concatenate.39), calls=%async_computation.3 | async-start | bytes 2228224 | tf_op jit(solution)/shard_map/all_to_all | solution.py:32
  118.4 101.0 %all-gather.10.cloned.1.call-start = ((), (), s32[]{:S(2)}) async-start(), calls=%async_computation.19 | async-start | bytes 3342336 | tf_op jit(solution)/shard_map/all_gather | solution.py:564
  134.7 89.6 %all-gather.12.cloned.1.call-start = ((), (), s32[]{:S(2)}) async-start(), calls=%async_computation.20 | async-start | bytes 3342336 | tf_op jit(solution)/shard_map/all_gather | solution.py:564
  170.0 14.9 %copy-start.10 = (bf16[256,640]{1,0:T(8,128)(2,1)}, bf16[256,640]{1,0:T(8,128)(2,1)S(1)}, u32[]{:S(2)}) copy-start(bf16[256,640]{1,0:T(8,128)(2,1)S(1)} %constant_dynamic-slice_fusion.refs_4_) | copy-start | bytes 983044
  177.0 24.6 %copy-start.23 = (bf16[32,3072]{1,0:T(8,128)(2,1)S(1)}, bf16[32,3072]{1,0:T(8,128)(2,1)}, u32[]{:S(2)}) copy-start(bf16[32,3072]{1,0:T(8,128)(2,1)} %copy-done.22) | copy-start | bytes 589828
  177.0 24.7 %copy-start.25 = (bf16[32,3072]{1,0:T(8,128)(2,1)S(1)}, bf16[32,3072]{1,0:T(8,128)(2,1)}, u32[]{:S(2)}) copy-start(bf16[32,3072]{1,0:T(8,128)(2,1)} %copy-done.24) | copy-start | bytes 589828
  177.0 17.5 %all-to-all-start.6 = ((bf16[8,32,1536]{2,1,0:T(8,128)(2,1)}), bf16[8,32,1536]{2,1,0:T(8,128)(2,1)S(1)}, u32[]{:S(2)}, u32[]{:S(2)}) async-start(bf16[8,32,1536]{2,1,0:T(8,128)(2,1)} %bitcast.24), calls=%async_computation.6 | async-start | bytes 1572864 | tf_op jit(solution)/shard_map/all_to_all | solution.py:32
  195.6 23.8 %all-to-all-start.7 = ((bf16[8,32,2048]{2,1,0:T(8,128)(2,1)}), bf16[8,32,2048]{2,1,0:T(8,128)(2,1)S(1)}, u32[]{:S(2)}, u32[]{:S(2)}) async-start(bf16[8,32,2048]{2,1,0:T(8,128)(2,1)} %bitcast.115), calls=%async_computation.7 | async-start | bytes 2097152 | tf_op jit(solution)/shard_map/all_to_all | solution.py:32
  201.6 101.2 %all-gather.14.cloned.1.call-start = ((), (), s32[]{:S(2)}) async-start(), calls=%async_computation.21 | async-start | bytes 6684672 | tf_op jit(solution)/shard_map/all_gather | solution.py:564
  230.3 25.1 %copy-start.19 = (f32[4,32,512]{2,1,0:T(8,128)}, f32[4,32,512]{2,1,0:T(8,128)S(1)}, u32[]{:S(2)}) copy-start(f32[4,32,512]{2,1,0:T(8,128)S(1)} %get-tuple-element.96.hidden_ref) | copy-start | bytes 786436
  255.4 6.2 %copy-start.5 = (bf16[8,32,2048]{2,1,0:T(8,128)(2,1)}, bf16[8,32,2048]{2,1,0:T(8,128)(2,1)S(1)}, u32[]{:S(2)}) copy-start(bf16[8,32,2048]{2,1,0:T(8,128)(2,1)S(1)} %all_to_all.128) | copy-start | bytes 3145732
  308.8 1.3 copy-start.7
  310.2 38.8 %all-to-all-start.10 = ((bf16[8,32,4224]{2,1,0:T(8,128)(2,1)}), bf16[8,32,4224]{2,1,0:T(8,128)(2,1)S(1)}, u32[]{:S(2)}, u32[]{:S(2)}) async-start(bf16[8,32,4224]{2,1,0:T(8,128)(2,1)} %bitcast.106), calls=%async_computation.10 | async-start | bytes 4325376 | tf_op jit(solution)/shard_map/all_to_all | solution.py:32
  317.1 198.6 %reduce-scatter.2.cloned.1.call-start = ((), (), s32[]{:S(2)}) async-start(), calls=%async_computation.22 | async-start | bytes 5570560 | tf_op jit(solution)/shard_map/reduce_scatter | solution.py:665
  349.9 1.1 copy-start.14
  363.4 20.9 %copy-start.2 = (bf16[512,3072]{1,0:T(8,128)(2,1)S(1)}, bf16[512,3072]{1,0:T(8,128)(2,1)}, u32[]{:S(2)}) copy-start(bf16[512,3072]{1,0:T(8,128)(2,1)} %all-gather.10.cloned.1.call-done.gram_in_ref.gram_ref) | copy-start | bytes 9437188
  363.5 50.1 %copy-start.6 = (bf16[8,32,2048]{2,1,0:T(8,128)(2,1)S(1)}, bf16[8,32,2048]{2,1,0:T(8,128)(2,1)}, u32[]{:S(2)}) copy-start(bf16[8,32,2048]{2,1,0:T(8,128)(2,1)} %copy-done.5) | copy-start | bytes 3145732
  363.5 50.1 %copy-start.9 = (bf16[4,256,640]{2,1,0:T(8,128)(2,1)S(1)}, bf16[4,256,640]{2,1,0:T(8,128)(2,1)}, u32[]{:S(2)}) copy-start(bf16[4,256,640]{2,1,0:T(8,128)(2,1)} %copy-done.8) | copy-start | bytes 3932164
  363.5 50.1 %copy-start.16 = (f32[256,640]{1,0:T(8,128)S(1)}, f32[256,640]{1,0:T(8,128)}, u32[]{:S(2)}) copy-start(f32[256,640]{1,0:T(8,128)} %copy-done.15) | copy-start | bytes 1966084
  425.8 6.3 %collective-permute-start.1 = (bf16[8,1280,128]{2,1,0:T(8,128)(2,1)}, bf16[8,1280,128]{2,1,0:T(8,128)(2,1)}, u32[]{:S(2)}, u32[]{:S(2)}) collective-permute-start(bf16[8,1280,128]{2,1,0:T(8,128)(2,1)} %get-tuple-element.103), channel_id=1, source_target_pairs={{0,1},{1,0},{2,3},{3,2},{4,5},{5,4},{6,7},{7,6},{8,9},{9,8},{10,11... | collective-permute-start | bytes 7864328 | tf_op jit(solution)/shard_map/ppermute | solution.py:464
  427.0 73.6 %all-to-all-start.13 = ((bf16[8,256,640]{2,1,0:T(8,128)(2,1)}), bf16[8,256,640]{2,1,0:T(8,128)(2,1)S(1)}, u32[]{:S(2)}, u32[]{:S(2)}) async-start(bf16[8,256,640]{2,1,0:T(8,128)(2,1)} %get-tuple-element.101), calls=%async_computation.13 | async-start | bytes 5242880 | tf_op jit(solution)/shard_map/all_to_all | solution.py:32
  436.2 60.6 %collective-permute-start.2 = (bf16[1280,128]{1,0:T(8,128)(2,1)}, bf16[1280,128]{1,0:T(8,128)(2,1)S(1)}, u32[]{:S(2)}, u32[]{:S(2)}) collective-permute-start(bf16[1280,128]{1,0:T(8,128)(2,1)} %get-tuple-element.105), channel_id=1, source_target_pairs={{0,2},{1,3},{2,0},{3,1},{4,6},{5,7},{6,4},{7,5},{8,10},{9,11},{10,... | collective-permute-start | bytes 983048 | tf_op jit(solution)/shard_map/ppermute | solution.py:493
  436.5 62.7 %collective-permute-start.3 = (bf16[1280,128]{1,0:T(8,128)(2,1)}, bf16[1280,128]{1,0:T(8,128)(2,1)S(1)}, u32[]{:S(2)}, u32[]{:S(2)}) collective-permute-start(bf16[1280,128]{1,0:T(8,128)(2,1)} %get-tuple-element.106), channel_id=1, source_target_pairs={{0,4},{1,5},{2,6},{3,7},{4,8},{5,9},{6,10},{7,11},{8,12},{9,13},{1... | collective-permute-start | bytes 983048 | tf_op jit(solution)/shard_map/ppermute | solution.py:493
  437.0 65.0 %collective-permute-start.4 = (bf16[1280,128]{1,0:T(8,128)(2,1)}, bf16[1280,128]{1,0:T(8,128)(2,1)}, u32[]{:S(2)}, u32[]{:S(2)}) collective-permute-start(bf16[1280,128]{1,0:T(8,128)(2,1)} %get-tuple-element.107), channel_id=1, source_target_pairs={{0,6},{1,7},{2,4},{3,5},{4,10},{5,11},{6,8},{7,9},{8,14},{9,15},{1... | collective-permute-start | bytes 983048 | tf_op jit(solution)/shard_map/ppermute | solution.py:493
  439.9 62.1 %collective-permute-start.5 = (bf16[1280,128]{1,0:T(8,128)(2,1)}, bf16[1280,128]{1,0:T(8,128)(2,1)}, u32[]{:S(2)}, u32[]{:S(2)}) collective-permute-start(bf16[1280,128]{1,0:T(8,128)(2,1)} %get-tuple-element.108), channel_id=1, source_target_pairs={{0,8},{1,9},{2,10},{3,11},{4,12},{5,13},{6,14},{7,15},{8,0},{9,1},... | collective-permute-start | bytes 983048 | tf_op jit(solution)/shard_map/ppermute | solution.py:493
  441.5 60.6 %collective-permute-start.6 = (bf16[1280,128]{1,0:T(8,128)(2,1)}, bf16[1280,128]{1,0:T(8,128)(2,1)}, u32[]{:S(2)}, u32[]{:S(2)}) collective-permute-start(bf16[1280,128]{1,0:T(8,128)(2,1)} %get-tuple-element.109), channel_id=1, source_target_pairs={{0,10},{1,11},{2,8},{3,9},{4,14},{5,15},{6,12},{7,13},{8,2},{9,3},... | collective-permute-start | bytes 983048 | tf_op jit(solution)/shard_map/ppermute | solution.py:493
  496.8 16.2 %copy-start.29 = (bf16[1280,128]{1,0:T(8,128)(2,1)}, bf16[1280,128]{1,0:T(8,128)(2,1)S(1)}, u32[]{:S(2)}) copy-start(bf16[1280,128]{1,0:T(8,128)(2,1)S(1)} %collective-permute-done.2.refs_1_) | copy-start | bytes 983044
  496.8 9.2 %collective-permute-start.7 = (bf16[1280,128]{1,0:T(8,128)(2,1)}, bf16[1280,128]{1,0:T(8,128)(2,1)}, u32[]{:S(2)}, u32[]{:S(2)}) collective-permute-start(bf16[1280,128]{1,0:T(8,128)(2,1)} %get-tuple-element.110), channel_id=1, source_target_pairs={{0,12},{1,13},{2,14},{3,15},{4,0},{5,1},{6,2},{7,3},{8,4},{9,5},{1... | collective-permute-start | bytes 983048 | tf_op jit(solution)/shard_map/ppermute | solution.py:493
  499.2 13.8 %copy-start.30 = (bf16[1280,128]{1,0:T(8,128)(2,1)}, bf16[1280,128]{1,0:T(8,128)(2,1)S(1)}, u32[]{:S(2)}) copy-start(bf16[1280,128]{1,0:T(8,128)(2,1)S(1)} %collective-permute-done.3.refs_2_) | copy-start | bytes 983044
  499.2 13.8 %collective-permute-start.8 = (bf16[1280,128]{1,0:T(8,128)(2,1)}, bf16[1280,128]{1,0:T(8,128)(2,1)}, u32[]{:S(2)}, u32[]{:S(2)}) collective-permute-start(bf16[1280,128]{1,0:T(8,128)(2,1)} %get-tuple-element.111), channel_id=1, source_target_pairs={{0,14},{1,15},{2,12},{3,13},{4,2},{5,3},{6,0},{7,1},{8,6},{9,7},{1... | collective-permute-start | bytes 983048 | tf_op jit(solution)/shard_map/ppermute | solution.py:493
  500.5 1.5 copy-start.3
  519.2 27.3 %all-to-all-start.14 = ((bf16[8,160,128]{2,1,0:T(8,128)(2,1)}), bf16[8,160,128]{2,1,0:T(8,128)(2,1)S(1)}, u32[]{:S(2)}, u32[]{:S(2)}) async-start(bf16[8,160,128]{2,1,0:T(8,128)(2,1)} %pad_maximum_fusion.3), calls=%async_computation.15 | async-start | bytes 655360 | tf_op jit(solution)/shard_map/all_to_all | solution.py:32
  527.5 10.1 %collective-permute-start.10 = (bf16[160,512]{1,0:T(8,128)(2,1)S(1)}, bf16[160,512]{1,0:T(8,128)(2,1)S(1)}, u32[]{:S(2)}, u32[]{:S(2)}) collective-permute-start(bf16[160,512]{1,0:T(8,128)(2,1)S(1)} %get-tuple-element.137), channel_id=1, source_target_pairs={{0,64},{1,0},{2,65},{3,1},{4,80},{5,16},{6,81},{7,17},{8,96},{9,32... | collective-permute-start | bytes 491528 | tf_op jit(solution)/shard_map/ppermute | solution.py:508
  529.2 17.3 %collective-permute-start.9 = (bf16[160,512]{1,0:T(8,128)(2,1)S(1)}, bf16[160,512]{1,0:T(8,128)(2,1)S(1)}, u32[]{:S(2)}, u32[]{:S(2)}) collective-permute-start(bf16[160,512]{1,0:T(8,128)(2,1)S(1)} %get-tuple-element.138), channel_id=1, source_target_pairs={{0,0},{1,64},{2,1},{3,65},{4,16},{5,80},{6,17},{7,81},{8,32},{9,96... | collective-permute-start | bytes 491528 | tf_op jit(solution)/shard_map/ppermute | solution.py:508
  537.5 9.0 %copy-start.32 = (bf16[160,512]{1,0:T(8,128)(2,1)}, bf16[160,512]{1,0:T(8,128)(2,1)S(1)}, u32[]{:S(2)}) copy-start(bf16[160,512]{1,0:T(8,128)(2,1)S(1)} %collective-permute-done.10.refs_2_) | copy-start | bytes 491524
  546.5 28.8 %copy-start.1 = (bf16[256,5120]{1,0:T(8,128)(2,1)S(1)}, bf16[256,5120]{1,0:T(8,128)(2,1)}, u32[]{:S(2)}) copy-start(bf16[256,5120]{1,0:T(8,128)(2,1)} %param.9) | copy-start | bytes 7864324
  552.5 21.8 %all-to-all-start.15 = ((bf16[16,2,32,320]{3,2,1,0:T(8,128)(2,1)}), bf16[16,2,32,320]{3,2,1,0:T(8,128)(2,1)S(1)}, u32[]{:S(2)}, u32[]{:S(2)}) async-start(bf16[16,2,32,320]{3,2,1,0:T(8,128)(2,1)} %get-tuple-element.132), calls=%async_computation.16 | async-start | bytes 1572864 | tf_op jit(solution)/shard_map/all_to_all | solution.py:32
  561.7 1.7 copy-start.4
  (15 other events, 12.3 us)
Sparse Core Ops, SparseCore 0:
  10.3 62.9 all-gather.7
  75.6 46.5 all-gather.5
  134.8 38.6 all-gather.9
  175.6 48.6 all-gather.11
  226.5 76.2 all-gather.13
  363.6 136.0 reduce-scatter.1

commit v12 on v11

--- a/solution.py
+++ b/solution.py
@@ -465,32 +465,31 @@
 
 
 def add_kernel(mine_ref, other_ref, *out_refs):
+    per = mine_ref.shape[0] // len(out_refs)
     for at in range(mine_ref.shape[0]):
         total = mine_ref[at].astype(jnp.float32) + other_ref[at].astype(jnp.float32)
-        if len(out_refs) == 1:
-            out_refs[0][at] = total.astype(jnp.bfloat16)
+        if per == 1:
+            out_refs[at][...] = total.astype(jnp.bfloat16)
         else:
-            out_refs[at][...] = total.astype(jnp.bfloat16)
+            out_refs[at // per][at % per] = total.astype(jnp.bfloat16)
 
 
 def added(mine, other, count):
-    shape = mine.shape if count == 1 else mine.shape[1:]
+    per = mine.shape[0] // count
+    shape = mine.shape[1:] if per == 1 else (per, *mine.shape[1:])
     shapes = [(shape, jnp.bfloat16)] * count
     return run(add_kernel, shapes, mine, other, vmem=VMEM_ALMOST_ALL)
 
 
-def chip_steps(n_dp):
-    return [(dx, dz) for dx in range(n_dp // 4) for dz in range(2)]
-
-
-def between_chips(blocks, n_dp):
+def between_chips(mine, other, n_dp):
+    xs = n_dp // 4
+    same, across = added(mine, other, 2)
+    across = lax.ppermute(across, "dp", [(j, j + 2 - 4 * (j // 2 % 2)) for j in range(n_dp)])
+    blocks = added(same, across, xs)
     arrived = [blocks[0]]
-    for (dx, dz), block in list(zip(chip_steps(n_dp), blocks))[1:]:
-        pairs = []
-        for j in range(n_dp):
-            x, z, core = j // 4, j // 2 % 2, j % 2
-            pairs.append((j, (x + dx) % (n_dp // 4) * 4 + (z ^ dz) * 2 + core))
-        arrived.append(lax.ppermute(block, "dp", pairs))
+    for dx in range(1, xs):
+        pairs = [(j, (j + 4 * dx) % n_dp) for j in range(n_dp)]
+        arrived.append(lax.ppermute(blocks[dx], "dp", pairs))
     return arrived
 
 
@@ -639,7 +638,7 @@
     core, chip = dp % 2, dp // 2
     chips = jnp.arange(n_dp // 2)
     xs = n_dp // 4
-    away = (chips // 2 - chip // 2 + xs) % xs * 2 + (chips % 2 + chip % 2) % 2
+    away = (chips % 2 + chip % 2) % 2 * xs + (chips // 2 - chip // 2 + xs) % xs
     place = jnp.concatenate([away, core[None]]).astype(jnp.int32)
 
     grads_high, upstream, packed, columns = run(
@@ -705,8 +704,7 @@
         )
         return sum_in, sum_out.reshape(group, -1, LANES)
 
-    blocks = added(mine, other_core(other, n_dp), mine.shape[0])
-    arrived_low = between_chips(blocks, n_dp)
+    arrived_low = between_chips(mine, other_core(other, n_dp), n_dp)
     input_grads = swap(grads, "pipe")
     input_grads, arrived_low = lax.optimization_barrier((input_grads, arrived_low))
     ins, outs = zip(unpacked(arrived_low, count), unpacked([packed], last - middle))

time: 585 us -> 597 us (1.021)
  waiting for transfers between devices: 193 us -> 212 us
  starting transfers between devices: 75.9 us -> 65.8 us
    ppermute x7 -> x4, waiting for transfers between devices: 65.1 us -> 82.3 us  [the longest x1 69.4 us: between_chips(): lax.ppermute(across, 'dp', [(j, j + 2 - 4 * (j // 2 % 2)) for j in range(...]
    ppermute x7 -> x4, starting transfers between devices: 10.1 us -> 4.16 us  [the longest x3 3.48 us: between_chips(): arrived.append(lax.ppermute(blocks[dx], 'dp', pairs))]
    pallas_call x13 -> x14, Pallas kernels: 56.1 us -> 58.6 us  [run(): pl.pallas_call(kernel, out_shape=[jax.ShapeDtypeStruct(shape, kind) for s...]
  transfers between devices with their start and end apart: 26 -> 23, of which waited for: 16 -> 16; matrix products, arithmetic and copies ran while one was open for 9% -> 9% of each run, Pallas kernels for 6% -> 6%
where the time goes in v12:
time: 597 us; the launch traced here: 594 us
  waiting for transfers between devices  212 us (36%)
  blocking collectives  168 us (28%)
  starting transfers between devices  65.8 us (11%)
  Pallas kernels  61.7 us (10%)
  matrix products  35.7 us (6%)
  local copies, waits for them, and re-layouts  25.4 us (4%)
  between operations  14.7 us (2%)
  other arithmetic  11.3 us (2%)
    all_to_all x7, blocking collectives, swap(): return lax.all_to_all(x, axis, 0, 0, tiled=True)  168 us
    all_to_all x9, waiting for transfers between devices, swap(): return lax.all_to_all(x, axis, 0, 0, tiled=True)  84 us
    ppermute x1, waiting for transfers between devices, between_chips(): lax.ppermute(across, 'dp', [(j, j + 2 - 4 * (j // 2 % 2)) for j in range(...  69.4 us
    pallas_call x14, Pallas kernels, run(): pl.pallas_call(kernel, out_shape=[jax.ShapeDtypeStruct(shape, kind) for s...  58.6 us
    all_to_all x9, starting transfers between devices, swap(): return lax.all_to_all(x, axis, 0, 0, tiled=True)  51.9 us
    dot_general x23, matrix products, dot(): lax.dot_general(left, right, (dims, ((), ())), preferred_element_type=jnp...  35.7 us
    all_gather x1, waiting for transfers between devices, on_device(): all_in = lax.all_gather(piece_in, 'dp', axis=0, tiled=True)  19.1 us
    unnamed x75, local copies, waits for them, and re-layouts  18.1 us
  transfers between devices with their start and end apart: 23, of which 16 were waited for; matrix products, arithmetic and copies ran while one was open for 9% of the time, Pallas kernels for 6%

profile of v12, /device:TPU:1, one launch (start us, length us, event | category | flops | bytes accessed | tf_op | source)
XLA Modules:
  0.0 594.5 jit_solution(7346115670683170160)
XLA Ops:
  11.2 37.5 %all_to_all.125 = bf16[8,32,640]{2,1,0:T(8,128)(2,1)S(1)} all-to-all(bf16[8,32,640]{2,1,0:T(8,128)(2,1)S(1)} %copy.30), channel_id=1, replica_groups=mesh['pipe'=8,'dp'=16] {'pipe'}, dimensions={0} | all-to-all | bytes 655360 | tf_op jit(solution)/shard_map/all_to_all | solution.py:32
  54.2 19.1 %all-gather.8.cloned.1.call-done.in_ref.refs_5_ = bf16[5120,512]{1,0:T(8,128)(2,1)} async-done(((bf16[320,512]{1,0:T(8,128)(2,1)}), bf16[5120,512]{1,0:T(8,128)(2,1)}) %all-gather.8.cloned.1.call-update) | async-done | bytes 5242896 | tf_op jit(solution)/shard_map/all_gather | solution.py:535
  82.2 6.4 %all-to-all-start.1 = ((bf16[8,48,512]{2,1,0:T(8,128)(2,1)}), bf16[8,48,512]{2,1,0:T(8,128)(2,1)}, u32[]{:S(2)}, u32[]{:S(2)}) async-start(bf16[8,48,512]{2,1,0:T(8,128)(2,1)} %bitcast.128), calls=%async_computation.1 | async-start | bytes 786432 | tf_op jit(solution)/shard_map/all_to_all | solution.py:32
  88.6 2.2 convolution_convert_fusion.2
  90.7 2.2 convolution_convert_fusion.1
  92.9 5.2 all-to-all-done.1
  99.9 4.2 all-to-all-start.2
  104.1 2.2 convolution_convert_fusion
  106.3 2.2 convolution_convert_fusion.3
  108.4 3.1 concatenate.39
  113.2 5.1 all-to-all-start.3
  119.8 2.4 all-gather.6.cloned.1.call-done.out_ref.refs_6_
  122.2 12.5 %all-to-all-done.3.down_ref = bf16[8,32,2176]{2,1,0:T(8,128)(2,1)} async-done(((bf16[8,32,2176]{2,1,0:T(8,128)(2,1)}), bf16[8,32,2176]{2,1,0:T(8,128)(2,1)}, u32[]{:S(2)}, u32[]{:S(2)}) %all-to-all-start.3) | async-done | bytes 1114144 | tf_op jit(solution)/shard_map/all_to_all | solution.py:32
  143.3 12.2 %all_to_all.126 = bf16[8,48,512]{2,1,0:T(8,128)(2,1)S(1)} all-to-all(bf16[8,48,512]{2,1,0:T(8,128)(2,1)S(1)} %bitcast.127), channel_id=1, replica_groups=mesh['pipe'=8,'dp'=16] {'pipe'}, dimensions={0} | all-to-all | bytes 786432 | tf_op jit(solution)/shard_map/all_to_all | solution.py:32
  155.6 12.9 %all_to_all.127 = bf16[8,48,512]{2,1,0:T(8,128)(2,1)S(1)} all-to-all(bf16[8,48,512]{2,1,0:T(8,128)(2,1)S(1)} %tile.5), channel_id=1, replica_groups=mesh['pipe'=8,'dp'=16] {'pipe'}, dimensions={0} | all-to-all | bytes 786432 | tf_op jit(solution)/shard_map/all_to_all | solution.py:32
  177.0 4.9 all-to-all-start.6
  186.4 8.1 %all-to-all-done.6.up_ref = bf16[8,32,1536]{2,1,0:T(8,128)(2,1)S(1)} async-done(((bf16[8,32,1536]{2,1,0:T(8,128)(2,1)}), bf16[8,32,1536]{2,1,0:T(8,128)(2,1)S(1)}, u32[]{:S(2)}, u32[]{:S(2)}) %all-to-all-start.6) | async-done | bytes 786464 | tf_op jit(solution)/shard_map/all_to_all | solution.py:32
  195.6 6.0 %all-to-all-start.7 = ((bf16[8,32,2048]{2,1,0:T(8,128)(2,1)}), bf16[8,32,2048]{2,1,0:T(8,128)(2,1)S(1)}, u32[]{:S(2)}, u32[]{:S(2)}) async-start(bf16[8,32,2048]{2,1,0:T(8,128)(2,1)} %bitcast.115), calls=%async_computation.7 | async-start | bytes 2097152 | tf_op jit(solution)/shard_map/all_to_all | solution.py:32
  202.4 17.0 %all-to-all-done.7.grad_ref = bf16[8,32,2048]{2,1,0:T(8,128)(2,1)S(1)} async-done(((bf16[8,32,2048]{2,1,0:T(8,128)(2,1)}), bf16[8,32,2048]{2,1,0:T(8,128)(2,1)S(1)}, u32[]{:S(2)}, u32[]{:S(2)}) %all-to-all-start.7) | async-done | bytes 1048608 | tf_op jit(solution)/shard_map/all_to_all | solution.py:32
  219.4 5.5 all-gather.12.cloned.1.call-done.gram_out_ref
  224.9 5.1 shard_map.153
  230.8 24.6 %all_to_all.128 = bf16[8,32,2048]{2,1,0:T(8,128)(2,1)S(1)} all-to-all(bf16[8,32,2048]{2,1,0:T(8,128)(2,1)S(1)} %bitcast.113), channel_id=1, replica_groups=mesh['pipe'=8,'dp'=16] {'pipe'}, dimensions={0} | all-to-all | bytes 2097152 | tf_op jit(solution)/shard_map/all_to_all | solution.py:32
  255.4 6.2 %shard_map.154 = (f32[256,640]{1,0:T(8,128)S(1)}, bf16[256,3712]{1,0:T(8,128)(2,1)S(1)}) custom-call(bf16[256,640]{1,0:T(8,128)(2,1)S(1)} %get-tuple-element.124.rows_ref.refs_1_, bf16[256,2048]{1,0:T(8,128)(2,1)S(1)} %bitcast.104, bf16[5120,512]{1,0:T(8,128)(2,1)} %all-gather.8.cloned.1.call-done.in_ref.refs_5_, ...), custom_call_target="tpu_custom_call" | custom-call | tf_op jit(solution)/shard_map/pallas_call | solution.py:72
  262.5 33.4 %all_to_all.129.sums_ref = bf16[8,32,3712]{2,1,0:T(8,128)(2,1)S(1)} all-to-all(bf16[8,32,3712]{2,1,0:T(8,128)(2,1)S(1)} %bitcast.109), channel_id=1, replica_groups=mesh['pipe'=8,'dp'=16] {'pipe'}, dimensions={0} | all-to-all | bytes 3801088 | tf_op jit(solution)/shard_map/all_to_all | solution.py:32
  295.9 6.9 %all-gather.14.cloned.1.call-done.gram_ref = bf16[512,6144]{1,0:T(8,128)(2,1)} async-done(((bf16[32,6144]{1,0:T(8,128)(2,1)}), bf16[512,6144]{1,0:T(8,128)(2,1)}) %all-gather.14.cloned.1.call-update) | async-done | bytes 6291472 | tf_op jit(solution)/shard_map/all_gather | solution.py:563
  302.8 6.0 %shard_map.155 = bf16[256,4224]{1,0:T(8,128)(2,1)S(1)} custom-call(bf16[8,32,3712]{2,1,0:T(8,128)(2,1)S(1)} %all_to_all.129.sums_ref, bf16[8,32,2048]{2,1,0:T(8,128)(2,1)S(1)} %all-to-all-done.7.grad_ref, bf16[512,6144]{1,0:T(8,128)(2,1)} %all-gather.14.cloned.1.call-done.gram_ref), custom_call_target="tpu_custom_call" | custom-call | tf_op jit(solution)/shard_map/pallas_call | solution.py:72
  310.2 6.9 %all-to-all-start.10 = ((bf16[8,32,4224]{2,1,0:T(8,128)(2,1)}), bf16[8,32,4224]{2,1,0:T(8,128)(2,1)S(1)}, u32[]{:S(2)}, u32[]{:S(2)}) async-start(bf16[8,32,4224]{2,1,0:T(8,128)(2,1)} %bitcast.106), calls=%async_computation.10 | async-start | bytes 4325376 | tf_op jit(solution)/shard_map/all_to_all | solution.py:32
  317.3 31.7 %all-to-all-done.10 = bf16[8,32,4224]{2,1,0:T(8,128)(2,1)S(1)} async-done(((bf16[8,32,4224]{2,1,0:T(8,128)(2,1)}), bf16[8,32,4224]{2,1,0:T(8,128)(2,1)S(1)}, u32[]{:S(2)}, u32[]{:S(2)}) %all-to-all-start.10) | async-done | bytes 2162720 | tf_op jit(solution)/shard_map/all_to_all | solution.py:32
  351.0 9.6 %shard_map.156 = (bf16[4,256,640]{2,1,0:T(8,128)(2,1)S(1)}, f32[256,640]{1,0:T(8,128)S(1)}, bf16[16,1280,128]{2,1,0:T(8,128)(2,1)}, bf16[256,2048]{1,0:T(8,128)(2,1)S(1)}) custom-call(s32[9]{0:T(128)S(1)} %pad_add_fusion.refs_0_, f32[256,640]{1,0:T(8,128)S(1)} %copy-done.14, bf16[256,4224]{1,0:T(8,128)(2,1)S(1)} %bitcast.102, ...), custom_call_target="tpu_custom_call" | custom-call | tf_op jit(solution)/shard_map/pallas_call | solution.py:72
  363.5 20.9 %all_to_all.130.grad_ref = bf16[8,32,2048]{2,1,0:T(8,128)(2,1)S(1)} all-to-all(bf16[8,32,2048]{2,1,0:T(8,128)(2,1)} %bitcast.112), channel_id=1, replica_groups=mesh['pipe'=8,'dp'=16] {'pipe'}, dimensions={0} | all-to-all | bytes 2097152 | tf_op jit(solution)/shard_map/all_to_all | solution.py:32
  387.7 26.1 %all_to_all.131 = bf16[8,32,2176]{2,1,0:T(8,128)(2,1)S(1)} all-to-all(bf16[8,32,2176]{2,1,0:T(8,128)(2,1)S(1)} %bitcast.108), channel_id=1, replica_groups=mesh['pipe'=8,'dp'=16] {'pipe'}, dimensions={0} | all-to-all | bytes 2228224 | tf_op jit(solution)/shard_map/all_to_all | solution.py:32
  413.8 12.2 %shard_map.158 = (bf16[8,256,640]{2,1,0:T(8,128)(2,1)}, f32[256,640]{1,0:T(8,128)}, bf16[8,1280,128]{2,1,0:T(8,128)(2,1)}, bf16[8,1280,128]{2,1,0:T(8,128)(2,1)}) custom-call(s32[9]{0:T(128)S(1)} %pad_add_fusion.refs_0_, bf16[256,640]{1,0:T(8,128)(2,1)S(1)} %get-tuple-element.124.rows_ref.refs_1_, bf16[256,2176]{1,0:T(8,128)(2,1)S(1)} %bitcast.107, ...), custom_call_target="tpu_custom_call" | custom-call | tf_op jit(solution)/shard_map/pallas_call | solution.py:72
  427.0 3.8 all-to-all-start.13
  431.9 4.4 shard_map.159
  436.9 69.4 %collective-permute-done.2.other_ref = bf16[4,1280,128]{2,1,0:T(8,128)(2,1)} collective-permute-done((bf16[4,1280,128]{2,1,0:T(8,128)(2,1)}, bf16[4,1280,128]{2,1,0:T(8,128)(2,1)}, u32[]{:S(2)}, u32[]{:S(2)}) %collective-permute-start.2) | collective-permute-done | bytes 1310752 | tf_op jit(solution)/shard_map/ppermute | solution.py:487
  506.4 2.8 shard_map.160
  509.2 3.4 collective-permute-start.4
  514.2 5.1 collective-permute-done.3.refs_1_
  519.3 7.7 %collective-permute-done.4.refs_2_ = bf16[1280,128]{1,0:T(8,128)(2,1)S(1)} collective-permute-done((bf16[1280,128]{1,0:T(8,128)(2,1)}, bf16[1280,128]{1,0:T(8,128)(2,1)S(1)}, u32[]{:S(2)}, u32[]{:S(2)}) %collective-permute-start.4) | collective-permute-done | bytes 327712 | tf_op jit(solution)/shard_map/ppermute | solution.py:492
  527.8 2.1 shard_map.163
  529.9 1.7 shard_map.162
  533.4 6.4 %all-to-all-start.14 = ((bf16[8,160,128]{2,1,0:T(8,128)(2,1)}), bf16[8,160,128]{2,1,0:T(8,128)(2,1)S(1)}, u32[]{:S(2)}, u32[]{:S(2)}) async-start(bf16[8,160,128]{2,1,0:T(8,128)(2,1)} %pad_maximum_fusion.3), calls=%async_computation.15 | async-start | bytes 655360 | tf_op jit(solution)/shard_map/all_to_all | solution.py:32
  542.4 6.3 %collective-permute-start.6 = (bf16[160,512]{1,0:T(8,128)(2,1)S(1)}, bf16[160,512]{1,0:T(8,128)(2,1)S(1)}, u32[]{:S(2)}, u32[]{:S(2)}) collective-permute-start(bf16[160,512]{1,0:T(8,128)(2,1)S(1)} %get-tuple-element.126), channel_id=1, source_target_pairs={{0,0},{1,64},{2,1},{3,65},{4,16},{5,80},{6,17},{7,81},{8,32},{9,96... | collective-permute-start | bytes 491528 | tf_op jit(solution)/shard_map/ppermute | solution.py:507
  548.8 11.0 %collective-permute-done.6.refs_1_ = bf16[160,512]{1,0:T(8,128)(2,1)S(1)} collective-permute-done((bf16[160,512]{1,0:T(8,128)(2,1)S(1)}, bf16[160,512]{1,0:T(8,128)(2,1)S(1)}, u32[]{:S(2)}, u32[]{:S(2)}) %collective-permute-start.6) | collective-permute-done | bytes 163872 | tf_op jit(solution)/shard_map/ppermute | solution.py:507
  560.5 5.3 shard_map.164
  565.8 8.2 %all-to-all-start.15 = ((bf16[16,2,32,320]{3,2,1,0:T(8,128)(2,1)}), bf16[16,2,32,320]{3,2,1,0:T(8,128)(2,1)S(1)}, u32[]{:S(2)}, u32[]{:S(2)}) async-start(bf16[16,2,32,320]{3,2,1,0:T(8,128)(2,1)} %get-tuple-element.120), calls=%async_computation.16 | async-start | bytes 1572864 | tf_op jit(solution)/shard_map/all_to_all | solution.py:32
  575.7 3.1 shard_map.161
  578.8 7.8 %all-to-all-done.15.pieces_ref = bf16[16,2,32,320]{3,2,1,0:T(8,128)(2,1)S(1)} async-done(((bf16[16,2,32,320]{3,2,1,0:T(8,128)(2,1)}), bf16[16,2,32,320]{3,2,1,0:T(8,128)(2,1)S(1)}, u32[]{:S(2)}, u32[]{:S(2)}) %all-to-all-start.15) | async-done | bytes 655392 | tf_op jit(solution)/shard_map/all_to_all | solution.py:32
  (151 shorter events, 70.7 us)
Async XLA Ops:
  7.2 162.7 %copy-start = (bf16[256,5120]{1,0:T(8,128)(2,1)S(1)}, bf16[256,5120]{1,0:T(8,128)(2,1)}, u32[]{:S(2)}) copy-start(bf16[256,5120]{1,0:T(8,128)(2,1)} %param.9) | copy-start | bytes 7864324
  7.2 66.1 %all-gather.8.cloned.1.call-start = ((), (), s32[]{:S(2)}) async-start(), calls=%async_computation.18 | async-start | bytes 5570560 | tf_op jit(solution)/shard_map/all_gather | solution.py:535
  8.5 0.7 collective-permute-start
  10.0 112.2 %all-gather.6.cloned.1.call-start = ((), (), s32[]{:S(2)}) async-start(), calls=%async_computation.17 | async-start | bytes 5570560 | tf_op jit(solution)/shard_map/all_gather | solution.py:536
  48.8 41.9 %copy-start.26 = (bf16[8,32,640]{2,1,0:T(8,128)(2,1)}, bf16[8,32,640]{2,1,0:T(8,128)(2,1)S(1)}, u32[]{:S(2)}) copy-start(bf16[8,32,640]{2,1,0:T(8,128)(2,1)S(1)} %all_to_all.125) | copy-start | bytes 983044
  54.2 45.7 %copy-start.34 = (bf16[3,32,640]{2,1,0:T(8,128)(2,1)}, bf16[3,32,640]{2,1,0:T(8,128)(2,1)S(1)}, u32[]{:S(2)}) copy-start(bf16[3,32,640]{2,1,0:T(8,128)(2,1)S(1)} %get-tuple-element.127) | copy-start | bytes 368644
  82.2 15.9 %all-to-all-start.1 = ((bf16[8,48,512]{2,1,0:T(8,128)(2,1)}), bf16[8,48,512]{2,1,0:T(8,128)(2,1)}, u32[]{:S(2)}, u32[]{:S(2)}) async-start(bf16[8,48,512]{2,1,0:T(8,128)(2,1)} %bitcast.128), calls=%async_computation.1 | async-start | bytes 786432 | tf_op jit(solution)/shard_map/all_to_all | solution.py:32
  99.9 13.3 %all-to-all-start.2 = ((bf16[8,48,512]{2,1,0:T(8,128)(2,1)}), bf16[8,48,512]{2,1,0:T(8,128)(2,1)S(1)}, u32[]{:S(2)}, u32[]{:S(2)}) async-start(bf16[8,48,512]{2,1,0:T(8,128)(2,1)} %tile.4), calls=%async_computation.2 | async-start | bytes 786432 | tf_op jit(solution)/shard_map/all_to_all | solution.py:32
  111.6 28.9 %copy-start.36 = (bf16[2,32,640]{2,1,0:T(8,128)(2,1)S(1)}, bf16[2,32,640]{2,1,0:T(8,128)(2,1)}, u32[]{:S(2)}) copy-start(bf16[2,32,640]{2,1,0:T(8,128)(2,1)} %get-tuple-element.129) | copy-start | bytes 245764
  111.6 30.3 %copy-start.35 = (bf16[3,32,640]{2,1,0:T(8,128)(2,1)S(1)}, bf16[3,32,640]{2,1,0:T(8,128)(2,1)}, u32[]{:S(2)}) copy-start(bf16[3,32,640]{2,1,0:T(8,128)(2,1)} %copy-done.34) | copy-start | bytes 368644
  113.2 21.5 %all-to-all-start.3 = ((bf16[8,32,2176]{2,1,0:T(8,128)(2,1)}), bf16[8,32,2176]{2,1,0:T(8,128)(2,1)}, u32[]{:S(2)}, u32[]{:S(2)}) async-start(bf16[8,32,2176]{2,1,0:T(8,128)(2,1)} %concatenate.39), calls=%async_computation.3 | async-start | bytes 2228224 | tf_op jit(solution)/shard_map/all_to_all | solution.py:32
  118.4 101.0 %all-gather.10.cloned.1.call-start = ((), (), s32[]{:S(2)}) async-start(), calls=%async_computation.19 | async-start | bytes 3342336 | tf_op jit(solution)/shard_map/all_gather | solution.py:563
  134.7 90.2 %all-gather.12.cloned.1.call-start = ((), (), s32[]{:S(2)}) async-start(), calls=%async_computation.20 | async-start | bytes 3342336 | tf_op jit(solution)/shard_map/all_gather | solution.py:563
  170.0 14.9 %copy-start.10 = (bf16[256,640]{1,0:T(8,128)(2,1)}, bf16[256,640]{1,0:T(8,128)(2,1)S(1)}, u32[]{:S(2)}) copy-start(bf16[256,640]{1,0:T(8,128)(2,1)S(1)} %constant_dynamic-slice_fusion.refs_4_) | copy-start | bytes 983044
  177.0 24.6 %copy-start.23 = (bf16[32,3072]{1,0:T(8,128)(2,1)S(1)}, bf16[32,3072]{1,0:T(8,128)(2,1)}, u32[]{:S(2)}) copy-start(bf16[32,3072]{1,0:T(8,128)(2,1)} %copy-done.22) | copy-start | bytes 589828
  177.0 24.7 %copy-start.25 = (bf16[32,3072]{1,0:T(8,128)(2,1)S(1)}, bf16[32,3072]{1,0:T(8,128)(2,1)}, u32[]{:S(2)}) copy-start(bf16[32,3072]{1,0:T(8,128)(2,1)} %copy-done.24) | copy-start | bytes 589828
  177.0 17.5 %all-to-all-start.6 = ((bf16[8,32,1536]{2,1,0:T(8,128)(2,1)}), bf16[8,32,1536]{2,1,0:T(8,128)(2,1)S(1)}, u32[]{:S(2)}, u32[]{:S(2)}) async-start(bf16[8,32,1536]{2,1,0:T(8,128)(2,1)} %bitcast.24), calls=%async_computation.6 | async-start | bytes 1572864 | tf_op jit(solution)/shard_map/all_to_all | solution.py:32
  195.6 23.8 %all-to-all-start.7 = ((bf16[8,32,2048]{2,1,0:T(8,128)(2,1)}), bf16[8,32,2048]{2,1,0:T(8,128)(2,1)S(1)}, u32[]{:S(2)}, u32[]{:S(2)}) async-start(bf16[8,32,2048]{2,1,0:T(8,128)(2,1)} %bitcast.115), calls=%async_computation.7 | async-start | bytes 2097152 | tf_op jit(solution)/shard_map/all_to_all | solution.py:32
  201.6 101.2 %all-gather.14.cloned.1.call-start = ((), (), s32[]{:S(2)}) async-start(), calls=%async_computation.21 | async-start | bytes 6684672 | tf_op jit(solution)/shard_map/all_gather | solution.py:563
  230.8 24.6 %copy-start.19 = (f32[4,32,512]{2,1,0:T(8,128)}, f32[4,32,512]{2,1,0:T(8,128)S(1)}, u32[]{:S(2)}) copy-start(f32[4,32,512]{2,1,0:T(8,128)S(1)} %get-tuple-element.90.hidden_ref) | copy-start | bytes 786436
  255.4 6.2 %copy-start.5 = (bf16[8,32,2048]{2,1,0:T(8,128)(2,1)}, bf16[8,32,2048]{2,1,0:T(8,128)(2,1)S(1)}, u32[]{:S(2)}) copy-start(bf16[8,32,2048]{2,1,0:T(8,128)(2,1)S(1)} %all_to_all.128) | copy-start | bytes 3145732
  308.8 1.3 copy-start.7
  310.2 38.8 %all-to-all-start.10 = ((bf16[8,32,4224]{2,1,0:T(8,128)(2,1)}), bf16[8,32,4224]{2,1,0:T(8,128)(2,1)S(1)}, u32[]{:S(2)}, u32[]{:S(2)}) async-start(bf16[8,32,4224]{2,1,0:T(8,128)(2,1)} %bitcast.106), calls=%async_computation.10 | async-start | bytes 4325376 | tf_op jit(solution)/shard_map/all_to_all | solution.py:32
  317.1 212.8 %reduce-scatter.2.cloned.1.call-start = ((), (), s32[]{:S(2)}) async-start(), calls=%async_computation.22 | async-start | bytes 5570560 | tf_op jit(solution)/shard_map/reduce_scatter | solution.py:664
  348.9 1.0 copy-start.11
  349.9 1.1 copy-start.14
  360.6 1.1 copy-start.8
  361.6 1.0 copy-start.12
  363.5 20.9 %copy-start.2 = (bf16[512,3072]{1,0:T(8,128)(2,1)S(1)}, bf16[512,3072]{1,0:T(8,128)(2,1)}, u32[]{:S(2)}) copy-start(bf16[512,3072]{1,0:T(8,128)(2,1)} %all-gather.10.cloned.1.call-done.gram_in_ref.gram_ref) | copy-start | bytes 9437188
  363.5 50.3 %copy-start.6 = (bf16[8,32,2048]{2,1,0:T(8,128)(2,1)S(1)}, bf16[8,32,2048]{2,1,0:T(8,128)(2,1)}, u32[]{:S(2)}) copy-start(bf16[8,32,2048]{2,1,0:T(8,128)(2,1)} %copy-done.5) | copy-start | bytes 3145732
  363.5 50.3 %copy-start.9 = (bf16[4,256,640]{2,1,0:T(8,128)(2,1)S(1)}, bf16[4,256,640]{2,1,0:T(8,128)(2,1)}, u32[]{:S(2)}) copy-start(bf16[4,256,640]{2,1,0:T(8,128)(2,1)} %copy-done.8) | copy-start | bytes 3932164
  363.5 50.3 %copy-start.16 = (f32[256,640]{1,0:T(8,128)S(1)}, f32[256,640]{1,0:T(8,128)}, u32[]{:S(2)}) copy-start(f32[256,640]{1,0:T(8,128)} %copy-done.15) | copy-start | bytes 1966084
  384.4 1.0 copy-start.18
  426.1 5.8 collective-permute-start.1
  427.0 85.7 %all-to-all-start.13 = ((bf16[8,256,640]{2,1,0:T(8,128)(2,1)}), bf16[8,256,640]{2,1,0:T(8,128)(2,1)S(1)}, u32[]{:S(2)}, u32[]{:S(2)}) async-start(bf16[8,256,640]{2,1,0:T(8,128)(2,1)} %get-tuple-element.95), calls=%async_computation.13 | async-start | bytes 5242880 | tf_op jit(solution)/shard_map/all_to_all | solution.py:32
  436.2 70.1 %collective-permute-start.2 = (bf16[4,1280,128]{2,1,0:T(8,128)(2,1)}, bf16[4,1280,128]{2,1,0:T(8,128)(2,1)}, u32[]{:S(2)}, u32[]{:S(2)}) collective-permute-start(bf16[4,1280,128]{2,1,0:T(8,128)(2,1)} %get-tuple-element.99), channel_id=1, source_target_pairs={{0,2},{1,3},{2,0},{3,1},{4,6},{5,7},{6,4},{7,5},{8,10},{9,11},{10,... | collective-permute-start | bytes 3932168 | tf_op jit(solution)/shard_map/ppermute | solution.py:487
  509.2 10.1 %collective-permute-start.3 = (bf16[1280,128]{1,0:T(8,128)(2,1)}, bf16[1280,128]{1,0:T(8,128)(2,1)S(1)}, u32[]{:S(2)}, u32[]{:S(2)}) collective-permute-start(bf16[1280,128]{1,0:T(8,128)(2,1)} %get-tuple-element.101), channel_id=1, source_target_pairs={{0,4},{1,5},{2,6},{3,7},{4,8},{5,9},{6,10},{7,11},{8,12},{9,13},{1... | collective-permute-start | bytes 983048 | tf_op jit(solution)/shard_map/ppermute | solution.py:492
  509.2 17.8 %collective-permute-start.4 = (bf16[1280,128]{1,0:T(8,128)(2,1)}, bf16[1280,128]{1,0:T(8,128)(2,1)S(1)}, u32[]{:S(2)}, u32[]{:S(2)}) collective-permute-start(bf16[1280,128]{1,0:T(8,128)(2,1)} %get-tuple-element.102), channel_id=1, source_target_pairs={{0,8},{1,9},{2,10},{3,11},{4,12},{5,13},{6,14},{7,15},{8,0},{9,1},... | collective-permute-start | bytes 983048 | tf_op jit(solution)/shard_map/ppermute | solution.py:492
  512.6 14.4 %collective-permute-start.5 = (bf16[1280,128]{1,0:T(8,128)(2,1)}, bf16[1280,128]{1,0:T(8,128)(2,1)}, u32[]{:S(2)}, u32[]{:S(2)}) collective-permute-start(bf16[1280,128]{1,0:T(8,128)(2,1)} %get-tuple-element.103), channel_id=1, source_target_pairs={{0,12},{1,13},{2,14},{3,15},{4,0},{5,1},{6,2},{7,3},{8,4},{9,5},{1... | collective-permute-start | bytes 983048 | tf_op jit(solution)/shard_map/ppermute | solution.py:492
  512.7 1.5 copy-start.3
  519.3 7.8 %copy-start.29 = (bf16[1280,128]{1,0:T(8,128)(2,1)}, bf16[1280,128]{1,0:T(8,128)(2,1)S(1)}, u32[]{:S(2)}) copy-start(bf16[1280,128]{1,0:T(8,128)(2,1)S(1)} %collective-permute-done.3.refs_1_) | copy-start | bytes 983044
  533.4 26.4 %all-to-all-start.14 = ((bf16[8,160,128]{2,1,0:T(8,128)(2,1)}), bf16[8,160,128]{2,1,0:T(8,128)(2,1)S(1)}, u32[]{:S(2)}, u32[]{:S(2)}) async-start(bf16[8,160,128]{2,1,0:T(8,128)(2,1)} %pad_maximum_fusion.3), calls=%async_computation.15 | async-start | bytes 655360 | tf_op jit(solution)/shard_map/all_to_all | solution.py:32
  540.8 7.9 %collective-permute-start.7 = (bf16[160,512]{1,0:T(8,128)(2,1)S(1)}, bf16[160,512]{1,0:T(8,128)(2,1)S(1)}, u32[]{:S(2)}, u32[]{:S(2)}) collective-permute-start(bf16[160,512]{1,0:T(8,128)(2,1)S(1)} %get-tuple-element.125), channel_id=1, source_target_pairs={{0,64},{1,0},{2,65},{3,1},{4,80},{5,16},{6,81},{7,17},{8,96},{9,32... | collective-permute-start | bytes 491528 | tf_op jit(solution)/shard_map/ppermute | solution.py:507
  542.4 17.3 %collective-permute-start.6 = (bf16[160,512]{1,0:T(8,128)(2,1)S(1)}, bf16[160,512]{1,0:T(8,128)(2,1)S(1)}, u32[]{:S(2)}, u32[]{:S(2)}) collective-permute-start(bf16[160,512]{1,0:T(8,128)(2,1)S(1)} %get-tuple-element.126), channel_id=1, source_target_pairs={{0,0},{1,64},{2,1},{3,65},{4,16},{5,80},{6,17},{7,81},{8,32},{9,96... | collective-permute-start | bytes 491528 | tf_op jit(solution)/shard_map/ppermute | solution.py:507
  548.7 11.0 %copy-start.32 = (bf16[160,512]{1,0:T(8,128)(2,1)}, bf16[160,512]{1,0:T(8,128)(2,1)S(1)}, u32[]{:S(2)}) copy-start(bf16[160,512]{1,0:T(8,128)(2,1)S(1)} %collective-permute-done.7.refs_2_) | copy-start | bytes 491524
  559.7 27.9 %copy-start.1 = (bf16[256,5120]{1,0:T(8,128)(2,1)S(1)}, bf16[256,5120]{1,0:T(8,128)(2,1)}, u32[]{:S(2)}) copy-start(bf16[256,5120]{1,0:T(8,128)(2,1)} %param.9) | copy-start | bytes 7864324
  565.8 20.9 %all-to-all-start.15 = ((bf16[16,2,32,320]{3,2,1,0:T(8,128)(2,1)}), bf16[16,2,32,320]{3,2,1,0:T(8,128)(2,1)S(1)}, u32[]{:S(2)}, u32[]{:S(2)}) async-start(bf16[16,2,32,320]{3,2,1,0:T(8,128)(2,1)} %get-tuple-element.120), calls=%async_computation.16 | async-start | bytes 1572864 | tf_op jit(solution)/shard_map/all_to_all | solution.py:32
  574.0 1.7 copy-start.4
  (12 other events, 9.0 us)
Sparse Core Ops, SparseCore 0:
  10.3 62.9 all-gather.7
  75.6 46.5 all-gather.5
  134.8 38.6 all-gather.9
  175.6 49.1 all-gather.11
  227.0 75.7 all-gather.13
  363.6 125.6 reduce-scatter.1

commit v13 on v11

--- a/solution.py
+++ b/solution.py
@@ -485,7 +485,8 @@
 
 def between_chips(blocks, n_dp):
     arrived = [blocks[0]]
-    for (dx, dz), block in list(zip(chip_steps(n_dp), blocks))[1:]:
+    steps = list(zip(chip_steps(n_dp), blocks))[1:]
+    for (dx, dz), block in sorted(steps, key=lambda step: (-step[0][1], step[0][0] % 2)):
         pairs = []
         for j in range(n_dp):
             x, z, core = j // 4, j // 2 % 2, j % 2

time: 585 us -> 586 us (level)
  transfers between devices with their start and end apart: 26 -> 26, of which waited for: 16 -> 15; matrix products, arithmetic and copies ran while one was open for 9% -> 9% of each run, Pallas kernels for 6% -> 6%
where the time goes in v13:
time: 586 us; the launch traced here: 583 us
  waiting for transfers between devices  196 us (33%)
  blocking collectives  168 us (29%)
  starting transfers between devices  73.7 us (13%)
  Pallas kernels  59.2 us (10%)
  matrix products  35.7 us (6%)
  local copies, waits for them, and re-layouts  24.7 us (4%)
  between operations  14.7 us (3%)
  other arithmetic  11.3 us (2%)
    all_to_all x7, blocking collectives, swap(): return lax.all_to_all(x, axis, 0, 0, tiled=True)  168 us
    all_to_all x9, waiting for transfers between devices, swap(): return lax.all_to_all(x, axis, 0, 0, tiled=True)  83.9 us
    ppermute x7, waiting for transfers between devices, between_chips(): arrived.append(lax.ppermute(block, 'dp', pairs))  66.2 us
    pallas_call x13, Pallas kernels, run(): pl.pallas_call(kernel, out_shape=[jax.ShapeDtypeStruct(shape, kind) for s...  56.1 us
    all_to_all x9, starting transfers between devices, swap(): return lax.all_to_all(x, axis, 0, 0, tiled=True)  53.3 us
    dot_general x23, matrix products, dot(): lax.dot_general(left, right, (dims, ((), ())), preferred_element_type=jnp...  35.7 us
    all_gather x1, waiting for transfers between devices, on_device(): all_in = lax.all_gather(piece_in, 'dp', axis=0, tiled=True)  19.1 us
    unnamed x75, local copies, waits for them, and re-layouts  17.4 us
  transfers between devices with their start and end apart: 26, of which 15 were waited for; matrix products, arithmetic and copies ran while one was open for 9% of the time, Pallas kernels for 6%

profile of v13, /device:TPU:1, one launch (start us, length us, event | category | flops | bytes accessed | tf_op | source)
XLA Modules:
  0.0 583.3 jit_solution(16732402398876899197)
XLA Ops:
  11.2 37.5 %all_to_all.125 = bf16[8,32,640]{2,1,0:T(8,128)(2,1)S(1)} all-to-all(bf16[8,32,640]{2,1,0:T(8,128)(2,1)S(1)} %copy.30), channel_id=1, replica_groups=mesh['pipe'=8,'dp'=16] {'pipe'}, dimensions={0} | all-to-all | bytes 655360 | tf_op jit(solution)/shard_map/all_to_all | solution.py:32
  54.2 19.1 %all-gather.8.cloned.1.call-done.in_ref.refs_5_ = bf16[5120,512]{1,0:T(8,128)(2,1)} async-done(((bf16[320,512]{1,0:T(8,128)(2,1)}), bf16[5120,512]{1,0:T(8,128)(2,1)}) %all-gather.8.cloned.1.call-update) | async-done | bytes 5242896 | tf_op jit(solution)/shard_map/all_gather | solution.py:537
  82.2 6.4 %all-to-all-start.1 = ((bf16[8,48,512]{2,1,0:T(8,128)(2,1)}), bf16[8,48,512]{2,1,0:T(8,128)(2,1)}, u32[]{:S(2)}, u32[]{:S(2)}) async-start(bf16[8,48,512]{2,1,0:T(8,128)(2,1)} %bitcast.128), calls=%async_computation.1 | async-start | bytes 786432 | tf_op jit(solution)/shard_map/all_to_all | solution.py:32
  88.6 2.2 convolution_convert_fusion.2
  90.7 2.2 convolution_convert_fusion.1
  92.9 5.2 all-to-all-done.1
  99.9 4.2 all-to-all-start.2
  104.1 2.2 convolution_convert_fusion
  106.3 2.2 convolution_convert_fusion.3
  108.4 3.1 concatenate.39
  113.2 5.1 all-to-all-start.3
  119.8 2.4 all-gather.6.cloned.1.call-done.out_ref.refs_6_
  122.2 12.5 %all-to-all-done.3.down_ref = bf16[8,32,2176]{2,1,0:T(8,128)(2,1)} async-done(((bf16[8,32,2176]{2,1,0:T(8,128)(2,1)}), bf16[8,32,2176]{2,1,0:T(8,128)(2,1)}, u32[]{:S(2)}, u32[]{:S(2)}) %all-to-all-start.3) | async-done | bytes 1114144 | tf_op jit(solution)/shard_map/all_to_all | solution.py:32
  143.3 12.2 %all_to_all.126 = bf16[8,48,512]{2,1,0:T(8,128)(2,1)S(1)} all-to-all(bf16[8,48,512]{2,1,0:T(8,128)(2,1)S(1)} %bitcast.127), channel_id=1, replica_groups=mesh['pipe'=8,'dp'=16] {'pipe'}, dimensions={0} | all-to-all | bytes 786432 | tf_op jit(solution)/shard_map/all_to_all | solution.py:32
  155.6 12.9 %all_to_all.127 = bf16[8,48,512]{2,1,0:T(8,128)(2,1)S(1)} all-to-all(bf16[8,48,512]{2,1,0:T(8,128)(2,1)S(1)} %tile.5), channel_id=1, replica_groups=mesh['pipe'=8,'dp'=16] {'pipe'}, dimensions={0} | all-to-all | bytes 786432 | tf_op jit(solution)/shard_map/all_to_all | solution.py:32
  177.0 4.9 all-to-all-start.6
  186.4 8.1 %all-to-all-done.6.up_ref = bf16[8,32,1536]{2,1,0:T(8,128)(2,1)S(1)} async-done(((bf16[8,32,1536]{2,1,0:T(8,128)(2,1)}), bf16[8,32,1536]{2,1,0:T(8,128)(2,1)S(1)}, u32[]{:S(2)}, u32[]{:S(2)}) %all-to-all-start.6) | async-done | bytes 786464 | tf_op jit(solution)/shard_map/all_to_all | solution.py:32
  195.6 6.0 %all-to-all-start.7 = ((bf16[8,32,2048]{2,1,0:T(8,128)(2,1)}), bf16[8,32,2048]{2,1,0:T(8,128)(2,1)S(1)}, u32[]{:S(2)}, u32[]{:S(2)}) async-start(bf16[8,32,2048]{2,1,0:T(8,128)(2,1)} %bitcast.115), calls=%async_computation.7 | async-start | bytes 2097152 | tf_op jit(solution)/shard_map/all_to_all | solution.py:32
  202.4 17.0 %all-to-all-done.7.grad_ref = bf16[8,32,2048]{2,1,0:T(8,128)(2,1)S(1)} async-done(((bf16[8,32,2048]{2,1,0:T(8,128)(2,1)}), bf16[8,32,2048]{2,1,0:T(8,128)(2,1)S(1)}, u32[]{:S(2)}, u32[]{:S(2)}) %all-to-all-start.7) | async-done | bytes 1048608 | tf_op jit(solution)/shard_map/all_to_all | solution.py:32
  219.4 4.9 all-gather.12.cloned.1.call-done.gram_out_ref
  224.4 5.1 shard_map.153
  230.3 25.1 %all_to_all.128 = bf16[8,32,2048]{2,1,0:T(8,128)(2,1)S(1)} all-to-all(bf16[8,32,2048]{2,1,0:T(8,128)(2,1)S(1)} %bitcast.113), channel_id=1, replica_groups=mesh['pipe'=8,'dp'=16] {'pipe'}, dimensions={0} | all-to-all | bytes 2097152 | tf_op jit(solution)/shard_map/all_to_all | solution.py:32
  255.4 6.2 %shard_map.154 = (f32[256,640]{1,0:T(8,128)S(1)}, bf16[256,3712]{1,0:T(8,128)(2,1)S(1)}) custom-call(bf16[256,640]{1,0:T(8,128)(2,1)S(1)} %get-tuple-element.136.rows_ref.refs_1_, bf16[256,2048]{1,0:T(8,128)(2,1)S(1)} %bitcast.104, bf16[5120,512]{1,0:T(8,128)(2,1)} %all-gather.8.cloned.1.call-done.in_ref.refs_5_, ...), custom_call_target="tpu_custom_call" | custom-call | tf_op jit(solution)/shard_map/pallas_call | solution.py:72
  262.5 33.5 %all_to_all.129.sums_ref = bf16[8,32,3712]{2,1,0:T(8,128)(2,1)S(1)} all-to-all(bf16[8,32,3712]{2,1,0:T(8,128)(2,1)S(1)} %bitcast.109), channel_id=1, replica_groups=mesh['pipe'=8,'dp'=16] {'pipe'}, dimensions={0} | all-to-all | bytes 3801088 | tf_op jit(solution)/shard_map/all_to_all | solution.py:32
  295.9 6.9 %all-gather.14.cloned.1.call-done.gram_ref = bf16[512,6144]{1,0:T(8,128)(2,1)} async-done(((bf16[32,6144]{1,0:T(8,128)(2,1)}), bf16[512,6144]{1,0:T(8,128)(2,1)}) %all-gather.14.cloned.1.call-update) | async-done | bytes 6291472 | tf_op jit(solution)/shard_map/all_gather | solution.py:565
  302.8 6.0 %shard_map.155 = bf16[256,4224]{1,0:T(8,128)(2,1)S(1)} custom-call(bf16[8,32,3712]{2,1,0:T(8,128)(2,1)S(1)} %all_to_all.129.sums_ref, bf16[8,32,2048]{2,1,0:T(8,128)(2,1)S(1)} %all-to-all-done.7.grad_ref, bf16[512,6144]{1,0:T(8,128)(2,1)} %all-gather.14.cloned.1.call-done.gram_ref), custom_call_target="tpu_custom_call" | custom-call | tf_op jit(solution)/shard_map/pallas_call | solution.py:72
  310.2 6.9 %all-to-all-start.10 = ((bf16[8,32,4224]{2,1,0:T(8,128)(2,1)}), bf16[8,32,4224]{2,1,0:T(8,128)(2,1)S(1)}, u32[]{:S(2)}, u32[]{:S(2)}) async-start(bf16[8,32,4224]{2,1,0:T(8,128)(2,1)} %bitcast.106), calls=%async_computation.10 | async-start | bytes 4325376 | tf_op jit(solution)/shard_map/all_to_all | solution.py:32
  317.3 31.7 %all-to-all-done.10 = bf16[8,32,4224]{2,1,0:T(8,128)(2,1)S(1)} async-done(((bf16[8,32,4224]{2,1,0:T(8,128)(2,1)}), bf16[8,32,4224]{2,1,0:T(8,128)(2,1)S(1)}, u32[]{:S(2)}, u32[]{:S(2)}) %all-to-all-start.10) | async-done | bytes 2162720 | tf_op jit(solution)/shard_map/all_to_all | solution.py:32
  351.0 9.6 %shard_map.156 = (bf16[4,256,640]{2,1,0:T(8,128)(2,1)S(1)}, f32[256,640]{1,0:T(8,128)S(1)}, bf16[16,1280,128]{2,1,0:T(8,128)(2,1)}, bf16[256,2048]{1,0:T(8,128)(2,1)S(1)}) custom-call(s32[9]{0:T(128)S(1)} %pad_add_fusion.refs_0_, f32[256,640]{1,0:T(8,128)S(1)} %copy-done.14, bf16[256,4224]{1,0:T(8,128)(2,1)S(1)} %bitcast.102, ...), custom_call_target="tpu_custom_call" | custom-call | tf_op jit(solution)/shard_map/pallas_call | solution.py:72
  363.5 20.9 %all_to_all.130.grad_ref = bf16[8,32,2048]{2,1,0:T(8,128)(2,1)S(1)} all-to-all(bf16[8,32,2048]{2,1,0:T(8,128)(2,1)} %bitcast.112), channel_id=1, replica_groups=mesh['pipe'=8,'dp'=16] {'pipe'}, dimensions={0} | all-to-all | bytes 2097152 | tf_op jit(solution)/shard_map/all_to_all | solution.py:32
  387.7 25.9 %all_to_all.131 = bf16[8,32,2176]{2,1,0:T(8,128)(2,1)S(1)} all-to-all(bf16[8,32,2176]{2,1,0:T(8,128)(2,1)S(1)} %bitcast.108), channel_id=1, replica_groups=mesh['pipe'=8,'dp'=16] {'pipe'}, dimensions={0} | all-to-all | bytes 2228224 | tf_op jit(solution)/shard_map/all_to_all | solution.py:32
  413.6 12.2 %shard_map.158 = (bf16[8,256,640]{2,1,0:T(8,128)(2,1)}, f32[256,640]{1,0:T(8,128)}, bf16[8,1280,128]{2,1,0:T(8,128)(2,1)}, bf16[8,1280,128]{2,1,0:T(8,128)(2,1)}) custom-call(s32[9]{0:T(128)S(1)} %pad_add_fusion.refs_0_, bf16[256,640]{1,0:T(8,128)(2,1)S(1)} %get-tuple-element.136.rows_ref.refs_1_, bf16[256,2176]{1,0:T(8,128)(2,1)S(1)} %bitcast.107, ...), custom_call_target="tpu_custom_call" | custom-call | tf_op jit(solution)/shard_map/pallas_call | solution.py:72
  427.0 3.7 all-to-all-start.13
  432.1 4.1 shard_map.159
  436.5 3.7 collective-permute-start.3
  440.6 3.2 collective-permute-start.5
  443.8 60.3 %collective-permute-done.2.refs_1_ = bf16[1280,128]{1,0:T(8,128)(2,1)S(1)} collective-permute-done((bf16[1280,128]{1,0:T(8,128)(2,1)}, bf16[1280,128]{1,0:T(8,128)(2,1)S(1)}, u32[]{:S(2)}, u32[]{:S(2)}) %collective-permute-start.2) | collective-permute-done | bytes 327712 | tf_op jit(solution)/shard_map/ppermute | solution.py:494
  504.2 2.7 collective-permute-start.8
  508.3 5.9 %collective-permute-done.7.refs_6_ = bf16[1280,128]{1,0:T(8,128)(2,1)} collective-permute-done((bf16[1280,128]{1,0:T(8,128)(2,1)}, bf16[1280,128]{1,0:T(8,128)(2,1)}, u32[]{:S(2)}, u32[]{:S(2)}) %collective-permute-start.7) | collective-permute-done | bytes 327712 | tf_op jit(solution)/shard_map/ppermute | solution.py:494
  514.2 2.7 shard_map.162
  516.9 1.7 shard_map.161
  520.4 7.9 %all-to-all-start.14 = ((bf16[8,160,128]{2,1,0:T(8,128)(2,1)}), bf16[8,160,128]{2,1,0:T(8,128)(2,1)S(1)}, u32[]{:S(2)}, u32[]{:S(2)}) async-start(bf16[8,160,128]{2,1,0:T(8,128)(2,1)} %pad_maximum_fusion.3), calls=%async_computation.15 | async-start | bytes 655360 | tf_op jit(solution)/shard_map/all_to_all | solution.py:32
  531.0 6.5 %collective-permute-start.9 = (bf16[160,512]{1,0:T(8,128)(2,1)S(1)}, bf16[160,512]{1,0:T(8,128)(2,1)S(1)}, u32[]{:S(2)}, u32[]{:S(2)}) collective-permute-start(bf16[160,512]{1,0:T(8,128)(2,1)S(1)} %get-tuple-element.138), channel_id=1, source_target_pairs={{0,0},{1,64},{2,1},{3,65},{4,16},{5,80},{6,17},{7,81},{8,32},{9,96... | collective-permute-start | bytes 491528 | tf_op jit(solution)/shard_map/ppermute | solution.py:509
  537.5 11.1 %collective-permute-done.9.refs_1_ = bf16[160,512]{1,0:T(8,128)(2,1)S(1)} collective-permute-done((bf16[160,512]{1,0:T(8,128)(2,1)S(1)}, bf16[160,512]{1,0:T(8,128)(2,1)S(1)}, u32[]{:S(2)}, u32[]{:S(2)}) %collective-permute-start.9) | collective-permute-done | bytes 163872 | tf_op jit(solution)/shard_map/ppermute | solution.py:509
  549.3 5.3 shard_map.163
  554.6 8.2 %all-to-all-start.15 = ((bf16[16,2,32,320]{3,2,1,0:T(8,128)(2,1)}), bf16[16,2,32,320]{3,2,1,0:T(8,128)(2,1)S(1)}, u32[]{:S(2)}, u32[]{:S(2)}) async-start(bf16[16,2,32,320]{3,2,1,0:T(8,128)(2,1)} %get-tuple-element.132), calls=%async_computation.16 | async-start | bytes 1572864 | tf_op jit(solution)/shard_map/all_to_all | solution.py:32
  564.5 3.1 shard_map.160
  567.6 7.8 %all-to-all-done.15.pieces_ref = bf16[16,2,32,320]{3,2,1,0:T(8,128)(2,1)S(1)} async-done(((bf16[16,2,32,320]{3,2,1,0:T(8,128)(2,1)}), bf16[16,2,32,320]{3,2,1,0:T(8,128)(2,1)S(1)}, u32[]{:S(2)}, u32[]{:S(2)}) %all-to-all-start.15) | async-done | bytes 655392 | tf_op jit(solution)/shard_map/all_to_all | solution.py:32
  (156 shorter events, 70.4 us)
Async XLA Ops:
  7.2 162.7 %copy-start = (bf16[256,5120]{1,0:T(8,128)(2,1)S(1)}, bf16[256,5120]{1,0:T(8,128)(2,1)}, u32[]{:S(2)}) copy-start(bf16[256,5120]{1,0:T(8,128)(2,1)} %param.9) | copy-start | bytes 7864324
  7.2 66.1 %all-gather.8.cloned.1.call-start = ((), (), s32[]{:S(2)}) async-start(), calls=%async_computation.18 | async-start | bytes 5570560 | tf_op jit(solution)/shard_map/all_gather | solution.py:537
  8.5 0.7 collective-permute-start
  10.0 112.2 %all-gather.6.cloned.1.call-start = ((), (), s32[]{:S(2)}) async-start(), calls=%async_computation.17 | async-start | bytes 5570560 | tf_op jit(solution)/shard_map/all_gather | solution.py:538
  48.8 41.9 %copy-start.26 = (bf16[8,32,640]{2,1,0:T(8,128)(2,1)}, bf16[8,32,640]{2,1,0:T(8,128)(2,1)S(1)}, u32[]{:S(2)}) copy-start(bf16[8,32,640]{2,1,0:T(8,128)(2,1)S(1)} %all_to_all.125) | copy-start | bytes 983044
  54.2 45.7 %copy-start.34 = (bf16[3,32,640]{2,1,0:T(8,128)(2,1)}, bf16[3,32,640]{2,1,0:T(8,128)(2,1)S(1)}, u32[]{:S(2)}) copy-start(bf16[3,32,640]{2,1,0:T(8,128)(2,1)S(1)} %get-tuple-element.139) | copy-start | bytes 368644
  82.2 15.9 %all-to-all-start.1 = ((bf16[8,48,512]{2,1,0:T(8,128)(2,1)}), bf16[8,48,512]{2,1,0:T(8,128)(2,1)}, u32[]{:S(2)}, u32[]{:S(2)}) async-start(bf16[8,48,512]{2,1,0:T(8,128)(2,1)} %bitcast.128), calls=%async_computation.1 | async-start | bytes 786432 | tf_op jit(solution)/shard_map/all_to_all | solution.py:32
  99.9 13.3 %all-to-all-start.2 = ((bf16[8,48,512]{2,1,0:T(8,128)(2,1)}), bf16[8,48,512]{2,1,0:T(8,128)(2,1)S(1)}, u32[]{:S(2)}, u32[]{:S(2)}) async-start(bf16[8,48,512]{2,1,0:T(8,128)(2,1)} %tile.4), calls=%async_computation.2 | async-start | bytes 786432 | tf_op jit(solution)/shard_map/all_to_all | solution.py:32
  111.6 28.9 %copy-start.36 = (bf16[2,32,640]{2,1,0:T(8,128)(2,1)S(1)}, bf16[2,32,640]{2,1,0:T(8,128)(2,1)}, u32[]{:S(2)}) copy-start(bf16[2,32,640]{2,1,0:T(8,128)(2,1)} %get-tuple-element.141) | copy-start | bytes 245764
  111.6 30.3 %copy-start.35 = (bf16[3,32,640]{2,1,0:T(8,128)(2,1)S(1)}, bf16[3,32,640]{2,1,0:T(8,128)(2,1)}, u32[]{:S(2)}) copy-start(bf16[3,32,640]{2,1,0:T(8,128)(2,1)} %copy-done.34) | copy-start | bytes 368644
  113.2 21.5 %all-to-all-start.3 = ((bf16[8,32,2176]{2,1,0:T(8,128)(2,1)}), bf16[8,32,2176]{2,1,0:T(8,128)(2,1)}, u32[]{:S(2)}, u32[]{:S(2)}) async-start(bf16[8,32,2176]{2,1,0:T(8,128)(2,1)} %concatenate.39), calls=%async_computation.3 | async-start | bytes 2228224 | tf_op jit(solution)/shard_map/all_to_all | solution.py:32
  118.4 101.0 %all-gather.10.cloned.1.call-start = ((), (), s32[]{:S(2)}) async-start(), calls=%async_computation.19 | async-start | bytes 3342336 | tf_op jit(solution)/shard_map/all_gather | solution.py:565
  134.7 89.6 %all-gather.12.cloned.1.call-start = ((), (), s32[]{:S(2)}) async-start(), calls=%async_computation.20 | async-start | bytes 3342336 | tf_op jit(solution)/shard_map/all_gather | solution.py:565
  170.0 14.9 %copy-start.10 = (bf16[256,640]{1,0:T(8,128)(2,1)}, bf16[256,640]{1,0:T(8,128)(2,1)S(1)}, u32[]{:S(2)}) copy-start(bf16[256,640]{1,0:T(8,128)(2,1)S(1)} %constant_dynamic-slice_fusion.refs_4_) | copy-start | bytes 983044
  177.0 24.6 %copy-start.23 = (bf16[32,3072]{1,0:T(8,128)(2,1)S(1)}, bf16[32,3072]{1,0:T(8,128)(2,1)}, u32[]{:S(2)}) copy-start(bf16[32,3072]{1,0:T(8,128)(2,1)} %copy-done.22) | copy-start | bytes 589828
  177.0 24.7 %copy-start.25 = (bf16[32,3072]{1,0:T(8,128)(2,1)S(1)}, bf16[32,3072]{1,0:T(8,128)(2,1)}, u32[]{:S(2)}) copy-start(bf16[32,3072]{1,0:T(8,128)(2,1)} %copy-done.24) | copy-start | bytes 589828
  177.0 17.5 %all-to-all-start.6 = ((bf16[8,32,1536]{2,1,0:T(8,128)(2,1)}), bf16[8,32,1536]{2,1,0:T(8,128)(2,1)S(1)}, u32[]{:S(2)}, u32[]{:S(2)}) async-start(bf16[8,32,1536]{2,1,0:T(8,128)(2,1)} %bitcast.24), calls=%async_computation.6 | async-start | bytes 1572864 | tf_op jit(solution)/shard_map/all_to_all | solution.py:32
  195.6 23.8 %all-to-all-start.7 = ((bf16[8,32,2048]{2,1,0:T(8,128)(2,1)}), bf16[8,32,2048]{2,1,0:T(8,128)(2,1)S(1)}, u32[]{:S(2)}, u32[]{:S(2)}) async-start(bf16[8,32,2048]{2,1,0:T(8,128)(2,1)} %bitcast.115), calls=%async_computation.7 | async-start | bytes 2097152 | tf_op jit(solution)/shard_map/all_to_all | solution.py:32
  201.6 101.2 %all-gather.14.cloned.1.call-start = ((), (), s32[]{:S(2)}) async-start(), calls=%async_computation.21 | async-start | bytes 6684672 | tf_op jit(solution)/shard_map/all_gather | solution.py:565
  230.3 25.1 %copy-start.19 = (f32[4,32,512]{2,1,0:T(8,128)}, f32[4,32,512]{2,1,0:T(8,128)S(1)}, u32[]{:S(2)}) copy-start(f32[4,32,512]{2,1,0:T(8,128)S(1)} %get-tuple-element.96.hidden_ref) | copy-start | bytes 786436
  255.4 6.2 %copy-start.5 = (bf16[8,32,2048]{2,1,0:T(8,128)(2,1)}, bf16[8,32,2048]{2,1,0:T(8,128)(2,1)S(1)}, u32[]{:S(2)}) copy-start(bf16[8,32,2048]{2,1,0:T(8,128)(2,1)S(1)} %all_to_all.128) | copy-start | bytes 3145732
  308.8 1.3 copy-start.7
  310.2 38.8 %all-to-all-start.10 = ((bf16[8,32,4224]{2,1,0:T(8,128)(2,1)}), bf16[8,32,4224]{2,1,0:T(8,128)(2,1)S(1)}, u32[]{:S(2)}, u32[]{:S(2)}) async-start(bf16[8,32,4224]{2,1,0:T(8,128)(2,1)} %bitcast.106), calls=%async_computation.10 | async-start | bytes 4325376 | tf_op jit(solution)/shard_map/all_to_all | solution.py:32
  317.1 199.8 %reduce-scatter.2.cloned.1.call-start = ((), (), s32[]{:S(2)}) async-start(), calls=%async_computation.22 | async-start | bytes 5570560 | tf_op jit(solution)/shard_map/reduce_scatter | solution.py:666
  349.9 1.1 copy-start.14
  363.4 20.9 %copy-start.2 = (bf16[512,3072]{1,0:T(8,128)(2,1)S(1)}, bf16[512,3072]{1,0:T(8,128)(2,1)}, u32[]{:S(2)}) copy-start(bf16[512,3072]{1,0:T(8,128)(2,1)} %all-gather.10.cloned.1.call-done.gram_in_ref.gram_ref) | copy-start | bytes 9437188
  363.5 50.1 %copy-start.6 = (bf16[8,32,2048]{2,1,0:T(8,128)(2,1)S(1)}, bf16[8,32,2048]{2,1,0:T(8,128)(2,1)}, u32[]{:S(2)}) copy-start(bf16[8,32,2048]{2,1,0:T(8,128)(2,1)} %copy-done.5) | copy-start | bytes 3145732
  363.5 50.1 %copy-start.9 = (bf16[4,256,640]{2,1,0:T(8,128)(2,1)S(1)}, bf16[4,256,640]{2,1,0:T(8,128)(2,1)}, u32[]{:S(2)}) copy-start(bf16[4,256,640]{2,1,0:T(8,128)(2,1)} %copy-done.8) | copy-start | bytes 3932164
  363.5 50.1 %copy-start.16 = (f32[256,640]{1,0:T(8,128)S(1)}, f32[256,640]{1,0:T(8,128)}, u32[]{:S(2)}) copy-start(f32[256,640]{1,0:T(8,128)} %copy-done.15) | copy-start | bytes 1966084
  425.8 6.3 %collective-permute-start.1 = (bf16[8,1280,128]{2,1,0:T(8,128)(2,1)}, bf16[8,1280,128]{2,1,0:T(8,128)(2,1)}, u32[]{:S(2)}, u32[]{:S(2)}) collective-permute-start(bf16[8,1280,128]{2,1,0:T(8,128)(2,1)} %get-tuple-element.103), channel_id=1, source_target_pairs={{0,1},{1,0},{2,3},{3,2},{4,5},{5,4},{6,7},{7,6},{8,9},{9,8},{10,11... | collective-permute-start | bytes 7864328 | tf_op jit(solution)/shard_map/ppermute | solution.py:464
  427.0 79.9 %all-to-all-start.13 = ((bf16[8,256,640]{2,1,0:T(8,128)(2,1)}), bf16[8,256,640]{2,1,0:T(8,128)(2,1)S(1)}, u32[]{:S(2)}, u32[]{:S(2)}) async-start(bf16[8,256,640]{2,1,0:T(8,128)(2,1)} %get-tuple-element.101), calls=%async_computation.13 | async-start | bytes 5242880 | tf_op jit(solution)/shard_map/all_to_all | solution.py:32
  436.2 67.9 %collective-permute-start.2 = (bf16[1280,128]{1,0:T(8,128)(2,1)}, bf16[1280,128]{1,0:T(8,128)(2,1)S(1)}, u32[]{:S(2)}, u32[]{:S(2)}) collective-permute-start(bf16[1280,128]{1,0:T(8,128)(2,1)} %get-tuple-element.105), channel_id=1, source_target_pairs={{0,2},{1,3},{2,0},{3,1},{4,6},{5,7},{6,4},{7,5},{8,10},{9,11},{10,... | collective-permute-start | bytes 983048 | tf_op jit(solution)/shard_map/ppermute | solution.py:494
  436.5 67.6 %collective-permute-start.3 = (bf16[1280,128]{1,0:T(8,128)(2,1)}, bf16[1280,128]{1,0:T(8,128)(2,1)S(1)}, u32[]{:S(2)}, u32[]{:S(2)}) collective-permute-start(bf16[1280,128]{1,0:T(8,128)(2,1)} %get-tuple-element.106), channel_id=1, source_target_pairs={{0,10},{1,11},{2,8},{3,9},{4,14},{5,15},{6,12},{7,13},{8,2},{9,3},... | collective-permute-start | bytes 983048 | tf_op jit(solution)/shard_map/ppermute | solution.py:494
  440.2 68.1 %collective-permute-start.4 = (bf16[1280,128]{1,0:T(8,128)(2,1)}, bf16[1280,128]{1,0:T(8,128)(2,1)}, u32[]{:S(2)}, u32[]{:S(2)}) collective-permute-start(bf16[1280,128]{1,0:T(8,128)(2,1)} %get-tuple-element.107), channel_id=1, source_target_pairs={{0,6},{1,7},{2,4},{3,5},{4,10},{5,11},{6,8},{7,9},{8,14},{9,15},{1... | collective-permute-start | bytes 983048 | tf_op jit(solution)/shard_map/ppermute | solution.py:494
  440.6 67.7 %collective-permute-start.5 = (bf16[1280,128]{1,0:T(8,128)(2,1)}, bf16[1280,128]{1,0:T(8,128)(2,1)}, u32[]{:S(2)}, u32[]{:S(2)}) collective-permute-start(bf16[1280,128]{1,0:T(8,128)(2,1)} %get-tuple-element.108), channel_id=1, source_target_pairs={{0,14},{1,15},{2,12},{3,13},{4,2},{5,3},{6,0},{7,1},{8,6},{9,7},{1... | collective-permute-start | bytes 983048 | tf_op jit(solution)/shard_map/ppermute | solution.py:494
  443.8 64.5 %collective-permute-start.6 = (bf16[1280,128]{1,0:T(8,128)(2,1)}, bf16[1280,128]{1,0:T(8,128)(2,1)}, u32[]{:S(2)}, u32[]{:S(2)}) collective-permute-start(bf16[1280,128]{1,0:T(8,128)(2,1)} %get-tuple-element.109), channel_id=1, source_target_pairs={{0,8},{1,9},{2,10},{3,11},{4,12},{5,13},{6,14},{7,15},{8,0},{9,1},... | collective-permute-start | bytes 983048 | tf_op jit(solution)/shard_map/ppermute | solution.py:494
  504.1 10.1 %copy-start.29 = (bf16[1280,128]{1,0:T(8,128)(2,1)}, bf16[1280,128]{1,0:T(8,128)(2,1)S(1)}, u32[]{:S(2)}) copy-start(bf16[1280,128]{1,0:T(8,128)(2,1)S(1)} %collective-permute-done.2.refs_1_) | copy-start | bytes 983044
  504.1 10.1 %collective-permute-start.7 = (bf16[1280,128]{1,0:T(8,128)(2,1)}, bf16[1280,128]{1,0:T(8,128)(2,1)}, u32[]{:S(2)}, u32[]{:S(2)}) collective-permute-start(bf16[1280,128]{1,0:T(8,128)(2,1)} %get-tuple-element.110), channel_id=1, source_target_pairs={{0,4},{1,5},{2,6},{3,7},{4,8},{5,9},{6,10},{7,11},{8,12},{9,13},{1... | collective-permute-start | bytes 983048 | tf_op jit(solution)/shard_map/ppermute | solution.py:494
  504.1 10.1 %copy-start.30 = (bf16[1280,128]{1,0:T(8,128)(2,1)}, bf16[1280,128]{1,0:T(8,128)(2,1)S(1)}, u32[]{:S(2)}) copy-start(bf16[1280,128]{1,0:T(8,128)(2,1)S(1)} %collective-permute-done.3.refs_2_) | copy-start | bytes 983044
  504.2 10.1 %collective-permute-start.8 = (bf16[1280,128]{1,0:T(8,128)(2,1)}, bf16[1280,128]{1,0:T(8,128)(2,1)}, u32[]{:S(2)}, u32[]{:S(2)}) collective-permute-start(bf16[1280,128]{1,0:T(8,128)(2,1)} %get-tuple-element.111), channel_id=1, source_target_pairs={{0,12},{1,13},{2,14},{3,15},{4,0},{5,1},{6,2},{7,3},{8,4},{9,5},{1... | collective-permute-start | bytes 983048 | tf_op jit(solution)/shard_map/ppermute | solution.py:494
  506.8 1.5 copy-start.3
  520.4 28.1 %all-to-all-start.14 = ((bf16[8,160,128]{2,1,0:T(8,128)(2,1)}), bf16[8,160,128]{2,1,0:T(8,128)(2,1)S(1)}, u32[]{:S(2)}, u32[]{:S(2)}) async-start(bf16[8,160,128]{2,1,0:T(8,128)(2,1)} %pad_maximum_fusion.3), calls=%async_computation.15 | async-start | bytes 655360 | tf_op jit(solution)/shard_map/all_to_all | solution.py:32
  529.4 8.1 %collective-permute-start.10 = (bf16[160,512]{1,0:T(8,128)(2,1)S(1)}, bf16[160,512]{1,0:T(8,128)(2,1)S(1)}, u32[]{:S(2)}, u32[]{:S(2)}) collective-permute-start(bf16[160,512]{1,0:T(8,128)(2,1)S(1)} %get-tuple-element.137), channel_id=1, source_target_pairs={{0,64},{1,0},{2,65},{3,1},{4,80},{5,16},{6,81},{7,17},{8,96},{9,32... | collective-permute-start | bytes 491528 | tf_op jit(solution)/shard_map/ppermute | solution.py:509
  531.0 17.6 %collective-permute-start.9 = (bf16[160,512]{1,0:T(8,128)(2,1)S(1)}, bf16[160,512]{1,0:T(8,128)(2,1)S(1)}, u32[]{:S(2)}, u32[]{:S(2)}) collective-permute-start(bf16[160,512]{1,0:T(8,128)(2,1)S(1)} %get-tuple-element.138), channel_id=1, source_target_pairs={{0,0},{1,64},{2,1},{3,65},{4,16},{5,80},{6,17},{7,81},{8,32},{9,96... | collective-permute-start | bytes 491528 | tf_op jit(solution)/shard_map/ppermute | solution.py:509
  537.5 11.1 %copy-start.32 = (bf16[160,512]{1,0:T(8,128)(2,1)}, bf16[160,512]{1,0:T(8,128)(2,1)S(1)}, u32[]{:S(2)}) copy-start(bf16[160,512]{1,0:T(8,128)(2,1)S(1)} %collective-permute-done.10.refs_2_) | copy-start | bytes 491524
  548.6 27.9 %copy-start.1 = (bf16[256,5120]{1,0:T(8,128)(2,1)S(1)}, bf16[256,5120]{1,0:T(8,128)(2,1)}, u32[]{:S(2)}) copy-start(bf16[256,5120]{1,0:T(8,128)(2,1)} %param.9) | copy-start | bytes 7864324
  554.6 20.8 %all-to-all-start.15 = ((bf16[16,2,32,320]{3,2,1,0:T(8,128)(2,1)}), bf16[16,2,32,320]{3,2,1,0:T(8,128)(2,1)S(1)}, u32[]{:S(2)}, u32[]{:S(2)}) async-start(bf16[16,2,32,320]{3,2,1,0:T(8,128)(2,1)} %get-tuple-element.132), calls=%async_computation.16 | async-start | bytes 1572864 | tf_op jit(solution)/shard_map/all_to_all | solution.py:32
  562.8 1.7 copy-start.4
  (15 other events, 12.3 us)
Sparse Core Ops, SparseCore 0:
  10.3 62.9 all-gather.7
  75.6 46.5 all-gather.5
  134.8 38.6 all-gather.9
  175.6 48.6 all-gather.11
  226.5 76.2 all-gather.13
  363.6 143.0 reduce-scatter.1
